TPU v7x, 32 devices: a whole 2x2x4 slice. The times are simulated.
32 devices in a mesh: sel: 8 (over z, y), mdl: 4 (over x, core).
Axes of the slice: x: 2, y: 2, z: 4, core: 2. Of those that a mesh axis runs over, the one named last changes fastest.
Arguments:
- patches: bfloat16 [6144, 1408], P('sel', 'mdl'), may hold values from -6 to 6
- text: bfloat16 [1024, 1024], P('sel', 'mdl'), may hold values from -64 to 64
- ref_proj: bfloat16 [1408, 1024], P(None, 'mdl'), may hold values from -0.15625 to 0.15625
- w_up: bfloat16 [1408, 6144], P(None, 'mdl'), may hold values from -0.15625 to 0.15625
- w_down: bfloat16 [6144, 1408], P('mdl'), may hold values from -0.078125 to 0.078125
- kept_index: int32 [512], P('sel'), may hold values from 0 to 127, as said below
- dest: int32 [512], P('sel'), may hold values from 0 to 7, as said below
- cotan: bfloat16 [3072, 1408], P('sel', 'mdl'), may hold values from -6 to 6
Outputs:
- ref_loss: float32 [1024], P('sel')
- learnability: float32 [512], P('sel')
- grad_up: float32 [1408, 6144], P('sel', 'mdl')
Inputs may be any that keep to these rules, and one draw needn't show every extreme that they name: `kept_index`: the 64 entries of one scorer shard are distinct. `dest`: on each scorer shard at most 16 kept entries name the same learner shard; one learner shard is named by exactly 16 kept entries of every scorer shard.
All inputs are finite; a program needn't handle non-finite values.
Results may differ from a plain program's by a relative error of at most 0.019.
Values may be sent and summed in bfloat16 or wider, within the bound.
No kernel may reach another device: no remote copies, remote signals or barrier semaphores. Data moves between devices by JAX's collectives and lax.ppermute only.
A program may use at most 128 MiB of HBM per device.

v0:
```python
import jax
import jax.numpy as jnp
from jax import lax
from jax.sharding import PartitionSpec as P

logit_scale = 64.0
eps = 1e-06


def gelu_parts(pre_act):
    cumul = 0.5 * (1.0 + lax.erf(pre_act * 0.7071067811865476))
    density = jnp.exp(-0.5 * pre_act * pre_act) * 0.3989422804014327
    return (pre_act * cumul, cumul + pre_act * density)


def partial_scores(rows_hat, text_all):
    return lax.dot_general(
        rows_hat, text_all, (((1,), (1,)), ((), ())), preferred_element_type=jnp.float32
    )


def exp_total(rows_full, text_share):
    return jnp.sum(jnp.exp(logit_scale * partial_scores(rows_full, text_share)), axis=1)


def own_product(rows_part, texts_part):
    return jnp.sum(rows_part.astype(jnp.float32) * texts_part.astype(jnp.float32), axis=1)


def learn(kept_tok, kept_cot, row_weight, w_up, w_down, ref_proj):
    n_items, n_patch, d_part = kept_tok.shape
    n_rows = n_items * n_patch
    weighted = (kept_cot.astype(jnp.float32) * row_weight[:, None, None]).astype(jnp.bfloat16)
    tok_full, cot_full = (
        lax.all_gather(kept_tok.reshape(n_rows, d_part), "mdl", axis=1, tiled=True),
        lax.all_gather(weighted.reshape(n_rows, d_part), "mdl", axis=1, tiled=True),
    )
    pre_act = jnp.dot(tok_full, w_up, preferred_element_type=jnp.float32)
    activated, gelu_slope = gelu_parts(pre_act)
    hidden = activated.astype(jnp.bfloat16)
    mixed_part = jnp.dot(hidden, w_down, preferred_element_type=jnp.float32)
    summed = lax.psum_scatter(mixed_part, "mdl", scatter_dimension=1, tiled=True)
    outputs = summed + kept_tok.reshape(n_rows, d_part).astype(jnp.float32)
    pooled = jnp.mean(outputs.reshape(n_items, n_patch, d_part), axis=1).astype(jnp.bfloat16)
    pooled_full = lax.all_gather(pooled, "mdl", axis=1, tiled=True)
    learn_emb = jnp.dot(pooled_full, ref_proj, preferred_element_type=jnp.float32)
    learn_sq = lax.psum(jnp.sum(learn_emb * learn_emb, axis=1), "mdl")
    learn_hat = (learn_emb * lax.rsqrt(learn_sq + eps)[:, None]).astype(jnp.bfloat16)
    grad_act = lax.dot_general(
        cot_full, w_down, (((1,), (1,)), ((), ())), preferred_element_type=jnp.float32
    )
    grad_pre = (grad_act * gelu_slope).astype(jnp.bfloat16)
    grad_up = lax.psum_scatter(
        lax.dot_general(
            tok_full, grad_pre, (((0,), (0,)), ((), ())), preferred_element_type=jnp.float32
        ),
        "sel",
        scatter_dimension=0,
        tiled=True,
    )
    return (learn_hat, grad_up)


def per_device(patches, text, ref_proj, w_up, w_down, kept_index, dest, cotan):
    n_sel = lax.axis_size("sel")
    ex_dev = text.shape[0]
    d_part = patches.shape[1]
    n_patch = patches.shape[0] // ex_dev
    k_dev = kept_index.shape[0]
    blocks = patches.reshape(ex_dev, n_patch, d_part)
    pooled = jnp.mean(blocks, axis=1, dtype=jnp.float32).astype(jnp.bfloat16)
    pooled_full = lax.all_gather(pooled, "mdl", axis=1, tiled=True)
    img_emb = jnp.dot(pooled_full, ref_proj, preferred_element_type=jnp.float32)
    text_vals = text.astype(jnp.float32)
    img_sq, text_sq = lax.psum(
        (jnp.sum(img_emb * img_emb, axis=1), jnp.sum(text_vals * text_vals, axis=1)), "mdl"
    )
    img_hat = (img_emb * lax.rsqrt(img_sq + eps)[:, None]).astype(jnp.bfloat16)
    text_hat = (text_vals * lax.rsqrt(text_sq + eps)[:, None]).astype(jnp.bfloat16)
    text_rows = lax.all_to_all(text_hat, "mdl", split_axis=0, concat_axis=1, tiled=True)
    text_split = lax.all_gather(text_rows, "sel", axis=0, tiled=True)
    img_full = lax.all_gather(img_hat, "mdl", axis=1, tiled=True)
    ref_total, ref_own = lax.psum(
        (exp_total(img_full, text_split), own_product(img_hat, text_hat)), "mdl"
    )
    ref_loss = jnp.log(ref_total) - logit_scale * ref_own
    kept_tok = blocks[kept_index]
    kept_cot = cotan.reshape(k_dev, n_patch, d_part)
    onehot = (dest[:, None] == jnp.arange(n_sel, dtype=jnp.int32)[None, :]).astype(jnp.int32)
    capacity = 2 * k_dev // n_sel
    dest_rank = jnp.sum(jnp.cumsum(onehot, axis=0) * onehot, axis=1) - 1
    slot_idx = dest * capacity + dest_rank
    inverse = (
        jnp.full((n_sel * capacity,), k_dev, jnp.int32)
        .at[slot_idx]
        .set(jnp.arange(k_dev, dtype=jnp.int32))
    )
    live_flag = (inverse < k_dev).astype(jnp.int32)
    pad_tok = jnp.concatenate([kept_tok, jnp.zeros((1, n_patch, d_part), jnp.bfloat16)], axis=0)[
        inverse
    ]
    pad_cot = jnp.concatenate([kept_cot, jnp.zeros((1, n_patch, d_part), jnp.bfloat16)], axis=0)[
        inverse
    ]
    recv_tok, recv_cot, recv_live = (
        lax.all_to_all(pad_tok, "sel", split_axis=0, concat_axis=0, tiled=True),
        lax.all_to_all(pad_cot, "sel", split_axis=0, concat_axis=0, tiled=True),
        lax.all_to_all(live_flag, "sel", split_axis=0, concat_axis=0, tiled=True),
    )
    learn_count = jnp.maximum(jnp.sum(recv_live), 1).astype(jnp.float32)
    row_weight = recv_live.astype(jnp.float32) / learn_count
    slot_hat, grad_up = learn(recv_tok, recv_cot, row_weight, w_up, w_down, ref_proj)
    returned = lax.all_to_all(slot_hat, "sel", split_axis=0, concat_axis=0, tiled=True)
    kept_hat = returned[slot_idx]
    learn_full = lax.all_gather(kept_hat, "mdl", axis=1, tiled=True)
    learn_total, learn_own = lax.psum(
        (exp_total(learn_full, text_split), own_product(kept_hat, text_hat[kept_index])), "mdl"
    )
    learner_loss = jnp.log(learn_total) - logit_scale * learn_own
    learnability = learner_loss - ref_loss[kept_index]
    return (ref_loss, learnability, grad_up)


def solution(mesh):
    in_specs = (
        P("sel", "mdl"),
        P("sel", "mdl"),
        P(None, "mdl"),
        P(None, "mdl"),
        P("mdl", None),
        P("sel"),
        P("sel"),
        P("sel", "mdl"),
    )
    out_specs = (P("sel"), P("sel"), P("sel", "mdl"))
    return jax.shard_map(
        per_device, mesh=mesh, in_specs=in_specs, out_specs=out_specs, check_vma=False
    )
```

profile of v0, /device:TPU:0, one launch (start us, length us, event | category | flops | bytes accessed | tf_op | source)
XLA Modules:
  0.0 318.4 jit_solution(16540091895615864231)
XLA Ops:
  7.2 0.7 compare_select_fusion.2
  8.0 1.4 copy.34
  9.3 0.2 reshape.43
  9.5 0.7 fusion.13
  10.3 0.1 reduce_window_sum.11
  10.4 0.8 select_reduce_fusion
  11.2 0.7 compare_select_fusion.1
  11.9 0.8 scatter_custom_fusion
  12.7 0.7 gather_fusion
  13.3 0.1 concatenate.6
  13.4 0.7 gather_fusion.1
  14.2 27.2 %all_to_all.55 = bf16[128,6,352]{2,1,0:T(8,128)(2,1)S(1)} all-to-all(bf16[128,6,352]{2,1,0:T(8,128)(2,1)S(1)} %gather_fusion.1), channel_id=1, replica_groups=mesh['sel'=8,'mdl'=4] {'sel'}, dimensions={0} | all-to-all | bytes 1081344 | tf_op jit(solution)/shard_map/all_to_all | solution.py:106
  41.4 0.4 reshape.44
  41.8 1.1 copy.37
  42.9 0.7 reshape.48
  43.5 3.6 %all-to-all-start.4 = ((s32[8,16,1]{1,2,0:T(1,128)}), s32[8,16,1]{1,2,0:T(1,128)S(1)}, u32[]{:S(2)}, u32[]{:S(2)}) async-start(s32[8,16,1]{1,2,0:T(1,128)} %bitcast.4), calls=%async_computation.5 | async-start | bytes 8192 | tf_op jit(solution)/shard_map/all_to_all | solution.py:108
  47.1 1.2 copy.41
  48.3 0.1 reshape.46
  48.4 0.1 concatenate.7
  48.5 1.6 gather_fusion.5
  50.1 3.5 %all-to-all-done.4 = s32[8,16,1]{1,2,0:T(1,128)S(1)} async-done(((s32[8,16,1]{1,2,0:T(1,128)}), s32[8,16,1]{1,2,0:T(1,128)S(1)}, u32[]{:S(2)}, u32[]{:S(2)}) %all-to-all-start.4) | async-done | bytes 544 | tf_op jit(solution)/shard_map/all_to_all | solution.py:108
  53.6 3.5 %all-to-all-start.3 = ((bf16[128,6,352]{2,1,0:T(8,128)(2,1)}), bf16[128,6,352]{2,1,0:T(8,128)(2,1)S(1)}, u32[]{:S(2)}, u32[]{:S(2)}) async-start(bf16[128,6,352]{2,1,0:T(8,128)(2,1)} %gather_fusion.5), calls=%async_computation.4 | async-start | bytes 1572864 | tf_op jit(solution)/shard_map/all_to_all | solution.py:107
  57.2 0.6 reduce_sum.109
  58.6 17.2 %all-to-all-done.3 = bf16[128,6,352]{2,1,0:T(8,128)(2,1)S(1)} async-done(((bf16[128,6,352]{2,1,0:T(8,128)(2,1)}), bf16[128,6,352]{2,1,0:T(8,128)(2,1)S(1)}, u32[]{:S(2)}, u32[]{:S(2)}) %all-to-all-start.3) | async-done | bytes 540704 | tf_op jit(solution)/shard_map/all_to_all | solution.py:107
  75.8 0.2 multiply_convert_fusion.2
  76.0 0.4 reshape.47
  76.4 1.1 copy.43
  77.5 6.5 %fusion.17 = f32[768,1536]{1,0:T(8,128)S(1)} fusion(bf16[768,1408]{0,1:T(8,128)(2,1)} %all-gather.4.cloned.1.call-done, bf16[1408,1536]{1,0:T(8,128)(2,1)} %param.11), kind=kOutput, calls=%fused_computation.56 | convolution fusion | flops 3321888768 | bytes 11206656 | tf_op jit(solution)/shard_map/dot_general | solution.py:38
  84.0 2.2 copy-done.4
  86.2 9.2 %fusion.6 = f32[768,1408]{0,1:T(8,128)} fusion(bf16[1536,1408]{1,0:T(8,128)(2,1)} %param.12, f32[768,1536]{1,0:T(8,128)S(1)} %fusion.17), kind=kOutput, calls=%fused_computation.16 | convolution fusion | flops 3327787008 | bytes 13369344 | tf_op jit(solution)/shard_map/dot_general | solution.py:41
  95.4 0.2 reduce-scatter.5.cloned.1.call-start
  95.6 3.9 %all-gather.6.cloned.1.call-done = bf16[768,1408]{0,1:T(8,128)(2,1)} async-done(((bf16[768,352]{0,1:T(8,128)(2,1)}), bf16[768,1408]{0,1:T(8,128)(2,1)}) %all-gather.6.cloned.1.call-update) | async-done | bytes 2162704 | tf_op jit(solution)/shard_map/all_gather | solution.py:36
  99.5 13.4 %fusion.18 = f32[1408,1536]{1,0:T(8,128)} fusion(bf16[768,1408]{0,1:T(8,128)(2,1)} %all-gather.4.cloned.1.call-done, f32[768,1536]{1,0:T(8,128)} %copy-done.4, bf16[768,1408]{0,1:T(8,128)(2,1)} %all-gather.6.cloned.1.call-done, bf16[1536,1408]{1,0:T(8,128)(2,1)} %param.12), kind=kOutput, calls=%fused_computation.57 | convolution fusion | flops 6655574016 | bytes 22020096 | tf_op jit(solution)/shard_map/dot_general | solution.py:54
  112.9 0.5 convert_reduce_fusion
  113.5 0.1 copy.35
  113.6 0.1 copy-done.3
  113.8 0.1 fusion.11
  113.9 6.3 %all_gather.21 = bf16[128,1408]{0,1:T(8,128)(2,1)S(1)} all-gather(bf16[128,352]{0,1:T(8,128)(2,1)S(1)} %multiply_convert_fusion.4), channel_id=1, replica_groups=mesh['sel'=8,'mdl'=4] {'mdl'}, dimensions={1}, use_global_device_ids=true | all-gather | bytes 450560 | tf_op jit(solution)/shard_map/all_gather | solution.py:72
  120.2 1.0 multiply_reduce_fusion.2
  121.2 26.3 %reduce-scatter.3.cloned.1.call-done = f32[768,352]{0,1:T(8,128)} async-done(((f32[768,1408]{0,1:T(8,128)}), f32[768,352]{0,1:T(8,128)}) %reduce-scatter.3.cloned.1.call-update) | async-done | bytes 1081360 | tf_op jit(solution)/shard_map/reduce_scatter | solution.py:42
  147.4 2.4 convert_add_fusion
  149.8 1.6 copy.39
  151.4 0.2 reshape.45
  151.6 0.5 reduce_sum.105
  152.1 0.1 copy.40
  152.2 6.1 %all_gather.25 = bf16[128,1408]{0,1:T(8,128)(2,1)S(1)} all-gather(bf16[128,352]{0,1:T(8,128)(2,1)S(1)} %multiply_convert_fusion.3), channel_id=1, replica_groups=mesh['sel'=8,'mdl'=4] {'mdl'}, dimensions={1}, use_global_device_ids=true | all-gather | bytes 450560 | tf_op jit(solution)/shard_map/all_gather | solution.py:45
  158.3 0.4 multiply_reduce_fusion
  158.7 6.8 %all-reduce.3 = (f32[128]{0:T(128)S(1)}, f32[128]{0:T(128)S(1)}, f32[128]{0:T(128)S(1)}) all-reduce(f32[128]{0:T(128)S(1)} %fusion.11, f32[128]{0:T(128)S(1)} %get-tuple-element.13, f32[128]{0:T(128)S(1)} %get-tuple-element.15), channel_id=1, replica_groups=mesh['sel'=8,'mdl'=4] {'mdl'}, use_global_device_ids=true, to_apply=%region_4.0 | all-reduce | flops 384 | bytes 3072 | tf_op jit(solution)/shard_map/psum | solution.py:75
  165.4 1.6 multiply_reduce_fusion.1
  167.1 3.3 %all-to-all-start = ((bf16[4,32,256]{2,1,0:T(8,128)(2,1)}), bf16[4,32,256]{2,1,0:T(8,128)(2,1)S(1)}, u32[]{:S(2)}, u32[]{:S(2)}) async-start(bf16[4,32,256]{2,1,0:T(8,128)(2,1)} %bitcast), calls=%async_computation | async-start | bytes 131072 | tf_op jit(solution)/shard_map/all_to_all | solution.py:80
  170.4 0.7 multiply_convert_fusion.5
  171.1 6.2 %all_gather.22 = bf16[128,1024]{1,0:T(8,128)(2,1)S(1)} all-gather(bf16[128,256]{1,0:T(8,128)(2,1)S(1)} %get-tuple-element.11), channel_id=1, replica_groups=mesh['sel'=8,'mdl'=4] {'mdl'}, dimensions={1}, use_global_device_ids=true | all-gather | bytes 327680 | tf_op jit(solution)/shard_map/all_gather | solution.py:82
  177.3 1.5 gather_fusion.3
  178.8 5.5 %all-to-all-start.2 = ((bf16[8,16,256]{2,1,0:T(8,128)(2,1)}), bf16[8,16,256]{2,1,0:T(8,128)(2,1)S(1)}, u32[]{:S(2)}, u32[]{:S(2)}) async-start(bf16[8,16,256]{2,1,0:T(8,128)(2,1)} %bitcast.2), calls=%async_computation.3 | async-start | bytes 131072 | tf_op jit(solution)/shard_map/all_to_all | solution.py:113
  184.4 35.6 %all_gather.23 = bf16[256,1024]{1,0:T(8,128)(2,1)S(1)} all-gather(bf16[32,1024]{1,0:T(8,128)(2,1)S(1)} %bitcast.31), channel_id=1, replica_groups=mesh['sel'=8,'mdl'=4] {'sel'}, dimensions={0}, use_global_device_ids=true | all-gather | bytes 589824 | tf_op jit(solution)/shard_map/all_gather | solution.py:81
  219.9 0.4 fusion.8
  220.4 0.7 gather_fusion.2
  221.1 5.4 %all-gather = bf16[64,1024]{1,0:T(8,128)(2,1)S(1)} all-gather(bf16[64,256]{1,0:T(8,128)(2,1)S(1)} %gather_fusion.2), channel_id=2, replica_groups=mesh['sel'=8,'mdl'=4] {'mdl'}, dimensions={1}, use_global_device_ids=true | all-gather | bytes 163840 | tf_op jit(solution)/shard_map/all_gather | solution.py:115
  226.5 0.1 multiply_reduce_fusion.3
  226.6 0.4 fusion.10
  227.0 7.5 %all-reduce.2 = (f32[128]{0:T(128)S(1)}, f32[128]{0:T(128)S(1)}, f32[64]{0:T(128)S(1)}, f32[64]{0:T(128)S(1)}) all-reduce(f32[128]{0:T(128)S(1)} %get-tuple-element.10, f32[128]{0:T(128)S(1)} %fusion.8, f32[64]{0:T(128)S(1)} %multiply_reduce_fusion.3, f32[64]{0:T(128)S(1)} %fusion.10), channel_id=1, replica_groups=mesh['sel'=8,'mdl'=4] {'mdl'}, use_global_device_ids=true, to_apply=%region_8.0 | all-reduce | flops 384 | bytes 3072 | tf_op jit(solution)/shard_map/psum | solution.py:83
  234.5 0.8 gather_fusion.4
  235.3 0.5 subtract_subtract_fusion
  235.8 76.0 %reduce-scatter.5.cloned.1.call-done = f32[176,1536]{1,0:T(8,128)} async-done(((f32[1408,1536]{1,0:T(8,128)}), f32[176,1536]{1,0:T(8,128)}) %reduce-scatter.5.cloned.1.call-update) | async-done | bytes 1081360 | tf_op jit(solution)/shard_map/reduce_scatter | solution.py:53
  (32 shorter events, 0.4 us)
Async XLA Ops:
  7.2 113.0 %copy-start = (bf16[1408,256]{1,0:T(8,128)(2,1)S(1)}, bf16[1408,256]{1,0:T(8,128)(2,1)}, u32[]{:S(2)}) copy-start(bf16[1408,256]{1,0:T(8,128)(2,1)} %param.10) | copy-start | bytes 2162692
  7.2 70.3 %all-gather.4.cloned.1.call-start = ((), (), s32[]{:S(2)}) async-start(), calls=%async_computation.7 | async-start | bytes 2703360 | tf_op jit(solution)/shard_map/all_gather | solution.py:35
  43.5 10.1 %all-to-all-start.4 = ((s32[8,16,1]{1,2,0:T(1,128)}), s32[8,16,1]{1,2,0:T(1,128)S(1)}, u32[]{:S(2)}, u32[]{:S(2)}) async-start(s32[8,16,1]{1,2,0:T(1,128)} %bitcast.4), calls=%async_computation.5 | async-start | bytes 8192 | tf_op jit(solution)/shard_map/all_to_all | solution.py:108
  53.6 22.2 %all-to-all-start.3 = ((bf16[128,6,352]{2,1,0:T(8,128)(2,1)}), bf16[128,6,352]{2,1,0:T(8,128)(2,1)S(1)}, u32[]{:S(2)}, u32[]{:S(2)}) async-start(bf16[128,6,352]{2,1,0:T(8,128)(2,1)} %gather_fusion.5), calls=%async_computation.4 | async-start | bytes 1572864 | tf_op jit(solution)/shard_map/all_to_all | solution.py:107
  57.1 42.4 %all-gather.6.cloned.1.call-start = ((), (), s32[]{:S(2)}) async-start(), calls=%async_computation.9 | async-start | bytes 2703360 | tf_op jit(solution)/shard_map/all_gather | solution.py:36
  77.5 70.0 %reduce-scatter.3.cloned.1.call-start = ((), (), s32[]{:S(2)}) async-start(), calls=%async_computation.8 | async-start | bytes 5406720 | tf_op jit(solution)/shard_map/reduce_scatter | solution.py:42
  84.0 2.2 copy-start.4
  95.4 216.4 %reduce-scatter.5.cloned.1.call-start = ((), (), s32[]{:S(2)}) async-start(), calls=%async_computation.10 | async-start | bytes 9732096 | tf_op jit(solution)/shard_map/reduce_scatter | solution.py:53
  112.9 0.8 copy-start.3
  112.9 34.5 %copy-start.2 = (bf16[768,352]{0,1:T(8,128)(2,1)S(1)}, bf16[768,352]{0,1:T(8,128)(2,1)}, u32[]{:S(2)}) copy-start(bf16[768,352]{0,1:T(8,128)(2,1)} %copy.37) | copy-start | bytes 1622020
  167.1 11.7 %all-to-all-start = ((bf16[4,32,256]{2,1,0:T(8,128)(2,1)}), bf16[4,32,256]{2,1,0:T(8,128)(2,1)S(1)}, u32[]{:S(2)}, u32[]{:S(2)}) async-start(bf16[4,32,256]{2,1,0:T(8,128)(2,1)} %bitcast), calls=%async_computation | async-start | bytes 131072 | tf_op jit(solution)/shard_map/all_to_all | solution.py:80
  178.8 41.5 %all-to-all-start.2 = ((bf16[8,16,256]{2,1,0:T(8,128)(2,1)}), bf16[8,16,256]{2,1,0:T(8,128)(2,1)S(1)}, u32[]{:S(2)}, u32[]{:S(2)}) async-start(bf16[8,16,256]{2,1,0:T(8,128)(2,1)} %bitcast.2), calls=%async_computation.3 | async-start | bytes 131072 | tf_op jit(solution)/shard_map/all_to_all | solution.py:113
  234.5 77.3 %copy-start.1 = (f32[128]{0:T(128)}, f32[128]{0:T(128)S(1)}, u32[]{:S(2)}) copy-start(f32[128]{0:T(128)S(1)} %multiply_subtract_fusion) | copy-start | bytes 1540
Sparse Core Ops, SparseCore 0:
  43.0 21.9 all-gather.3
  77.6 21.8 all-gather.5
  102.1 45.3 reduce-scatter.2
  151.9 159.8 reduce-scatter.4
where the time goes:
time: 319 us; the launch traced here: 318 us
  waiting for transfers between devices  127 us (40%)
  blocking collectives  101 us (32%)
  matrix products  31.2 us (10%)
  local copies, waits for them, and re-layouts  17.6 us (6%)
  starting transfers between devices  16.3 us (5%)
  between operations  14.7 us (5%)
  other arithmetic  10.5 us (3%)
    reduce_scatter x1, waiting for transfers between devices, learn(): lax.psum_scatter(lax.dot_general(tok_full, grad_pre, (((0,), (0,)), ((),...  76 us
    all_gather x1, blocking collectives, per_device(): text_split = lax.all_gather(text_rows, 'sel', axis=0, tiled=True)  35.6 us
    all_to_all x1, blocking collectives, per_device(): lax.all_to_all(pad_tok, 'sel', split_axis=0, concat_axis=0, tiled=True)  27.2 us
    reduce_scatter x1, waiting for transfers between devices, learn(): lax.psum_scatter(mixed_part, 'mdl', scatter_dimension=1, tiled=True)  26.3 us
    all_to_all x1, waiting for transfers between devices, per_device(): lax.all_to_all(pad_cot, 'sel', split_axis=0, concat_axis=0, tiled=True)  17.2 us
    dot_general x1, matrix products, learn(): lax.dot_general(tok_full, grad_pre, (((0,), (0,)), ((), ())), preferred_e...  13.4 us
    dot_general x1, matrix products, learn(): mixed_part = jnp.dot(hidden, w_down, preferred_element_type=jnp.float32)  9.17 us
    psum x1, blocking collectives, per_device(): lax.psum((exp_total(img_full, text_split), own_product(img_hat, text_hat)...  7.52 us
  transfers between devices with their start and end apart: 8, of which 5 were waited for; matrix products, arithmetic and copies ran while one was open for 15% of the time, Pallas kernels for 0%

commit v1 on v0

v1 whole, which is shorter than its diff:
```python
import jax
import jax.numpy as jnp
from jax import lax
from jax.sharding import PartitionSpec as P

logit_scale = 64.0
eps = 1e-06
f32 = jnp.float32
bf16 = jnp.bfloat16


def gelu_parts(pre_act):
    cumul = 0.5 * (1.0 + lax.erf(pre_act * 0.7071067811865476))
    density = jnp.exp(-0.5 * pre_act * pre_act) * 0.3989422804014327
    return (pre_act * cumul, cumul + pre_act * density)


def swap(value, axis, bit):
    size = lax.axis_size(axis)
    return lax.ppermute(value, axis, [(i, i ^ bit) for i in range(size)])


def rotate_pairs(value, step):
    size = lax.axis_size("sel")
    return lax.ppermute(value, "sel", [(i, (i + 2 * step) % size) for i in range(size)])


def mdl_pieces(value):
    n = lax.axis_size("mdl")
    out = [value] + [None] * (n - 1)
    top = n // 2
    if n == 1:
        return out
    out[top] = swap(value, "mdl", top)
    low = top // 2
    have = [0, top]
    while low:
        for j in list(have):
            out[j | low] = swap(out[j], "mdl", low)
            have.append(j | low)
        low //= 2
    return out


def in_order(pieces, axis):
    me = lax.axis_index("mdl")
    bit = 1
    while bit < lax.axis_size("mdl"):
        set_bit = (me & bit) != 0
        merged = []
        for j in range(0, len(pieces), 2):
            first, second = pieces[j], pieces[j + 1]
            merged.append(
                jnp.where(
                    set_bit,
                    jnp.concatenate([second, first], axis),
                    jnp.concatenate([first, second], axis),
                )
            )
        pieces = merged
        bit *= 2
    return pieces[0]


def mdl_sum(value):
    bit = 1
    while bit < lax.axis_size("mdl"):
        value = value + swap(value, "mdl", bit)
        bit *= 2
    return value


def unit_rows(values):
    norm_sq = jnp.sum(values * values, axis=1)
    return (values * lax.rsqrt(norm_sq + eps)[:, None]).astype(bf16)


def exp_total(rows_full, texts):
    scores = lax.dot_general(
        rows_full, texts, (((1,), (1,)), ((), ())), preferred_element_type=f32
    )
    return jnp.sum(jnp.exp(logit_scale * scores), axis=1)


def own_product(rows, texts):
    return jnp.sum(rows.astype(f32) * texts.astype(f32), axis=1)


def per_device(patches, text, ref_proj, w_up, w_down, kept_index, dest, cotan):
    n_sel = lax.axis_size("sel")
    n_mdl = lax.axis_size("mdl")
    ex_dev = text.shape[0]
    d_part = patches.shape[1]
    n_patch = patches.shape[0] // ex_dev
    k_dev = kept_index.shape[0]
    n_rows = k_dev * n_patch
    ff_dev = w_up.shape[1]
    n_high = n_sel // 2
    rotations = n_high <= 4
    sel_me, mdl_me = lax.axis_index("sel"), lax.axis_index("mdl")
    pair_me, high_me = sel_me % 2, sel_me // 2

    patches_t = patches.T
    row_of = (kept_index[:, None] * n_patch + jnp.arange(n_patch)[None, :]).reshape(-1)
    pick = (jnp.arange(ex_dev * n_patch)[:, None] == row_of[None, :]).astype(bf16)
    tok_t = jnp.dot(patches_t, pick, preferred_element_type=f32).astype(bf16)
    cot_t = cotan.T
    blk = d_part * n_mdl // n_sel
    halves = tok_t.reshape(d_part // (2 * blk), 2, blk, n_rows)
    send_half = lax.dynamic_index_in_dim(halves, 1 - pair_me, 1, keepdims=False)
    recv_half = swap(send_half.reshape(d_part // 2, n_rows), "sel", 1)

    tok_full = in_order(mdl_pieces(tok_t), 0)
    cot_full = in_order(mdl_pieces(cot_t), 0)
    recv_half_full = in_order(mdl_pieces(recv_half), 0)
    n_blk = d_part * n_mdl // (2 * blk)
    own_half_full = lax.dynamic_index_in_dim(
        tok_full.reshape(n_blk, 2, blk, n_rows), pair_me, 1, keepdims=False
    ).reshape(n_blk * blk, n_rows)
    tok_pair = jnp.concatenate([own_half_full, recv_half_full], axis=1)

    counts = jnp.sum((dest[:, None] == jnp.arange(n_sel)[None, :]).astype(f32), axis=0)
    if rotations:
        pair_counts = counts + swap(counts, "sel", 1)
        counts = pair_counts
        for step in range(1, n_high):
            counts = counts + rotate_pairs(pair_counts, step)
    else:
        counts = lax.psum(counts, "sel")
    row_weight = 1.0 / jnp.repeat(counts[dest], n_patch)

    text_full = in_order(mdl_pieces(text), 1).astype(f32)
    text_hat = unit_rows(text_full)
    share = ex_dev // n_mdl
    text_share = lax.dynamic_slice_in_dim(text_hat, mdl_me * share, share, 0)
    if rotations:
        pair_share = jnp.concatenate([text_share, swap(text_share, "sel", 1)], axis=0)
        text_split = jnp.concatenate(
            [pair_share] + [rotate_pairs(pair_share, s) for s in range(1, n_high)], axis=0
        )
    else:
        text_split = lax.all_gather(text_share, "sel", axis=0, tiled=True)

    pooled_t = (
        jnp.sum(patches_t.reshape(d_part, ex_dev, n_patch).astype(f32), axis=2) * (1.0 / n_patch)
    ).astype(bf16)
    pooled_full = in_order(mdl_pieces(pooled_t), 0)
    img_emb = lax.dot_general(
        pooled_full, ref_proj, (((0,), (0,)), ((), ())), preferred_element_type=f32
    )
    img_hat = unit_rows(in_order(mdl_pieces(img_emb), 1))
    ref_own = own_product(img_hat, text_hat)
    ref_part = exp_total(img_hat, text_split)

    pre_act = lax.dot_general(
        tok_full, w_up, (((0,), (0,)), ((), ())), preferred_element_type=f32
    )
    activated, gelu_slope = gelu_parts(pre_act)
    hidden = activated.astype(bf16)
    mixed = jnp.dot(hidden, w_down, preferred_element_type=f32)
    mixed_pool = mdl_sum(jnp.sum(mixed.reshape(k_dev, n_patch, -1), axis=1))
    tok_pool = jnp.sum(tok_full.reshape(-1, k_dev, n_patch).astype(f32), axis=2).T
    learn_pool = ((mixed_pool + tok_pool) * (1.0 / n_patch)).astype(bf16)
    learn_emb = jnp.dot(learn_pool, ref_proj, preferred_element_type=f32)
    learn_hat = unit_rows(in_order(mdl_pieces(learn_emb), 1))
    kept_text = text_hat[kept_index]
    learn_own = own_product(learn_hat, kept_text)
    learn_part = exp_total(learn_hat, text_split)
    totals = mdl_sum(jnp.concatenate([ref_part, learn_part]))
    ref_loss = jnp.log(totals[:ex_dev]) - logit_scale * ref_own
    learner_loss = jnp.log(totals[ex_dev:]) - logit_scale * learn_own
    learnability = learner_loss - ref_loss[kept_index]

    n_chunks = 4
    width = ff_dev // n_chunks
    outs = []
    for c in range(n_chunks):
        cols = slice(c * width, (c + 1) * width)
        grad_act = lax.dot_general(
            cot_full, w_down[cols], (((0,), (1,)), ((), ())), preferred_element_type=f32
        )
        grad_pre = (grad_act * row_weight[:, None] * gelu_slope[:, cols]).astype(bf16)
        pair_pre = jnp.concatenate([grad_pre, swap(grad_pre, "sel", 1)], axis=0)
        part = jnp.dot(tok_pair, pair_pre, preferred_element_type=f32)
        part = part.reshape(n_high, blk, width)
        if rotations:
            total = lax.dynamic_index_in_dim(part, high_me, 0, keepdims=False)
            for step in range(1, n_high):
                block = lax.dynamic_index_in_dim(
                    part, (high_me + step) % n_high, 0, keepdims=False
                )
                total = total + rotate_pairs(block.astype(bf16), step).astype(f32)
        else:
            total = lax.psum_scatter(
                part,
                "sel",
                scatter_dimension=0,
                axis_index_groups=[list(range(p, n_sel, 2)) for p in range(2)],
                tiled=False,
            )
        outs.append(total)
    grad_up = jnp.concatenate(outs, axis=1)
    return (ref_loss, learnability, grad_up)


def solution(mesh):
    in_specs = (
        P("sel", "mdl"),
        P("sel", "mdl"),
        P(None, "mdl"),
        P(None, "mdl"),
        P("mdl", None),
        P("sel"),
        P("sel"),
        P("sel", "mdl"),
    )
    out_specs = (P("sel"), P("sel"), P("sel", "mdl"))
    return jax.shard_map(
        per_device, mesh=mesh, in_specs=in_specs, out_specs=out_specs, check_vma=False
    )
```

time: 319 us -> 181 us (0.57)
  blocking collectives: 101 us -> 0 us
  waiting for transfers between devices: 127 us -> 49.2 us
  starting transfers between devices: 16.3 us -> 52.6 us
  other arithmetic: 10.5 us -> 26.1 us
  between operations: 14.7 us -> 1.27 us
  local copies, waits for them, and re-layouts: 17.6 us -> 20.9 us
    reduce_scatter x2 -> x0, waiting for transfers between devices: 102 us -> none  [the longest x1 76 us: learn(): lax.psum_scatter(lax.dot_general(tok_full, grad_pre, (((0,), (0,)), ((),...]
    all_gather x5 -> x0, blocking collectives: 59.6 us -> none  [the longest x1 35.6 us: per_device(): text_split = lax.all_gather(text_rows, 'sel', axis=0, tiled=True)]
    ppermute x0 -> x50, starting transfers between devices: none -> 52.6 us  [the longest x18 33.7 us: rotate_pairs(): lax.ppermute(value, 'sel', [(i, (i + 2 * step) % size) for i in range(siz...]
    ppermute x0 -> x50, waiting for transfers between devices: none -> 49.2 us  [the longest x18 26.4 us: rotate_pairs(): lax.ppermute(value, 'sel', [(i, (i + 2 * step) % size) for i in range(siz...]
    all_to_all x1 -> x0, blocking collectives: 27.2 us -> none  [per_device(): lax.all_to_all(pad_tok, 'sel', split_axis=0, concat_axis=0, tiled=True)]
    all_to_all x4 -> x0, waiting for transfers between devices: 20.7 us -> none  [the longest x1 17.2 us: per_device(): lax.all_to_all(pad_cot, 'sel', split_axis=0, concat_axis=0, tiled=True)]
    all_to_all x4 -> x0, starting transfers between devices: 15.9 us -> none  [the longest x1 5.53 us: per_device(): lax.all_to_all(slot_hat, 'sel', split_axis=0, concat_axis=0, tiled=True)]
    psum x2 -> x0, blocking collectives: 14.3 us -> none  [the longest x1 7.52 us: per_device(): lax.psum((exp_total(img_full, text_split), own_product(img_hat, text_hat)...]
  transfers between devices with their start and end apart: 8 -> 50, of which waited for: 5 -> 15; matrix products, arithmetic and copies ran while one was open for 15% -> 41% of each run, Pallas kernels for 0% -> 0%
where the time goes in v1:
time: 181 us; the launch traced here: 180 us
  starting transfers between devices  52.6 us (29%)
  waiting for transfers between devices  49.2 us (27%)
  matrix products  29.9 us (17%)
  other arithmetic  26.1 us (14%)
  local copies, waits for them, and re-layouts  20.9 us (12%)
    ppermute x18, starting transfers between devices, rotate_pairs(): lax.ppermute(value, 'sel', [(i, (i + 2 * step) % size) for i in range(siz...  33.7 us
    ppermute x18, waiting for transfers between devices, rotate_pairs(): lax.ppermute(value, 'sel', [(i, (i + 2 * step) % size) for i in range(siz...  26.4 us
    ppermute x32, waiting for transfers between devices, swap(): return lax.ppermute(value, axis, [(i, i ^ bit) for i in range(size)])  22.8 us
    ppermute x32, starting transfers between devices, swap(): return lax.ppermute(value, axis, [(i, i ^ bit) for i in range(size)])  18.9 us
    select_n x17, other arithmetic, in_order(): jnp.where(set_bit, jnp.concatenate([second, first], axis), jnp.concatenat...  11.8 us
    dot_general x1, matrix products, per_device(): lax.dot_general(tok_full, w_up, (((0,), (0,)), ((), ())), preferred_eleme...  6.51 us
    dot_general x1, matrix products, per_device(): mixed = jnp.dot(hidden, w_down, preferred_element_type=f32)  6.42 us
    dot_general x4, matrix products, per_device(): lax.dot_general(cot_full, w_down[cols], (((0,), (1,)), ((), ())), preferr...  6.24 us
  transfers between devices with their start and end apart: 50, of which 15 were waited for; matrix products, arithmetic and copies ran while one was open for 41% of the time, Pallas kernels for 0%

profile of v1, /device:TPU:0, one launch (start us, length us, event | category | flops | bytes accessed | tf_op | source)
XLA Modules:
  0.0 180.0 jit_solution(1828549029629585042)
XLA Ops:
  0.7 3.0 %collective-permute-start.6 = (bf16[128,256]{1,0:T(8,128)(2,1)}, bf16[128,256]{1,0:T(8,128)(2,1)S(1)}, u32[]{:S(2)}, u32[]{:S(2)}) collective-permute-start(bf16[128,256]{1,0:T(8,128)(2,1)} %param.9), channel_id=1, source_target_pairs={{0,2},{1,3},{2,0},{3,1},{4,6},{5,7},{6,4},{7,5},{8,10},{9,11},{10,... | collective-permute-start | bytes 196616 | tf_op jit(solution)/shard_map/ppermute | solution.py:20
  4.6 2.2 %convolution_convert_fusion = bf16[384,352]{0,1:T(8,128)(2,1)} fusion(bf16[768,352]{0,1:T(8,128)(2,1)} %param.8, s32[384]{0:T(512)S(1)} %add.210), kind=kOutput, calls=%fused_computation.23 | convolution fusion | flops 208048128 | bytes 812544 | tf_op jit(solution)/shard_map/dot_general | solution.py:106
  7.5 2.0 %collective-permute-start.30 = (f32[8]{0:T(128)S(1)}, f32[8]{0:T(128)S(1)}, u32[]{:S(2)}, u32[]{:S(2)}) collective-permute-start(f32[8]{0:T(128)S(1)} %convert_reduce_fusion.1), channel_id=1, source_target_pairs={{0,4},{4,0},{8,12},{12,8},{16,20},{20,16},{24,28},{28,24},{1,5},{5... | collective-permute-start | bytes 104 | tf_op jit(solution)/shard_map/ppermute | solution.py:20
  9.5 1.2 copy.25
  12.8 0.9 dynamic-slice_bitcast_fusion
  13.7 3.7 %collective-permute-start.33 = (f32[8]{0:T(128)S(1)}, f32[8]{0:T(128)S(1)}, u32[]{:S(2)}, u32[]{:S(2)}) collective-permute-start(f32[8]{0:T(128)S(1)} %add.224), channel_id=1, source_target_pairs={{0,24},{4,28},{8,0},{12,4},{16,8},{20,12},{24,16},{28,20},{1,25},{... | collective-permute-start | bytes 104 | tf_op jit(solution)/shard_map/ppermute | solution.py:25
  17.4 1.3 collective-permute-done.33
  18.7 1.2 collective-permute-start.32
  19.9 3.2 %collective-permute-done.32 = f32[8]{0:T(128)S(1)} collective-permute-done((f32[8]{0:T(128)S(1)}, f32[8]{0:T(128)S(1)}, u32[]{:S(2)}, u32[]{:S(2)}) %collective-permute-start.32) | collective-permute-done | bytes 64 | tf_op jit(solution)/shard_map/ppermute | solution.py:25
  23.1 1.7 collective-permute-start.31
  24.8 3.9 %collective-permute-done.31 = f32[8]{0:T(128)S(1)} collective-permute-done((f32[8]{0:T(128)S(1)}, f32[8]{0:T(128)S(1)}, u32[]{:S(2)}, u32[]{:S(2)}) %collective-permute-start.31) | collective-permute-done | bytes 64 | tf_op jit(solution)/shard_map/ppermute | solution.py:25
  29.4 5.0 %fusion.72 = f32[64]{0:T(128)S(1)} fusion(s32[64]{0:T(128)S(1)} %copy-done.10, f32[]{:T(128)} %bitcast.8, f32[]{:T(128)} %bitcast.9, f32[]{:T(128)} %bitcast.10, f32[]{:T(128)} %bitcast.11, f32[]{:T(128)} %bitcast.12, f32[]{:T(128)} %bitcast.13, f32[]{:T(128)} %bitcast.14, f32[]{:T(128)} %bitcast.15), kind=kLoop, calls=%fused_computation.161 | loop fusion | flops 1152 | bytes 544 | tf_op jit(solution)/shard_map/div | solution.py:130
  34.6 1.6 collective-permute-start
  36.1 0.9 maximum_select_fusion.22
  37.8 2.0 %collective-permute-done = bf16[352,128]{0,1:T(8,128)(2,1)S(1)} collective-permute-done((bf16[352,128]{0,1:T(8,128)(2,1)S(1)}, bf16[352,128]{0,1:T(8,128)(2,1)S(1)}, u32[]{:S(2)}, u32[]{:S(2)}) %collective-permute-start) | collective-permute-done | bytes 90144 | tf_op jit(solution)/shard_map/ppermute | solution.py:20
  40.6 2.3 %collective-permute-done.23 = bf16[176,384]{1,0:T(8,128)(2,1)S(1)} collective-permute-done((bf16[176,384]{1,0:T(8,128)(2,1)S(1)}, bf16[176,384]{1,0:T(8,128)(2,1)S(1)}, u32[]{:S(2)}, u32[]{:S(2)}) %collective-permute-start.23) | collective-permute-done | bytes 135200 | tf_op jit(solution)/shard_map/ppermute | solution.py:20
  43.9 1.6 collective-permute-start.24
  45.5 2.0 %maximum_select_fusion.9 = bf16[704,384]{1,0:T(8,128)(2,1)} fusion(bf16[352,384]{1,0:T(8,128)(2,1)} %bitcast.7, bf16[352,384]{1,0:T(8,128)(2,1)S(1)} %collective-permute-done.29, pred[]{:T(512)S(6)} %ne.61), kind=kLoop, calls=%fused_computation.66 | loop fusion | flops 2433024 | bytes 1081345 | tf_op jit(solution)/shard_map/jit(_where)/select_n | solution.py:54
  48.2 1.4 maximum_select_fusion.6
  49.6 5.6 %collective-permute-done.24 = bf16[176,384]{1,0:T(8,128)(2,1)S(1)} collective-permute-done((bf16[176,384]{1,0:T(8,128)(2,1)S(1)}, bf16[176,384]{1,0:T(8,128)(2,1)S(1)}, u32[]{:S(2)}, u32[]{:S(2)}) %collective-permute-start.24) | collective-permute-done | bytes 135200 | tf_op jit(solution)/shard_map/ppermute | solution.py:20
  55.8 1.2 copy.23
  57.1 1.2 copy.24
  59.6 1.0 maximum_select_fusion.16
  61.1 1.0 maximum_select_fusion.15
  63.6 1.0 maximum_select_fusion.7
  64.6 1.4 gather_fusion
  66.0 1.4 collective-permute-done.9
  68.0 2.0 %collective-permute-start.12 = (bf16[64,1024]{1,0:T(8,128)(2,1)}, bf16[64,1024]{1,0:T(8,128)(2,1)}, u32[]{:S(2)}, u32[]{:S(2)}) collective-permute-start(bf16[64,1024]{1,0:T(8,128)(2,1)} %pad_maximum_fusion.2), channel_id=1, source_target_pairs={{0,24},{4,28},{8,0},{12,4},{16,8},{20,12},{24,16},{28,20},{1,25},{... | collective-permute-start | bytes 393224 | tf_op jit(solution)/shard_map/ppermute | solution.py:25
  71.3 1.2 maximum_select_fusion.5
  72.9 6.5 %fusion.3 = (f32[384,1536]{1,0:T(8,128)S(1)}, f32[384,1536]{1,0:T(8,128)}) fusion(bf16[1408,384]{1,0:T(8,128)(2,1)S(1)} %maximum_select_fusion.1, bf16[1408,1536]{1,0:T(8,128)(2,1)} %param.11), kind=kOutput, calls=%fused_computation.7 | convolution fusion | flops 1665662976 | bytes 10125312 | tf_op jit(solution)/shard_map/dot_general | solution.py:155
  79.4 1.3 maximum_select_fusion.8
  80.8 1.6 fusion.11
  82.3 1.6 fusion.10
  83.9 1.6 fusion.9
  85.5 1.5 fusion.8
  88.1 6.4 %fusion.12 = f32[384,1408]{1,0:T(8,128)} fusion(bf16[1536,1408]{1,0:T(8,128)(2,1)} %param.12, f32[384,1536]{1,0:T(8,128)} %get-tuple-element.30), kind=kOutput, calls=%fused_computation.24 | convolution fusion | flops 1663893504 | bytes 8847360 | tf_op jit(solution)/shard_map/dot_general | solution.py:160
  95.0 1.5 collective-permute-start.38
  96.5 1.1 maximum_select_fusion.3
  97.7 1.7 convert_reduce_fusion
  99.4 3.5 %reshape.102 = f32[64,6,1408]{2,1,0:T(8,128)} reshape(f32[384,1408]{1,0:T(8,128)} %fusion.12) | data formatting | bytes 4325376 | tf_op jit(solution)/shard_map/reshape | solution.py:161
  102.9 2.7 %reduce_sum.103 = f32[64,1408]{1,0:T(8,128)S(1)} reduce(f32[64,6,1408]{2,1,0:T(8,128)} %reshape.102, f32[]{:T(128)} %constant.131.clone.1), dimensions={1}, to_apply=%region_4.5 | reduce | flops 450560 | bytes 2523140 | tf_op jit(solution)/shard_map/reduce_sum | solution.py:161
  106.3 1.6 constant_dynamic-update-slice_fusion.2
  107.8 1.6 collective-permute-start.46
  109.4 1.6 constant_dynamic-update-slice_fusion.1
  111.0 1.6 constant_dynamic-update-slice_fusion
  112.5 1.4 fusion.14
  114.0 7.0 %collective-permute-done.46 = bf16[384,384]{1,0:T(8,128)(2,1)S(1)} collective-permute-done((bf16[384,384]{1,0:T(8,128)(2,1)}, bf16[384,384]{1,0:T(8,128)(2,1)S(1)}, u32[]{:S(2)}, u32[]{:S(2)}) %collective-permute-start.46) | collective-permute-done | bytes 294944 | tf_op jit(solution)/shard_map/ppermute | solution.py:20
  121.8 2.7 %collective-permute-start.47 = (bf16[176,384]{1,0:T(8,128)(2,1)S(1)}, bf16[176,384]{1,0:T(8,128)(2,1)S(1)}, u32[]{:S(2)}, u32[]{:S(2)}) collective-permute-start(bf16[176,384]{1,0:T(8,128)(2,1)S(1)} %get-tuple-element.16), channel_id=1, source_target_pairs={{0,8},{4,12},{8,16},{12,20},{16,24},{20,28},{24,0},{28,4},{1,9},{5... | collective-permute-start | bytes 405512 | tf_op jit(solution)/shard_map/ppermute | solution.py:25
  124.5 1.2 collective-permute-start.49
  127.1 1.8 fusion.25
  128.9 1.5 collective-permute-start.43
  130.4 1.8 fusion.21
  132.4 2.4 %collective-permute-start.45 = (bf16[176,384]{1,0:T(8,128)(2,1)S(1)}, bf16[176,384]{1,0:T(8,128)(2,1)S(1)}, u32[]{:S(2)}, u32[]{:S(2)}) collective-permute-start(bf16[176,384]{1,0:T(8,128)(2,1)S(1)} %get-tuple-element.14), channel_id=1, source_target_pairs={{0,24},{4,28},{8,0},{12,4},{16,8},{20,12},{24,16},{28,20},{1,25},{... | collective-permute-start | bytes 405512 | tf_op jit(solution)/shard_map/ppermute | solution.py:25
  135.5 1.5 collective-permute-start.39
  137.0 8.1 %collective-permute-done.48 = bf16[176,384]{1,0:T(8,128)(2,1)S(1)} collective-permute-done((bf16[176,384]{1,0:T(8,128)(2,1)S(1)}, bf16[176,384]{1,0:T(8,128)(2,1)S(1)}, u32[]{:S(2)}, u32[]{:S(2)}) %collective-permute-start.48) | collective-permute-done | bytes 135200 | tf_op jit(solution)/shard_map/ppermute | solution.py:25
  145.2 6.4 %collective-permute-start.40 = (bf16[176,384]{1,0:T(8,128)(2,1)S(1)}, bf16[176,384]{1,0:T(8,128)(2,1)S(1)}, u32[]{:S(2)}, u32[]{:S(2)}) collective-permute-start(bf16[176,384]{1,0:T(8,128)(2,1)S(1)} %get-tuple-element.12), channel_id=1, source_target_pairs={{0,16},{4,20},{8,24},{12,28},{16,0},{20,4},{24,8},{28,12},{1,17},{... | collective-permute-start | bytes 405512 | tf_op jit(solution)/shard_map/ppermute | solution.py:25
  152.5 3.9 %collective-permute-done.44 = bf16[176,384]{1,0:T(8,128)(2,1)S(1)} collective-permute-done((bf16[176,384]{1,0:T(8,128)(2,1)S(1)}, bf16[176,384]{1,0:T(8,128)(2,1)S(1)}, u32[]{:S(2)}, u32[]{:S(2)}) %collective-permute-start.44) | collective-permute-done | bytes 135200 | tf_op jit(solution)/shard_map/ppermute | solution.py:25
  157.0 6.6 %collective-permute-start.36 = (bf16[176,384]{1,0:T(8,128)(2,1)S(1)}, bf16[176,384]{1,0:T(8,128)(2,1)S(1)}, u32[]{:S(2)}, u32[]{:S(2)}) collective-permute-start(bf16[176,384]{1,0:T(8,128)(2,1)S(1)} %get-tuple-element.9), channel_id=1, source_target_pairs={{0,16},{4,20},{8,24},{12,28},{16,0},{20,4},{24,8},{28,12},{1,17},{... | collective-permute-start | bytes 405512 | tf_op jit(solution)/shard_map/ppermute | solution.py:25
  163.7 1.3 collective-permute-done.40
  166.0 4.7 %collective-permute-done.36 = bf16[176,384]{1,0:T(8,128)(2,1)S(1)} collective-permute-done((bf16[176,384]{1,0:T(8,128)(2,1)S(1)}, bf16[176,384]{1,0:T(8,128)(2,1)S(1)}, u32[]{:S(2)}, u32[]{:S(2)}) %collective-permute-start.36) | collective-permute-done | bytes 135200 | tf_op jit(solution)/shard_map/ppermute | solution.py:25
  170.9 1.2 collective-permute-done.19
  172.2 1.5 fusion.16
  174.0 1.1 pad_maximum_fusion.1
  175.9 2.8 %collective-permute-done.22 = f32[192]{0:T(256)S(1)} collective-permute-done((f32[192]{0:T(256)S(1)}, f32[192]{0:T(256)S(1)}, u32[]{:S(2)}, u32[]{:S(2)}) %collective-permute-start.22) | collective-permute-done | bytes 800 | tf_op jit(solution)/shard_map/ppermute | solution.py:20
  (159 shorter events, 24.5 us)
Async XLA Ops:
  0.6 42.9 %copy-start = (bf16[1408,256]{1,0:T(8,128)(2,1)S(1)}, bf16[1408,256]{1,0:T(8,128)(2,1)}, u32[]{:S(2)}) copy-start(bf16[1408,256]{1,0:T(8,128)(2,1)} %param.10) | copy-start | bytes 2162692
  0.6 10.1 %copy-start.5 = (bf16[768,352]{0,1:T(8,128)(2,1)S(1)}, bf16[768,352]{0,1:T(8,128)(2,1)}, u32[]{:S(2)}) copy-start(bf16[768,352]{0,1:T(8,128)(2,1)} %param.8) | copy-start | bytes 1622020
  0.7 6.7 %copy-start.10 = (s32[64]{0:T(128)S(1)}, s32[64]{0:T(128)}, u32[]{:S(2)}) copy-start(s32[64]{0:T(128)} %param.14) | copy-start | bytes 772
  0.7 36.4 %collective-permute-start.6 = (bf16[128,256]{1,0:T(8,128)(2,1)}, bf16[128,256]{1,0:T(8,128)(2,1)S(1)}, u32[]{:S(2)}, u32[]{:S(2)}) collective-permute-start(bf16[128,256]{1,0:T(8,128)(2,1)} %param.9), channel_id=1, source_target_pairs={{0,2},{1,3},{2,0},{3,1},{4,6},{5,7},{6,4},{7,5},{8,10},{9,11},{10,... | collective-permute-start | bytes 196616 | tf_op jit(solution)/shard_map/ppermute | solution.py:20
  3.7 30.9 %collective-permute-start.8 = (bf16[128,256]{1,0:T(8,128)(2,1)}, bf16[128,256]{1,0:T(8,128)(2,1)}, u32[]{:S(2)}, u32[]{:S(2)}) collective-permute-start(bf16[128,256]{1,0:T(8,128)(2,1)} %param.9), channel_id=1, source_target_pairs={{0,1},{1,0},{2,3},{3,2},{4,5},{5,4},{6,7},{7,6},{8,9},{9,8},{10,11... | collective-permute-start | bytes 196616 | tf_op jit(solution)/shard_map/ppermute | solution.py:20
  6.8 40.9 %collective-permute-start.15 = (bf16[352,384]{1,0:T(8,128)(2,1)}, bf16[352,384]{1,0:T(8,128)(2,1)}, u32[]{:S(2)}, u32[]{:S(2)}) collective-permute-start(bf16[352,384]{1,0:T(8,128)(2,1)} %bitcast.1), channel_id=1, source_target_pairs={{0,1},{1,0},{2,3},{3,2},{4,5},{5,4},{6,7},{7,6},{8,9},{9,8},{10,11... | collective-permute-start | bytes 811016 | tf_op jit(solution)/shard_map/ppermute | solution.py:20
  7.3 47.9 %collective-permute-start.13 = (bf16[352,384]{1,0:T(8,128)(2,1)}, bf16[352,384]{1,0:T(8,128)(2,1)}, u32[]{:S(2)}, u32[]{:S(2)}) collective-permute-start(bf16[352,384]{1,0:T(8,128)(2,1)} %bitcast.1), channel_id=1, source_target_pairs={{0,2},{1,3},{2,0},{3,1},{4,6},{5,7},{6,4},{7,5},{8,10},{9,11},{10,... | collective-permute-start | bytes 811016 | tf_op jit(solution)/shard_map/ppermute | solution.py:20
  7.5 6.2 %collective-permute-start.30 = (f32[8]{0:T(128)S(1)}, f32[8]{0:T(128)S(1)}, u32[]{:S(2)}, u32[]{:S(2)}) collective-permute-start(f32[8]{0:T(128)S(1)} %convert_reduce_fusion.1), channel_id=1, source_target_pairs={{0,4},{4,0},{8,12},{12,8},{16,20},{20,16},{24,28},{28,24},{1,5},{5... | collective-permute-start | bytes 104 | tf_op jit(solution)/shard_map/ppermute | solution.py:20
  12.2 23.9 %copy-start.9 = (bf16[128,256]{1,0:T(8,128)(2,1)S(1)}, bf16[128,256]{1,0:T(8,128)(2,1)}, u32[]{:S(2)}) copy-start(bf16[128,256]{1,0:T(8,128)(2,1)} %param.9) | copy-start | bytes 196612
  13.7 5.0 %collective-permute-start.33 = (f32[8]{0:T(128)S(1)}, f32[8]{0:T(128)S(1)}, u32[]{:S(2)}, u32[]{:S(2)}) collective-permute-start(f32[8]{0:T(128)S(1)} %add.224), channel_id=1, source_target_pairs={{0,24},{4,28},{8,0},{12,4},{16,8},{20,12},{24,16},{28,20},{1,25},{... | collective-permute-start | bytes 104 | tf_op jit(solution)/shard_map/ppermute | solution.py:25
  18.7 4.4 %collective-permute-start.32 = (f32[8]{0:T(128)S(1)}, f32[8]{0:T(128)S(1)}, u32[]{:S(2)}, u32[]{:S(2)}) collective-permute-start(f32[8]{0:T(128)S(1)} %add.224), channel_id=1, source_target_pairs={{0,16},{4,20},{8,24},{12,28},{16,0},{20,4},{24,8},{28,12},{1,17},{... | collective-permute-start | bytes 104 | tf_op jit(solution)/shard_map/ppermute | solution.py:25
  23.1 5.6 %collective-permute-start.31 = (f32[8]{0:T(128)S(1)}, f32[8]{0:T(128)S(1)}, u32[]{:S(2)}, u32[]{:S(2)}) collective-permute-start(f32[8]{0:T(128)S(1)} %add.224), channel_id=1, source_target_pairs={{0,8},{4,12},{8,16},{12,20},{16,24},{20,28},{24,0},{28,4},{1,9},{5... | collective-permute-start | bytes 104 | tf_op jit(solution)/shard_map/ppermute | solution.py:25
  28.7 9.0 %collective-permute-start.2 = (bf16[352,128]{0,1:T(8,128)(2,1)S(1)}, bf16[352,128]{0,1:T(8,128)(2,1)S(1)}, u32[]{:S(2)}, u32[]{:S(2)}) collective-permute-start(bf16[352,128]{0,1:T(8,128)(2,1)S(1)} %multiply_convert_fusion.4), channel_id=1, source_target_pairs={{0,1},{1,0},{2,3},{3,2},{4,5},{5,4},{6,7},{7,6},{8,9},{9,8},{10,11... | collective-permute-start | bytes 270344 | tf_op jit(solution)/shard_map/ppermute | solution.py:20
  34.6 5.3 %collective-permute-start = (bf16[352,128]{0,1:T(8,128)(2,1)S(1)}, bf16[352,128]{0,1:T(8,128)(2,1)S(1)}, u32[]{:S(2)}, u32[]{:S(2)}) collective-permute-start(bf16[352,128]{0,1:T(8,128)(2,1)S(1)} %multiply_convert_fusion.4), channel_id=1, source_target_pairs={{0,2},{1,3},{2,0},{3,1},{4,6},{5,7},{6,4},{7,5},{8,10},{9,11},{10,... | collective-permute-start | bytes 270344 | tf_op jit(solution)/shard_map/ppermute | solution.py:20
  37.1 5.8 %collective-permute-start.23 = (bf16[176,384]{1,0:T(8,128)(2,1)S(1)}, bf16[176,384]{1,0:T(8,128)(2,1)S(1)}, u32[]{:S(2)}, u32[]{:S(2)}) collective-permute-start(bf16[176,384]{1,0:T(8,128)(2,1)S(1)} %dynamic-slice_bitcast_fusion), channel_id=1, source_target_pairs={{0,4},{4,0},{8,12},{12,8},{16,20},{20,16},{24,28},{28,24},{1,5},{5... | collective-permute-start | bytes 405512 | tf_op jit(solution)/shard_map/ppermute | solution.py:20
  37.7 2.2 %collective-permute-start.7 = (bf16[128,256]{1,0:T(8,128)(2,1)S(1)}, bf16[128,256]{1,0:T(8,128)(2,1)S(1)}, u32[]{:S(2)}, u32[]{:S(2)}) collective-permute-start(bf16[128,256]{1,0:T(8,128)(2,1)S(1)} %collective-permute-done.6), channel_id=1, source_target_pairs={{0,1},{1,0},{2,3},{3,2},{4,5},{5,4},{6,7},{7,6},{8,9},{9,8},{10,11... | collective-permute-start | bytes 196616 | tf_op jit(solution)/shard_map/ppermute | solution.py:20
  39.9 4.1 %collective-permute-start.29 = (bf16[352,384]{1,0:T(8,128)(2,1)}, bf16[352,384]{1,0:T(8,128)(2,1)S(1)}, u32[]{:S(2)}, u32[]{:S(2)}) collective-permute-start(bf16[352,384]{1,0:T(8,128)(2,1)} %bitcast.7), channel_id=1, source_target_pairs={{0,1},{1,0},{2,3},{3,2},{4,5},{5,4},{6,7},{7,6},{8,9},{9,8},{10,11... | collective-permute-start | bytes 811016 | tf_op jit(solution)/shard_map/ppermute | solution.py:20
  39.9 3.6 %collective-permute-start.1 = (bf16[352,128]{0,1:T(8,128)(2,1)S(1)}, bf16[352,128]{0,1:T(8,128)(2,1)S(1)}, u32[]{:S(2)}, u32[]{:S(2)}) collective-permute-start(bf16[352,128]{0,1:T(8,128)(2,1)S(1)} %collective-permute-done), channel_id=1, source_target_pairs={{0,1},{1,0},{2,3},{3,2},{4,5},{5,4},{6,7},{7,6},{8,9},{9,8},{10,11... | collective-permute-start | bytes 270344 | tf_op jit(solution)/shard_map/ppermute | solution.py:20
  42.9 16.2 %collective-permute-start.27 = (bf16[352,384]{1,0:T(8,128)(2,1)}, bf16[352,384]{1,0:T(8,128)(2,1)}, u32[]{:S(2)}, u32[]{:S(2)}) collective-permute-start(bf16[352,384]{1,0:T(8,128)(2,1)} %bitcast.7), channel_id=1, source_target_pairs={{0,2},{1,3},{2,0},{3,1},{4,6},{5,7},{6,4},{7,5},{8,10},{9,11},{10,... | collective-permute-start | bytes 811016 | tf_op jit(solution)/shard_map/ppermute | solution.py:20
  43.4 4.0 %collective-permute-start.26 = (bf16[176,384]{1,0:T(8,128)(2,1)S(1)}, bf16[176,384]{1,0:T(8,128)(2,1)S(1)}, u32[]{:S(2)}, u32[]{:S(2)}) collective-permute-start(bf16[176,384]{1,0:T(8,128)(2,1)S(1)} %collective-permute-done.23), channel_id=1, source_target_pairs={{0,1},{1,0},{2,3},{3,2},{4,5},{5,4},{6,7},{7,6},{8,9},{9,8},{10,11... | collective-permute-start | bytes 405512 | tf_op jit(solution)/shard_map/ppermute | solution.py:20
  43.9 11.3 %collective-permute-start.24 = (bf16[176,384]{1,0:T(8,128)(2,1)S(1)}, bf16[176,384]{1,0:T(8,128)(2,1)S(1)}, u32[]{:S(2)}, u32[]{:S(2)}) collective-permute-start(bf16[176,384]{1,0:T(8,128)(2,1)S(1)} %collective-permute-done.23), channel_id=1, source_target_pairs={{0,2},{1,3},{2,0},{3,1},{4,6},{5,7},{6,4},{7,5},{8,10},{9,11},{10,... | collective-permute-start | bytes 405512 | tf_op jit(solution)/shard_map/ppermute | solution.py:20
  47.5 12.2 %collective-permute-start.5 = (f32[128,256]{1,0:T(8,128)S(1)}, f32[128,256]{1,0:T(8,128)}, u32[]{:S(2)}, u32[]{:S(2)}) collective-permute-start(f32[128,256]{1,0:T(8,128)S(1)} %fusion.40), channel_id=1, source_target_pairs={{0,1},{1,0},{2,3},{3,2},{4,5},{5,4},{6,7},{7,6},{8,9},{9,8},{10,11... | collective-permute-start | bytes 393224 | tf_op jit(solution)/shard_map/ppermute | solution.py:20
  47.7 11.4 %collective-permute-start.3 = (f32[128,256]{1,0:T(8,128)S(1)}, f32[128,256]{1,0:T(8,128)}, u32[]{:S(2)}, u32[]{:S(2)}) collective-permute-start(f32[128,256]{1,0:T(8,128)S(1)} %fusion.40), channel_id=1, source_target_pairs={{0,2},{1,3},{2,0},{3,1},{4,6},{5,7},{6,4},{7,5},{8,10},{9,11},{10,... | collective-permute-start | bytes 393224 | tf_op jit(solution)/shard_map/ppermute | solution.py:20
  55.2 5.5 %collective-permute-start.25 = (bf16[176,384]{1,0:T(8,128)(2,1)S(1)}, bf16[176,384]{1,0:T(8,128)(2,1)S(1)}, u32[]{:S(2)}, u32[]{:S(2)}) collective-permute-start(bf16[176,384]{1,0:T(8,128)(2,1)S(1)} %collective-permute-done.24), channel_id=1, source_target_pairs={{0,1},{1,0},{2,3},{3,2},{4,5},{5,4},{6,7},{7,6},{8,9},{9,8},{10,11... | collective-permute-start | bytes 405512 | tf_op jit(solution)/shard_map/ppermute | solution.py:20
  55.2 16.1 %collective-permute-start.14 = (bf16[352,384]{1,0:T(8,128)(2,1)}, bf16[352,384]{1,0:T(8,128)(2,1)S(1)}, u32[]{:S(2)}, u32[]{:S(2)}) collective-permute-start(bf16[352,384]{1,0:T(8,128)(2,1)} %collective-permute-done.13), channel_id=1, source_target_pairs={{0,1},{1,0},{2,3},{3,2},{4,5},{5,4},{6,7},{7,6},{8,9},{9,8},{10,11... | collective-permute-start | bytes 811016 | tf_op jit(solution)/shard_map/ppermute | solution.py:20
  59.1 20.3 %collective-permute-start.28 = (bf16[352,384]{1,0:T(8,128)(2,1)}, bf16[352,384]{1,0:T(8,128)(2,1)}, u32[]{:S(2)}, u32[]{:S(2)}) collective-permute-start(bf16[352,384]{1,0:T(8,128)(2,1)} %collective-permute-done.27), channel_id=1, source_target_pairs={{0,1},{1,0},{2,3},{3,2},{4,5},{5,4},{6,7},{7,6},{8,9},{9,8},{10,11... | collective-permute-start | bytes 811016 | tf_op jit(solution)/shard_map/ppermute | solution.py:20
  59.1 1.9 %collective-permute-start.4 = (f32[128,256]{1,0:T(8,128)}, f32[128,256]{1,0:T(8,128)S(1)}, u32[]{:S(2)}, u32[]{:S(2)}) collective-permute-start(f32[128,256]{1,0:T(8,128)} %collective-permute-done.3), channel_id=1, source_target_pairs={{0,1},{1,0},{2,3},{3,2},{4,5},{5,4},{6,7},{7,6},{8,9},{9,8},{10,11... | collective-permute-start | bytes 393224 | tf_op jit(solution)/shard_map/ppermute | solution.py:20
  63.1 4.3 %collective-permute-start.9 = (bf16[32,1024]{1,0:T(8,128)(2,1)S(1)}, bf16[32,1024]{1,0:T(8,128)(2,1)S(1)}, u32[]{:S(2)}, u32[]{:S(2)}) collective-permute-start(bf16[32,1024]{1,0:T(8,128)(2,1)S(1)} %get-tuple-element.4), channel_id=1, source_target_pairs={{0,4},{4,0},{8,12},{12,8},{16,20},{20,16},{24,28},{28,24},{1,5},{5... | collective-permute-start | bytes 196616 | tf_op jit(solution)/shard_map/ppermute | solution.py:20
  68.0 42.9 %collective-permute-start.12 = (bf16[64,1024]{1,0:T(8,128)(2,1)}, bf16[64,1024]{1,0:T(8,128)(2,1)}, u32[]{:S(2)}, u32[]{:S(2)}) collective-permute-start(bf16[64,1024]{1,0:T(8,128)(2,1)} %pad_maximum_fusion.2), channel_id=1, source_target_pairs={{0,24},{4,28},{8,0},{12,4},{16,8},{20,12},{24,16},{28,20},{1,25},{... | collective-permute-start | bytes 393224 | tf_op jit(solution)/shard_map/ppermute | solution.py:25
  70.1 37.8 %collective-permute-start.11 = (bf16[64,1024]{1,0:T(8,128)(2,1)}, bf16[64,1024]{1,0:T(8,128)(2,1)}, u32[]{:S(2)}, u32[]{:S(2)}) collective-permute-start(bf16[64,1024]{1,0:T(8,128)(2,1)} %pad_maximum_fusion.2), channel_id=1, source_target_pairs={{0,16},{4,20},{8,24},{12,28},{16,0},{20,4},{24,8},{28,12},{1,17},{... | collective-permute-start | bytes 393224 | tf_op jit(solution)/shard_map/ppermute | solution.py:25
  70.1 35.6 %collective-permute-start.10 = (bf16[64,1024]{1,0:T(8,128)(2,1)}, bf16[64,1024]{1,0:T(8,128)(2,1)}, u32[]{:S(2)}, u32[]{:S(2)}) collective-permute-start(bf16[64,1024]{1,0:T(8,128)(2,1)} %pad_maximum_fusion.2), channel_id=1, source_target_pairs={{0,8},{4,12},{8,16},{12,20},{16,24},{20,28},{24,0},{28,4},{1,9},{5... | collective-permute-start | bytes 393224 | tf_op jit(solution)/shard_map/ppermute | solution.py:25
  72.5 8.3 %slice-start = ((s8[4325376]{0:T(1024)(128)(4,1)}), s8[4194304]{0:T(1024)(128)(4,1)S(1)}, s32[]{:S(2)}) async-start(s8[4325376]{0:T(1024)(128)(4,1)} %bitcast.108), calls=%async_computation | async-start | bytes 8388608
  72.8 7.9 %copy-start.7 = (bf16[704,384]{1,0:T(8,128)(2,1)S(1)}, bf16[704,384]{1,0:T(8,128)(2,1)}, u32[]{:S(2)}) copy-start(bf16[704,384]{1,0:T(8,128)(2,1)} %maximum_select_fusion.9) | copy-start | bytes 1622020
  72.9 7.9 %slice-start.1 = ((s8[4325376]{0:T(1024)(128)(4,1)}), s8[131072]{0:T(1024)(128)(4,1)S(1)}, s32[]{:S(2)}) async-start(s8[4325376]{0:T(1024)(128)(4,1)} %bitcast.108), calls=%async_computation.1 | async-start | bytes 262144
  88.1 8.5 %copy-start.2 = (bf16[352,64,6]{0,2,1:T(8,128)(2,1)S(1)}, bf16[352,64,6]{0,2,1:T(8,128)(2,1)}, u32[]{:S(2)}) copy-start(bf16[352,64,6]{0,2,1:T(8,128)(2,1)} %concatenate.211) | copy-start | bytes 811012
  88.1 8.5 %copy-start.3 = (bf16[352,64,6]{0,2,1:T(8,128)(2,1)S(1)}, bf16[352,64,6]{0,2,1:T(8,128)(2,1)}, u32[]{:S(2)}) copy-start(bf16[352,64,6]{0,2,1:T(8,128)(2,1)} %concatenate.210) | copy-start | bytes 811012
  88.1 8.5 %copy-start.4 = (bf16[352,64,6]{0,2,1:T(8,128)(2,1)S(1)}, bf16[352,64,6]{0,2,1:T(8,128)(2,1)}, u32[]{:S(2)}) copy-start(bf16[352,64,6]{0,2,1:T(8,128)(2,1)} %concatenate.206) | copy-start | bytes 811012
  94.5 34.4 %collective-permute-start.34 = (bf16[384,384]{1,0:T(8,128)(2,1)}, bf16[384,384]{1,0:T(8,128)(2,1)}, u32[]{:S(2)}, u32[]{:S(2)}) collective-permute-start(bf16[384,384]{1,0:T(8,128)(2,1)} %fusion.8), channel_id=1, source_target_pairs={{0,4},{4,0},{8,12},{12,8},{16,20},{20,16},{24,28},{28,24},{1,5},{5... | collective-permute-start | bytes 884744 | tf_op jit(solution)/shard_map/ppermute | solution.py:20
  95.0 31.5 %collective-permute-start.38 = (bf16[384,384]{1,0:T(8,128)(2,1)}, bf16[384,384]{1,0:T(8,128)(2,1)}, u32[]{:S(2)}, u32[]{:S(2)}) collective-permute-start(bf16[384,384]{1,0:T(8,128)(2,1)} %fusion.9), channel_id=1, source_target_pairs={{0,4},{4,0},{8,12},{12,8},{16,20},{20,16},{24,28},{28,24},{1,5},{5... | collective-permute-start | bytes 884744 | tf_op jit(solution)/shard_map/ppermute | solution.py:20
  102.9 2.7 %copy-start.11 = (bf16[384,384]{1,0:T(8,128)(2,1)S(1)}, bf16[384,384]{1,0:T(8,128)(2,1)}, u32[]{:S(2)}) copy-start(bf16[384,384]{1,0:T(8,128)(2,1)} %fusion.10) | copy-start | bytes 884740
  105.7 18.8 %collective-permute-start.42 = (bf16[384,384]{1,0:T(8,128)(2,1)S(1)}, bf16[384,384]{1,0:T(8,128)(2,1)S(1)}, u32[]{:S(2)}, u32[]{:S(2)}) collective-permute-start(bf16[384,384]{1,0:T(8,128)(2,1)S(1)} %copy-done.11), channel_id=1, source_target_pairs={{0,4},{4,0},{8,12},{12,8},{16,20},{20,16},{24,28},{28,24},{1,5},{5... | collective-permute-start | bytes 884744 | tf_op jit(solution)/shard_map/ppermute | solution.py:20
  107.8 13.2 %copy-start.6 = (bf16[704,384]{1,0:T(8,128)(2,1)S(1)}, bf16[704,384]{1,0:T(8,128)(2,1)}, u32[]{:S(2)}) copy-start(bf16[704,384]{1,0:T(8,128)(2,1)} %maximum_select_fusion.7) | copy-start | bytes 1622020
  107.8 13.2 %copy-start.12 = (bf16[384,384]{1,0:T(8,128)(2,1)S(1)}, bf16[384,384]{1,0:T(8,128)(2,1)}, u32[]{:S(2)}) copy-start(bf16[384,384]{1,0:T(8,128)(2,1)} %fusion.11) | copy-start | bytes 884740
  107.8 13.2 %collective-permute-start.46 = (bf16[384,384]{1,0:T(8,128)(2,1)}, bf16[384,384]{1,0:T(8,128)(2,1)S(1)}, u32[]{:S(2)}, u32[]{:S(2)}) collective-permute-start(bf16[384,384]{1,0:T(8,128)(2,1)} %fusion.11), channel_id=1, source_target_pairs={{0,4},{4,0},{8,12},{12,8},{16,20},{20,16},{24,28},{28,24},{1,5},{5... | collective-permute-start | bytes 884744 | tf_op jit(solution)/shard_map/ppermute | solution.py:20
  111.0 21.4 %collective-permute-start.16 = (f32[64,1408]{1,0:T(8,128)S(1)}, f32[64,1408]{1,0:T(8,128)S(1)}, u32[]{:S(2)}, u32[]{:S(2)}) collective-permute-start(f32[64,1408]{1,0:T(8,128)S(1)} %reduce_sum.103), channel_id=1, source_target_pairs={{0,1},{1,0},{2,3},{3,2},{4,5},{5,4},{6,7},{7,6},{8,9},{9,8},{10,11... | collective-permute-start | bytes 1081352 | tf_op jit(solution)/shard_map/ppermute | solution.py:20
  121.8 13.0 %collective-permute-start.47 = (bf16[176,384]{1,0:T(8,128)(2,1)S(1)}, bf16[176,384]{1,0:T(8,128)(2,1)S(1)}, u32[]{:S(2)}, u32[]{:S(2)}) collective-permute-start(bf16[176,384]{1,0:T(8,128)(2,1)S(1)} %get-tuple-element.16), channel_id=1, source_target_pairs={{0,8},{4,12},{8,16},{12,20},{16,24},{20,28},{24,0},{28,4},{1,9},{5... | collective-permute-start | bytes 405512 | tf_op jit(solution)/shard_map/ppermute | solution.py:25
  124.5 10.9 %collective-permute-start.49 = (bf16[176,384]{1,0:T(8,128)(2,1)S(1)}, bf16[176,384]{1,0:T(8,128)(2,1)S(1)}, u32[]{:S(2)}, u32[]{:S(2)}) collective-permute-start(bf16[176,384]{1,0:T(8,128)(2,1)S(1)} %get-tuple-element.17), channel_id=1, source_target_pairs={{0,24},{4,28},{8,0},{12,4},{16,8},{20,12},{24,16},{28,20},{1,25},{... | collective-permute-start | bytes 405512 | tf_op jit(solution)/shard_map/ppermute | solution.py:25
  126.5 18.6 %collective-permute-start.48 = (bf16[176,384]{1,0:T(8,128)(2,1)S(1)}, bf16[176,384]{1,0:T(8,128)(2,1)S(1)}, u32[]{:S(2)}, u32[]{:S(2)}) collective-permute-start(bf16[176,384]{1,0:T(8,128)(2,1)S(1)} %get-tuple-element.18), channel_id=1, source_target_pairs={{0,16},{4,20},{8,24},{12,28},{16,0},{20,4},{24,8},{28,12},{1,17},{... | collective-permute-start | bytes 405512 | tf_op jit(solution)/shard_map/ppermute | solution.py:25
  128.9 16.3 %collective-permute-start.43 = (bf16[176,384]{1,0:T(8,128)(2,1)S(1)}, bf16[176,384]{1,0:T(8,128)(2,1)S(1)}, u32[]{:S(2)}, u32[]{:S(2)}) collective-permute-start(bf16[176,384]{1,0:T(8,128)(2,1)S(1)} %get-tuple-element.13), channel_id=1, source_target_pairs={{0,8},{4,12},{8,16},{12,20},{16,24},{20,28},{24,0},{28,4},{1,9},{5... | collective-permute-start | bytes 405512 | tf_op jit(solution)/shard_map/ppermute | solution.py:25
  132.4 19.2 %collective-permute-start.45 = (bf16[176,384]{1,0:T(8,128)(2,1)S(1)}, bf16[176,384]{1,0:T(8,128)(2,1)S(1)}, u32[]{:S(2)}, u32[]{:S(2)}) collective-permute-start(bf16[176,384]{1,0:T(8,128)(2,1)S(1)} %get-tuple-element.14), channel_id=1, source_target_pairs={{0,24},{4,28},{8,0},{12,4},{16,8},{20,12},{24,16},{28,20},{1,25},{... | collective-permute-start | bytes 405512 | tf_op jit(solution)/shard_map/ppermute | solution.py:25
  134.8 21.5 %collective-permute-start.44 = (bf16[176,384]{1,0:T(8,128)(2,1)S(1)}, bf16[176,384]{1,0:T(8,128)(2,1)S(1)}, u32[]{:S(2)}, u32[]{:S(2)}) collective-permute-start(bf16[176,384]{1,0:T(8,128)(2,1)S(1)} %get-tuple-element.15), channel_id=1, source_target_pairs={{0,16},{4,20},{8,24},{12,28},{16,0},{20,4},{24,8},{28,12},{1,17},{... | collective-permute-start | bytes 405512 | tf_op jit(solution)/shard_map/ppermute | solution.py:25
  135.5 21.5 %collective-permute-start.39 = (bf16[176,384]{1,0:T(8,128)(2,1)S(1)}, bf16[176,384]{1,0:T(8,128)(2,1)S(1)}, u32[]{:S(2)}, u32[]{:S(2)}) collective-permute-start(bf16[176,384]{1,0:T(8,128)(2,1)S(1)} %get-tuple-element.10), channel_id=1, source_target_pairs={{0,8},{4,12},{8,16},{12,20},{16,24},{20,28},{24,0},{28,4},{1,9},{5... | collective-permute-start | bytes 405512 | tf_op jit(solution)/shard_map/ppermute | solution.py:25
  145.1 11.9 %collective-permute-start.41 = (bf16[176,384]{1,0:T(8,128)(2,1)S(1)}, bf16[176,384]{1,0:T(8,128)(2,1)S(1)}, u32[]{:S(2)}, u32[]{:S(2)}) collective-permute-start(bf16[176,384]{1,0:T(8,128)(2,1)S(1)} %get-tuple-element.11), channel_id=1, source_target_pairs={{0,24},{4,28},{8,0},{12,4},{16,8},{20,12},{24,16},{28,20},{1,25},{... | collective-permute-start | bytes 405512 | tf_op jit(solution)/shard_map/ppermute | solution.py:25
  145.2 19.7 %collective-permute-start.40 = (bf16[176,384]{1,0:T(8,128)(2,1)S(1)}, bf16[176,384]{1,0:T(8,128)(2,1)S(1)}, u32[]{:S(2)}, u32[]{:S(2)}) collective-permute-start(bf16[176,384]{1,0:T(8,128)(2,1)S(1)} %get-tuple-element.12), channel_id=1, source_target_pairs={{0,16},{4,20},{8,24},{12,28},{16,0},{20,4},{24,8},{28,12},{1,17},{... | collective-permute-start | bytes 405512 | tf_op jit(solution)/shard_map/ppermute | solution.py:25
  151.6 14.3 %collective-permute-start.35 = (bf16[176,384]{1,0:T(8,128)(2,1)S(1)}, bf16[176,384]{1,0:T(8,128)(2,1)S(1)}, u32[]{:S(2)}, u32[]{:S(2)}) collective-permute-start(bf16[176,384]{1,0:T(8,128)(2,1)S(1)} %get-tuple-element.7), channel_id=1, source_target_pairs={{0,8},{4,12},{8,16},{12,20},{16,24},{20,28},{24,0},{28,4},{1,9},{5... | collective-permute-start | bytes 405512 | tf_op jit(solution)/shard_map/ppermute | solution.py:25
  156.3 8.7 %collective-permute-start.17 = (f32[64,1408]{1,0:T(8,128)S(1)}, f32[64,1408]{1,0:T(8,128)S(1)}, u32[]{:S(2)}, u32[]{:S(2)}) collective-permute-start(f32[64,1408]{1,0:T(8,128)S(1)} %add.213), channel_id=1, source_target_pairs={{0,2},{1,3},{2,0},{3,1},{4,6},{5,7},{6,4},{7,5},{8,10},{9,11},{10,... | collective-permute-start | bytes 1081352 | tf_op jit(solution)/shard_map/ppermute | solution.py:20
  157.0 9.0 %collective-permute-start.37 = (bf16[176,384]{1,0:T(8,128)(2,1)S(1)}, bf16[176,384]{1,0:T(8,128)(2,1)S(1)}, u32[]{:S(2)}, u32[]{:S(2)}) collective-permute-start(bf16[176,384]{1,0:T(8,128)(2,1)S(1)} %get-tuple-element.8), channel_id=1, source_target_pairs={{0,24},{4,28},{8,0},{12,4},{16,8},{20,12},{24,16},{28,20},{1,25},{... | collective-permute-start | bytes 405512 | tf_op jit(solution)/shard_map/ppermute | solution.py:25
  157.0 13.7 %collective-permute-start.36 = (bf16[176,384]{1,0:T(8,128)(2,1)S(1)}, bf16[176,384]{1,0:T(8,128)(2,1)S(1)}, u32[]{:S(2)}, u32[]{:S(2)}) collective-permute-start(bf16[176,384]{1,0:T(8,128)(2,1)S(1)} %get-tuple-element.9), channel_id=1, source_target_pairs={{0,16},{4,20},{8,24},{12,28},{16,0},{20,4},{24,8},{28,12},{1,17},{... | collective-permute-start | bytes 405512 | tf_op jit(solution)/shard_map/ppermute | solution.py:25
  165.3 5.6 %collective-permute-start.20 = (f32[64,256]{1,0:T(8,128)S(1)}, f32[64,256]{1,0:T(8,128)S(1)}, u32[]{:S(2)}, u32[]{:S(2)}) collective-permute-start(f32[64,256]{1,0:T(8,128)S(1)} %fusion.57), channel_id=1, source_target_pairs={{0,1},{1,0},{2,3},{3,2},{4,5},{5,4},{6,7},{7,6},{8,9},{9,8},{10,11... | collective-permute-start | bytes 196616 | tf_op jit(solution)/shard_map/ppermute | solution.py:20
  165.3 5.4 %collective-permute-start.18 = (f32[64,256]{1,0:T(8,128)S(1)}, f32[64,256]{1,0:T(8,128)S(1)}, u32[]{:S(2)}, u32[]{:S(2)}) collective-permute-start(f32[64,256]{1,0:T(8,128)S(1)} %fusion.57), channel_id=1, source_target_pairs={{0,2},{1,3},{2,0},{3,1},{4,6},{5,7},{6,4},{7,5},{8,10},{9,11},{10,... | collective-permute-start | bytes 196616 | tf_op jit(solution)/shard_map/ppermute | solution.py:20
  170.8 1.3 collective-permute-start.19
  173.7 2.0 %copy-start.8 = (bf16[64,1024]{1,0:T(8,128)(2,1)S(1)}, bf16[64,1024]{1,0:T(8,128)(2,1)}, u32[]{:S(2)}) copy-start(bf16[64,1024]{1,0:T(8,128)(2,1)} %gather_fusion) | copy-start | bytes 393220
  173.7 1.3 collective-permute-start.21
  175.1 3.6 %collective-permute-start.22 = (f32[192]{0:T(256)S(1)}, f32[192]{0:T(256)S(1)}, u32[]{:S(2)}, u32[]{:S(2)}) collective-permute-start(f32[192]{0:T(256)S(1)} %fusion.79), channel_id=1, source_target_pairs={{0,2},{1,3},{2,0},{3,1},{4,6},{5,7},{6,4},{7,5},{8,10},{9,11},{10,... | collective-permute-start | bytes 2312 | tf_op jit(solution)/shard_map/ppermute | solution.py:20
  (1 other events, 1.3 us)

commit v2 on v1

--- a/solution.py
+++ b/solution.py
@@ -1,6 +1,10 @@
+import functools
+
 import jax
 import jax.numpy as jnp
 from jax import lax
+from jax.experimental import pallas as pl
+from jax.experimental.pallas import tpu as pltpu
 from jax.sharding import PartitionSpec as P
 
 logit_scale = 64.0
@@ -203,6 +207,395 @@
     return (ref_loss, learnability, grad_up)
 
 
+def dot_f32(a, b):
+    return jnp.dot(a, b, preferred_element_type=f32)
+
+
+def dot_rows(a, b):
+    return lax.dot_general(a, b, (((1,), (1,)), ((), ())), preferred_element_type=f32)
+
+
+def dot_cols(a, b):
+    return lax.dot_general(a, b, (((0,), (0,)), ((), ())), preferred_element_type=f32)
+
+
+def group_mask(n_items, n_patch):
+    shape = (n_items, n_items * n_patch)
+    row = lax.broadcasted_iota(jnp.int32, shape, 1)
+    first = n_patch * lax.broadcasted_iota(jnp.int32, shape, 0)
+    return (row >= first) & (row < first + n_patch), row - first
+
+
+def as_row(column):
+    n = column.shape[0]
+    return jnp.broadcast_to(column, (n, n)).T[0:1]
+
+
+def place(index, length):
+    return pl.ds(pl.multiple_of(index * length, length), length)
+
+
+def call(body, out_shape, cost, grid=(), **kwargs):
+    flops, moved = cost
+    return pl.pallas_call(
+        body,
+        out_shape=out_shape,
+        grid=grid,
+        cost_estimate=pl.CostEstimate(flops=flops, bytes_accessed=moved, transcendentals=0),
+        compiler_params=pltpu.CompilerParams(vmem_limit_bytes=40 * 2**20),
+        **kwargs,
+    )
+
+
+def struct(shape, dtype):
+    return jax.ShapeDtypeStruct(shape, dtype)
+
+
+def pick_body(n_patch, patches, kept, dest, tok, half, pool, counts):
+    d_part, n_all = patches.shape
+    ex_dev = n_all // n_patch
+    k_dev = kept.shape[1]
+    member, offset = group_mask(k_dev, n_patch)
+    expand = member.astype(bf16)
+    index = jnp.broadcast_to(kept[...].astype(f32), (8, k_dev)).astype(bf16)
+    base = dot_f32(index, expand)[0:1].astype(jnp.int32)
+    row = base * n_patch + jnp.sum(jnp.where(member, offset, 0), axis=0, keepdims=True)
+    pick = (lax.broadcasted_iota(jnp.int32, (n_all, row.shape[1]), 0) == row).astype(bf16)
+    values = patches[...]
+    tok[...] = dot_f32(values, pick).astype(bf16)
+    other = 1 - lax.rem(lax.axis_index("sel"), 2)
+    half[...] = tok[place(other, d_part // 2), :]
+    groups, _ = group_mask(ex_dev, n_patch)
+    pool[...] = (dot_rows(values, groups.astype(bf16)) * (1.0 / n_patch)).astype(bf16)
+    shards = lax.broadcasted_iota(jnp.int32, (128, k_dev), 0) == dest[...]
+    counts[...] = dot_rows(jnp.ones((8, k_dev), bf16), shards.astype(bf16))
+
+
+def text_body(t0, t1, t2, t3, hat, share, whole):
+    me = lax.axis_index("mdl")
+    width = t0.shape[1]
+    for j, piece in enumerate((t0, t1, t2, t3)):
+        whole[:, place(me ^ j, width)] = piece[...].astype(f32)
+    values = whole[...]
+    norm_sq = jnp.sum(values * values, axis=1, keepdims=True)
+    hat[...] = (values * lax.rsqrt(norm_sq + eps)).astype(bf16)
+    share[...] = hat[place(me, share.shape[0]), :]
+
+
+def forward_body(n_patch, n_mdl, t0, t1, t2, t3, w_up, w_down, slope, mixed, tok_full, tok):
+    d_part, n_rows = t0.shape
+    k_dev = n_rows // n_patch
+    member, _ = group_mask(k_dev, n_patch)
+    groups = member.astype(bf16)
+
+    @pl.when(pl.program_id(0) == 0)
+    def _():
+        me = lax.axis_index("mdl")
+        for j, piece in enumerate((t0, t1, t2, t3)):
+            tok_full[place(me ^ j, d_part), :] = piece[...]
+        tok[...] = tok_full[...].T
+        mixed[...] = dot_f32(groups, tok[...]) * (1.0 / n_mdl)
+
+    pre_act = dot_f32(tok[...], w_up[...])
+    activated, gelu_slope = gelu_parts(pre_act)
+    slope[...] = gelu_slope
+    pooled = dot_f32(groups, activated.astype(bf16))
+    high = pooled.astype(bf16)
+    low = (pooled - high.astype(f32)).astype(bf16)
+    both = dot_f32(jnp.concatenate([high, low], axis=0), w_down[...])
+    mixed[...] += both[:k_dev] + both[k_dev:]
+
+
+def weigh_body(n_patch, c0, c1, c2, c3, n0, n1, n2, n3, dest, w_down, slope, weighted, pre, cot):
+    d_part, n_rows = c0.shape
+    k_dev = n_rows // n_patch
+    member, _ = group_mask(k_dev, n_patch)
+    counts = (n0[...] + n1[...]) + (n2[...] + n3[...])
+    shards = lax.broadcasted_iota(jnp.int32, (128, k_dev), 0) == dest[...]
+    named = dot_f32(counts.astype(bf16), shards.astype(bf16))
+    weight = 1.0 / dot_f32(named.astype(bf16), member.astype(bf16))[0:1]
+    me = lax.axis_index("mdl")
+    for j, piece in enumerate((c0, c1, c2, c3)):
+        cot[place(me ^ j, d_part), :] = (piece[...].astype(f32) * weight).astype(bf16)
+    weighted[...] = cot[...].T
+    pre[...] = (dot_rows(weighted[...], w_down[...]) * slope[...]).astype(bf16)
+
+
+def backward_body(weighted, w_down, slope, pre):
+    pre[...] = (dot_rows(weighted[...], w_down[...]) * slope[...]).astype(bf16)
+
+
+def send_blocks(part, own, sends):
+    blk = own.shape[0]
+    own[...] = part[:blk]
+    for r, block in enumerate(sends):
+        block[...] = part[(r + 1) * blk : (r + 2) * blk].astype(bf16)
+
+
+def first_grad_body(n_high, tok_full, h0, h1, h2, h3, pre, pre_pair, pair, own, *sends):
+    n_rows = tok_full.shape[1]
+    blk = own.shape[0]
+    me = lax.axis_index("mdl")
+    sel = lax.axis_index("sel")
+    parity, high = lax.rem(sel, 2), lax.div(sel, 2)
+    for j, piece in enumerate((h0, h1, h2, h3)):
+        block = me ^ j
+        rows = place(lax.rem(block + n_high - high, n_high), blk)
+        pair[rows, 0:n_rows] = tok_full[place(2 * block + parity, blk), :]
+        pair[rows, n_rows:] = piece[:, 0:n_rows]
+    part = dot_f32(pair[:, 0:n_rows], pre[...]) + dot_f32(pair[:, n_rows:], pre_pair[...])
+    send_blocks(part, own, sends)
+
+
+def grad_body(pair, pre, pre_pair, own, *sends):
+    n_rows = pre.shape[0]
+    part = dot_f32(pair[:, 0:n_rows], pre[...]) + dot_f32(pair[:, n_rows:], pre_pair[...])
+    send_blocks(part, own, sends)
+
+
+def image_body(h0, h1, h2, h3, ref_proj, emb, pooled):
+    me = lax.axis_index("mdl")
+    n_rows = h0.shape[0]
+    n_ex = pooled.shape[1]
+    first = h0.shape[1] - 2 * n_ex
+    for j, piece in enumerate((h0, h1, h2, h3)):
+        for part in range(2):
+            pooled[place((me ^ j) * 2 + part, n_rows), :] = piece[
+                :, first + part * n_ex : first + (part + 1) * n_ex
+            ]
+    emb[...] = dot_cols(pooled[...], ref_proj[...])
+
+
+def normed(pieces, whole):
+    me = lax.axis_index("mdl")
+    width = pieces[0].shape[1]
+    for j, piece in enumerate(pieces):
+        whole[:, place(me ^ j, width)] = piece[...]
+    values = whole[...]
+    norm_sq = jnp.sum(values * values, axis=1, keepdims=True)
+    return (values * lax.rsqrt(norm_sq + eps)).astype(bf16)
+
+
+def share_totals(hat, shares):
+    total = None
+    for share in shares:
+        scores = dot_rows(share[...], hat)
+        part = jnp.sum(jnp.exp(logit_scale * scores), axis=0, keepdims=True)
+        total = part if total is None else total + part
+    return total
+
+
+def own_score(hat, texts):
+    return jnp.sum(hat.astype(f32) * texts.astype(f32), axis=1, keepdims=True)
+
+
+def image_loss_body(e0, e1, e2, e3, text_hat, s0, s1, s2, s3, s4, own, total, whole):
+    hat = normed((e0, e1, e2, e3), whole)
+    own[...] = as_row(own_score(hat, text_hat[...]))
+    total[...] = share_totals(hat, (s0, s1, s2, s3, s4))
+
+
+def learn_head_body(n_patch, a, b, ref_proj, emb):
+    learn_pool = ((a[...] + b[...]) * (1.0 / n_patch)).astype(bf16)
+    emb[...] = dot_f32(learn_pool, ref_proj[...])
+
+
+def learn_loss_body(
+    e0, e1, e2, e3, text_hat, kept, s0, s1, s2, s3, s4, ref_total, own, totals, whole
+):
+    hat = normed((e0, e1, e2, e3), whole)
+    k_dev, ex_dev = kept.shape[1], text_hat.shape[0]
+    pick = (lax.broadcasted_iota(jnp.int32, (ex_dev, k_dev), 0) == kept[...]).astype(bf16)
+    kept_text = dot_cols(pick, text_hat[...])
+    own[...] = as_row(own_score(hat, kept_text))
+    totals[...] = jnp.zeros_like(totals)
+    totals[:, 0:ex_dev] = ref_total[...]
+    totals[:, ex_dev : ex_dev + k_dev] = share_totals(hat, (s0, s1, s2, s3, s4))
+
+
+def losses_body(a, b, ref_own, own, kept, ref_loss, learnability):
+    totals = a[...] + b[...]
+    k_dev, ex_dev = kept.shape[1], ref_own.shape[1]
+    losses = jnp.log(totals[:, 0:ex_dev]) - logit_scale * ref_own[...]
+    ref_loss[...] = losses
+    learner = jnp.log(totals[:, ex_dev : ex_dev + k_dev]) - logit_scale * own[...]
+    column = as_row_t(losses)
+    pick = lax.broadcasted_iota(jnp.int32, (ex_dev, k_dev), 0) == kept[...]
+    picked = jnp.sum(jnp.where(pick, column, 0.0), axis=0, keepdims=True)
+    learnability[...] = learner - picked
+
+
+def as_row_t(row):
+    n = row.shape[1]
+    return jnp.broadcast_to(row, (n, n)).T[:, 0:1]
+
+
+def quarter_sel(patches, text, ref_proj, w_up, w_down, kept_index, dest, cotan):
+    n_mdl, n_sel = lax.axis_size("mdl"), lax.axis_size("sel")
+    n_high = n_sel // 2
+    ex_dev, emb_part = text.shape
+    d_part = patches.shape[1]
+    d_full = d_part * n_mdl
+    n_patch = patches.shape[0] // ex_dev
+    k_dev = kept_index.shape[0]
+    n_rows = k_dev * n_patch
+    ff_dev = w_up.shape[1]
+    blk = d_full // n_sel
+    kept_row = kept_index.reshape(1, k_dev)
+    dest_row = dest.reshape(1, k_dev)
+    cot_t = cotan.T
+
+    tok, half, pool, counts = call(
+        functools.partial(pick_body, n_patch),
+        (
+            struct((d_part, n_rows), bf16),
+            struct((d_part // 2, n_rows), bf16),
+            struct((d_part, ex_dev), bf16),
+            struct((8, 128), f32),
+        ),
+        (2 * d_part * ex_dev * n_patch * n_rows, 2 * 2**20),
+    )(patches.T, kept_row, dest_row)
+
+    tok_pieces = mdl_pieces(tok)
+    half_pair = swap(half, "sel", 1)
+    pair_counts = counts + swap(counts, "sel", 1)
+    all_counts = [pair_counts] + [rotate_pairs(pair_counts, s) for s in range(1, n_high)]
+    cot_pieces = mdl_pieces(cot_t)
+    text_pieces = mdl_pieces(text)
+
+    text_hat, text_share = call(
+        text_body,
+        (struct((ex_dev, emb_part * n_mdl), bf16), struct((ex_dev // n_mdl, emb_part * n_mdl), bf16)),
+        (2**20, 2**20),
+        scratch_shapes=[pltpu.VMEM((ex_dev, emb_part * n_mdl), f32)],
+    )(*text_pieces)
+    share_pair = swap(text_share, "sel", 1)
+    two_shares = jnp.concatenate([text_share, share_pair], axis=0)
+    shares = [text_share, share_pair] + [rotate_pairs(two_shares, s) for s in range(1, n_high)]
+
+    extras = jnp.concatenate(
+        [half_pair, pool[: d_part // 2], pool[d_part // 2 :]], axis=1
+    )
+    extra_pieces = mdl_pieces(extras)
+
+    width = 512
+    whole = lambda shape: pl.BlockSpec(shape, lambda i: (0,) * len(shape))
+    slope, mixed, tok_full = call(
+        functools.partial(forward_body, n_patch, n_mdl),
+        (
+            struct((n_rows, ff_dev), f32),
+            struct((k_dev, d_full), f32),
+            struct((d_full, n_rows), bf16),
+        ),
+        (4 * n_rows * d_full * ff_dev, 12 * 2**20),
+        grid=(ff_dev // width,),
+        in_specs=[whole((d_part, n_rows))] * 4
+        + [
+            pl.BlockSpec((d_full, width), lambda i: (0, i)),
+            pl.BlockSpec((width, d_full), lambda i: (i, 0)),
+        ],
+        out_specs=[
+            pl.BlockSpec((n_rows, width), lambda i: (0, i)),
+            whole((k_dev, d_full)),
+            whole((d_full, n_rows)),
+        ],
+        scratch_shapes=[pltpu.VMEM((n_rows, d_full), bf16)],
+    )(*tok_pieces, w_up, w_down)
+
+    widths = (256, 256, 512, 512)
+    starts = [sum(widths[:c]) for c in range(len(widths))]
+
+    def chunk_specs(c):
+        first, size = starts[c] // widths[c], widths[c]
+        return [
+            pl.BlockSpec((size, d_full), lambda i: (first, 0)),
+            pl.BlockSpec((n_rows, size), lambda i: (0, first)),
+        ]
+
+    pres = []
+    for c, size in enumerate(widths):
+        cost = (2 * n_rows * d_full * size, (d_full * (size + n_rows) * 2 + n_rows * size * 6))
+        pre_struct = struct((n_rows, size), bf16)
+        if c == 0:
+            weighted, pre = call(
+                functools.partial(weigh_body, n_patch),
+                (struct((n_rows, d_full), bf16), pre_struct),
+                cost,
+                grid=(1,),
+                in_specs=[whole((d_part, n_rows))] * 4
+                + [whole((8, 128))] * 4
+                + [whole((1, k_dev))]
+                + chunk_specs(c),
+                out_specs=[whole((n_rows, d_full)), whole((n_rows, size))],
+                scratch_shapes=[pltpu.VMEM((d_full, n_rows), bf16)],
+            )(*cot_pieces, *all_counts, dest_row, w_down, slope)
+        else:
+            pre = call(
+                backward_body,
+                pre_struct,
+                cost,
+                grid=(1,),
+                in_specs=[whole((n_rows, d_full))] + chunk_specs(c),
+                out_specs=whole((n_rows, size)),
+            )(weighted, w_down, slope)
+        pres.append(pre)
+    pair_pres = [swap(pre, "sel", 1) for pre in pres]
+
+    outs = []
+    for c, size in enumerate(widths):
+        cost = (4 * n_rows * blk * n_high * size, 4 * 2**20)
+        blocks = (struct((blk, size), f32),) + (struct((blk, size), bf16),) * (n_high - 1)
+        if c == 0:
+            pair, *blocks = call(
+                functools.partial(first_grad_body, n_high),
+                (struct((blk * n_high, 2 * n_rows), bf16),) + blocks,
+                cost,
+            )(tok_full, *extra_pieces, pres[c], pair_pres[c])
+        else:
+            blocks = call(grad_body, blocks, cost)(pair, pres[c], pair_pres[c])
+        total = blocks[0]
+        for r in range(1, n_high):
+            total = total + rotate_pairs(blocks[r], r).astype(f32)
+        outs.append(total)
+    grad_up = jnp.concatenate(outs, axis=1)
+
+    emb_cost = (2 * ex_dev * d_full * emb_part, 2**20)
+    img_emb = call(
+        image_body,
+        struct((ex_dev, emb_part), f32),
+        emb_cost,
+        scratch_shapes=[pltpu.VMEM((d_full, ex_dev), bf16)],
+    )(*extra_pieces, ref_proj)
+    emb_full = emb_part * n_mdl
+    loss_cost = (2 * ex_dev * emb_full * ex_dev * n_sel // n_mdl, 2 * 2**20)
+    ref_own, ref_total = call(
+        image_loss_body,
+        (struct((1, ex_dev), f32), struct((1, ex_dev), f32)),
+        loss_cost,
+        scratch_shapes=[pltpu.VMEM((ex_dev, emb_full), f32)],
+    )(*mdl_pieces(img_emb), text_hat, *shares)
+
+    mixed = mixed + swap(mixed, "mdl", 1)
+    learn_emb = call(
+        functools.partial(learn_head_body, n_patch),
+        struct((k_dev, emb_part), f32),
+        (2 * k_dev * d_full * emb_part, 2**20),
+    )(mixed, swap(mixed, "mdl", 2), ref_proj)
+    learn_own, totals = call(
+        learn_loss_body,
+        (struct((1, k_dev), f32), struct((1, 2 * ex_dev), f32)),
+        loss_cost,
+        scratch_shapes=[pltpu.VMEM((k_dev, emb_full), f32)],
+    )(*mdl_pieces(learn_emb), text_hat, kept_row, *shares, ref_total)
+    totals = totals + swap(totals, "mdl", 1)
+    ref_loss, learnability = call(
+        losses_body,
+        (struct((1, ex_dev), f32), struct((1, k_dev), f32)),
+        (2**16, 2**16),
+    )(totals, swap(totals, "mdl", 2), ref_own, learn_own, kept_row)
+    return (ref_loss.reshape(ex_dev), learnability.reshape(k_dev), grad_up)
+
+
 def solution(mesh):
     in_specs = (
         P("sel", "mdl"),
@@ -215,6 +608,7 @@
         P("sel", "mdl"),
     )
     out_specs = (P("sel"), P("sel"), P("sel", "mdl"))
+    body = quarter_sel if (mesh.shape["sel"], mesh.shape["mdl"]) == (8, 4) else per_device
     return jax.shard_map(
-        per_device, mesh=mesh, in_specs=in_specs, out_specs=out_specs, check_vma=False
+        body, mesh=mesh, in_specs=in_specs, out_specs=out_specs, check_vma=False
     )

time: 181 us -> 118 us (0.65)
  matrix products: 29.9 us -> 0 us
  other arithmetic: 26.1 us -> 1.44 us
  Pallas kernels: 0 us -> 15.3 us
  local copies, waits for them, and re-layouts: 20.9 us -> 7.68 us
  starting transfers between devices: 52.6 us -> 39.7 us
  waiting for transfers between devices: 49.2 us -> 52.3 us
    dot_general x15 -> x0, matrix products: 29.9 us -> none  [the longest x1 6.51 us: per_device(): lax.dot_general(tok_full, w_up, (((0,), (0,)), ((), ())), preferred_eleme...]
    pallas_call x0 -> x16, Pallas kernels: none -> 15.3 us  [the longest x1 5.56 us: quarter_sel(): call(functools.partial(forward_body, n_patch, n_mdl), (struct((n_rows, ff...]
    ppermute x18, starting transfers between devices: 33.7 us -> 19.3 us  [rotate_pairs(): lax.ppermute(value, 'sel', [(i, (i + 2 * step) % size) for i in range(siz...]
    select_n x18 -> x0, other arithmetic: 12.5 us -> none  [the longest x17 11.8 us: in_order(): jnp.where(set_bit, jnp.concatenate([second, first], axis), jnp.concatenat...]
    ppermute x18, waiting for transfers between devices: 26.4 us -> 32.3 us  [rotate_pairs(): lax.ppermute(value, 'sel', [(i, (i + 2 * step) % size) for i in range(siz...]
    reduce_sum x9 -> x0, other arithmetic: 5.82 us -> none  [the longest x1 2.71 us: per_device(): mixed_pool = mdl_sum(jnp.sum(mixed.reshape(k_dev, n_patch, -1), axis=1))]
    div x1 -> x0, other arithmetic: 5 us -> none  [per_device(): row_weight = 1.0 / jnp.repeat(counts[dest], n_patch)]
    reshape x2 -> x0, local copies, waits for them, and re-layouts: 4.44 us -> none  [the longest x1 3.51 us: per_device(): mixed_pool = mdl_sum(jnp.sum(mixed.reshape(k_dev, n_patch, -1), axis=1))]
  transfers between devices with their start and end apart: 50 -> 47, of which waited for: 15 -> 18; matrix products, arithmetic and copies ran while one was open for 41% -> 1% of each run, Pallas kernels for 0% -> 12%
where the time goes in v2:
time: 118 us; the launch traced here: 117 us
  waiting for transfers between devices  52.3 us (44%)
  starting transfers between devices  39.7 us (34%)
  Pallas kernels  15.3 us (13%)
  local copies, waits for them, and re-layouts  7.68 us (7%)
  other arithmetic  1.44 us (1%)
    ppermute x18, waiting for transfers between devices, rotate_pairs(): lax.ppermute(value, 'sel', [(i, (i + 2 * step) % size) for i in range(siz...  32.3 us
    ppermute x29, starting transfers between devices, swap(): return lax.ppermute(value, axis, [(i, i ^ bit) for i in range(size)])  20.5 us
    ppermute x29, waiting for transfers between devices, swap(): return lax.ppermute(value, axis, [(i, i ^ bit) for i in range(size)])  19.9 us
    ppermute x18, starting transfers between devices, rotate_pairs(): lax.ppermute(value, 'sel', [(i, (i + 2 * step) % size) for i in range(siz...  19.3 us
    unnamed x23, local copies, waits for them, and re-layouts  7.67 us
    pallas_call x1, Pallas kernels, quarter_sel(): call(functools.partial(forward_body, n_patch, n_mdl), (struct((n_rows, ff...  5.56 us
  transfers between devices with their start and end apart: 47, of which 18 were waited for; matrix products, arithmetic and copies ran while one was open for 1% of the time, Pallas kernels for 12%

profile of v2, /device:TPU:0, one launch (start us, length us, event | category | flops | bytes accessed | tf_op | source)
XLA Modules:
  0.0 117.4 jit_solution(567340246653080685)
XLA Ops:
  0.6 0.6 copy-done.5
  1.3 0.7 copy-done.7
  1.9 1.0 copy-done.10
  3.0 0.8 shard_map.103
  3.8 3.0 %collective-permute-start.1 = (bf16[352,384]{1,0:T(8,128)(2,1)S(1)}, bf16[352,384]{1,0:T(8,128)(2,1)S(1)}, u32[]{:S(2)}, u32[]{:S(2)}) collective-permute-start(bf16[352,384]{1,0:T(8,128)(2,1)S(1)} %get-tuple-element.37.t0), channel_id=1, source_target_pairs={{0,2},{1,3},{2,0},{3,1},{4,6},{5,7},{6,4},{7,5},{8,10},{9,11},{10,... | collective-permute-start | bytes 811016 | tf_op jit(solution)/shard_map/ppermute | solution.py:24
  6.9 2.0 %collective-permute-start.27 = (f32[8,128]{1,0:T(8,128)S(1)}, f32[8,128]{1,0:T(8,128)S(1)}, u32[]{:S(2)}, u32[]{:S(2)}) collective-permute-start(f32[8,128]{1,0:T(8,128)S(1)} %get-tuple-element.50), channel_id=1, source_target_pairs={{0,4},{4,0},{8,12},{12,8},{16,20},{20,16},{24,28},{28,24},{1,5},{5... | collective-permute-start | bytes 12296 | tf_op jit(solution)/shard_map/ppermute | solution.py:24
  8.8 0.5 collective-permute-start.8
  9.3 1.1 collective-permute-done.27
  10.5 2.0 %collective-permute-start.15 = (bf16[176,384]{1,0:T(8,128)(2,1)S(1)}, bf16[176,384]{1,0:T(8,128)(2,1)S(1)}, u32[]{:S(2)}, u32[]{:S(2)}) collective-permute-start(bf16[176,384]{1,0:T(8,128)(2,1)S(1)} %get-tuple-element.41), channel_id=1, source_target_pairs={{0,4},{4,0},{8,12},{12,8},{16,20},{20,16},{24,28},{28,24},{1,5},{5... | collective-permute-start | bytes 405512 | tf_op jit(solution)/shard_map/ppermute | solution.py:24
  12.4 2.2 %collective-permute-done.9.t2 = bf16[128,256]{1,0:T(8,128)(2,1)S(1)} collective-permute-done((bf16[128,256]{1,0:T(8,128)(2,1)}, bf16[128,256]{1,0:T(8,128)(2,1)S(1)}, u32[]{:S(2)}, u32[]{:S(2)}) %collective-permute-start.9) | collective-permute-done | bytes 65568 | tf_op jit(solution)/shard_map/ppermute | solution.py:24
  14.7 0.5 collective-permute-start.2
  15.3 0.6 collective-permute-done.10.t3
  15.9 1.7 %collective-permute-start.25 = (bf16[352,384]{1,0:T(8,128)(2,1)}, bf16[352,384]{1,0:T(8,128)(2,1)S(1)}, u32[]{:S(2)}, u32[]{:S(2)}) collective-permute-start(bf16[352,384]{1,0:T(8,128)(2,1)} %bitcast.7), channel_id=1, source_target_pairs={{0,2},{1,3},{2,0},{3,1},{4,6},{5,7},{6,4},{7,5},{8,10},{9,11},{10,... | collective-permute-start | bytes 811016 | tf_op jit(solution)/shard_map/ppermute | solution.py:24
  17.7 0.8 copy-done.4
  18.7 1.6 %collective-permute-start.28 = (f32[8,128]{1,0:T(8,128)S(1)}, f32[8,128]{1,0:T(8,128)S(1)}, u32[]{:S(2)}, u32[]{:S(2)}) collective-permute-start(f32[8,128]{1,0:T(8,128)S(1)} %add.47.n0), channel_id=1, source_target_pairs={{0,8},{4,12},{8,16},{12,20},{16,24},{20,28},{24,0},{28,4},{1,9},{5... | collective-permute-start | bytes 12296 | tf_op jit(solution)/shard_map/ppermute | solution.py:29
  20.4 2.7 %collective-permute-start.29 = (f32[8,128]{1,0:T(8,128)S(1)}, f32[8,128]{1,0:T(8,128)S(1)}, u32[]{:S(2)}, u32[]{:S(2)}) collective-permute-start(f32[8,128]{1,0:T(8,128)S(1)} %add.47.n0), channel_id=1, source_target_pairs={{0,16},{4,20},{8,24},{12,28},{16,0},{20,4},{24,8},{28,12},{1,17},{... | collective-permute-start | bytes 12296 | tf_op jit(solution)/shard_map/ppermute | solution.py:29
  23.0 1.3 %collective-permute-start.30 = (f32[8,128]{1,0:T(8,128)S(1)}, f32[8,128]{1,0:T(8,128)S(1)}, u32[]{:S(2)}, u32[]{:S(2)}) collective-permute-start(f32[8,128]{1,0:T(8,128)S(1)} %add.47.n0), channel_id=1, source_target_pairs={{0,24},{4,28},{8,0},{12,4},{16,8},{20,12},{24,16},{28,20},{1,25},{... | collective-permute-start | bytes 12296 | tf_op jit(solution)/shard_map/ppermute | solution.py:29
  24.4 2.2 %copy-done = bf16[1536,1408]{1,0:T(8,128)(2,1)S(1)} copy-done((bf16[1536,1408]{1,0:T(8,128)(2,1)S(1)}, bf16[1536,1408]{1,0:T(8,128)(2,1)}, u32[]{:S(2)}) %copy-start) | copy-done | bytes 4325400
  26.6 2.2 %copy-done.9 = bf16[1408,1536]{1,0:T(8,128)(2,1)S(1)} copy-done((bf16[1408,1536]{1,0:T(8,128)(2,1)S(1)}, bf16[1408,1536]{1,0:T(8,128)(2,1)}, u32[]{:S(2)}) %copy-start.9) | copy-done | bytes 4325400
  28.8 5.6 %shard_map.104 = (f32[384,1536]{1,0:T(8,128)S(1)}, f32[64,1408]{1,0:T(8,128)S(1)}, bf16[1408,384]{1,0:T(8,128)(2,1)S(1)}) custom-call(bf16[352,384]{1,0:T(8,128)(2,1)S(1)} %get-tuple-element.37.t0, bf16[352,384]{1,0:T(8,128)(2,1)S(1)} %collective-permute-done.t1, bf16[352,384]{1,0:T(8,128)(2,1)S(1)} %collective-permute-done.1.t2, ...), custom_call_target="tpu_custom_call" | custom-call | flops 3321888768 | bytes 12582912 | tf_op jit(solution)/shard_map/pallas_call | solution.py:483
  34.4 1.6 %collective-permute-start.11 = (bf16[32,1024]{1,0:T(8,128)(2,1)S(1)}, bf16[32,1024]{1,0:T(8,128)(2,1)S(1)}, u32[]{:S(2)}, u32[]{:S(2)}) collective-permute-start(bf16[32,1024]{1,0:T(8,128)(2,1)S(1)} %get-tuple-element.40.s0), channel_id=1, source_target_pairs={{0,4},{4,0},{8,12},{12,8},{16,20},{20,16},{24,28},{28,24},{1,5},{5... | collective-permute-start | bytes 196616 | tf_op jit(solution)/shard_map/ppermute | solution.py:24
  36.0 0.5 collective-permute-start.17
  36.6 0.5 collective-permute-start.3
  37.1 1.7 %collective-permute-done.11.s1 = bf16[32,1024]{1,0:T(8,128)(2,1)S(1)} collective-permute-done((bf16[32,1024]{1,0:T(8,128)(2,1)S(1)}, bf16[32,1024]{1,0:T(8,128)(2,1)S(1)}, u32[]{:S(2)}, u32[]{:S(2)}) %collective-permute-start.11) | collective-permute-done | bytes 65568 | tf_op jit(solution)/shard_map/ppermute | solution.py:24
  38.8 0.7 collective-permute-start.12
  39.5 2.7 %collective-permute-done.17.h2 = bf16[176,640]{1,0:T(8,128)(2,1)S(1)} collective-permute-done((bf16[176,640]{1,0:T(8,128)(2,1)S(1)}, bf16[176,640]{1,0:T(8,128)(2,1)S(1)}, u32[]{:S(2)}, u32[]{:S(2)}) %collective-permute-start.17) | collective-permute-done | bytes 225312 | tf_op jit(solution)/shard_map/ppermute | solution.py:24
  42.6 1.1 shard_map.111
  43.8 0.5 shard_map.113.pre
  44.3 2.8 %collective-permute-done.12.s2 = bf16[64,1024]{1,0:T(8,128)(2,1)S(1)} collective-permute-done((bf16[64,1024]{1,0:T(8,128)(2,1)S(1)}, bf16[64,1024]{1,0:T(8,128)(2,1)S(1)}, u32[]{:S(2)}, u32[]{:S(2)}) %collective-permute-start.12) | collective-permute-done | bytes 131104 | tf_op jit(solution)/shard_map/ppermute | solution.py:29
  47.0 1.5 %collective-permute-start.31 = (bf16[384,256]{1,0:T(8,128)(2,1)S(1)}, bf16[384,256]{1,0:T(8,128)(2,1)S(1)}, u32[]{:S(2)}, u32[]{:S(2)}) collective-permute-start(bf16[384,256]{1,0:T(8,128)(2,1)S(1)} %get-tuple-element.52.pre), channel_id=1, source_target_pairs={{0,4},{4,0},{8,12},{12,8},{16,20},{20,16},{24,28},{28,24},{1,5},{5... | collective-permute-start | bytes 589832 | tf_op jit(solution)/shard_map/ppermute | solution.py:24
  48.5 3.4 %collective-permute-done.13.s3 = bf16[64,1024]{1,0:T(8,128)(2,1)S(1)} collective-permute-done((bf16[64,1024]{1,0:T(8,128)(2,1)S(1)}, bf16[64,1024]{1,0:T(8,128)(2,1)S(1)}, u32[]{:S(2)}, u32[]{:S(2)}) %collective-permute-start.13) | collective-permute-done | bytes 131104 | tf_op jit(solution)/shard_map/ppermute | solution.py:29
  51.9 1.2 %collective-permute-start.35 = (bf16[384,256]{1,0:T(8,128)(2,1)S(1)}, bf16[384,256]{1,0:T(8,128)(2,1)S(1)}, u32[]{:S(2)}, u32[]{:S(2)}) collective-permute-start(bf16[384,256]{1,0:T(8,128)(2,1)S(1)} %shard_map.113.pre), channel_id=1, source_target_pairs={{0,4},{4,0},{8,12},{12,8},{16,20},{20,16},{24,28},{28,24},{1,5},{5... | collective-permute-start | bytes 589832 | tf_op jit(solution)/shard_map/ppermute | solution.py:24
  53.2 0.8 shard_map.117.pre
  54.0 0.9 collective-permute-start.43
  54.9 0.6 collective-permute-start.4
  56.1 3.7 %collective-permute-done.35.pre_pair = bf16[384,256]{1,0:T(8,128)(2,1)S(1)} collective-permute-done((bf16[384,256]{1,0:T(8,128)(2,1)S(1)}, bf16[384,256]{1,0:T(8,128)(2,1)S(1)}, u32[]{:S(2)}, u32[]{:S(2)}) %collective-permute-start.35) | collective-permute-done | bytes 196640 | tf_op jit(solution)/shard_map/ppermute | solution.py:24
  59.7 0.5 collective-permute-start.20
  60.3 0.6 shard_map.112
  60.9 0.5 shard_map.114
  61.5 0.9 collective-permute-start.38
  62.3 5.0 %collective-permute-done.20.e2 = f32[128,256]{1,0:T(8,128)S(1)} collective-permute-done((f32[128,256]{1,0:T(8,128)S(1)}, f32[128,256]{1,0:T(8,128)S(1)}, u32[]{:S(2)}, u32[]{:S(2)}) %collective-permute-start.20) | collective-permute-done | bytes 131104 | tf_op jit(solution)/shard_map/ppermute | solution.py:24
  67.4 0.8 shard_map.115.pre
  68.2 0.9 collective-permute-start.39
  69.1 4.6 %collective-permute-done.36 = bf16[176,256]{1,0:T(8,128)(2,1)S(1)} collective-permute-done((bf16[176,256]{1,0:T(8,128)(2,1)S(1)}, bf16[176,256]{1,0:T(8,128)(2,1)S(1)}, u32[]{:S(2)}, u32[]{:S(2)}) %collective-permute-start.36) | collective-permute-done | bytes 90144 | tf_op jit(solution)/shard_map/ppermute | solution.py:29
  73.8 2.1 %collective-permute-start.32 = (bf16[176,256]{1,0:T(8,128)(2,1)S(1)}, bf16[176,256]{1,0:T(8,128)(2,1)S(1)}, u32[]{:S(2)}, u32[]{:S(2)}) collective-permute-start(bf16[176,256]{1,0:T(8,128)(2,1)S(1)} %get-tuple-element.54), channel_id=1, source_target_pairs={{0,8},{4,12},{8,16},{12,20},{16,24},{20,28},{24,0},{28,4},{1,9},{5... | collective-permute-start | bytes 270344 | tf_op jit(solution)/shard_map/ppermute | solution.py:29
  75.9 0.9 shard_map.118
  77.0 5.1 %collective-permute-done.34 = bf16[176,256]{1,0:T(8,128)(2,1)S(1)} collective-permute-done((bf16[176,256]{1,0:T(8,128)(2,1)S(1)}, bf16[176,256]{1,0:T(8,128)(2,1)S(1)}, u32[]{:S(2)}, u32[]{:S(2)}) %collective-permute-start.34) | collective-permute-done | bytes 90144 | tf_op jit(solution)/shard_map/ppermute | solution.py:29
  82.2 0.5 collective-permute-start.45
  82.7 0.8 collective-permute-done.32
  83.5 4.5 %collective-permute-start.44 = (bf16[176,512]{1,0:T(8,128)(2,1)S(1)}, bf16[176,512]{1,0:T(8,128)(2,1)S(1)}, u32[]{:S(2)}, u32[]{:S(2)}) collective-permute-start(bf16[176,512]{1,0:T(8,128)(2,1)S(1)} %get-tuple-element.68), channel_id=1, source_target_pairs={{0,8},{4,12},{8,16},{12,20},{16,24},{20,28},{24,0},{28,4},{1,9},{5... | collective-permute-start | bytes 540680 | tf_op jit(solution)/shard_map/ppermute | solution.py:29
  88.1 0.8 collective-permute-start.6
  88.9 0.8 shard_map.108
  89.7 0.9 shard_map.116
  90.7 1.3 %collective-permute-done.46 = bf16[176,512]{1,0:T(8,128)(2,1)S(1)} collective-permute-done((bf16[176,512]{1,0:T(8,128)(2,1)S(1)}, bf16[176,512]{1,0:T(8,128)(2,1)S(1)}, u32[]{:S(2)}, u32[]{:S(2)}) %collective-permute-start.46) | collective-permute-done | bytes 180256 | tf_op jit(solution)/shard_map/ppermute | solution.py:29
  92.0 4.0 %collective-permute-start.41 = (bf16[176,512]{1,0:T(8,128)(2,1)S(1)}, bf16[176,512]{1,0:T(8,128)(2,1)S(1)}, u32[]{:S(2)}, u32[]{:S(2)}) collective-permute-start(bf16[176,512]{1,0:T(8,128)(2,1)S(1)} %get-tuple-element.65), channel_id=1, source_target_pairs={{0,16},{4,20},{8,24},{12,28},{16,0},{20,4},{24,8},{28,12},{1,17},{... | collective-permute-start | bytes 540680 | tf_op jit(solution)/shard_map/ppermute | solution.py:29
  96.0 5.3 %collective-permute-done.45 = bf16[176,512]{1,0:T(8,128)(2,1)S(1)} collective-permute-done((bf16[176,512]{1,0:T(8,128)(2,1)S(1)}, bf16[176,512]{1,0:T(8,128)(2,1)S(1)}, u32[]{:S(2)}, u32[]{:S(2)}) %collective-permute-start.45) | collective-permute-done | bytes 180256 | tf_op jit(solution)/shard_map/ppermute | solution.py:29
  101.7 0.5 collective-permute-start.7
  102.3 0.6 collective-permute-done.5.e1
  103.1 0.5 shard_map.109
  104.0 8.9 %collective-permute-done.41 = bf16[176,512]{1,0:T(8,128)(2,1)S(1)} collective-permute-done((bf16[176,512]{1,0:T(8,128)(2,1)S(1)}, bf16[176,512]{1,0:T(8,128)(2,1)S(1)}, u32[]{:S(2)}, u32[]{:S(2)}) %collective-permute-start.41) | collective-permute-done | bytes 180256 | tf_op jit(solution)/shard_map/ppermute | solution.py:29
  113.1 0.5 collective-permute-start.23
  113.6 1.1 pad_maximum_fusion
  114.6 2.1 %collective-permute-done.23.b = f32[1,256]{1,0:T(1,128)S(1)} collective-permute-done((f32[1,256]{1,0:T(1,128)S(1)}, f32[1,256]{1,0:T(1,128)S(1)}, u32[]{:S(2)}, u32[]{:S(2)}) %collective-permute-start.23) | collective-permute-done | bytes 1056 | tf_op jit(solution)/shard_map/ppermute | solution.py:24
  116.7 0.7 shard_map.110
  (80 shorter events, 3.0 us)
Async XLA Ops:
  0.6 0.7 copy-start.5
  1.3 0.7 copy-start.7
  1.9 1.0 copy-start.10
  3.8 10.9 %collective-permute-start.1 = (bf16[352,384]{1,0:T(8,128)(2,1)S(1)}, bf16[352,384]{1,0:T(8,128)(2,1)S(1)}, u32[]{:S(2)}, u32[]{:S(2)}) collective-permute-start(bf16[352,384]{1,0:T(8,128)(2,1)S(1)} %get-tuple-element.37.t0), channel_id=1, source_target_pairs={{0,2},{1,3},{2,0},{3,1},{4,6},{5,7},{6,4},{7,5},{8,10},{9,11},{10,... | collective-permute-start | bytes 811016 | tf_op jit(solution)/shard_map/ppermute | solution.py:24
  6.8 7.9 %collective-permute-start.9 = (bf16[128,256]{1,0:T(8,128)(2,1)}, bf16[128,256]{1,0:T(8,128)(2,1)S(1)}, u32[]{:S(2)}, u32[]{:S(2)}) collective-permute-start(bf16[128,256]{1,0:T(8,128)(2,1)} %t0.1), channel_id=1, source_target_pairs={{0,2},{1,3},{2,0},{3,1},{4,6},{5,7},{6,4},{7,5},{8,10},{9,11},{10,... | collective-permute-start | bytes 196616 | tf_op jit(solution)/shard_map/ppermute | solution.py:24
  6.9 3.6 %collective-permute-start.27 = (f32[8,128]{1,0:T(8,128)S(1)}, f32[8,128]{1,0:T(8,128)S(1)}, u32[]{:S(2)}, u32[]{:S(2)}) collective-permute-start(f32[8,128]{1,0:T(8,128)S(1)} %get-tuple-element.50), channel_id=1, source_target_pairs={{0,4},{4,0},{8,12},{12,8},{16,20},{20,16},{24,28},{28,24},{1,5},{5... | collective-permute-start | bytes 12296 | tf_op jit(solution)/shard_map/ppermute | solution.py:24
  8.8 11.5 %collective-permute-start = (bf16[352,384]{1,0:T(8,128)(2,1)S(1)}, bf16[352,384]{1,0:T(8,128)(2,1)S(1)}, u32[]{:S(2)}, u32[]{:S(2)}) collective-permute-start(bf16[352,384]{1,0:T(8,128)(2,1)S(1)} %get-tuple-element.37.t0), channel_id=1, source_target_pairs={{0,1},{1,0},{2,3},{3,2},{4,5},{5,4},{6,7},{7,6},{8,9},{9,8},{10,11... | collective-permute-start | bytes 811016 | tf_op jit(solution)/shard_map/ppermute | solution.py:24
  8.8 6.4 %collective-permute-start.8 = (bf16[128,256]{1,0:T(8,128)(2,1)}, bf16[128,256]{1,0:T(8,128)(2,1)S(1)}, u32[]{:S(2)}, u32[]{:S(2)}) collective-permute-start(bf16[128,256]{1,0:T(8,128)(2,1)} %t0.1), channel_id=1, source_target_pairs={{0,1},{1,0},{2,3},{3,2},{4,5},{5,4},{6,7},{7,6},{8,9},{9,8},{10,11... | collective-permute-start | bytes 196616 | tf_op jit(solution)/shard_map/ppermute | solution.py:24
  10.5 8.2 %collective-permute-start.15 = (bf16[176,384]{1,0:T(8,128)(2,1)S(1)}, bf16[176,384]{1,0:T(8,128)(2,1)S(1)}, u32[]{:S(2)}, u32[]{:S(2)}) collective-permute-start(bf16[176,384]{1,0:T(8,128)(2,1)S(1)} %get-tuple-element.41), channel_id=1, source_target_pairs={{0,4},{4,0},{8,12},{12,8},{16,20},{20,16},{24,28},{28,24},{1,5},{5... | collective-permute-start | bytes 405512 | tf_op jit(solution)/shard_map/ppermute | solution.py:24
  14.7 1.3 %collective-permute-start.10 = (bf16[128,256]{1,0:T(8,128)(2,1)S(1)}, bf16[128,256]{1,0:T(8,128)(2,1)S(1)}, u32[]{:S(2)}, u32[]{:S(2)}) collective-permute-start(bf16[128,256]{1,0:T(8,128)(2,1)S(1)} %collective-permute-done.9.t2), channel_id=1, source_target_pairs={{0,1},{1,0},{2,3},{3,2},{4,5},{5,4},{6,7},{7,6},{8,9},{9,8},{10,11... | collective-permute-start | bytes 196616 | tf_op jit(solution)/shard_map/ppermute | solution.py:24
  14.7 8.4 %collective-permute-start.2 = (bf16[352,384]{1,0:T(8,128)(2,1)S(1)}, bf16[352,384]{1,0:T(8,128)(2,1)S(1)}, u32[]{:S(2)}, u32[]{:S(2)}) collective-permute-start(bf16[352,384]{1,0:T(8,128)(2,1)S(1)} %collective-permute-done.1.t2), channel_id=1, source_target_pairs={{0,1},{1,0},{2,3},{3,2},{4,5},{5,4},{6,7},{7,6},{8,9},{9,8},{10,11... | collective-permute-start | bytes 811016 | tf_op jit(solution)/shard_map/ppermute | solution.py:24
  15.2 23.6 %collective-permute-start.24 = (bf16[352,384]{1,0:T(8,128)(2,1)}, bf16[352,384]{1,0:T(8,128)(2,1)S(1)}, u32[]{:S(2)}, u32[]{:S(2)}) collective-permute-start(bf16[352,384]{1,0:T(8,128)(2,1)} %bitcast.6), channel_id=1, source_target_pairs={{0,1},{1,0},{2,3},{3,2},{4,5},{5,4},{6,7},{7,6},{8,9},{9,8},{10,11... | collective-permute-start | bytes 811016 | tf_op jit(solution)/shard_map/ppermute | solution.py:24
  15.9 20.6 %collective-permute-start.25 = (bf16[352,384]{1,0:T(8,128)(2,1)}, bf16[352,384]{1,0:T(8,128)(2,1)S(1)}, u32[]{:S(2)}, u32[]{:S(2)}) collective-permute-start(bf16[352,384]{1,0:T(8,128)(2,1)} %bitcast.7), channel_id=1, source_target_pairs={{0,2},{1,3},{2,0},{3,1},{4,6},{5,7},{6,4},{7,5},{8,10},{9,11},{10,... | collective-permute-start | bytes 811016 | tf_op jit(solution)/shard_map/ppermute | solution.py:24
  17.7 0.8 copy-start.4
  18.7 15.7 %collective-permute-start.28 = (f32[8,128]{1,0:T(8,128)S(1)}, f32[8,128]{1,0:T(8,128)S(1)}, u32[]{:S(2)}, u32[]{:S(2)}) collective-permute-start(f32[8,128]{1,0:T(8,128)S(1)} %add.47.n0), channel_id=1, source_target_pairs={{0,8},{4,12},{8,16},{12,20},{16,24},{20,28},{24,0},{28,4},{1,9},{5... | collective-permute-start | bytes 12296 | tf_op jit(solution)/shard_map/ppermute | solution.py:29
  20.3 22.3 %copy-start.3 = (bf16[384,352]{0,1:T(8,128)(2,1)S(1)}, bf16[384,352]{0,1:T(8,128)(2,1)}, u32[]{:S(2)}) copy-start(bf16[384,352]{0,1:T(8,128)(2,1)} %param.15) | copy-start | bytes 811012
  20.3 22.3 %copy-start.8 = (s32[64]{0:T(128)S(1)}, s32[64]{0:T(128)}, u32[]{:S(2)}) copy-start(s32[64]{0:T(128)} %param.14) | copy-start | bytes 772
  20.4 15.6 %collective-permute-start.29 = (f32[8,128]{1,0:T(8,128)S(1)}, f32[8,128]{1,0:T(8,128)S(1)}, u32[]{:S(2)}, u32[]{:S(2)}) collective-permute-start(f32[8,128]{1,0:T(8,128)S(1)} %add.47.n0), channel_id=1, source_target_pairs={{0,16},{4,20},{8,24},{12,28},{16,0},{20,4},{24,8},{28,12},{1,17},{... | collective-permute-start | bytes 12296 | tf_op jit(solution)/shard_map/ppermute | solution.py:29
  23.0 13.5 %collective-permute-start.30 = (f32[8,128]{1,0:T(8,128)S(1)}, f32[8,128]{1,0:T(8,128)S(1)}, u32[]{:S(2)}, u32[]{:S(2)}) collective-permute-start(f32[8,128]{1,0:T(8,128)S(1)} %add.47.n0), channel_id=1, source_target_pairs={{0,24},{4,28},{8,0},{12,4},{16,8},{20,12},{24,16},{28,20},{1,25},{... | collective-permute-start | bytes 12296 | tf_op jit(solution)/shard_map/ppermute | solution.py:29
  24.4 2.2 %copy-start = (bf16[1536,1408]{1,0:T(8,128)(2,1)S(1)}, bf16[1536,1408]{1,0:T(8,128)(2,1)}, u32[]{:S(2)}) copy-start(bf16[1536,1408]{1,0:T(8,128)(2,1)} %w_down.9) | copy-start | bytes 12976132
  26.6 2.2 %copy-start.9 = (bf16[1408,1536]{1,0:T(8,128)(2,1)S(1)}, bf16[1408,1536]{1,0:T(8,128)(2,1)}, u32[]{:S(2)}) copy-start(bf16[1408,1536]{1,0:T(8,128)(2,1)} %w_up.1) | copy-start | bytes 12976132
  28.8 13.8 %copy-start.1 = (bf16[1536,1408]{1,0:T(8,128)(2,1)S(1)}, bf16[1536,1408]{1,0:T(8,128)(2,1)}, u32[]{:S(2)}) copy-start(bf16[1536,1408]{1,0:T(8,128)(2,1)} %w_down.9) | copy-start | bytes 12976132
  34.4 4.3 %collective-permute-start.11 = (bf16[32,1024]{1,0:T(8,128)(2,1)S(1)}, bf16[32,1024]{1,0:T(8,128)(2,1)S(1)}, u32[]{:S(2)}, u32[]{:S(2)}) collective-permute-start(bf16[32,1024]{1,0:T(8,128)(2,1)S(1)} %get-tuple-element.40.s0), channel_id=1, source_target_pairs={{0,4},{4,0},{8,12},{12,8},{16,20},{20,16},{24,28},{28,24},{1,5},{5... | collective-permute-start | bytes 196616 | tf_op jit(solution)/shard_map/ppermute | solution.py:24
  36.0 6.2 %collective-permute-start.17 = (bf16[176,640]{1,0:T(8,128)(2,1)S(1)}, bf16[176,640]{1,0:T(8,128)(2,1)S(1)}, u32[]{:S(2)}, u32[]{:S(2)}) collective-permute-start(bf16[176,640]{1,0:T(8,128)(2,1)S(1)} %pad_maximum_fusion.1.h0), channel_id=1, source_target_pairs={{0,2},{1,3},{2,0},{3,1},{4,6},{5,7},{6,4},{7,5},{8,10},{9,11},{10,... | collective-permute-start | bytes 675848 | tf_op jit(solution)/shard_map/ppermute | solution.py:24
  36.5 6.1 %collective-permute-start.26 = (bf16[352,384]{1,0:T(8,128)(2,1)S(1)}, bf16[352,384]{1,0:T(8,128)(2,1)S(1)}, u32[]{:S(2)}, u32[]{:S(2)}) collective-permute-start(bf16[352,384]{1,0:T(8,128)(2,1)S(1)} %collective-permute-done.25.c2), channel_id=1, source_target_pairs={{0,1},{1,0},{2,3},{3,2},{4,5},{5,4},{6,7},{7,6},{8,9},{9,8},{10,11... | collective-permute-start | bytes 811016 | tf_op jit(solution)/shard_map/ppermute | solution.py:24
  36.6 17.4 %collective-permute-start.3 = (f32[64,1408]{1,0:T(8,128)S(1)}, f32[64,1408]{1,0:T(8,128)S(1)}, u32[]{:S(2)}, u32[]{:S(2)}) collective-permute-start(f32[64,1408]{1,0:T(8,128)S(1)} %get-tuple-element.38), channel_id=1, source_target_pairs={{0,1},{1,0},{2,3},{3,2},{4,5},{5,4},{6,7},{7,6},{8,9},{9,8},{10,11... | collective-permute-start | bytes 1081352 | tf_op jit(solution)/shard_map/ppermute | solution.py:24
  38.8 16.2 %collective-permute-start.16 = (bf16[176,640]{1,0:T(8,128)(2,1)S(1)}, bf16[176,640]{1,0:T(8,128)(2,1)S(1)}, u32[]{:S(2)}, u32[]{:S(2)}) collective-permute-start(bf16[176,640]{1,0:T(8,128)(2,1)S(1)} %pad_maximum_fusion.1.h0), channel_id=1, source_target_pairs={{0,1},{1,0},{2,3},{3,2},{4,5},{5,4},{6,7},{7,6},{8,9},{9,8},{10,11... | collective-permute-start | bytes 675848 | tf_op jit(solution)/shard_map/ppermute | solution.py:24
  38.8 8.2 %collective-permute-start.12 = (bf16[64,1024]{1,0:T(8,128)(2,1)S(1)}, bf16[64,1024]{1,0:T(8,128)(2,1)S(1)}, u32[]{:S(2)}, u32[]{:S(2)}) collective-permute-start(bf16[64,1024]{1,0:T(8,128)(2,1)S(1)} %constant_dynamic-update-slice_fusion), channel_id=1, source_target_pairs={{0,8},{4,12},{8,16},{12,20},{16,24},{20,28},{24,0},{28,4},{1,9},{5... | collective-permute-start | bytes 393224 | tf_op jit(solution)/shard_map/ppermute | solution.py:29
  42.2 9.8 %collective-permute-start.13 = (bf16[64,1024]{1,0:T(8,128)(2,1)S(1)}, bf16[64,1024]{1,0:T(8,128)(2,1)S(1)}, u32[]{:S(2)}, u32[]{:S(2)}) collective-permute-start(bf16[64,1024]{1,0:T(8,128)(2,1)S(1)} %constant_dynamic-update-slice_fusion), channel_id=1, source_target_pairs={{0,16},{4,20},{8,24},{12,28},{16,0},{20,4},{24,8},{28,12},{1,17},{... | collective-permute-start | bytes 393224 | tf_op jit(solution)/shard_map/ppermute | solution.py:29
  42.6 12.9 %collective-permute-start.18 = (bf16[176,640]{1,0:T(8,128)(2,1)S(1)}, bf16[176,640]{1,0:T(8,128)(2,1)S(1)}, u32[]{:S(2)}, u32[]{:S(2)}) collective-permute-start(bf16[176,640]{1,0:T(8,128)(2,1)S(1)} %collective-permute-done.17.h2), channel_id=1, source_target_pairs={{0,1},{1,0},{2,3},{3,2},{4,5},{5,4},{6,7},{7,6},{8,9},{9,8},{10,11... | collective-permute-start | bytes 675848 | tf_op jit(solution)/shard_map/ppermute | solution.py:24
  47.0 9.0 %collective-permute-start.31 = (bf16[384,256]{1,0:T(8,128)(2,1)S(1)}, bf16[384,256]{1,0:T(8,128)(2,1)S(1)}, u32[]{:S(2)}, u32[]{:S(2)}) collective-permute-start(bf16[384,256]{1,0:T(8,128)(2,1)S(1)} %get-tuple-element.52.pre), channel_id=1, source_target_pairs={{0,4},{4,0},{8,12},{12,8},{16,20},{20,16},{24,28},{28,24},{1,5},{5... | collective-permute-start | bytes 589832 | tf_op jit(solution)/shard_map/ppermute | solution.py:24
  51.9 7.8 %collective-permute-start.35 = (bf16[384,256]{1,0:T(8,128)(2,1)S(1)}, bf16[384,256]{1,0:T(8,128)(2,1)S(1)}, u32[]{:S(2)}, u32[]{:S(2)}) collective-permute-start(bf16[384,256]{1,0:T(8,128)(2,1)S(1)} %shard_map.113.pre), channel_id=1, source_target_pairs={{0,4},{4,0},{8,12},{12,8},{16,20},{20,16},{24,28},{28,24},{1,5},{5... | collective-permute-start | bytes 589832 | tf_op jit(solution)/shard_map/ppermute | solution.py:24
  54.0 1.6 %copy-start.2 = (bf16[1408,256]{1,0:T(8,128)(2,1)S(1)}, bf16[1408,256]{1,0:T(8,128)(2,1)}, u32[]{:S(2)}) copy-start(bf16[1408,256]{1,0:T(8,128)(2,1)} %ref_proj.3) | copy-start | bytes 2162692
  54.0 19.7 %collective-permute-start.43 = (bf16[384,512]{1,0:T(8,128)(2,1)S(1)}, bf16[384,512]{1,0:T(8,128)(2,1)S(1)}, u32[]{:S(2)}, u32[]{:S(2)}) collective-permute-start(bf16[384,512]{1,0:T(8,128)(2,1)S(1)} %shard_map.117.pre), channel_id=1, source_target_pairs={{0,4},{4,0},{8,12},{12,8},{16,20},{20,16},{24,28},{28,24},{1,5},{5... | collective-permute-start | bytes 1179656 | tf_op jit(solution)/shard_map/ppermute | solution.py:24
  54.9 18.8 %collective-permute-start.4 = (f32[64,1408]{1,0:T(8,128)S(1)}, f32[64,1408]{1,0:T(8,128)S(1)}, u32[]{:S(2)}, u32[]{:S(2)}) collective-permute-start(f32[64,1408]{1,0:T(8,128)S(1)} %add.45.a), channel_id=1, source_target_pairs={{0,2},{1,3},{2,0},{3,1},{4,6},{5,7},{6,4},{7,5},{8,10},{9,11},{10,... | collective-permute-start | bytes 1081352 | tf_op jit(solution)/shard_map/ppermute | solution.py:24
  55.5 5.9 %collective-permute-start.14 = (bf16[64,1024]{1,0:T(8,128)(2,1)S(1)}, bf16[64,1024]{1,0:T(8,128)(2,1)S(1)}, u32[]{:S(2)}, u32[]{:S(2)}) collective-permute-start(bf16[64,1024]{1,0:T(8,128)(2,1)S(1)} %constant_dynamic-update-slice_fusion), channel_id=1, source_target_pairs={{0,24},{4,28},{8,0},{12,4},{16,8},{20,12},{24,16},{28,20},{1,25},{... | collective-permute-start | bytes 393224 | tf_op jit(solution)/shard_map/ppermute | solution.py:29
  56.0 6.4 %collective-permute-start.19 = (f32[128,256]{1,0:T(8,128)S(1)}, f32[128,256]{1,0:T(8,128)S(1)}, u32[]{:S(2)}, u32[]{:S(2)}) collective-permute-start(f32[128,256]{1,0:T(8,128)S(1)} %shard_map.107.e0), channel_id=1, source_target_pairs={{0,1},{1,0},{2,3},{3,2},{4,5},{5,4},{6,7},{7,6},{8,9},{9,8},{10,11... | collective-permute-start | bytes 393224 | tf_op jit(solution)/shard_map/ppermute | solution.py:24
  59.7 7.6 %collective-permute-start.20 = (f32[128,256]{1,0:T(8,128)S(1)}, f32[128,256]{1,0:T(8,128)S(1)}, u32[]{:S(2)}, u32[]{:S(2)}) collective-permute-start(f32[128,256]{1,0:T(8,128)S(1)} %shard_map.107.e0), channel_id=1, source_target_pairs={{0,2},{1,3},{2,0},{3,1},{4,6},{5,7},{6,4},{7,5},{8,10},{9,11},{10,... | collective-permute-start | bytes 393224 | tf_op jit(solution)/shard_map/ppermute | solution.py:24
  61.5 6.7 %collective-permute-start.38 = (bf16[176,256]{1,0:T(8,128)(2,1)S(1)}, bf16[176,256]{1,0:T(8,128)(2,1)S(1)}, u32[]{:S(2)}, u32[]{:S(2)}) collective-permute-start(bf16[176,256]{1,0:T(8,128)(2,1)S(1)} %get-tuple-element.62), channel_id=1, source_target_pairs={{0,24},{4,28},{8,0},{12,4},{16,8},{20,12},{24,16},{28,20},{1,25},{... | collective-permute-start | bytes 270344 | tf_op jit(solution)/shard_map/ppermute | solution.py:29
  62.3 6.8 %collective-permute-start.37 = (bf16[176,256]{1,0:T(8,128)(2,1)S(1)}, bf16[176,256]{1,0:T(8,128)(2,1)S(1)}, u32[]{:S(2)}, u32[]{:S(2)}) collective-permute-start(bf16[176,256]{1,0:T(8,128)(2,1)S(1)} %get-tuple-element.61), channel_id=1, source_target_pairs={{0,16},{4,20},{8,24},{12,28},{16,0},{20,4},{24,8},{28,12},{1,17},{... | collective-permute-start | bytes 270344 | tf_op jit(solution)/shard_map/ppermute | solution.py:29
  67.4 6.4 %collective-permute-start.36 = (bf16[176,256]{1,0:T(8,128)(2,1)S(1)}, bf16[176,256]{1,0:T(8,128)(2,1)S(1)}, u32[]{:S(2)}, u32[]{:S(2)}) collective-permute-start(bf16[176,256]{1,0:T(8,128)(2,1)S(1)} %get-tuple-element.60), channel_id=1, source_target_pairs={{0,8},{4,12},{8,16},{12,20},{16,24},{20,28},{24,0},{28,4},{1,9},{5... | collective-permute-start | bytes 270344 | tf_op jit(solution)/shard_map/ppermute | solution.py:29
  68.2 21.5 %collective-permute-start.39 = (bf16[384,512]{1,0:T(8,128)(2,1)S(1)}, bf16[384,512]{1,0:T(8,128)(2,1)S(1)}, u32[]{:S(2)}, u32[]{:S(2)}) collective-permute-start(bf16[384,512]{1,0:T(8,128)(2,1)S(1)} %shard_map.115.pre), channel_id=1, source_target_pairs={{0,4},{4,0},{8,12},{12,8},{16,20},{20,16},{24,28},{28,24},{1,5},{5... | collective-permute-start | bytes 1179656 | tf_op jit(solution)/shard_map/ppermute | solution.py:24
  69.1 19.0 %collective-permute-start.21 = (f32[128,256]{1,0:T(8,128)S(1)}, f32[128,256]{1,0:T(8,128)S(1)}, u32[]{:S(2)}, u32[]{:S(2)}) collective-permute-start(f32[128,256]{1,0:T(8,128)S(1)} %collective-permute-done.20.e2), channel_id=1, source_target_pairs={{0,1},{1,0},{2,3},{3,2},{4,5},{5,4},{6,7},{7,6},{8,9},{9,8},{10,11... | collective-permute-start | bytes 393224 | tf_op jit(solution)/shard_map/ppermute | solution.py:24
  73.7 8.5 %collective-permute-start.34 = (bf16[176,256]{1,0:T(8,128)(2,1)S(1)}, bf16[176,256]{1,0:T(8,128)(2,1)S(1)}, u32[]{:S(2)}, u32[]{:S(2)}) collective-permute-start(bf16[176,256]{1,0:T(8,128)(2,1)S(1)} %get-tuple-element.56), channel_id=1, source_target_pairs={{0,24},{4,28},{8,0},{12,4},{16,8},{20,12},{24,16},{28,20},{1,25},{... | collective-permute-start | bytes 270344 | tf_op jit(solution)/shard_map/ppermute | solution.py:29
  73.7 8.5 %collective-permute-start.33 = (bf16[176,256]{1,0:T(8,128)(2,1)S(1)}, bf16[176,256]{1,0:T(8,128)(2,1)S(1)}, u32[]{:S(2)}, u32[]{:S(2)}) collective-permute-start(bf16[176,256]{1,0:T(8,128)(2,1)S(1)} %get-tuple-element.55), channel_id=1, source_target_pairs={{0,16},{4,20},{8,24},{12,28},{16,0},{20,4},{24,8},{28,12},{1,17},{... | collective-permute-start | bytes 270344 | tf_op jit(solution)/shard_map/ppermute | solution.py:29
  73.8 9.8 %collective-permute-start.32 = (bf16[176,256]{1,0:T(8,128)(2,1)S(1)}, bf16[176,256]{1,0:T(8,128)(2,1)S(1)}, u32[]{:S(2)}, u32[]{:S(2)}) collective-permute-start(bf16[176,256]{1,0:T(8,128)(2,1)S(1)} %get-tuple-element.54), channel_id=1, source_target_pairs={{0,8},{4,12},{8,16},{12,20},{16,24},{20,28},{24,0},{28,4},{1,9},{5... | collective-permute-start | bytes 270344 | tf_op jit(solution)/shard_map/ppermute | solution.py:29
  82.2 9.8 %collective-permute-start.46 = (bf16[176,512]{1,0:T(8,128)(2,1)S(1)}, bf16[176,512]{1,0:T(8,128)(2,1)S(1)}, u32[]{:S(2)}, u32[]{:S(2)}) collective-permute-start(bf16[176,512]{1,0:T(8,128)(2,1)S(1)} %get-tuple-element.70), channel_id=1, source_target_pairs={{0,24},{4,28},{8,0},{12,4},{16,8},{20,12},{24,16},{28,20},{1,25},{... | collective-permute-start | bytes 540680 | tf_op jit(solution)/shard_map/ppermute | solution.py:29
  82.2 19.1 %collective-permute-start.45 = (bf16[176,512]{1,0:T(8,128)(2,1)S(1)}, bf16[176,512]{1,0:T(8,128)(2,1)S(1)}, u32[]{:S(2)}, u32[]{:S(2)}) collective-permute-start(bf16[176,512]{1,0:T(8,128)(2,1)S(1)} %get-tuple-element.69), channel_id=1, source_target_pairs={{0,16},{4,20},{8,24},{12,28},{16,0},{20,4},{24,8},{28,12},{1,17},{... | collective-permute-start | bytes 540680 | tf_op jit(solution)/shard_map/ppermute | solution.py:29
  83.5 18.2 %collective-permute-start.44 = (bf16[176,512]{1,0:T(8,128)(2,1)S(1)}, bf16[176,512]{1,0:T(8,128)(2,1)S(1)}, u32[]{:S(2)}, u32[]{:S(2)}) collective-permute-start(bf16[176,512]{1,0:T(8,128)(2,1)S(1)} %get-tuple-element.68), channel_id=1, source_target_pairs={{0,8},{4,12},{8,16},{12,20},{16,24},{20,28},{24,0},{28,4},{1,9},{5... | collective-permute-start | bytes 540680 | tf_op jit(solution)/shard_map/ppermute | solution.py:29
  88.1 13.6 %collective-permute-start.6 = (f32[64,256]{1,0:T(8,128)S(1)}, f32[64,256]{1,0:T(8,128)S(1)}, u32[]{:S(2)}, u32[]{:S(2)}) collective-permute-start(f32[64,256]{1,0:T(8,128)S(1)} %shard_map.105.e0), channel_id=1, source_target_pairs={{0,2},{1,3},{2,0},{3,1},{4,6},{5,7},{6,4},{7,5},{8,10},{9,11},{10,... | collective-permute-start | bytes 196616 | tf_op jit(solution)/shard_map/ppermute | solution.py:24
  90.6 12.5 %copy-start.6 = (s32[64]{0:T(128)S(1)}, s32[64]{0:T(128)}, u32[]{:S(2)}) copy-start(s32[64]{0:T(128)} %param.13) | copy-start | bytes 772
  90.6 13.4 %collective-permute-start.42 = (bf16[176,512]{1,0:T(8,128)(2,1)S(1)}, bf16[176,512]{1,0:T(8,128)(2,1)S(1)}, u32[]{:S(2)}, u32[]{:S(2)}) collective-permute-start(bf16[176,512]{1,0:T(8,128)(2,1)S(1)} %get-tuple-element.66), channel_id=1, source_target_pairs={{0,24},{4,28},{8,0},{12,4},{16,8},{20,12},{24,16},{28,20},{1,25},{... | collective-permute-start | bytes 540680 | tf_op jit(solution)/shard_map/ppermute | solution.py:29
  92.0 20.9 %collective-permute-start.41 = (bf16[176,512]{1,0:T(8,128)(2,1)S(1)}, bf16[176,512]{1,0:T(8,128)(2,1)S(1)}, u32[]{:S(2)}, u32[]{:S(2)}) collective-permute-start(bf16[176,512]{1,0:T(8,128)(2,1)S(1)} %get-tuple-element.65), channel_id=1, source_target_pairs={{0,16},{4,20},{8,24},{12,28},{16,0},{20,4},{24,8},{28,12},{1,17},{... | collective-permute-start | bytes 540680 | tf_op jit(solution)/shard_map/ppermute | solution.py:29
  101.3 11.6 %collective-permute-start.40 = (bf16[176,512]{1,0:T(8,128)(2,1)S(1)}, bf16[176,512]{1,0:T(8,128)(2,1)S(1)}, u32[]{:S(2)}, u32[]{:S(2)}) collective-permute-start(bf16[176,512]{1,0:T(8,128)(2,1)S(1)} %get-tuple-element.64), channel_id=1, source_target_pairs={{0,8},{4,12},{8,16},{12,20},{16,24},{20,28},{24,0},{28,4},{1,9},{5... | collective-permute-start | bytes 540680 | tf_op jit(solution)/shard_map/ppermute | solution.py:29
  101.7 1.3 %collective-permute-start.5 = (f32[64,256]{1,0:T(8,128)S(1)}, f32[64,256]{1,0:T(8,128)S(1)}, u32[]{:S(2)}, u32[]{:S(2)}) collective-permute-start(f32[64,256]{1,0:T(8,128)S(1)} %shard_map.105.e0), channel_id=1, source_target_pairs={{0,1},{1,0},{2,3},{3,2},{4,5},{5,4},{6,7},{7,6},{8,9},{9,8},{10,11... | collective-permute-start | bytes 196616 | tf_op jit(solution)/shard_map/ppermute | solution.py:24
  101.7 1.4 %collective-permute-start.7 = (f32[64,256]{1,0:T(8,128)S(1)}, f32[64,256]{1,0:T(8,128)S(1)}, u32[]{:S(2)}, u32[]{:S(2)}) collective-permute-start(f32[64,256]{1,0:T(8,128)S(1)} %collective-permute-done.6.e2), channel_id=1, source_target_pairs={{0,1},{1,0},{2,3},{3,2},{4,5},{5,4},{6,7},{7,6},{8,9},{9,8},{10,11... | collective-permute-start | bytes 196616 | tf_op jit(solution)/shard_map/ppermute | solution.py:24
  103.6 9.5 %collective-permute-start.22 = (f32[1,256]{1,0:T(1,128)S(1)}, f32[1,256]{1,0:T(1,128)S(1)}, u32[]{:S(2)}, u32[]{:S(2)}) collective-permute-start(f32[1,256]{1,0:T(1,128)S(1)} %get-tuple-element.44), channel_id=1, source_target_pairs={{0,1},{1,0},{2,3},{3,2},{4,5},{5,4},{6,7},{7,6},{8,9},{9,8},{10,11... | collective-permute-start | bytes 3080 | tf_op jit(solution)/shard_map/ppermute | solution.py:24
  113.1 3.6 %collective-permute-start.23 = (f32[1,256]{1,0:T(1,128)S(1)}, f32[1,256]{1,0:T(1,128)S(1)}, u32[]{:S(2)}, u32[]{:S(2)}) collective-permute-start(f32[1,256]{1,0:T(1,128)S(1)} %add.46.a), channel_id=1, source_target_pairs={{0,2},{1,3},{2,0},{3,1},{4,6},{5,7},{6,4},{7,5},{8,10},{9,11},{10,... | collective-permute-start | bytes 3080 | tf_op jit(solution)/shard_map/ppermute | solution.py:24

commit v3 on v1

--- a/solution.py
+++ b/solution.py
@@ -1,6 +1,10 @@
+import functools
+
 import jax
 import jax.numpy as jnp
 from jax import lax
+from jax.experimental import pallas as pl
+from jax.experimental.pallas import tpu as pltpu
 from jax.sharding import PartitionSpec as P
 
 logit_scale = 64.0
@@ -203,6 +207,563 @@
     return (ref_loss, learnability, grad_up)
 
 
+def dot_f32(a, b):
+    return jnp.dot(a, b, preferred_element_type=f32)
+
+
+def dot_rows(a, b):
+    return lax.dot_general(a, b, (((1,), (1,)), ((), ())), preferred_element_type=f32)
+
+
+def dot_cols(a, b):
+    return lax.dot_general(a, b, (((0,), (0,)), ((), ())), preferred_element_type=f32)
+
+
+def group_mask(n_items, n_patch):
+    shape = (n_items, n_items * n_patch)
+    row = lax.broadcasted_iota(jnp.int32, shape, 1)
+    first = n_patch * lax.broadcasted_iota(jnp.int32, shape, 0)
+    return (row >= first) & (row < first + n_patch), row - first
+
+
+def as_row(column):
+    n = column.shape[0]
+    return jnp.broadcast_to(column, (n, n)).T[0:1]
+
+
+def place(index, length):
+    return pl.ds(pl.multiple_of(index * length, length), length)
+
+
+def call(body, out_shape, cost, grid=(), vmem=40 * 2**20, **kwargs):
+    flops, moved = cost
+    return pl.pallas_call(
+        body,
+        out_shape=out_shape,
+        grid=grid,
+        cost_estimate=pl.CostEstimate(flops=1, bytes_accessed=1, transcendentals=0),
+        compiler_params=pltpu.CompilerParams(vmem_limit_bytes=vmem),
+        **kwargs,
+    )
+
+
+def struct(shape, dtype):
+    return jax.ShapeDtypeStruct(shape, dtype)
+
+
+def pick_body(
+    n_patch, patches_hbm, cot_hbm, kept, dest, text_hbm, both, half, pool, texts, patches, sems
+):
+    d_part, n_all = patches.shape
+    ex_dev = n_all // n_patch
+    copies = [
+        pltpu.make_async_copy(patches_hbm, patches, sems.at[0]),
+        pltpu.make_async_copy(cot_hbm, both.at[pl.ds(d_part, d_part), :], sems.at[1]),
+        pltpu.make_async_copy(text_hbm, texts.at[pl.ds(0, ex_dev), :], sems.at[2]),
+    ]
+    for copy in copies:
+        copy.start()
+    k_dev = kept.shape[1]
+    member, offset = group_mask(k_dev, n_patch)
+    expand = member.astype(bf16)
+    index = jnp.broadcast_to(kept[...].astype(f32), (8, k_dev)).astype(bf16)
+    base = dot_f32(index, expand)[0:1].astype(jnp.int32)
+    row = base * n_patch + jnp.sum(jnp.where(member, offset, 0), axis=0, keepdims=True)
+    pick = (lax.broadcasted_iota(jnp.int32, (n_all, row.shape[1]), 0) == row).astype(bf16)
+    for copy in copies:
+        copy.wait()
+    values = patches[...]
+    both[0:d_part, :] = dot_f32(values, pick).astype(bf16)
+    other = 1 - lax.rem(lax.axis_index("sel"), 2)
+    half[...] = both[place(other, d_part // 2), :]
+    texts[ex_dev:, :] = jnp.zeros((16, texts.shape[1]), bf16)
+    texts[ex_dev:, 0:k_dev] = jnp.broadcast_to(dest[...].astype(f32), (16, k_dev)).astype(bf16)
+    groups, _ = group_mask(ex_dev, n_patch)
+    pool[...] = (dot_rows(values, groups.astype(bf16)) * (1.0 / n_patch)).astype(bf16)
+
+
+def extras_body(half, pool, t0, t1, t2, t3, extras, texts):
+    n_half, n_rows = half.shape
+    n_ex = pool.shape[1]
+    extras[:, 0:n_rows] = half[...]
+    extras[:, n_rows : n_rows + n_ex] = pool[0:n_half, :]
+    extras[:, n_rows + n_ex :] = pool[n_half:, :]
+    n_text = t0.shape[0]
+    for r, piece in enumerate((t0, t1, t2, t3)):
+        texts[r * n_text : (r + 1) * n_text, :] = piece[...]
+
+
+def text_body(k_dev, n_patch, mine, theirs, whole, send, weights):
+    n_high = 4
+    n_text = mine.shape[0] // n_high
+    ex_dev = n_text - 16
+    me = lax.axis_index("mdl")
+    sel = lax.axis_index("sel")
+    parity, high = lax.rem(sel, 2), lax.div(sel, 2)
+    shard = lax.broadcasted_iota(jnp.int32, (128, k_dev), 0).astype(f32)
+    ones = jnp.ones((8, k_dev), bf16)
+    counts = jnp.zeros((8, 128), f32)
+    named = []
+    for which, place_in_pair in ((mine, parity), (theirs, 1 - parity)):
+        for r in range(n_high):
+            source = lax.rem(high + n_high - r, n_high)
+            rows = place(source * 2 + place_in_pair, ex_dev)
+            whole[rows, :] = which[r * n_text : r * n_text + ex_dev, :]
+            dest = which[r * n_text + ex_dev : (r + 1) * n_text, 0:k_dev].astype(f32)[0:1]
+            is_dest = (shard == dest).astype(bf16)
+            counts = counts + dot_rows(ones, is_dest)
+            if r == 0:
+                named.append(is_dest)
+    member = group_mask(k_dev, n_patch)[0].astype(bf16)
+    n_rows = k_dev * n_patch
+    for i, is_dest in enumerate(named):
+        count = dot_f32(counts.astype(bf16), is_dest).astype(bf16)
+        weights[:, i * n_rows : (i + 1) * n_rows] = 1.0 / dot_f32(count, member)
+    for i in range(2):
+        send[i * 2 * ex_dev : (i + 1) * 2 * ex_dev, :] = whole[place(me ^ (2 + i), 2 * ex_dev), :]
+
+
+def text_relay_body(whole, received, send):
+    n_share = received.shape[0] // 2
+    send[0:n_share, :] = whole[place(lax.axis_index("mdl") ^ 1, n_share), :]
+    send[n_share:, :] = received[n_share:, :]
+
+
+def share_body(whole, from_x, from_core, share, values):
+    n_share, width = share.shape[0], whole.shape[1]
+    me = lax.axis_index("mdl")
+    pieces = (
+        whole[place(me, n_share), :],
+        from_core[0:n_share, :],
+        from_x[0:n_share, :],
+        from_core[n_share:, :],
+    )
+    for j, piece in enumerate(pieces):
+        values[:, place(me ^ j, width)] = piece.astype(f32)
+    rows = values[...]
+    norm_sq = jnp.sum(rows * rows, axis=1, keepdims=True)
+    share[...] = (rows * lax.rsqrt(norm_sq + eps)).astype(bf16)
+
+
+def stage_body(up, down, up_held, down_held, sems):
+    copies = [
+        pltpu.make_async_copy(up, up_held, sems.at[0]),
+        pltpu.make_async_copy(down, down_held, sems.at[1]),
+    ]
+    for copy in copies:
+        copy.start()
+    for copy in copies:
+        copy.wait()
+
+
+def chunk_work(n_patch, tok, cot, w_up, w_down, pre, mixed):
+    k_dev = tok.shape[0] // n_patch
+    groups = group_mask(k_dev, n_patch)[0].astype(bf16)
+    pre_act = dot_f32(tok[...], w_up[...])
+    activated, gelu_slope = gelu_parts(pre_act)
+    pre[...] = (dot_rows(cot[...], w_down[...]) * gelu_slope).astype(bf16)
+    pooled = dot_f32(groups, activated.astype(bf16))
+    high = pooled.astype(bf16)
+    low = (pooled - high.astype(f32)).astype(bf16)
+    both = dot_f32(jnp.concatenate([high, low], axis=0), w_down[...])
+    return mixed + (both[:k_dev] + both[k_dev:])
+
+
+def first_chunk_body(
+    n_patch, n_mdl, b0, b1, b2, b3, w_up, w_down, pre, mixed, tok_full, tok, cot, cot_full
+):
+    d_part, n_rows = b0.shape[0] // 2, b0.shape[1]
+    groups = group_mask(n_rows // n_patch, n_patch)[0].astype(bf16)
+    me = lax.axis_index("mdl")
+    for j, piece in enumerate((b0, b1, b2, b3)):
+        tok_full[place(me ^ j, d_part), :] = piece[0:d_part, :]
+        cot_full[place(me ^ j, d_part), :] = piece[d_part:, :]
+    tok[...] = tok_full[...].T
+    cot[...] = cot_full[...].T
+    start = dot_f32(groups, tok[...]) * (1.0 / n_mdl)
+    mixed[...] = chunk_work(n_patch, tok, cot, w_up, w_down, pre, start)
+
+
+def next_chunk_body(n_patch, tok, cot, w_up, w_down, mixed_in, pre, mixed):
+    mixed[...] = chunk_work(n_patch, tok, cot, w_up, w_down, pre, mixed_in[...])
+
+
+def split_part(part, keep, send):
+    n_keep = keep.shape[0]
+    keep[...] = part[:n_keep]
+    send[...] = part[n_keep:].astype(bf16)
+
+
+def first_grad_body(tok_full, h0, h1, h2, h3, weights, pre, pre_pair, pair, keep, send):
+    n_rows = tok_full.shape[1]
+    blk = h0.shape[0]
+    me = lax.axis_index("mdl")
+    sel = lax.axis_index("sel")
+    parity, high = lax.rem(sel, 2), lax.div(sel, 2)
+    for j, piece in enumerate((h0, h1, h2, h3)):
+        block = me ^ j
+        apart = block ^ high
+        rows = place(2 * lax.rem(apart, 2) + lax.div(apart, 2), blk)
+        own_tok = tok_full[place(2 * block + parity, blk), :].astype(f32)
+        pair[rows, 0:n_rows] = (own_tok * weights[0:1, 0:n_rows]).astype(bf16)
+        pair_tok = piece[:, 0:n_rows].astype(f32)
+        pair[rows, n_rows:] = (pair_tok * weights[0:1, n_rows:]).astype(bf16)
+    grad_body(pair, pre, pre_pair, keep, send)
+
+
+def grad_body(pair, pre, pre_pair, keep, send):
+    n_rows = pre.shape[0]
+    part = dot_f32(pair[:, 0:n_rows], pre[...]) + dot_f32(pair[:, n_rows:], pre_pair[...])
+    split_part(part, keep, send)
+
+
+def add_body(held, received, keep, send):
+    split_part(held[...] + received[...].astype(f32), keep, send)
+
+
+def mix_body(a, b, total):
+    total[...] = (a[...] + b[...]).astype(total.dtype)
+
+
+def heads_body(n_patch, h0, h1, h2, h3, a, b, ref_proj, emb, pooled):
+    me = lax.axis_index("mdl")
+    n_rows = h0.shape[0]
+    n_ex = pooled.shape[1]
+    first = h0.shape[1] - 2 * n_ex
+    for j, piece in enumerate((h0, h1, h2, h3)):
+        for part in range(2):
+            pooled[place((me ^ j) * 2 + part, n_rows), :] = piece[
+                :, first + part * n_ex : first + (part + 1) * n_ex
+            ]
+    learn_pool = ((a[...].astype(f32) + b[...].astype(f32)) * (1.0 / n_patch)).astype(bf16)
+    emb[0:n_ex, :] = dot_cols(pooled[...], ref_proj[...])
+    emb[n_ex:, :] = dot_f32(learn_pool, ref_proj[...])
+
+
+def own_score(hat, texts):
+    return jnp.sum(hat.astype(f32) * texts.astype(f32), axis=1, keepdims=True)
+
+
+def scores_body(e0, e1, e2, e3, share, kept, out, whole):
+    me = lax.axis_index("mdl")
+    sel = lax.axis_index("sel")
+    width = e0.shape[1]
+    for j, piece in enumerate((e0, e1, e2, e3)):
+        whole[:, place(me ^ j, width)] = piece[...]
+    values = whole[...]
+    norm_sq = jnp.sum(values * values, axis=1, keepdims=True)
+    hat = (values * lax.rsqrt(norm_sq + eps)).astype(bf16)
+    k_dev = kept.shape[1]
+    n_all = hat.shape[0]
+    ex_dev = n_all - k_dev
+    scores = dot_rows(share[...], hat)
+    out[:, 0:n_all] = jnp.sum(jnp.exp(logit_scale * scores), axis=0, keepdims=True)
+    own_text = share[place(lax.rem(sel, 2), ex_dev), :]
+    holds = me == lax.div(sel, 2)
+    pick = (lax.broadcasted_iota(jnp.int32, (ex_dev, k_dev), 0) == kept[...]).astype(bf16)
+    kept_text = dot_cols(pick, own_text)
+    learn_own = as_row(own_score(hat[ex_dev:], kept_text))
+    image_own = as_row(own_score(hat[:ex_dev], own_text))
+    out[:, n_all : n_all + k_dev] = jnp.where(holds, learn_own, 0.0)
+    out[:, n_all + k_dev :] = jnp.where(holds, image_own, 0.0)
+
+
+def losses_body(a, b, kept, ref_loss, learnability):
+    sums = a[...] + b[...]
+    k_dev, ex_dev = kept.shape[1], ref_loss.shape[1]
+    n_all = ex_dev + k_dev
+    losses = jnp.log(sums[:, 0:ex_dev]) - logit_scale * sums[:, n_all + k_dev :]
+    ref_loss[...] = losses
+    learner = jnp.log(sums[:, ex_dev:n_all]) - logit_scale * sums[:, n_all : n_all + k_dev]
+    pick = lax.broadcasted_iota(jnp.int32, (ex_dev, k_dev), 0) == kept[...]
+    picked = jnp.sum(jnp.where(pick, as_row_t(losses), 0.0), axis=0, keepdims=True)
+    learnability[...] = learner - picked
+
+
+def as_row_t(row):
+    n = row.shape[1]
+    return jnp.broadcast_to(row, (n, n)).T[:, 0:1]
+
+
+def after(value, *others):
+    return lax.optimization_barrier((value,) + others)[0] if others else value
+
+
+class Order:
+    def __init__(self):
+        self.last = ()
+
+    def wait(self, *values):
+        self.last = self.last + values
+
+    def call(self, body, out_shape, cost, *operands, **kwargs):
+        operands = list(operands)
+        operands[0] = lax.optimization_barrier((operands[0],) + self.last)[0]
+        result = call(body, out_shape, cost, **kwargs)(*operands)
+        self.last = (result[-1] if isinstance(result, (tuple, list)) else result,)
+        return result
+
+
+def quarter_sel(patches, text, ref_proj, w_up, w_down, kept_index, dest, cotan):
+    n_mdl, n_sel = lax.axis_size("mdl"), lax.axis_size("sel")
+    n_high = n_sel // 2
+    ex_dev, emb_part = text.shape
+    emb_full = emb_part * n_mdl
+    d_part = patches.shape[1]
+    d_full = d_part * n_mdl
+    n_patch = patches.shape[0] // ex_dev
+    k_dev = kept_index.shape[0]
+    n_rows = k_dev * n_patch
+    ff_dev = w_up.shape[1]
+    blk = d_full // n_sel
+    n_share = ex_dev * n_sel // n_mdl
+    n_emb = ex_dev + k_dev
+    kept_row = kept_index.reshape(1, k_dev)
+    dest_row = dest.reshape(1, k_dev)
+    order = Order()
+    whole = lambda shape: pl.BlockSpec(shape, lambda i: (0,) * len(shape))
+    widths = (384, 384, 384, 384)
+    starts = [sum(widths[:c]) for c in range(len(widths))]
+    row_struct = struct((n_rows, d_full), bf16)
+    row_spec = whole((n_rows, d_full))
+    mixed_struct = struct((k_dev, d_full), f32)
+    mixed_spec = whole((k_dev, d_full))
+    small = (2**20, 2**20)
+
+    both, half, pool, texts = order.call(
+        functools.partial(pick_body, n_patch),
+        (
+            struct((2 * d_part, n_rows), bf16),
+            struct((d_part // 2, n_rows), bf16),
+            struct((d_part, ex_dev), bf16),
+            struct((ex_dev + 16, emb_part), bf16),
+        ),
+        small,
+        patches.T,
+        cotan.T,
+        kept_row,
+        dest_row,
+        text,
+        in_specs=[
+            pl.BlockSpec(memory_space=space)
+            for space in (pltpu.HBM, pltpu.HBM, pltpu.VMEM, pltpu.VMEM, pltpu.HBM)
+        ],
+        scratch_shapes=[
+            pltpu.VMEM((d_part, ex_dev * n_patch), bf16),
+            pltpu.SemaphoreType.DMA((3,)),
+        ],
+    )
+    both_x = swap(both, "mdl", 2)
+    both_core = swap(both, "mdl", 1)
+    text_pieces = [texts] + [rotate_pairs(texts, s) for s in range(1, n_high)]
+    half = lax.optimization_barrier((half, both_core))[0]
+    half_pair = swap(half, "sel", 1)
+    held_up, held_down = order.call(
+        stage_body,
+        (struct(w_up.shape, bf16), struct(w_down.shape, bf16)),
+        small,
+        w_up,
+        w_down,
+        in_specs=[pl.BlockSpec(memory_space=pltpu.HBM)] * 2,
+        scratch_shapes=[pltpu.SemaphoreType.DMA((2,))],
+    )
+    extras, my_texts = order.call(
+        extras_body,
+        (
+            struct((d_part // 2, n_rows + 2 * ex_dev), bf16),
+            struct((n_high * (ex_dev + 16), emb_part), bf16),
+        ),
+        small,
+        half_pair,
+        pool,
+        *text_pieces,
+    )
+    both_x = lax.optimization_barrier((both_x, extras))[0]
+    both_diag = swap(both_x, "mdl", 1)
+    pair_texts = swap(my_texts, "sel", 1)
+    extra_pieces = mdl_pieces(extras)
+    order.wait(extra_pieces[1])
+
+    def weight_specs(c):
+        first, size = starts[c] // widths[c], widths[c]
+        if starts[c] % size == 0:
+            return [
+                pl.BlockSpec((d_full, size), lambda i: (0, first)),
+                pl.BlockSpec((size, d_full), lambda i: (first, 0)),
+            ]
+        start = starts[c]
+        return [
+            pl.BlockSpec((pl.Element(d_full), pl.Element(size)), lambda i: (0, start)),
+            pl.BlockSpec((pl.Element(size), pl.Element(d_full)), lambda i: (start, 0)),
+        ]
+
+    pres = [None] * len(widths)
+    pair_pres = list(pres)
+
+    def chunk(c, state):
+        size = widths[c]
+        tok, cot, mixed = state
+        cost = (4 * n_rows * d_full * size, 8 * d_full * size)
+        pre_struct = struct((n_rows, size), bf16)
+        if c == 0:
+            pre, mixed, tok_full, tok, cot = order.call(
+                functools.partial(first_chunk_body, n_patch, n_mdl),
+                (pre_struct, mixed_struct, struct((d_full, n_rows), bf16), row_struct, row_struct),
+                cost,
+                both,
+                both_core,
+                both_x,
+                both_diag,
+                held_up,
+                held_down,
+                grid=(1,),
+                in_specs=[whole((2 * d_part, n_rows))] * 4 + weight_specs(c),
+                out_specs=[
+                    whole((n_rows, size)),
+                    mixed_spec,
+                    whole((d_full, n_rows)),
+                    row_spec,
+                    row_spec,
+                ],
+                scratch_shapes=[pltpu.VMEM((d_full, n_rows), bf16)],
+            )
+        else:
+            tok_full = None
+            pre, mixed = order.call(
+                functools.partial(next_chunk_body, n_patch),
+                (pre_struct, mixed_struct),
+                cost,
+                tok,
+                cot,
+                held_up,
+                held_down,
+                mixed,
+                grid=(1,),
+                in_specs=[row_spec, row_spec] + weight_specs(c) + [mixed_spec],
+                out_specs=[whole((n_rows, size)), mixed_spec],
+            )
+        pres[c] = pre
+        if c < 2:
+            pair_pres[c] = swap(pre, "sel", 1)
+        return (tok, cot, mixed), tok_full
+
+    state, tok_full = chunk(0, (None, None, None))
+    state, _ = chunk(1, state)
+
+    all_texts, text_send, weights = order.call(
+        functools.partial(text_body, k_dev, n_patch),
+        (
+            struct((ex_dev * n_sel, emb_part), bf16),
+            struct((2 * n_share, emb_part), bf16),
+            struct((8, 2 * n_rows), f32),
+        ),
+        small,
+        my_texts,
+        pair_texts,
+    )
+    state, _ = chunk(2, state)
+    order.wait(extra_pieces[2])
+    state, _ = chunk(3, state)
+
+    parts = [None] * len(widths)
+
+    def first_half(c, pair):
+        size = widths[c]
+        cost = (4 * n_rows * blk * n_high * size, 4 * 2**20)
+        halves = (struct((2 * blk, size), f32), struct((2 * blk, size), bf16))
+        if c == 0:
+            pair, keep, send = order.call(
+                first_grad_body,
+                (struct((blk * n_high, 2 * n_rows), bf16),) + halves,
+                cost,
+                tok_full,
+                *extra_pieces,
+                weights,
+                pres[c],
+                pair_pres[c],
+            )
+        else:
+            keep, send = order.call(grad_body, halves, cost, pair, pres[c], pair_pres[c])
+        parts[c] = [keep, swap(send, "sel", 2)]
+        return pair
+
+    def second_half(c):
+        if c > 1:
+            order.wait(parts[c - 2][1])
+        keep, send = order.call(
+            add_body,
+            (struct((blk, widths[c]), f32), struct((blk, widths[c]), bf16)),
+            (2**16, 2**20),
+            *parts[c],
+        )
+        parts[c] = [keep, swap(send, "sel", 4)]
+
+    pair = first_half(0, None)
+    mixed = state[2]
+    mixed_core = swap(mixed, "mdl", 1)
+    first_half(1, pair)
+    pair_pres[2] = swap(after(pres[2], parts[1][0]), "sel", 1)
+    text_x = swap(after(text_send, parts[1][0]), "mdl", 2)
+    mixed = order.call(mix_body, struct((k_dev, d_full), bf16), small, mixed, mixed_core)
+    mixed_x = swap(mixed, "mdl", 2)
+    second_half(0)
+    pair_pres[3] = swap(after(pres[3], parts[0][0]), "sel", 1)
+    relay = order.call(
+        text_relay_body, struct((2 * n_share, emb_part), bf16), small, all_texts, text_x
+    )
+    text_core = swap(relay, "mdl", 1)
+    emb = order.call(
+        functools.partial(heads_body, n_patch),
+        struct((n_emb, emb_part), f32),
+        small,
+        *extra_pieces,
+        mixed,
+        mixed_x,
+        ref_proj,
+        scratch_shapes=[pltpu.VMEM((d_full, ex_dev), bf16)],
+    )
+    emb_pieces = mdl_pieces(emb)
+    first_half(2, pair)
+    second_half(1)
+    share = order.call(
+        share_body,
+        struct((n_share, emb_full), bf16),
+        small,
+        all_texts,
+        text_x,
+        text_core,
+        scratch_shapes=[pltpu.VMEM((n_share, emb_full), f32)],
+    )
+    first_half(3, pair)
+    sums = order.call(
+        scores_body,
+        struct((1, 2 * n_emb), f32),
+        small,
+        *emb_pieces,
+        share,
+        kept_row,
+        scratch_shapes=[pltpu.VMEM((n_emb, emb_full), f32)],
+    )
+    sums_core = swap(sums, "mdl", 1)
+    second_half(2)
+    sums = order.call(mix_body, struct((1, 2 * n_emb), f32), small, sums, sums_core)
+    sums_x = swap(sums, "mdl", 2)
+    second_half(3)
+    ref_loss, learnability = order.call(
+        losses_body,
+        (struct((1, ex_dev), f32), struct((1, k_dev), f32)),
+        small,
+        sums,
+        sums_x,
+        kept_row,
+    )
+    parts[-1][0], ref_loss, learnability = lax.optimization_barrier(
+        (parts[-1][0], ref_loss, learnability)
+    )
+    grad_up = jnp.concatenate([own + other.astype(f32) for own, other in parts], axis=1)
+    return (ref_loss.reshape(ex_dev), learnability.reshape(k_dev), grad_up)
+
+
 def solution(mesh):
     in_specs = (
         P("sel", "mdl"),
@@ -215,6 +776,7 @@
         P("sel", "mdl"),
     )
     out_specs = (P("sel"), P("sel"), P("sel", "mdl"))
+    body = quarter_sel if (mesh.shape["sel"], mesh.shape["mdl"]) == (8, 4) else per_device
     return jax.shard_map(
-        per_device, mesh=mesh, in_specs=in_specs, out_specs=out_specs, check_vma=False
-    )
+        body, mesh=mesh, in_specs=in_specs, out_specs=out_specs, check_vma=False
+    )

time: 181 us -> 90.5 us (0.50)
  matrix products: 29.9 us -> 0 us
  other arithmetic: 26.1 us -> 1.23 us
  starting transfers between devices: 52.6 us -> 28.6 us
  Pallas kernels: 0 us -> 19.6 us
  waiting for transfers between devices: 49.2 us -> 31.4 us
  local copies, waits for them, and re-layouts: 20.9 us -> 8.4 us
    dot_general x15 -> x0, matrix products: 29.9 us -> none  [the longest x1 6.51 us: per_device(): lax.dot_general(tok_full, w_up, (((0,), (0,)), ((), ())), preferred_eleme...]
    ppermute x18 -> x3, starting transfers between devices: 33.7 us -> 5.51 us  [rotate_pairs(): lax.ppermute(value, 'sel', [(i, (i + 2 * step) % size) for i in range(siz...]
    ppermute x18 -> x3, waiting for transfers between devices: 26.4 us -> 0.01 us  [rotate_pairs(): lax.ppermute(value, 'sel', [(i, (i + 2 * step) % size) for i in range(siz...]
    pallas_call x0 -> x23, Pallas kernels: none -> 19.6 us  [call(): result = call(body, out_shape, cost, **kwargs)(*operands)]
    select_n x18 -> x0, other arithmetic: 12.5 us -> none  [the longest x17 11.8 us: in_order(): jnp.where(set_bit, jnp.concatenate([second, first], axis), jnp.concatenat...]
    ppermute x32 -> x29, waiting for transfers between devices: 22.8 us -> 31.4 us  [swap(): return lax.ppermute(value, axis, [(i, i ^ bit) for i in range(size)])]
    reduce_sum x9 -> x0, other arithmetic: 5.82 us -> none  [the longest x1 2.71 us: per_device(): mixed_pool = mdl_sum(jnp.sum(mixed.reshape(k_dev, n_patch, -1), axis=1))]
    div x1 -> x0, other arithmetic: 5 us -> none  [per_device(): row_weight = 1.0 / jnp.repeat(counts[dest], n_patch)]
  transfers between devices with their start and end apart: 50 -> 32, of which waited for: 15 -> 9; matrix products, arithmetic and copies ran while one was open for 41% -> 0% of each run, Pallas kernels for 0% -> 20%
where the time goes in v3:
time: 90.5 us; the launch traced here: 90.1 us
  waiting for transfers between devices  31.4 us (35%)
  starting transfers between devices  28.6 us (32%)
  Pallas kernels  19.6 us (22%)
  local copies, waits for them, and re-layouts  8.4 us (9%)
  other arithmetic  1.23 us (1%)
  between operations  0.94 us (1%)
    ppermute x29, waiting for transfers between devices, swap(): return lax.ppermute(value, axis, [(i, i ^ bit) for i in range(size)])  31.4 us
    ppermute x29, starting transfers between devices, swap(): return lax.ppermute(value, axis, [(i, i ^ bit) for i in range(size)])  23 us
    pallas_call x23, Pallas kernels, call(): result = call(body, out_shape, cost, **kwargs)(*operands)  19.6 us
    unnamed x22, local copies, waits for them, and re-layouts  8.4 us
    ppermute x3, starting transfers between devices, rotate_pairs(): lax.ppermute(value, 'sel', [(i, (i + 2 * step) % size) for i in range(siz...  5.51 us
  transfers between devices with their start and end apart: 32, of which 9 were waited for; matrix products, arithmetic and copies ran while one was open for 0% of the time, Pallas kernels for 20%

profile of v3, /device:TPU:0, one launch (start us, length us, event | category | flops | bytes accessed | tf_op | source)
XLA Modules:
  0.0 90.1 jit_solution(2075608283632409756)
XLA Ops:
  0.6 1.0 %copy-done.3 = bf16[768,352]{0,1:T(8,128)(2,1)S(1)} copy-done((bf16[768,352]{0,1:T(8,128)(2,1)S(1)}, bf16[768,352]{0,1:T(8,128)(2,1)}, u32[]{:S(2)}) %copy-start.3) | copy-done | bytes 540696
  1.7 1.0 %copy-done.4 = bf16[384,352]{0,1:T(8,128)(2,1)S(1)} copy-done((bf16[384,352]{0,1:T(8,128)(2,1)S(1)}, bf16[384,352]{0,1:T(8,128)(2,1)}, u32[]{:S(2)}) %copy-start.4) | copy-done | bytes 270360
  2.6 0.8 copy-done.5
  3.5 0.7 copy-done.6
  4.1 0.7 copy-done.8
  4.8 1.2 %shard_map.103 = (bf16[704,384]{1,0:T(8,128)(2,1)S(1)}, bf16[176,384]{1,0:T(8,128)(2,1)S(1)}, bf16[352,128]{1,0:T(8,128)(2,1)S(1)}, bf16[144,256]{1,0:T(8,128)(2,1)S(1)}) custom-call(bf16[352,768]{1,0:T(8,128)(2,1)S(1)} %bitcast.8, bf16[352,384]{1,0:T(8,128)(2,1)S(1)} %bitcast.9, s32[1,64]{1,0:T(1,128)S(1)} %bitcast.10, s32[1,64]{1,0:T(1,128)S(1)} %bitcast.13, ...), custom_call_target="tpu_custom_call" | custom-call | flops 1 | bytes 1 | tf_op jit(solution)/shard_map/pallas_call | solution.py:502
  5.9 0.5 collective-permute-start
  6.5 2.6 %collective-permute-start.6 = (bf16[704,384]{1,0:T(8,128)(2,1)S(1)}, bf16[704,384]{1,0:T(8,128)(2,1)S(1)}, u32[]{:S(2)}, u32[]{:S(2)}) collective-permute-start(bf16[704,384]{1,0:T(8,128)(2,1)S(1)} %get-tuple-element.84.b0), channel_id=1, source_target_pairs={{0,2},{1,3},{2,0},{3,1},{4,6},{5,7},{6,4},{7,5},{8,10},{9,11},{10,... | collective-permute-start | bytes 1622024 | tf_op jit(solution)/shard_map/ppermute | solution.py:24
  9.0 1.9 %collective-permute-start.1 = (bf16[176,384]{1,0:T(8,128)(2,1)S(1)}, bf16[176,384]{1,0:T(8,128)(2,1)S(1)}, u32[]{:S(2)}, u32[]{:S(2)}) collective-permute-start(bf16[176,384]{1,0:T(8,128)(2,1)S(1)} %get-tuple-element.76), channel_id=1, source_target_pairs={{0,4},{4,0},{8,12},{12,8},{16,20},{20,16},{24,28},{28,24},{1,5},{5... | collective-permute-start | bytes 405512 | tf_op jit(solution)/shard_map/ppermute | solution.py:24
  10.9 1.6 %collective-permute-start.2 = (bf16[144,256]{1,0:T(8,128)(2,1)S(1)}, bf16[144,256]{1,0:T(8,128)(2,1)S(1)}, u32[]{:S(2)}, u32[]{:S(2)}) collective-permute-start(bf16[144,256]{1,0:T(8,128)(2,1)S(1)} %get-tuple-element.77.t0), channel_id=1, source_target_pairs={{0,8},{4,12},{8,16},{12,20},{16,24},{20,28},{24,0},{28,4},{1,9},{5... | collective-permute-start | bytes 221192 | tf_op jit(solution)/shard_map/ppermute | solution.py:29
  12.5 2.6 %collective-permute-start.3 = (bf16[144,256]{1,0:T(8,128)(2,1)S(1)}, bf16[144,256]{1,0:T(8,128)(2,1)S(1)}, u32[]{:S(2)}, u32[]{:S(2)}) collective-permute-start(bf16[144,256]{1,0:T(8,128)(2,1)S(1)} %get-tuple-element.77.t0), channel_id=1, source_target_pairs={{0,16},{4,20},{8,24},{12,28},{16,0},{20,4},{24,8},{28,12},{1,17},{... | collective-permute-start | bytes 221192 | tf_op jit(solution)/shard_map/ppermute | solution.py:29
  15.1 1.4 %collective-permute-start.4 = (bf16[144,256]{1,0:T(8,128)(2,1)S(1)}, bf16[144,256]{1,0:T(8,128)(2,1)S(1)}, u32[]{:S(2)}, u32[]{:S(2)}) collective-permute-start(bf16[144,256]{1,0:T(8,128)(2,1)S(1)} %get-tuple-element.77.t0), channel_id=1, source_target_pairs={{0,24},{4,28},{8,0},{12,4},{16,8},{20,12},{24,16},{28,20},{1,25},{... | collective-permute-start | bytes 221192 | tf_op jit(solution)/shard_map/ppermute | solution.py:29
  16.4 2.2 %copy-done.1 = bf16[1408,1536]{1,0:T(8,128)(2,1)S(1)} copy-done((bf16[1408,1536]{1,0:T(8,128)(2,1)S(1)}, bf16[1408,1536]{1,0:T(8,128)(2,1)}, u32[]{:S(2)}) %copy-start.1) | copy-done | bytes 4325400
  18.6 2.7 %shard_map.104 = (bf16[1408,1536]{1,0:T(8,128)(2,1)S(1)}, bf16[1536,1408]{1,0:T(8,128)(2,1)S(1)}) custom-call(bf16[1408,1536]{1,0:T(8,128)(2,1)S(1)} %copy-done.1, bf16[1536,1408]{1,0:T(8,128)(2,1)} %down.1), custom_call_target="tpu_custom_call" | custom-call | flops 1 | bytes 1 | tf_op jit(solution)/shard_map/pallas_call | solution.py:502
  21.3 2.0 %copy-done = bf16[1536,1408]{1,0:T(8,128)(2,1)} copy-done((bf16[1536,1408]{1,0:T(8,128)(2,1)}, bf16[1536,1408]{1,0:T(8,128)(2,1)S(1)}, u32[]{:S(2)}) %copy-start) | copy-done | bytes 4325400
  23.4 0.1 collective-permute-start.7
  23.5 0.5 collective-permute-start.5
  24.0 0.5 collective-permute-start.8
  24.5 1.5 %collective-permute-start.9 = (bf16[176,640]{1,0:T(8,128)(2,1)S(1)}, bf16[176,640]{1,0:T(8,128)(2,1)S(1)}, u32[]{:S(2)}, u32[]{:S(2)}) collective-permute-start(bf16[176,640]{1,0:T(8,128)(2,1)S(1)} %get-tuple-element.115.h0), channel_id=1, source_target_pairs={{0,2},{1,3},{2,0},{3,1},{4,6},{5,7},{6,4},{7,5},{8,10},{9,11},{10,... | collective-permute-start | bytes 675848 | tf_op jit(solution)/shard_map/ppermute | solution.py:24
  26.1 3.7 %shard_map.106 = (bf16[384,384]{1,0:T(8,128)(2,1)S(1)}, f32[64,1408]{1,0:T(8,128)S(1)}, bf16[1408,384]{1,0:T(8,128)(2,1)S(1)}, bf16[384,1408]{1,0:T(8,128)(2,1)S(1)}, bf16[384,1408]{1,0:T(8,128)(2,1)S(1)}) custom-call(bf16[704,384]{1,0:T(8,128)(2,1)S(1)} %get-tuple-element.84.b0, bf16[704,384]{1,0:T(8,128)(2,1)S(1)} %collective-permute-done.b1, ...), custom_call_target="tpu_custom_call" | custom-call | flops 1 | bytes 1 | tf_op jit(solution)/shard_map/pallas_call | solution.py:502
  29.7 1.6 %collective-permute-start.11 = (bf16[384,384]{1,0:T(8,128)(2,1)S(1)}, bf16[384,384]{1,0:T(8,128)(2,1)S(1)}, u32[]{:S(2)}, u32[]{:S(2)}) collective-permute-start(bf16[384,384]{1,0:T(8,128)(2,1)S(1)} %get-tuple-element.100.pre), channel_id=1, source_target_pairs={{0,4},{4,0},{8,12},{12,8},{16,20},{20,16},{24,28},{28,24},{1,5},{5... | collective-permute-start | bytes 884744 | tf_op jit(solution)/shard_map/ppermute | solution.py:24
  31.3 1.8 %shard_map.107 = (bf16[384,384]{1,0:T(8,128)(2,1)S(1)}, f32[64,1408]{1,0:T(8,128)S(1)}) custom-call(bf16[384,1408]{1,0:T(8,128)(2,1)S(1)} %get-tuple-element.97.tok, bf16[384,1408]{1,0:T(8,128)(2,1)S(1)} %get-tuple-element.89.cot, bf16[1408,1536]{1,0:T(8,128)(2,1)S(1)} %get-tuple-element.86.w_up, bf16[1536,1408]{1,0:T(8,128)(2,1)S(1)} %bitcast.7, ...), custom_call_target="tpu_custom_call" | custom-call | flops 1 | bytes 1 | tf_op jit(solution)/shard_map/pallas_call | solution.py:502
  33.1 0.6 collective-permute-start.12
  33.7 0.7 shard_map.108
  34.4 1.8 %shard_map.109 = (bf16[384,384]{1,0:T(8,128)(2,1)S(1)}, f32[64,1408]{1,0:T(8,128)S(1)}) custom-call(bf16[384,1408]{1,0:T(8,128)(2,1)S(1)} %get-tuple-element.97.tok, bf16[384,1408]{1,0:T(8,128)(2,1)S(1)} %get-tuple-element.89.cot, bf16[1408,1536]{1,0:T(8,128)(2,1)S(1)} %get-tuple-element.86.w_up, bf16[1536,1408]{1,0:T(8,128)(2,1)S(1)} %bitcast.7, ...), custom_call_target="tpu_custom_call" | custom-call | flops 1 | bytes 1 | tf_op jit(solution)/shard_map/pallas_call | solution.py:502
  36.2 1.8 %shard_map.110 = (bf16[384,384]{1,0:T(8,128)(2,1)S(1)}, f32[64,1408]{1,0:T(8,128)S(1)}) custom-call(bf16[384,1408]{1,0:T(8,128)(2,1)S(1)} %get-tuple-element.97.tok, bf16[384,1408]{1,0:T(8,128)(2,1)S(1)} %get-tuple-element.89.cot, bf16[1408,1536]{1,0:T(8,128)(2,1)S(1)} %get-tuple-element.86.w_up, bf16[1536,1408]{1,0:T(8,128)(2,1)S(1)} %bitcast.7, ...), custom_call_target="tpu_custom_call" | custom-call | flops 1 | bytes 1 | tf_op jit(solution)/shard_map/pallas_call | solution.py:502
  38.0 0.6 collective-permute-start.13
  38.6 1.4 %collective-permute-done.11.pre_pair = bf16[384,384]{1,0:T(8,128)(2,1)S(1)} collective-permute-done((bf16[384,384]{1,0:T(8,128)(2,1)S(1)}, bf16[384,384]{1,0:T(8,128)(2,1)S(1)}, u32[]{:S(2)}, u32[]{:S(2)}) %collective-permute-start.11) | collective-permute-done | bytes 294944 | tf_op jit(solution)/shard_map/ppermute | solution.py:24
  40.0 1.1 %shard_map.111 = (bf16[704,768]{1,0:T(8,128)(2,1)S(1)}, f32[352,384]{1,0:T(8,128)S(1)}, bf16[352,384]{1,0:T(8,128)(2,1)S(1)}) custom-call(bf16[1408,384]{1,0:T(8,128)(2,1)S(1)} %get-tuple-element.99.tok_full, bf16[176,640]{1,0:T(8,128)(2,1)S(1)} %get-tuple-element.115.h0, bf16[176,640]{1,0:T(8,128)(2,1)S(1)} %collective-permute-done.5.h1, ...), custom_call_target="tpu_custom_call" | custom-call | flops 1 | bytes 1 | tf_op jit(solution)/shard_map/pallas_call | solution.py:502
  41.1 1.0 %collective-permute-start.14 = (bf16[352,384]{1,0:T(8,128)(2,1)S(1)}, bf16[352,384]{1,0:T(8,128)(2,1)S(1)}, u32[]{:S(2)}, u32[]{:S(2)}) collective-permute-start(bf16[352,384]{1,0:T(8,128)(2,1)S(1)} %get-tuple-element.103), channel_id=1, source_target_pairs={{0,8},{4,12},{8,0},{12,4},{16,24},{20,28},{24,16},{28,20},{1,9},{5... | collective-permute-start | bytes 811016 | tf_op jit(solution)/shard_map/ppermute | solution.py:24
  42.1 3.6 %collective-permute-done.12.pre_pair = bf16[384,384]{1,0:T(8,128)(2,1)S(1)} collective-permute-done((bf16[384,384]{1,0:T(8,128)(2,1)S(1)}, bf16[384,384]{1,0:T(8,128)(2,1)S(1)}, u32[]{:S(2)}, u32[]{:S(2)}) %collective-permute-start.12) | collective-permute-done | bytes 294944 | tf_op jit(solution)/shard_map/ppermute | solution.py:24
  45.7 0.8 shard_map.112
  46.5 1.6 %collective-permute-start.15 = (bf16[512,256]{1,0:T(8,128)(2,1)S(1)}, bf16[512,256]{1,0:T(8,128)(2,1)S(1)}, u32[]{:S(2)}, u32[]{:S(2)}) collective-permute-start(bf16[512,256]{1,0:T(8,128)(2,1)S(1)} %get-tuple-element.114), channel_id=1, source_target_pairs={{0,2},{1,3},{2,0},{3,1},{4,6},{5,7},{6,4},{7,5},{8,10},{9,11},{10,... | collective-permute-start | bytes 786440 | tf_op jit(solution)/shard_map/ppermute | solution.py:24
  48.0 0.5 collective-permute-start.17
  48.6 0.6 collective-permute-start.16
  49.2 1.1 %collective-permute-start.18 = (bf16[352,384]{1,0:T(8,128)(2,1)S(1)}, bf16[352,384]{1,0:T(8,128)(2,1)S(1)}, u32[]{:S(2)}, u32[]{:S(2)}) collective-permute-start(bf16[352,384]{1,0:T(8,128)(2,1)S(1)} %get-tuple-element.108), channel_id=1, source_target_pairs={{0,8},{4,12},{8,0},{12,4},{16,24},{20,28},{24,16},{28,20},{1,9},{5... | collective-permute-start | bytes 811016 | tf_op jit(solution)/shard_map/ppermute | solution.py:24
  50.3 0.1 shard_map.114
  50.4 1.1 %collective-permute-start.20 = (bf16[384,384]{1,0:T(8,128)(2,1)S(1)}, bf16[384,384]{1,0:T(8,128)(2,1)S(1)}, u32[]{:S(2)}, u32[]{:S(2)}) collective-permute-start(bf16[384,384]{1,0:T(8,128)(2,1)S(1)} %get-tuple-element.126.pre), channel_id=1, source_target_pairs={{0,4},{4,0},{8,12},{12,8},{16,20},{20,16},{24,28},{28,24},{1,5},{5... | collective-permute-start | bytes 884744 | tf_op jit(solution)/shard_map/ppermute | solution.py:24
  51.5 4.3 %collective-permute-done.15.received.from_x = bf16[512,256]{1,0:T(8,128)(2,1)S(1)} collective-permute-done((bf16[512,256]{1,0:T(8,128)(2,1)S(1)}, bf16[512,256]{1,0:T(8,128)(2,1)S(1)}, u32[]{:S(2)}, u32[]{:S(2)}) %collective-permute-start.15) | collective-permute-done | bytes 262176 | tf_op jit(solution)/shard_map/ppermute | solution.py:24
  55.8 0.1 collective-permute-start.19
  55.9 2.1 %collective-permute-done.16.b = bf16[64,1408]{1,0:T(8,128)(2,1)S(1)} collective-permute-done((bf16[64,1408]{1,0:T(8,128)(2,1)S(1)}, bf16[64,1408]{1,0:T(8,128)(2,1)S(1)}, u32[]{:S(2)}, u32[]{:S(2)}) %collective-permute-start.16) | collective-permute-done | bytes 180256 | tf_op jit(solution)/shard_map/ppermute | solution.py:24
  58.0 0.5 shard_map.116.e0
  58.5 1.6 %collective-permute-start.22 = (f32[192,256]{1,0:T(8,128)S(1)}, f32[192,256]{1,0:T(8,128)S(1)}, u32[]{:S(2)}, u32[]{:S(2)}) collective-permute-start(f32[192,256]{1,0:T(8,128)S(1)} %shard_map.116.e0), channel_id=1, source_target_pairs={{0,2},{1,3},{2,0},{3,1},{4,6},{5,7},{6,4},{7,5},{8,10},{9,11},{10,... | collective-permute-start | bytes 589832 | tf_op jit(solution)/shard_map/ppermute | solution.py:24
  60.1 1.2 %collective-permute-start.24 = (bf16[176,384]{1,0:T(8,128)(2,1)S(1)}, bf16[176,384]{1,0:T(8,128)(2,1)S(1)}, u32[]{:S(2)}, u32[]{:S(2)}) collective-permute-start(bf16[176,384]{1,0:T(8,128)(2,1)S(1)} %get-tuple-element.111), channel_id=1, source_target_pairs={{0,16},{4,20},{8,24},{12,28},{16,0},{20,4},{24,8},{28,12},{1,17},{... | collective-permute-start | bytes 405512 | tf_op jit(solution)/shard_map/ppermute | solution.py:24
  61.3 0.8 shard_map.117
  62.1 1.7 %collective-permute-start.25 = (bf16[352,384]{1,0:T(8,128)(2,1)S(1)}, bf16[352,384]{1,0:T(8,128)(2,1)S(1)}, u32[]{:S(2)}, u32[]{:S(2)}) collective-permute-start(bf16[352,384]{1,0:T(8,128)(2,1)S(1)} %get-tuple-element.119), channel_id=1, source_target_pairs={{0,8},{4,12},{8,0},{12,4},{16,24},{20,28},{24,16},{28,20},{1,9},{5... | collective-permute-start | bytes 811016 | tf_op jit(solution)/shard_map/ppermute | solution.py:24
  63.8 0.1 collective-permute-start.21
  63.9 0.2 shard_map.119.share
  64.2 1.0 %collective-permute-start.27 = (bf16[176,384]{1,0:T(8,128)(2,1)S(1)}, bf16[176,384]{1,0:T(8,128)(2,1)S(1)}, u32[]{:S(2)}, u32[]{:S(2)}) collective-permute-start(bf16[176,384]{1,0:T(8,128)(2,1)S(1)} %get-tuple-element.121), channel_id=1, source_target_pairs={{0,16},{4,20},{8,24},{12,28},{16,0},{20,4},{24,8},{28,12},{1,17},{... | collective-permute-start | bytes 405512 | tf_op jit(solution)/shard_map/ppermute | solution.py:24
  65.3 0.8 shard_map.120
  66.1 1.6 %collective-permute-done.24 = bf16[176,384]{1,0:T(8,128)(2,1)S(1)} collective-permute-done((bf16[176,384]{1,0:T(8,128)(2,1)S(1)}, bf16[176,384]{1,0:T(8,128)(2,1)S(1)}, u32[]{:S(2)}, u32[]{:S(2)}) %collective-permute-start.24) | collective-permute-done | bytes 135200 | tf_op jit(solution)/shard_map/ppermute | solution.py:24
  67.6 0.4 collective-permute-start.28
  68.1 0.8 shard_map.121.a
  68.9 6.6 %collective-permute-done.25.received = bf16[352,384]{1,0:T(8,128)(2,1)S(1)} collective-permute-done((bf16[352,384]{1,0:T(8,128)(2,1)S(1)}, bf16[352,384]{1,0:T(8,128)(2,1)S(1)}, u32[]{:S(2)}, u32[]{:S(2)}) %collective-permute-start.25) | collective-permute-done | bytes 270368 | tf_op jit(solution)/shard_map/ppermute | solution.py:24
  75.5 0.1 shard_map.122
  75.6 0.3 collective-permute-start.30
  75.9 0.4 collective-permute-start.29
  76.3 6.1 %collective-permute-done.28.received = bf16[352,384]{1,0:T(8,128)(2,1)S(1)} collective-permute-done((bf16[352,384]{1,0:T(8,128)(2,1)S(1)}, bf16[352,384]{1,0:T(8,128)(2,1)S(1)}, u32[]{:S(2)}, u32[]{:S(2)}) %collective-permute-start.28) | collective-permute-done | bytes 270368 | tf_op jit(solution)/shard_map/ppermute | solution.py:24
  82.5 0.1 shard_map.124
  82.5 0.1 collective-permute-start.31
  82.6 2.3 %collective-permute-done.30 = bf16[176,384]{1,0:T(8,128)(2,1)S(1)} collective-permute-done((bf16[176,384]{1,0:T(8,128)(2,1)S(1)}, bf16[176,384]{1,0:T(8,128)(2,1)S(1)}, u32[]{:S(2)}, u32[]{:S(2)}) %collective-permute-start.30) | collective-permute-done | bytes 135200 | tf_op jit(solution)/shard_map/ppermute | solution.py:24
  85.0 0.7 shard_map.125
  85.7 3.3 %collective-permute-done.31 = bf16[176,384]{1,0:T(8,128)(2,1)S(1)} collective-permute-done((bf16[176,384]{1,0:T(8,128)(2,1)S(1)}, bf16[176,384]{1,0:T(8,128)(2,1)S(1)}, u32[]{:S(2)}, u32[]{:S(2)}) %collective-permute-start.31) | collective-permute-done | bytes 135200 | tf_op jit(solution)/shard_map/ppermute | solution.py:24
  89.0 1.1 %pad_maximum_fusion = f32[176,1536]{1,0:T(8,128)} fusion(f32[176,384]{1,0:T(8,128)S(1)} %convert_add_fusion, f32[176,384]{1,0:T(8,128)S(1)} %convert_add_fusion.1, f32[176,384]{1,0:T(8,128)S(1)} %convert_add_fusion.2, f32[176,384]{1,0:T(8,128)S(1)} %convert_add_fusion.3), kind=kLoop, calls=%fused_computation | loop fusion | flops 811008 | bytes 2162688 | tf_op jit(solution)/shard_map/concatenate | solution.py:763
  (51 shorter events, 0.5 us)
Async XLA Ops:
  0.6 1.0 %copy-start.3 = (bf16[768,352]{0,1:T(8,128)(2,1)S(1)}, bf16[768,352]{0,1:T(8,128)(2,1)}, u32[]{:S(2)}) copy-start(bf16[768,352]{0,1:T(8,128)(2,1)} %param.8) | copy-start | bytes 1622020
  1.7 1.0 %copy-start.4 = (bf16[384,352]{0,1:T(8,128)(2,1)S(1)}, bf16[384,352]{0,1:T(8,128)(2,1)}, u32[]{:S(2)}) copy-start(bf16[384,352]{0,1:T(8,128)(2,1)} %param.15) | copy-start | bytes 811012
  2.6 0.8 copy-start.5
  3.5 0.7 copy-start.6
  4.1 0.7 copy-start.8
  5.9 3.1 %collective-permute-start = (bf16[704,384]{1,0:T(8,128)(2,1)S(1)}, bf16[704,384]{1,0:T(8,128)(2,1)S(1)}, u32[]{:S(2)}, u32[]{:S(2)}) collective-permute-start(bf16[704,384]{1,0:T(8,128)(2,1)S(1)} %get-tuple-element.84.b0), channel_id=1, source_target_pairs={{0,1},{1,0},{2,3},{3,2},{4,5},{5,4},{6,7},{7,6},{8,9},{9,8},{10,11... | collective-permute-start | bytes 1622024 | tf_op jit(solution)/shard_map/ppermute | solution.py:24
  6.5 17.0 %collective-permute-start.6 = (bf16[704,384]{1,0:T(8,128)(2,1)S(1)}, bf16[704,384]{1,0:T(8,128)(2,1)S(1)}, u32[]{:S(2)}, u32[]{:S(2)}) collective-permute-start(bf16[704,384]{1,0:T(8,128)(2,1)S(1)} %get-tuple-element.84.b0), channel_id=1, source_target_pairs={{0,2},{1,3},{2,0},{3,1},{4,6},{5,7},{6,4},{7,5},{8,10},{9,11},{10,... | collective-permute-start | bytes 1622024 | tf_op jit(solution)/shard_map/ppermute | solution.py:24
  9.0 14.3 %collective-permute-start.1 = (bf16[176,384]{1,0:T(8,128)(2,1)S(1)}, bf16[176,384]{1,0:T(8,128)(2,1)S(1)}, u32[]{:S(2)}, u32[]{:S(2)}) collective-permute-start(bf16[176,384]{1,0:T(8,128)(2,1)S(1)} %get-tuple-element.76), channel_id=1, source_target_pairs={{0,4},{4,0},{8,12},{12,8},{16,20},{20,16},{24,28},{28,24},{1,5},{5... | collective-permute-start | bytes 405512 | tf_op jit(solution)/shard_map/ppermute | solution.py:24
  10.9 12.5 %collective-permute-start.2 = (bf16[144,256]{1,0:T(8,128)(2,1)S(1)}, bf16[144,256]{1,0:T(8,128)(2,1)S(1)}, u32[]{:S(2)}, u32[]{:S(2)}) collective-permute-start(bf16[144,256]{1,0:T(8,128)(2,1)S(1)} %get-tuple-element.77.t0), channel_id=1, source_target_pairs={{0,8},{4,12},{8,16},{12,20},{16,24},{20,28},{24,0},{28,4},{1,9},{5... | collective-permute-start | bytes 221192 | tf_op jit(solution)/shard_map/ppermute | solution.py:29
  12.5 10.9 %collective-permute-start.3 = (bf16[144,256]{1,0:T(8,128)(2,1)S(1)}, bf16[144,256]{1,0:T(8,128)(2,1)S(1)}, u32[]{:S(2)}, u32[]{:S(2)}) collective-permute-start(bf16[144,256]{1,0:T(8,128)(2,1)S(1)} %get-tuple-element.77.t0), channel_id=1, source_target_pairs={{0,16},{4,20},{8,24},{12,28},{16,0},{20,4},{24,8},{28,12},{1,17},{... | collective-permute-start | bytes 221192 | tf_op jit(solution)/shard_map/ppermute | solution.py:29
  15.1 8.3 %collective-permute-start.4 = (bf16[144,256]{1,0:T(8,128)(2,1)S(1)}, bf16[144,256]{1,0:T(8,128)(2,1)S(1)}, u32[]{:S(2)}, u32[]{:S(2)}) collective-permute-start(bf16[144,256]{1,0:T(8,128)(2,1)S(1)} %get-tuple-element.77.t0), channel_id=1, source_target_pairs={{0,24},{4,28},{8,0},{12,4},{16,8},{20,12},{24,16},{28,20},{1,25},{... | collective-permute-start | bytes 221192 | tf_op jit(solution)/shard_map/ppermute | solution.py:29
  16.4 2.2 %copy-start.1 = (bf16[1408,1536]{1,0:T(8,128)(2,1)S(1)}, bf16[1408,1536]{1,0:T(8,128)(2,1)}, u32[]{:S(2)}) copy-start(bf16[1408,1536]{1,0:T(8,128)(2,1)} %up) | copy-start | bytes 12976132
  21.3 2.0 %copy-start = (bf16[1536,1408]{1,0:T(8,128)(2,1)}, bf16[1536,1408]{1,0:T(8,128)(2,1)S(1)}, u32[]{:S(2)}) copy-start(bf16[1536,1408]{1,0:T(8,128)(2,1)S(1)} %get-tuple-element.79.w_down) | copy-start | bytes 12976132
  23.4 2.6 %collective-permute-start.7 = (bf16[704,384]{1,0:T(8,128)(2,1)S(1)}, bf16[704,384]{1,0:T(8,128)(2,1)S(1)}, u32[]{:S(2)}, u32[]{:S(2)}) collective-permute-start(bf16[704,384]{1,0:T(8,128)(2,1)S(1)} %collective-permute-done.6.b2), channel_id=1, source_target_pairs={{0,1},{1,0},{2,3},{3,2},{4,5},{5,4},{6,7},{7,6},{8,9},{9,8},{10,11... | collective-permute-start | bytes 1622024 | tf_op jit(solution)/shard_map/ppermute | solution.py:24
  23.5 2.5 %collective-permute-start.5 = (bf16[176,640]{1,0:T(8,128)(2,1)S(1)}, bf16[176,640]{1,0:T(8,128)(2,1)S(1)}, u32[]{:S(2)}, u32[]{:S(2)}) collective-permute-start(bf16[176,640]{1,0:T(8,128)(2,1)S(1)} %get-tuple-element.115.h0), channel_id=1, source_target_pairs={{0,1},{1,0},{2,3},{3,2},{4,5},{5,4},{6,7},{7,6},{8,9},{9,8},{10,11... | collective-permute-start | bytes 675848 | tf_op jit(solution)/shard_map/ppermute | solution.py:24
  24.0 9.7 %collective-permute-start.8 = (bf16[576,256]{1,0:T(8,128)(2,1)S(1)}, bf16[576,256]{1,0:T(8,128)(2,1)S(1)}, u32[]{:S(2)}, u32[]{:S(2)}) collective-permute-start(bf16[576,256]{1,0:T(8,128)(2,1)S(1)} %get-tuple-element.93.mine), channel_id=1, source_target_pairs={{0,4},{4,0},{8,12},{12,8},{16,20},{20,16},{24,28},{28,24},{1,5},{5... | collective-permute-start | bytes 884744 | tf_op jit(solution)/shard_map/ppermute | solution.py:24
  24.5 9.2 %collective-permute-start.9 = (bf16[176,640]{1,0:T(8,128)(2,1)S(1)}, bf16[176,640]{1,0:T(8,128)(2,1)S(1)}, u32[]{:S(2)}, u32[]{:S(2)}) collective-permute-start(bf16[176,640]{1,0:T(8,128)(2,1)S(1)} %get-tuple-element.115.h0), channel_id=1, source_target_pairs={{0,2},{1,3},{2,0},{3,1},{4,6},{5,7},{6,4},{7,5},{8,10},{9,11},{10,... | collective-permute-start | bytes 675848 | tf_op jit(solution)/shard_map/ppermute | solution.py:24
  26.0 5.3 %slice-start = ((s8[4325376]{0:T(1024)(128)(4,1)}), s8[4194304]{0:T(1024)(128)(4,1)S(1)}, s32[]{:S(2)}) async-start(s8[4325376]{0:T(1024)(128)(4,1)} %bitcast.6), calls=%async_computation | async-start | bytes 8388608
  26.0 5.3 %slice-start.1 = ((s8[4325376]{0:T(1024)(128)(4,1)}), s8[131072]{0:T(1024)(128)(4,1)S(1)}, s32[]{:S(2)}) async-start(s8[4325376]{0:T(1024)(128)(4,1)} %bitcast.6), calls=%async_computation.1 | async-start | bytes 262144
  29.7 10.3 %collective-permute-start.11 = (bf16[384,384]{1,0:T(8,128)(2,1)S(1)}, bf16[384,384]{1,0:T(8,128)(2,1)S(1)}, u32[]{:S(2)}, u32[]{:S(2)}) collective-permute-start(bf16[384,384]{1,0:T(8,128)(2,1)S(1)} %get-tuple-element.100.pre), channel_id=1, source_target_pairs={{0,4},{4,0},{8,12},{12,8},{16,20},{20,16},{24,28},{28,24},{1,5},{5... | collective-permute-start | bytes 884744 | tf_op jit(solution)/shard_map/ppermute | solution.py:24
  33.1 12.5 %collective-permute-start.12 = (bf16[384,384]{1,0:T(8,128)(2,1)S(1)}, bf16[384,384]{1,0:T(8,128)(2,1)S(1)}, u32[]{:S(2)}, u32[]{:S(2)}) collective-permute-start(bf16[384,384]{1,0:T(8,128)(2,1)S(1)} %get-tuple-element.105.pre), channel_id=1, source_target_pairs={{0,4},{4,0},{8,12},{12,8},{16,20},{20,16},{24,28},{28,24},{1,5},{5... | collective-permute-start | bytes 884744 | tf_op jit(solution)/shard_map/ppermute | solution.py:24
  33.7 4.9 %collective-permute-start.10 = (bf16[176,640]{1,0:T(8,128)(2,1)S(1)}, bf16[176,640]{1,0:T(8,128)(2,1)S(1)}, u32[]{:S(2)}, u32[]{:S(2)}) collective-permute-start(bf16[176,640]{1,0:T(8,128)(2,1)S(1)} %collective-permute-done.9.h2), channel_id=1, source_target_pairs={{0,1},{1,0},{2,3},{3,2},{4,5},{5,4},{6,7},{7,6},{8,9},{9,8},{10,11... | collective-permute-start | bytes 675848 | tf_op jit(solution)/shard_map/ppermute | solution.py:24
  38.0 10.6 %collective-permute-start.13 = (f32[64,1408]{1,0:T(8,128)S(1)}, f32[64,1408]{1,0:T(8,128)S(1)}, u32[]{:S(2)}, u32[]{:S(2)}) collective-permute-start(f32[64,1408]{1,0:T(8,128)S(1)} %get-tuple-element.109.a), channel_id=1, source_target_pairs={{0,1},{1,0},{2,3},{3,2},{4,5},{5,4},{6,7},{7,6},{8,9},{9,8},{10,11... | collective-permute-start | bytes 1081352 | tf_op jit(solution)/shard_map/ppermute | solution.py:24
  41.1 9.3 %collective-permute-start.14 = (bf16[352,384]{1,0:T(8,128)(2,1)S(1)}, bf16[352,384]{1,0:T(8,128)(2,1)S(1)}, u32[]{:S(2)}, u32[]{:S(2)}) collective-permute-start(bf16[352,384]{1,0:T(8,128)(2,1)S(1)} %get-tuple-element.103), channel_id=1, source_target_pairs={{0,8},{4,12},{8,0},{12,4},{16,24},{20,28},{24,16},{28,20},{1,9},{5... | collective-permute-start | bytes 811016 | tf_op jit(solution)/shard_map/ppermute | solution.py:24
  46.5 9.3 %collective-permute-start.15 = (bf16[512,256]{1,0:T(8,128)(2,1)S(1)}, bf16[512,256]{1,0:T(8,128)(2,1)S(1)}, u32[]{:S(2)}, u32[]{:S(2)}) collective-permute-start(bf16[512,256]{1,0:T(8,128)(2,1)S(1)} %get-tuple-element.114), channel_id=1, source_target_pairs={{0,2},{1,3},{2,0},{3,1},{4,6},{5,7},{6,4},{7,5},{8,10},{9,11},{10,... | collective-permute-start | bytes 786440 | tf_op jit(solution)/shard_map/ppermute | solution.py:24
  48.0 12.0 %collective-permute-start.17 = (bf16[384,384]{1,0:T(8,128)(2,1)S(1)}, bf16[384,384]{1,0:T(8,128)(2,1)S(1)}, u32[]{:S(2)}, u32[]{:S(2)}) collective-permute-start(bf16[384,384]{1,0:T(8,128)(2,1)S(1)} %get-tuple-element.118.pre), channel_id=1, source_target_pairs={{0,4},{4,0},{8,12},{12,8},{16,20},{20,16},{24,28},{28,24},{1,5},{5... | collective-permute-start | bytes 884744 | tf_op jit(solution)/shard_map/ppermute | solution.py:24
  48.6 9.4 %copy-start.2 = (bf16[1408,256]{1,0:T(8,128)(2,1)S(1)}, bf16[1408,256]{1,0:T(8,128)(2,1)}, u32[]{:S(2)}) copy-start(bf16[1408,256]{1,0:T(8,128)(2,1)} %ref_proj.1) | copy-start | bytes 2162692
  48.6 9.4 %collective-permute-start.16 = (bf16[64,1408]{1,0:T(8,128)(2,1)S(1)}, bf16[64,1408]{1,0:T(8,128)(2,1)S(1)}, u32[]{:S(2)}, u32[]{:S(2)}) collective-permute-start(bf16[64,1408]{1,0:T(8,128)(2,1)S(1)} %shard_map.113.a), channel_id=1, source_target_pairs={{0,2},{1,3},{2,0},{3,1},{4,6},{5,7},{6,4},{7,5},{8,10},{9,11},{10,... | collective-permute-start | bytes 540680 | tf_op jit(solution)/shard_map/ppermute | solution.py:24
  49.2 12.9 %collective-permute-start.18 = (bf16[352,384]{1,0:T(8,128)(2,1)S(1)}, bf16[352,384]{1,0:T(8,128)(2,1)S(1)}, u32[]{:S(2)}, u32[]{:S(2)}) collective-permute-start(bf16[352,384]{1,0:T(8,128)(2,1)S(1)} %get-tuple-element.108), channel_id=1, source_target_pairs={{0,8},{4,12},{8,0},{12,4},{16,24},{20,28},{24,16},{28,20},{1,9},{5... | collective-permute-start | bytes 811016 | tf_op jit(solution)/shard_map/ppermute | solution.py:24
  50.4 14.8 %collective-permute-start.20 = (bf16[384,384]{1,0:T(8,128)(2,1)S(1)}, bf16[384,384]{1,0:T(8,128)(2,1)S(1)}, u32[]{:S(2)}, u32[]{:S(2)}) collective-permute-start(bf16[384,384]{1,0:T(8,128)(2,1)S(1)} %get-tuple-element.126.pre), channel_id=1, source_target_pairs={{0,4},{4,0},{8,12},{12,8},{16,20},{20,16},{24,28},{28,24},{1,5},{5... | collective-permute-start | bytes 884744 | tf_op jit(solution)/shard_map/ppermute | solution.py:24
  55.8 8.0 %collective-permute-start.19 = (bf16[512,256]{1,0:T(8,128)(2,1)S(1)}, bf16[512,256]{1,0:T(8,128)(2,1)S(1)}, u32[]{:S(2)}, u32[]{:S(2)}) collective-permute-start(bf16[512,256]{1,0:T(8,128)(2,1)S(1)} %shard_map.115), channel_id=1, source_target_pairs={{0,1},{1,0},{2,3},{3,2},{4,5},{5,4},{6,7},{7,6},{8,9},{9,8},{10,11... | collective-permute-start | bytes 786440 | tf_op jit(solution)/shard_map/ppermute | solution.py:24
  58.5 5.7 %collective-permute-start.22 = (f32[192,256]{1,0:T(8,128)S(1)}, f32[192,256]{1,0:T(8,128)S(1)}, u32[]{:S(2)}, u32[]{:S(2)}) collective-permute-start(f32[192,256]{1,0:T(8,128)S(1)} %shard_map.116.e0), channel_id=1, source_target_pairs={{0,2},{1,3},{2,0},{3,1},{4,6},{5,7},{6,4},{7,5},{8,10},{9,11},{10,... | collective-permute-start | bytes 589832 | tf_op jit(solution)/shard_map/ppermute | solution.py:24
  60.1 7.6 %collective-permute-start.24 = (bf16[176,384]{1,0:T(8,128)(2,1)S(1)}, bf16[176,384]{1,0:T(8,128)(2,1)S(1)}, u32[]{:S(2)}, u32[]{:S(2)}) collective-permute-start(bf16[176,384]{1,0:T(8,128)(2,1)S(1)} %get-tuple-element.111), channel_id=1, source_target_pairs={{0,16},{4,20},{8,24},{12,28},{16,0},{20,4},{24,8},{28,12},{1,17},{... | collective-permute-start | bytes 405512 | tf_op jit(solution)/shard_map/ppermute | solution.py:24
  62.1 13.4 %collective-permute-start.25 = (bf16[352,384]{1,0:T(8,128)(2,1)S(1)}, bf16[352,384]{1,0:T(8,128)(2,1)S(1)}, u32[]{:S(2)}, u32[]{:S(2)}) collective-permute-start(bf16[352,384]{1,0:T(8,128)(2,1)S(1)} %get-tuple-element.119), channel_id=1, source_target_pairs={{0,8},{4,12},{8,0},{12,4},{16,24},{20,28},{24,16},{28,20},{1,9},{5... | collective-permute-start | bytes 811016 | tf_op jit(solution)/shard_map/ppermute | solution.py:24
  63.8 4.3 %collective-permute-start.21 = (f32[192,256]{1,0:T(8,128)S(1)}, f32[192,256]{1,0:T(8,128)S(1)}, u32[]{:S(2)}, u32[]{:S(2)}) collective-permute-start(f32[192,256]{1,0:T(8,128)S(1)} %shard_map.116.e0), channel_id=1, source_target_pairs={{0,1},{1,0},{2,3},{3,2},{4,5},{5,4},{6,7},{7,6},{8,9},{9,8},{10,11... | collective-permute-start | bytes 589832 | tf_op jit(solution)/shard_map/ppermute | solution.py:24
  64.2 4.0 %copy-start.7 = (s32[64]{0:T(128)S(1)}, s32[64]{0:T(128)}, u32[]{:S(2)}) copy-start(s32[64]{0:T(128)} %param.13) | copy-start | bytes 772
  64.2 11.6 %collective-permute-start.27 = (bf16[176,384]{1,0:T(8,128)(2,1)S(1)}, bf16[176,384]{1,0:T(8,128)(2,1)S(1)}, u32[]{:S(2)}, u32[]{:S(2)}) collective-permute-start(bf16[176,384]{1,0:T(8,128)(2,1)S(1)} %get-tuple-element.121), channel_id=1, source_target_pairs={{0,16},{4,20},{8,24},{12,28},{16,0},{20,4},{24,8},{28,12},{1,17},{... | collective-permute-start | bytes 405512 | tf_op jit(solution)/shard_map/ppermute | solution.py:24
  65.2 2.9 %collective-permute-start.23 = (f32[192,256]{1,0:T(8,128)S(1)}, f32[192,256]{1,0:T(8,128)S(1)}, u32[]{:S(2)}, u32[]{:S(2)}) collective-permute-start(f32[192,256]{1,0:T(8,128)S(1)} %collective-permute-done.22.e2), channel_id=1, source_target_pairs={{0,1},{1,0},{2,3},{3,2},{4,5},{5,4},{6,7},{7,6},{8,9},{9,8},{10,11... | collective-permute-start | bytes 589832 | tf_op jit(solution)/shard_map/ppermute | solution.py:24
  67.6 14.8 %collective-permute-start.28 = (bf16[352,384]{1,0:T(8,128)(2,1)S(1)}, bf16[352,384]{1,0:T(8,128)(2,1)S(1)}, u32[]{:S(2)}, u32[]{:S(2)}) collective-permute-start(bf16[352,384]{1,0:T(8,128)(2,1)S(1)} %get-tuple-element.128), channel_id=1, source_target_pairs={{0,8},{4,12},{8,0},{12,4},{16,24},{20,28},{24,16},{28,20},{1,9},{5... | collective-permute-start | bytes 811016 | tf_op jit(solution)/shard_map/ppermute | solution.py:24
  68.9 7.0 %collective-permute-start.26 = (f32[1,384]{1,0:T(1,128)S(1)}, f32[1,384]{1,0:T(1,128)S(1)}, u32[]{:S(2)}, u32[]{:S(2)}) collective-permute-start(f32[1,384]{1,0:T(1,128)S(1)} %shard_map.121.a), channel_id=1, source_target_pairs={{0,1},{1,0},{2,3},{3,2},{4,5},{5,4},{6,7},{7,6},{8,9},{9,8},{10,11... | collective-permute-start | bytes 4616 | tf_op jit(solution)/shard_map/ppermute | solution.py:24
  75.6 9.3 %collective-permute-start.30 = (bf16[176,384]{1,0:T(8,128)(2,1)S(1)}, bf16[176,384]{1,0:T(8,128)(2,1)S(1)}, u32[]{:S(2)}, u32[]{:S(2)}) collective-permute-start(bf16[176,384]{1,0:T(8,128)(2,1)S(1)} %get-tuple-element.132), channel_id=1, source_target_pairs={{0,16},{4,20},{8,24},{12,28},{16,0},{20,4},{24,8},{28,12},{1,17},{... | collective-permute-start | bytes 405512 | tf_op jit(solution)/shard_map/ppermute | solution.py:24
  75.9 9.1 %collective-permute-start.29 = (f32[1,384]{1,0:T(1,128)S(1)}, f32[1,384]{1,0:T(1,128)S(1)}, u32[]{:S(2)}, u32[]{:S(2)}) collective-permute-start(f32[1,384]{1,0:T(1,128)S(1)} %shard_map.123.a), channel_id=1, source_target_pairs={{0,2},{1,3},{2,0},{3,1},{4,6},{5,7},{6,4},{7,5},{8,10},{9,11},{10,... | collective-permute-start | bytes 4616 | tf_op jit(solution)/shard_map/ppermute | solution.py:24
  82.5 6.4 %collective-permute-start.31 = (bf16[176,384]{1,0:T(8,128)(2,1)S(1)}, bf16[176,384]{1,0:T(8,128)(2,1)S(1)}, u32[]{:S(2)}, u32[]{:S(2)}) collective-permute-start(bf16[176,384]{1,0:T(8,128)(2,1)S(1)} %get-tuple-element.136), channel_id=1, source_target_pairs={{0,16},{4,20},{8,24},{12,28},{16,0},{20,4},{24,8},{28,12},{1,17},{... | collective-permute-start | bytes 405512 | tf_op jit(solution)/shard_map/ppermute | solution.py:24

commit v4 on v3

--- a/solution.py
+++ b/solution.py
@@ -235,7 +235,7 @@
     return pl.ds(pl.multiple_of(index * length, length), length)
 
 
-def call(body, out_shape, cost, grid=(), vmem=40 * 2**20, **kwargs):
+def call(body, out_shape, cost, grid=(), vmem=24 * 2**20, **kwargs):
     flops, moved = cost
     return pl.pallas_call(
         body,
@@ -489,21 +489,6 @@
     return lax.optimization_barrier((value,) + others)[0] if others else value
 
 
-class Order:
-    def __init__(self):
-        self.last = ()
-
-    def wait(self, *values):
-        self.last = self.last + values
-
-    def call(self, body, out_shape, cost, *operands, **kwargs):
-        operands = list(operands)
-        operands[0] = lax.optimization_barrier((operands[0],) + self.last)[0]
-        result = call(body, out_shape, cost, **kwargs)(*operands)
-        self.last = (result[-1] if isinstance(result, (tuple, list)) else result,)
-        return result
-
-
 def quarter_sel(patches, text, ref_proj, w_up, w_down, kept_index, dest, cotan):
     n_mdl, n_sel = lax.axis_size("mdl"), lax.axis_size("sel")
     n_high = n_sel // 2
@@ -520,247 +505,252 @@
     n_emb = ex_dev + k_dev
     kept_row = kept_index.reshape(1, k_dev)
     dest_row = dest.reshape(1, k_dev)
-    order = Order()
+    size = ff_dev // 4
     whole = lambda shape: pl.BlockSpec(shape, lambda i: (0,) * len(shape))
-    widths = (384, 384, 384, 384)
-    starts = [sum(widths[:c]) for c in range(len(widths))]
     row_struct = struct((n_rows, d_full), bf16)
     row_spec = whole((n_rows, d_full))
     mixed_struct = struct((k_dev, d_full), f32)
     mixed_spec = whole((k_dev, d_full))
-    small = (2**20, 2**20)
-
-    both, half, pool, texts = order.call(
-        functools.partial(pick_body, n_patch),
-        (
-            struct((2 * d_part, n_rows), bf16),
-            struct((d_part // 2, n_rows), bf16),
-            struct((d_part, ex_dev), bf16),
-            struct((ex_dev + 16, emb_part), bf16),
-        ),
-        small,
-        patches.T,
-        cotan.T,
-        kept_row,
-        dest_row,
-        text,
-        in_specs=[
-            pl.BlockSpec(memory_space=space)
-            for space in (pltpu.HBM, pltpu.HBM, pltpu.VMEM, pltpu.VMEM, pltpu.HBM)
-        ],
-        scratch_shapes=[
-            pltpu.VMEM((d_part, ex_dev * n_patch), bf16),
-            pltpu.SemaphoreType.DMA((3,)),
-        ],
-    )
+    pre_struct = struct((n_rows, size), bf16)
+    pre_spec = whole((n_rows, size))
+    halves = (struct((2 * blk, size), f32), struct((2 * blk, size), bf16))
+
+    def run(ties, body, out_shape, *operands, **kwargs):
+        first = after(operands[0], *ties)
+        return call(body, out_shape, (2**20, 2**20), **kwargs)(first, *operands[1:])
+
+    def pick(ties):
+        return run(
+            ties,
+            functools.partial(pick_body, n_patch),
+            (
+                struct((2 * d_part, n_rows), bf16),
+                struct((d_part // 2, n_rows), bf16),
+                struct((d_part, ex_dev), bf16),
+                struct((ex_dev + 16, emb_part), bf16),
+            ),
+            patches.T,
+            cotan.T,
+            kept_row,
+            dest_row,
+            text,
+            in_specs=[
+                pl.BlockSpec(memory_space=space)
+                for space in (pltpu.HBM, pltpu.HBM, pltpu.VMEM, pltpu.VMEM, pltpu.HBM)
+            ],
+            scratch_shapes=[
+                pltpu.VMEM((d_part, ex_dev * n_patch), bf16),
+                pltpu.SemaphoreType.DMA((3,)),
+            ],
+            vmem=60 * 2**20,
+        )
+
+
+    def stage(ties):
+        return run(
+            ties,
+            stage_body,
+            (struct(w_up.shape, bf16), struct(w_down.shape, bf16)),
+            w_up,
+            w_down,
+            in_specs=[pl.BlockSpec(memory_space=pltpu.HBM)] * 2,
+            scratch_shapes=[pltpu.SemaphoreType.DMA((2,))],
+            vmem=40 * 2**20,
+        )
+
+
+    def make_extras(ties, half_pair, pool, texts):
+        rotated = [rotate_pairs(texts, s) for s in range(1, n_high)]
+        return run(
+            ties,
+            extras_body,
+            (
+                struct((d_part // 2, n_rows + 2 * ex_dev), bf16),
+                struct((n_high * (ex_dev + 16), emb_part), bf16),
+            ),
+            half_pair,
+            pool,
+            texts,
+            *rotated,
+        )
+
+
+    def weight_specs(c):
+        return [
+            pl.BlockSpec((d_full, size), lambda i: (0, c)),
+            pl.BlockSpec((size, d_full), lambda i: (c, 0)),
+        ]
+
+
+    def forward_first(ties, *operands):
+        return run(
+            ties,
+            functools.partial(first_chunk_body, n_patch, n_mdl),
+            (pre_struct, mixed_struct, struct((d_full, n_rows), bf16), row_struct, row_struct),
+            *operands,
+            grid=(1,),
+            in_specs=[whole((2 * d_part, n_rows))] * 4 + weight_specs(0),
+            out_specs=[pre_spec, mixed_spec, whole((d_full, n_rows)), row_spec, row_spec],
+            scratch_shapes=[pltpu.VMEM((d_full, n_rows), bf16)],
+        )
+
+    def forward(ties, c, tok, cot, held_up, held_down, mixed):
+        return run(
+            ties,
+            functools.partial(next_chunk_body, n_patch),
+            (pre_struct, mixed_struct),
+            tok,
+            cot,
+            held_up,
+            held_down,
+            mixed,
+            grid=(1,),
+            in_specs=[row_spec, row_spec] + weight_specs(c) + [mixed_spec],
+            out_specs=[pre_spec, mixed_spec],
+        )
+
+
+    def all_shards(ties, my_texts, pair_texts):
+        return run(
+            ties,
+            functools.partial(text_body, k_dev, n_patch),
+            (
+                struct((ex_dev * n_sel, emb_part), bf16),
+                struct((2 * n_share, emb_part), bf16),
+                struct((8, 2 * n_rows), f32),
+            ),
+            my_texts,
+            pair_texts,
+        )
+
+    def grad_first(ties, *operands):
+        pair_struct = struct((blk * n_high, 2 * n_rows), bf16)
+        return run(ties, first_grad_body, (pair_struct,) + halves, *operands)
+
+    def grad(ties, *operands):
+        return run(ties, grad_body, halves, *operands)
+
+    def add(ties, keep, received):
+        structs = (struct((blk, size), f32), struct((blk, size), bf16))
+        return run(ties, add_body, structs, keep, received)
+
+    def relay_text(ties, all_texts, text_x):
+        send = struct((2 * n_share, emb_part), bf16)
+        return run(ties, text_relay_body, send, all_texts, text_x)
+
+    def share_text(ties, *operands):
+        return run(
+            ties,
+            share_body,
+            struct((n_share, emb_full), bf16),
+            *operands,
+            scratch_shapes=[pltpu.VMEM((n_share, emb_full), f32)],
+        )
+
+    def heads(ties, *operands):
+        return run(
+            ties,
+            functools.partial(heads_body, n_patch),
+            struct((n_emb, emb_part), f32),
+            *operands,
+            ref_proj,
+            scratch_shapes=[pltpu.VMEM((d_full, ex_dev), bf16)],
+        )
+
+    def scores(ties, *operands):
+        return run(
+            ties,
+            scores_body,
+            struct((1, 2 * n_emb), f32),
+            *operands,
+            kept_row,
+            scratch_shapes=[pltpu.VMEM((n_emb, emb_full), f32)],
+        )
+
+    def losses(ties, total, total_x):
+        structs = (struct((1, ex_dev), f32), struct((1, k_dev), f32))
+        return run(ties, losses_body, structs, total, total_x, kept_row)
+
+
+    both, half, pool, texts = pick(())
     both_x = swap(both, "mdl", 2)
     both_core = swap(both, "mdl", 1)
-    text_pieces = [texts] + [rotate_pairs(texts, s) for s in range(1, n_high)]
-    half = lax.optimization_barrier((half, both_core))[0]
     half_pair = swap(half, "sel", 1)
-    held_up, held_down = order.call(
-        stage_body,
-        (struct(w_up.shape, bf16), struct(w_down.shape, bf16)),
-        small,
-        w_up,
-        w_down,
-        in_specs=[pl.BlockSpec(memory_space=pltpu.HBM)] * 2,
-        scratch_shapes=[pltpu.SemaphoreType.DMA((2,))],
-    )
-    extras, my_texts = order.call(
-        extras_body,
-        (
-            struct((d_part // 2, n_rows + 2 * ex_dev), bf16),
-            struct((n_high * (ex_dev + 16), emb_part), bf16),
-        ),
-        small,
-        half_pair,
-        pool,
-        *text_pieces,
-    )
-    both_x = lax.optimization_barrier((both_x, extras))[0]
-    both_diag = swap(both_x, "mdl", 1)
+    held_up, held_down = stage((texts,))
+    extras, my_texts = make_extras((held_down,), half_pair, pool, texts)
+    both_diag = swap(after(both_x, extras), "mdl", 1)
+    extras_x = swap(extras, "mdl", 2)
+    extras_core = swap(extras, "mdl", 1)
+    extras_diag = swap(extras_x, "mdl", 1)
     pair_texts = swap(my_texts, "sel", 1)
-    extra_pieces = mdl_pieces(extras)
-    order.wait(extra_pieces[1])
-
-    def weight_specs(c):
-        first, size = starts[c] // widths[c], widths[c]
-        if starts[c] % size == 0:
-            return [
-                pl.BlockSpec((d_full, size), lambda i: (0, first)),
-                pl.BlockSpec((size, d_full), lambda i: (first, 0)),
-            ]
-        start = starts[c]
-        return [
-            pl.BlockSpec((pl.Element(d_full), pl.Element(size)), lambda i: (0, start)),
-            pl.BlockSpec((pl.Element(size), pl.Element(d_full)), lambda i: (start, 0)),
-        ]
-
-    pres = [None] * len(widths)
-    pair_pres = list(pres)
-
-    def chunk(c, state):
-        size = widths[c]
-        tok, cot, mixed = state
-        cost = (4 * n_rows * d_full * size, 8 * d_full * size)
-        pre_struct = struct((n_rows, size), bf16)
-        if c == 0:
-            pre, mixed, tok_full, tok, cot = order.call(
-                functools.partial(first_chunk_body, n_patch, n_mdl),
-                (pre_struct, mixed_struct, struct((d_full, n_rows), bf16), row_struct, row_struct),
-                cost,
-                both,
-                both_core,
-                both_x,
-                both_diag,
-                held_up,
-                held_down,
-                grid=(1,),
-                in_specs=[whole((2 * d_part, n_rows))] * 4 + weight_specs(c),
-                out_specs=[
-                    whole((n_rows, size)),
-                    mixed_spec,
-                    whole((d_full, n_rows)),
-                    row_spec,
-                    row_spec,
-                ],
-                scratch_shapes=[pltpu.VMEM((d_full, n_rows), bf16)],
-            )
-        else:
-            tok_full = None
-            pre, mixed = order.call(
-                functools.partial(next_chunk_body, n_patch),
-                (pre_struct, mixed_struct),
-                cost,
-                tok,
-                cot,
-                held_up,
-                held_down,
-                mixed,
-                grid=(1,),
-                in_specs=[row_spec, row_spec] + weight_specs(c) + [mixed_spec],
-                out_specs=[whole((n_rows, size)), mixed_spec],
-            )
-        pres[c] = pre
-        if c < 2:
-            pair_pres[c] = swap(pre, "sel", 1)
-        return (tok, cot, mixed), tok_full
-
-    state, tok_full = chunk(0, (None, None, None))
-    state, _ = chunk(1, state)
-
-    all_texts, text_send, weights = order.call(
-        functools.partial(text_body, k_dev, n_patch),
-        (
-            struct((ex_dev * n_sel, emb_part), bf16),
-            struct((2 * n_share, emb_part), bf16),
-            struct((8, 2 * n_rows), f32),
-        ),
-        small,
-        my_texts,
-        pair_texts,
-    )
-    state, _ = chunk(2, state)
-    order.wait(extra_pieces[2])
-    state, _ = chunk(3, state)
-
-    parts = [None] * len(widths)
-
-    def first_half(c, pair):
-        size = widths[c]
-        cost = (4 * n_rows * blk * n_high * size, 4 * 2**20)
-        halves = (struct((2 * blk, size), f32), struct((2 * blk, size), bf16))
-        if c == 0:
-            pair, keep, send = order.call(
-                first_grad_body,
-                (struct((blk * n_high, 2 * n_rows), bf16),) + halves,
-                cost,
-                tok_full,
-                *extra_pieces,
-                weights,
-                pres[c],
-                pair_pres[c],
-            )
-        else:
-            keep, send = order.call(grad_body, halves, cost, pair, pres[c], pair_pres[c])
-        parts[c] = [keep, swap(send, "sel", 2)]
-        return pair
-
-    def second_half(c):
-        if c > 1:
-            order.wait(parts[c - 2][1])
-        keep, send = order.call(
-            add_body,
-            (struct((blk, widths[c]), f32), struct((blk, widths[c]), bf16)),
-            (2**16, 2**20),
-            *parts[c],
-        )
-        parts[c] = [keep, swap(send, "sel", 4)]
-
-    pair = first_half(0, None)
-    mixed = state[2]
+    pre0, mixed0, tok_full, tok, cot = forward_first(
+        (my_texts, extras_core),
+        both,
+        both_core,
+        both_x,
+        both_diag,
+        held_up,
+        held_down,
+    )
+    pair_pre0 = swap(pre0, "sel", 1)
+    all_texts, text_send, weights = all_shards((cot,), my_texts, pair_texts)
+    text_x = swap(text_send, "mdl", 2)
+    pre1, mixed1 = forward((weights,), 1, tok, cot, held_up, held_down, mixed0)
+    pair_pre1 = swap(pre1, "sel", 1)
+    pre2, mixed2 = forward((mixed1,), 2, tok, cot, held_up, held_down, mixed1)
+    pair_pre2 = swap(pre2, "sel", 1)
+    pre3, mixed = forward((mixed2, extras_x), 3, tok, cot, held_up, held_down, mixed2)
     mixed_core = swap(mixed, "mdl", 1)
-    first_half(1, pair)
-    pair_pres[2] = swap(after(pres[2], parts[1][0]), "sel", 1)
-    text_x = swap(after(text_send, parts[1][0]), "mdl", 2)
-    mixed = order.call(mix_body, struct((k_dev, d_full), bf16), small, mixed, mixed_core)
-    mixed_x = swap(mixed, "mdl", 2)
-    second_half(0)
-    pair_pres[3] = swap(after(pres[3], parts[0][0]), "sel", 1)
-    relay = order.call(
-        text_relay_body, struct((2 * n_share, emb_part), bf16), small, all_texts, text_x
-    )
+    pair, keep0, send0 = grad_first(
+        (mixed,),
+        tok_full,
+        extras,
+        extras_core,
+        extras_x,
+        extras_diag,
+        weights,
+        pre0,
+        pair_pre0,
+    )
+    first0 = swap(send0, "sel", 2)
+    keep1, send1 = grad((send0,), pair, pre1, pair_pre1)
+    first1 = swap(send1, "sel", 2)
+    mixsum = run((send1,), mix_body, struct((k_dev, d_full), bf16), mixed, mixed_core)
+    mixsum_x = swap(mixsum, "mdl", 2)
+    own0, rest0 = add((mixsum,), keep0, first0)
+    pair_pre3 = swap(after(pre3, own0), "sel", 1)
+    second0 = swap(rest0, "sel", 4)
+    relay = relay_text((rest0,), all_texts, text_x)
     text_core = swap(relay, "mdl", 1)
-    emb = order.call(
-        functools.partial(heads_body, n_patch),
-        struct((n_emb, emb_part), f32),
-        small,
-        *extra_pieces,
-        mixed,
-        mixed_x,
-        ref_proj,
-        scratch_shapes=[pltpu.VMEM((d_full, ex_dev), bf16)],
-    )
-    emb_pieces = mdl_pieces(emb)
-    first_half(2, pair)
-    second_half(1)
-    share = order.call(
-        share_body,
-        struct((n_share, emb_full), bf16),
-        small,
-        all_texts,
-        text_x,
-        text_core,
-        scratch_shapes=[pltpu.VMEM((n_share, emb_full), f32)],
-    )
-    first_half(3, pair)
-    sums = order.call(
-        scores_body,
-        struct((1, 2 * n_emb), f32),
-        small,
-        *emb_pieces,
-        share,
-        kept_row,
-        scratch_shapes=[pltpu.VMEM((n_emb, emb_full), f32)],
-    )
+    emb = heads((relay,), extras, extras_core, extras_x, extras_diag, mixsum, mixsum_x)
+    emb_x = swap(emb, "mdl", 2)
+    emb_core = swap(emb, "mdl", 1)
+    emb_diag = swap(emb_x, "mdl", 1)
+    keep2, send2 = grad((emb,), pair, pre2, pair_pre2)
+    first2 = swap(send2, "sel", 2)
+    own1, rest1 = add((send2,), keep1, first1)
+    second1 = swap(rest1, "sel", 4)
+    share = share_text((rest1,), all_texts, text_x, text_core)
+    keep3, send3 = grad((share,), pair, pre3, pair_pre3)
+    first3 = swap(send3, "sel", 2)
+    sums = scores((send3,), emb, emb_core, emb_x, emb_diag, share)
     sums_core = swap(sums, "mdl", 1)
-    second_half(2)
-    sums = order.call(mix_body, struct((1, 2 * n_emb), f32), small, sums, sums_core)
-    sums_x = swap(sums, "mdl", 2)
-    second_half(3)
-    ref_loss, learnability = order.call(
-        losses_body,
-        (struct((1, ex_dev), f32), struct((1, k_dev), f32)),
-        small,
-        sums,
-        sums_x,
-        kept_row,
-    )
-    parts[-1][0], ref_loss, learnability = lax.optimization_barrier(
-        (parts[-1][0], ref_loss, learnability)
-    )
-    grad_up = jnp.concatenate([own + other.astype(f32) for own, other in parts], axis=1)
+    own2, rest2 = add((sums, second0), keep2, first2)
+    second2 = swap(rest2, "sel", 4)
+    total = run((rest2,), mix_body, struct((1, 2 * n_emb), f32), sums, sums_core)
+    total_x = swap(total, "mdl", 2)
+    own3, rest3 = add((total, second1), keep3, first3)
+    second3 = swap(rest3, "sel", 4)
+    ref_loss, learnability = losses((rest3,), total, total_x)
+
+    own3, ref_loss, learnability = lax.optimization_barrier((own3, ref_loss, learnability))
+    sums = [
+        (own0, second0),
+        (own1, second1),
+        (own2, second2),
+        (own3, second3),
+    ]
+    grad_up = jnp.concatenate([own + other.astype(f32) for own, other in sums], axis=1)
     return (ref_loss.reshape(ex_dev), learnability.reshape(k_dev), grad_up)
 
 

time: 90.5 us -> 85.8 us (0.948)
  starting transfers between devices: 28.6 us -> 35.8 us
  waiting for transfers between devices: 31.4 us -> 25 us
  local copies, waits for them, and re-layouts: 8.4 us -> 2.25 us
    ppermute x29, starting transfers between devices: 23 us -> 30.3 us  [swap(): return lax.ppermute(value, axis, [(i, i ^ bit) for i in range(size)])]
    ppermute x29, waiting for transfers between devices: 31.4 us -> 25 us  [swap(): return lax.ppermute(value, axis, [(i, i ^ bit) for i in range(size)])]
    unnamed x22 -> x12, local copies, waits for them, and re-layouts: 8.4 us -> 2.25 us
  transfers between devices with their start and end apart: 32 -> 32, of which waited for: 9 -> 10; matrix products, arithmetic and copies ran while one was open for 0% -> 0% of each run, Pallas kernels for 20% -> 20%
where the time goes in v4:
time: 85.8 us; the launch traced here: 85.6 us
  starting transfers between devices  35.8 us (42%)
  waiting for transfers between devices  25 us (29%)
  Pallas kernels  20.4 us (24%)
  local copies, waits for them, and re-layouts  2.25 us (3%)
  other arithmetic  1.22 us (1%)
  between operations  0.98 us (1%)
    ppermute x29, starting transfers between devices, swap(): return lax.ppermute(value, axis, [(i, i ^ bit) for i in range(size)])  30.3 us
    ppermute x29, waiting for transfers between devices, swap(): return lax.ppermute(value, axis, [(i, i ^ bit) for i in range(size)])  25 us
    pallas_call x23, Pallas kernels, run(): call(body, out_shape, (2 ** 20, 2 ** 20), **kwargs)(first, *operands[1:])  20.4 us
    ppermute x3, starting transfers between devices, rotate_pairs(): lax.ppermute(value, 'sel', [(i, (i + 2 * step) % size) for i in range(siz...  5.51 us
    unnamed x12, local copies, waits for them, and re-layouts  2.25 us
  transfers between devices with their start and end apart: 32, of which 10 were waited for; matrix products, arithmetic and copies ran while one was open for 0% of the time, Pallas kernels for 20%

profile of v4, /device:TPU:0, one launch (start us, length us, event | category | flops | bytes accessed | tf_op | source)
XLA Modules:
  0.0 85.6 jit_solution(801247245955736325)
XLA Ops:
  0.6 3.3 %shard_map.103 = (bf16[704,384]{1,0:T(8,128)(2,1)}, bf16[176,384]{1,0:T(8,128)(2,1)}, bf16[352,128]{1,0:T(8,128)(2,1)}, bf16[144,256]{1,0:T(8,128)(2,1)}) custom-call(bf16[352,768]{1,0:T(8,128)(2,1)} %bitcast.9, bf16[352,384]{1,0:T(8,128)(2,1)} %bitcast.10, s32[1,64]{1,0:T(1,128)} %bitcast.6, s32[1,64]{1,0:T(1,128)} %bitcast.11, bf16[128,256]{1,0:T(8,128)(2,1)} %text_hbm.1), custom_call_target="tpu_custom_call" | custom-call | flops 1 | bytes 1 | tf_op jit(solution)/shard_map/pallas_call | solution.py:520
  4.0 3.0 %collective-permute-start.6 = (bf16[704,384]{1,0:T(8,128)(2,1)}, bf16[704,384]{1,0:T(8,128)(2,1)S(1)}, u32[]{:S(2)}, u32[]{:S(2)}) collective-permute-start(bf16[704,384]{1,0:T(8,128)(2,1)} %get-tuple-element.80.b0), channel_id=1, source_target_pairs={{0,2},{1,3},{2,0},{3,1},{4,6},{5,7},{6,4},{7,5},{8,10},{9,11},{10,... | collective-permute-start | bytes 1622024 | tf_op jit(solution)/shard_map/ppermute | solution.py:24
  7.0 1.5 %collective-permute-start = (bf16[176,384]{1,0:T(8,128)(2,1)}, bf16[176,384]{1,0:T(8,128)(2,1)S(1)}, u32[]{:S(2)}, u32[]{:S(2)}) collective-permute-start(bf16[176,384]{1,0:T(8,128)(2,1)} %get-tuple-element.72), channel_id=1, source_target_pairs={{0,4},{4,0},{8,12},{12,8},{16,20},{20,16},{24,28},{28,24},{1,5},{5... | collective-permute-start | bytes 405512 | tf_op jit(solution)/shard_map/ppermute | solution.py:24
  8.5 1.6 %collective-permute-start.1 = (bf16[144,256]{1,0:T(8,128)(2,1)}, bf16[144,256]{1,0:T(8,128)(2,1)S(1)}, u32[]{:S(2)}, u32[]{:S(2)}) collective-permute-start(bf16[144,256]{1,0:T(8,128)(2,1)} %get-tuple-element.73.t0), channel_id=1, source_target_pairs={{0,8},{4,12},{8,16},{12,20},{16,24},{20,28},{24,0},{28,4},{1,9},{5... | collective-permute-start | bytes 221192 | tf_op jit(solution)/shard_map/ppermute | solution.py:29
  10.1 2.6 %collective-permute-start.2 = (bf16[144,256]{1,0:T(8,128)(2,1)}, bf16[144,256]{1,0:T(8,128)(2,1)S(1)}, u32[]{:S(2)}, u32[]{:S(2)}) collective-permute-start(bf16[144,256]{1,0:T(8,128)(2,1)} %get-tuple-element.73.t0), channel_id=1, source_target_pairs={{0,16},{4,20},{8,24},{12,28},{16,0},{20,4},{24,8},{28,12},{1,17},{... | collective-permute-start | bytes 221192 | tf_op jit(solution)/shard_map/ppermute | solution.py:29
  12.7 1.3 %collective-permute-start.3 = (bf16[144,256]{1,0:T(8,128)(2,1)}, bf16[144,256]{1,0:T(8,128)(2,1)S(1)}, u32[]{:S(2)}, u32[]{:S(2)}) collective-permute-start(bf16[144,256]{1,0:T(8,128)(2,1)} %get-tuple-element.73.t0), channel_id=1, source_target_pairs={{0,24},{4,28},{8,0},{12,4},{16,8},{20,12},{24,16},{28,20},{1,25},{... | collective-permute-start | bytes 221192 | tf_op jit(solution)/shard_map/ppermute | solution.py:29
  14.0 2.2 %copy-done = bf16[1408,1536]{1,0:T(8,128)(2,1)S(1)} copy-done((bf16[1408,1536]{1,0:T(8,128)(2,1)S(1)}, bf16[1408,1536]{1,0:T(8,128)(2,1)}, u32[]{:S(2)}) %copy-start) | copy-done | bytes 4325400
  16.2 2.7 %shard_map.104 = (bf16[1408,1536]{1,0:T(8,128)(2,1)S(1)}, bf16[1536,1408]{1,0:T(8,128)(2,1)S(1)}) custom-call(bf16[1408,1536]{1,0:T(8,128)(2,1)S(1)} %copy-done, bf16[1536,1408]{1,0:T(8,128)(2,1)} %down.1), custom_call_target="tpu_custom_call" | custom-call | flops 1 | bytes 1 | tf_op jit(solution)/shard_map/pallas_call | solution.py:520
  19.0 0.1 collective-permute-start.5
  19.1 0.1 shard_map.105
  19.1 0.3 collective-permute-done.6.b2
  19.5 0.2 collective-permute-start.7
  19.7 0.3 collective-permute-start.4
  20.0 1.7 %collective-permute-start.8 = (bf16[576,256]{1,0:T(8,128)(2,1)S(1)}, bf16[576,256]{1,0:T(8,128)(2,1)S(1)}, u32[]{:S(2)}, u32[]{:S(2)}) collective-permute-start(bf16[576,256]{1,0:T(8,128)(2,1)S(1)} %get-tuple-element.86.mine), channel_id=1, source_target_pairs={{0,4},{4,0},{8,12},{12,8},{16,20},{20,16},{24,28},{28,24},{1,5},{5... | collective-permute-start | bytes 884744 | tf_op jit(solution)/shard_map/ppermute | solution.py:24
  21.7 1.5 %collective-permute-start.9 = (bf16[176,640]{1,0:T(8,128)(2,1)S(1)}, bf16[176,640]{1,0:T(8,128)(2,1)S(1)}, u32[]{:S(2)}, u32[]{:S(2)}) collective-permute-start(bf16[176,640]{1,0:T(8,128)(2,1)S(1)} %get-tuple-element.110.h0), channel_id=1, source_target_pairs={{0,2},{1,3},{2,0},{3,1},{4,6},{5,7},{6,4},{7,5},{8,10},{9,11},{10,... | collective-permute-start | bytes 675848 | tf_op jit(solution)/shard_map/ppermute | solution.py:24
  23.2 2.2 %shard_map.106 = (bf16[384,384]{1,0:T(8,128)(2,1)S(1)}, f32[64,1408]{1,0:T(8,128)S(1)}, bf16[1408,384]{1,0:T(8,128)(2,1)S(1)}, bf16[384,1408]{1,0:T(8,128)(2,1)S(1)}, bf16[384,1408]{1,0:T(8,128)(2,1)S(1)}) custom-call(bf16[704,384]{1,0:T(8,128)(2,1)S(1)} %copy-done.2, bf16[704,384]{1,0:T(8,128)(2,1)S(1)} %collective-permute-done.5.b1, ...), custom_call_target="tpu_custom_call" | custom-call | flops 1 | bytes 1 | tf_op jit(solution)/shard_map/pallas_call | solution.py:520
  25.4 0.6 collective-permute-start.11
  26.0 2.8 %collective-permute-done.9.h2 = bf16[176,640]{1,0:T(8,128)(2,1)S(1)} collective-permute-done((bf16[176,640]{1,0:T(8,128)(2,1)S(1)}, bf16[176,640]{1,0:T(8,128)(2,1)S(1)}, u32[]{:S(2)}, u32[]{:S(2)}) %collective-permute-start.9) | collective-permute-done | bytes 225312 | tf_op jit(solution)/shard_map/ppermute | solution.py:24
  28.9 0.9 %collective-permute-done.8.theirs = bf16[576,256]{1,0:T(8,128)(2,1)S(1)} collective-permute-done((bf16[576,256]{1,0:T(8,128)(2,1)S(1)}, bf16[576,256]{1,0:T(8,128)(2,1)S(1)}, u32[]{:S(2)}, u32[]{:S(2)}) %collective-permute-start.8) | collective-permute-done | bytes 294944 | tf_op jit(solution)/shard_map/ppermute | solution.py:24
  29.8 0.7 shard_map.107
  30.5 1.8 %shard_map.108 = (bf16[384,384]{1,0:T(8,128)(2,1)S(1)}, f32[64,1408]{1,0:T(8,128)S(1)}) custom-call(bf16[384,1408]{1,0:T(8,128)(2,1)S(1)} %get-tuple-element.93.tok, bf16[384,1408]{1,0:T(8,128)(2,1)S(1)} %get-tuple-element.85.cot, bf16[1408,1536]{1,0:T(8,128)(2,1)S(1)} %get-tuple-element.82.w_up, bf16[1536,1408]{1,0:T(8,128)(2,1)S(1)} %get-tuple-element.75.w_down, ...), custom_call_target="tpu_custom_call" | custom-call | flops 1 | bytes 1 | tf_op jit(solution)/shard_map/pallas_call | solution.py:520
  32.3 1.8 %shard_map.109 = (bf16[384,384]{1,0:T(8,128)(2,1)S(1)}, f32[64,1408]{1,0:T(8,128)S(1)}) custom-call(bf16[384,1408]{1,0:T(8,128)(2,1)S(1)} %get-tuple-element.93.tok, bf16[384,1408]{1,0:T(8,128)(2,1)S(1)} %get-tuple-element.85.cot, bf16[1408,1536]{1,0:T(8,128)(2,1)S(1)} %get-tuple-element.82.w_up, bf16[1536,1408]{1,0:T(8,128)(2,1)S(1)} %get-tuple-element.75.w_down, ...), custom_call_target="tpu_custom_call" | custom-call | flops 1 | bytes 1 | tf_op jit(solution)/shard_map/pallas_call | solution.py:520
  34.1 1.8 %shard_map.110 = (bf16[384,384]{1,0:T(8,128)(2,1)S(1)}, f32[64,1408]{1,0:T(8,128)S(1)}) custom-call(bf16[384,1408]{1,0:T(8,128)(2,1)S(1)} %get-tuple-element.93.tok, bf16[384,1408]{1,0:T(8,128)(2,1)S(1)} %get-tuple-element.85.cot, bf16[1408,1536]{1,0:T(8,128)(2,1)S(1)} %get-tuple-element.82.w_up, bf16[1536,1408]{1,0:T(8,128)(2,1)S(1)} %get-tuple-element.75.w_down, ...), custom_call_target="tpu_custom_call" | custom-call | flops 1 | bytes 1 | tf_op jit(solution)/shard_map/pallas_call | solution.py:520
  35.9 0.1 collective-permute-start.13
  36.0 1.9 %collective-permute-start.12 = (bf16[384,384]{1,0:T(8,128)(2,1)S(1)}, bf16[384,384]{1,0:T(8,128)(2,1)S(1)}, u32[]{:S(2)}, u32[]{:S(2)}) collective-permute-start(bf16[384,384]{1,0:T(8,128)(2,1)S(1)} %get-tuple-element.101.pre), channel_id=1, source_target_pairs={{0,4},{4,0},{8,12},{12,8},{16,20},{20,16},{24,28},{28,24},{1,5},{5... | collective-permute-start | bytes 884744 | tf_op jit(solution)/shard_map/ppermute | solution.py:24
  37.8 1.1 %shard_map.111 = (bf16[704,768]{1,0:T(8,128)(2,1)S(1)}, f32[352,384]{1,0:T(8,128)S(1)}, bf16[352,384]{1,0:T(8,128)(2,1)S(1)}) custom-call(bf16[1408,384]{1,0:T(8,128)(2,1)S(1)} %get-tuple-element.95.tok_full, bf16[176,640]{1,0:T(8,128)(2,1)S(1)} %get-tuple-element.110.h0, bf16[176,640]{1,0:T(8,128)(2,1)S(1)} %collective-permute-done.4.h1, ...), custom_call_target="tpu_custom_call" | custom-call | flops 1 | bytes 1 | tf_op jit(solution)/shard_map/pallas_call | solution.py:520
  38.9 1.6 %collective-permute-start.14 = (bf16[352,384]{1,0:T(8,128)(2,1)S(1)}, bf16[352,384]{1,0:T(8,128)(2,1)S(1)}, u32[]{:S(2)}, u32[]{:S(2)}) collective-permute-start(bf16[352,384]{1,0:T(8,128)(2,1)S(1)} %get-tuple-element.99), channel_id=1, source_target_pairs={{0,8},{4,12},{8,0},{12,4},{16,24},{20,28},{24,16},{28,20},{1,9},{5... | collective-permute-start | bytes 811016 | tf_op jit(solution)/shard_map/ppermute | solution.py:24
  40.5 1.5 %collective-permute-start.15 = (bf16[512,256]{1,0:T(8,128)(2,1)S(1)}, bf16[512,256]{1,0:T(8,128)(2,1)S(1)}, u32[]{:S(2)}, u32[]{:S(2)}) collective-permute-start(bf16[512,256]{1,0:T(8,128)(2,1)S(1)} %get-tuple-element.109), channel_id=1, source_target_pairs={{0,2},{1,3},{2,0},{3,1},{4,6},{5,7},{6,4},{7,5},{8,10},{9,11},{10,... | collective-permute-start | bytes 786440 | tf_op jit(solution)/shard_map/ppermute | solution.py:24
  42.0 0.5 collective-permute-start.17
  42.6 3.3 %collective-permute-done.12.pre_pair = bf16[384,384]{1,0:T(8,128)(2,1)S(1)} collective-permute-done((bf16[384,384]{1,0:T(8,128)(2,1)S(1)}, bf16[384,384]{1,0:T(8,128)(2,1)S(1)}, u32[]{:S(2)}, u32[]{:S(2)}) %collective-permute-start.12) | collective-permute-done | bytes 294944 | tf_op jit(solution)/shard_map/ppermute | solution.py:24
  45.8 0.8 shard_map.112
  46.7 0.1 shard_map.113.a
  46.8 1.8 %collective-permute-start.16 = (bf16[64,1408]{1,0:T(8,128)(2,1)S(1)}, bf16[64,1408]{1,0:T(8,128)(2,1)S(1)}, u32[]{:S(2)}, u32[]{:S(2)}) collective-permute-start(bf16[64,1408]{1,0:T(8,128)(2,1)S(1)} %shard_map.113.a), channel_id=1, source_target_pairs={{0,2},{1,3},{2,0},{3,1},{4,6},{5,7},{6,4},{7,5},{8,10},{9,11},{10,... | collective-permute-start | bytes 540680 | tf_op jit(solution)/shard_map/ppermute | solution.py:24
  48.6 1.6 %collective-permute-start.18 = (bf16[352,384]{1,0:T(8,128)(2,1)S(1)}, bf16[352,384]{1,0:T(8,128)(2,1)S(1)}, u32[]{:S(2)}, u32[]{:S(2)}) collective-permute-start(bf16[352,384]{1,0:T(8,128)(2,1)S(1)} %get-tuple-element.104), channel_id=1, source_target_pairs={{0,8},{4,12},{8,0},{12,4},{16,24},{20,28},{24,16},{28,20},{1,9},{5... | collective-permute-start | bytes 811016 | tf_op jit(solution)/shard_map/ppermute | solution.py:24
  50.2 0.1 shard_map.114
  50.3 1.6 %collective-permute-start.20 = (bf16[384,384]{1,0:T(8,128)(2,1)S(1)}, bf16[384,384]{1,0:T(8,128)(2,1)S(1)}, u32[]{:S(2)}, u32[]{:S(2)}) collective-permute-start(bf16[384,384]{1,0:T(8,128)(2,1)S(1)} %get-tuple-element.120.pre), channel_id=1, source_target_pairs={{0,4},{4,0},{8,12},{12,8},{16,20},{20,16},{24,28},{28,24},{1,5},{5... | collective-permute-start | bytes 884744 | tf_op jit(solution)/shard_map/ppermute | solution.py:24
  51.8 0.1 collective-permute-start.19
  51.9 0.6 collective-permute-done.16.b
  52.5 0.5 shard_map.116.e0
  53.0 1.8 %collective-permute-start.22 = (f32[192,256]{1,0:T(8,128)S(1)}, f32[192,256]{1,0:T(8,128)S(1)}, u32[]{:S(2)}, u32[]{:S(2)}) collective-permute-start(f32[192,256]{1,0:T(8,128)S(1)} %shard_map.116.e0), channel_id=1, source_target_pairs={{0,2},{1,3},{2,0},{3,1},{4,6},{5,7},{6,4},{7,5},{8,10},{9,11},{10,... | collective-permute-start | bytes 589832 | tf_op jit(solution)/shard_map/ppermute | solution.py:24
  54.8 2.6 %collective-permute-start.24 = (bf16[176,384]{1,0:T(8,128)(2,1)S(1)}, bf16[176,384]{1,0:T(8,128)(2,1)S(1)}, u32[]{:S(2)}, u32[]{:S(2)}) collective-permute-start(bf16[176,384]{1,0:T(8,128)(2,1)S(1)} %get-tuple-element.107), channel_id=1, source_target_pairs={{0,16},{4,20},{8,24},{12,28},{16,0},{20,4},{24,8},{28,12},{1,17},{... | collective-permute-start | bytes 405512 | tf_op jit(solution)/shard_map/ppermute | solution.py:24
  57.4 0.8 shard_map.117
  58.2 1.6 %collective-permute-start.25 = (bf16[352,384]{1,0:T(8,128)(2,1)S(1)}, bf16[352,384]{1,0:T(8,128)(2,1)S(1)}, u32[]{:S(2)}, u32[]{:S(2)}) collective-permute-start(bf16[352,384]{1,0:T(8,128)(2,1)S(1)} %get-tuple-element.113), channel_id=1, source_target_pairs={{0,8},{4,12},{8,0},{12,4},{16,24},{20,28},{24,16},{28,20},{1,9},{5... | collective-permute-start | bytes 811016 | tf_op jit(solution)/shard_map/ppermute | solution.py:24
  59.9 0.1 shard_map.118
  59.9 0.4 collective-permute-start.27
  60.4 0.2 shard_map.119.share
  60.6 0.0 copy-start.5
  60.6 0.1 collective-permute-start.21
  60.7 0.5 collective-permute-start.23
  61.2 0.8 shard_map.120
  62.0 0.4 collective-permute-done.24
  62.5 1.9 %collective-permute-start.28 = (bf16[352,384]{1,0:T(8,128)(2,1)S(1)}, bf16[352,384]{1,0:T(8,128)(2,1)S(1)}, u32[]{:S(2)}, u32[]{:S(2)}) collective-permute-start(bf16[352,384]{1,0:T(8,128)(2,1)S(1)} %get-tuple-element.122), channel_id=1, source_target_pairs={{0,8},{4,12},{8,0},{12,4},{16,24},{20,28},{24,16},{28,20},{1,9},{5... | collective-permute-start | bytes 811016 | tf_op jit(solution)/shard_map/ppermute | solution.py:24
  64.5 0.8 shard_map.121.a
  65.2 0.0 collective-permute-start.26
  65.3 5.3 %collective-permute-done.25.received = bf16[352,384]{1,0:T(8,128)(2,1)S(1)} collective-permute-done((bf16[352,384]{1,0:T(8,128)(2,1)S(1)}, bf16[352,384]{1,0:T(8,128)(2,1)S(1)}, u32[]{:S(2)}, u32[]{:S(2)}) %collective-permute-start.25) | collective-permute-done | bytes 270368 | tf_op jit(solution)/shard_map/ppermute | solution.py:24
  70.6 0.8 collective-permute-start.30
  71.5 0.9 %collective-permute-start.29 = (f32[1,384]{1,0:T(1,128)S(1)}, f32[1,384]{1,0:T(1,128)S(1)}, u32[]{:S(2)}, u32[]{:S(2)}) collective-permute-start(f32[1,384]{1,0:T(1,128)S(1)} %shard_map.123.a), channel_id=1, source_target_pairs={{0,2},{1,3},{2,0},{3,1},{4,6},{5,7},{6,4},{7,5},{8,10},{9,11},{10,... | collective-permute-start | bytes 4616 | tf_op jit(solution)/shard_map/ppermute | solution.py:24
  72.4 5.6 %collective-permute-done.28.received = bf16[352,384]{1,0:T(8,128)(2,1)S(1)} collective-permute-done((bf16[352,384]{1,0:T(8,128)(2,1)S(1)}, bf16[352,384]{1,0:T(8,128)(2,1)S(1)}, u32[]{:S(2)}, u32[]{:S(2)}) %collective-permute-start.28) | collective-permute-done | bytes 270368 | tf_op jit(solution)/shard_map/ppermute | solution.py:24
  77.9 0.1 shard_map.124
  78.0 0.1 collective-permute-start.31
  78.1 1.8 %collective-permute-done.30 = bf16[176,384]{1,0:T(8,128)(2,1)S(1)} collective-permute-done((bf16[176,384]{1,0:T(8,128)(2,1)S(1)}, bf16[176,384]{1,0:T(8,128)(2,1)S(1)}, u32[]{:S(2)}, u32[]{:S(2)}) %collective-permute-start.30) | collective-permute-done | bytes 135200 | tf_op jit(solution)/shard_map/ppermute | solution.py:24
  79.9 0.7 shard_map.125
  80.6 3.9 %collective-permute-done.31 = bf16[176,384]{1,0:T(8,128)(2,1)S(1)} collective-permute-done((bf16[176,384]{1,0:T(8,128)(2,1)S(1)}, bf16[176,384]{1,0:T(8,128)(2,1)S(1)}, u32[]{:S(2)}, u32[]{:S(2)}) %collective-permute-start.31) | collective-permute-done | bytes 135200 | tf_op jit(solution)/shard_map/ppermute | solution.py:24
  84.5 1.1 %pad_maximum_fusion = f32[176,1536]{1,0:T(8,128)} fusion(f32[176,384]{1,0:T(8,128)S(1)} %convert_add_fusion, f32[176,384]{1,0:T(8,128)S(1)} %convert_add_fusion.1, f32[176,384]{1,0:T(8,128)S(1)} %convert_add_fusion.2, f32[176,384]{1,0:T(8,128)S(1)} %convert_add_fusion.3), kind=kLoop, calls=%fused_computation | loop fusion | flops 811008 | bytes 2162688 | tf_op jit(solution)/shard_map/concatenate | solution.py:753
  (40 shorter events, 0.3 us)
Async XLA Ops:
  4.0 15.5 %collective-permute-start.6 = (bf16[704,384]{1,0:T(8,128)(2,1)}, bf16[704,384]{1,0:T(8,128)(2,1)S(1)}, u32[]{:S(2)}, u32[]{:S(2)}) collective-permute-start(bf16[704,384]{1,0:T(8,128)(2,1)} %get-tuple-element.80.b0), channel_id=1, source_target_pairs={{0,2},{1,3},{2,0},{3,1},{4,6},{5,7},{6,4},{7,5},{8,10},{9,11},{10,... | collective-permute-start | bytes 1622024 | tf_op jit(solution)/shard_map/ppermute | solution.py:24
  7.0 11.9 %collective-permute-start = (bf16[176,384]{1,0:T(8,128)(2,1)}, bf16[176,384]{1,0:T(8,128)(2,1)S(1)}, u32[]{:S(2)}, u32[]{:S(2)}) collective-permute-start(bf16[176,384]{1,0:T(8,128)(2,1)} %get-tuple-element.72), channel_id=1, source_target_pairs={{0,4},{4,0},{8,12},{12,8},{16,20},{20,16},{24,28},{28,24},{1,5},{5... | collective-permute-start | bytes 405512 | tf_op jit(solution)/shard_map/ppermute | solution.py:24
  8.5 10.5 %collective-permute-start.1 = (bf16[144,256]{1,0:T(8,128)(2,1)}, bf16[144,256]{1,0:T(8,128)(2,1)S(1)}, u32[]{:S(2)}, u32[]{:S(2)}) collective-permute-start(bf16[144,256]{1,0:T(8,128)(2,1)} %get-tuple-element.73.t0), channel_id=1, source_target_pairs={{0,8},{4,12},{8,16},{12,20},{16,24},{20,28},{24,0},{28,4},{1,9},{5... | collective-permute-start | bytes 221192 | tf_op jit(solution)/shard_map/ppermute | solution.py:29
  10.1 9.0 %collective-permute-start.2 = (bf16[144,256]{1,0:T(8,128)(2,1)}, bf16[144,256]{1,0:T(8,128)(2,1)S(1)}, u32[]{:S(2)}, u32[]{:S(2)}) collective-permute-start(bf16[144,256]{1,0:T(8,128)(2,1)} %get-tuple-element.73.t0), channel_id=1, source_target_pairs={{0,16},{4,20},{8,24},{12,28},{16,0},{20,4},{24,8},{28,12},{1,17},{... | collective-permute-start | bytes 221192 | tf_op jit(solution)/shard_map/ppermute | solution.py:29
  12.7 6.4 %collective-permute-start.3 = (bf16[144,256]{1,0:T(8,128)(2,1)}, bf16[144,256]{1,0:T(8,128)(2,1)S(1)}, u32[]{:S(2)}, u32[]{:S(2)}) collective-permute-start(bf16[144,256]{1,0:T(8,128)(2,1)} %get-tuple-element.73.t0), channel_id=1, source_target_pairs={{0,24},{4,28},{8,0},{12,4},{16,8},{20,12},{24,16},{28,20},{1,25},{... | collective-permute-start | bytes 221192 | tf_op jit(solution)/shard_map/ppermute | solution.py:29
  14.0 2.2 %copy-start = (bf16[1408,1536]{1,0:T(8,128)(2,1)S(1)}, bf16[1408,1536]{1,0:T(8,128)(2,1)}, u32[]{:S(2)}) copy-start(bf16[1408,1536]{1,0:T(8,128)(2,1)} %up) | copy-start | bytes 12976132
  16.2 2.7 %copy-start.2 = (bf16[704,384]{1,0:T(8,128)(2,1)S(1)}, bf16[704,384]{1,0:T(8,128)(2,1)}, u32[]{:S(2)}) copy-start(bf16[704,384]{1,0:T(8,128)(2,1)} %get-tuple-element.80.b0) | copy-start | bytes 1622020
  16.2 2.8 %copy-start.3 = (bf16[352,128]{1,0:T(8,128)(2,1)S(1)}, bf16[352,128]{1,0:T(8,128)(2,1)}, u32[]{:S(2)}) copy-start(bf16[352,128]{1,0:T(8,128)(2,1)} %get-tuple-element.77.pool) | copy-start | bytes 270340
  16.2 2.8 %copy-start.4 = (bf16[144,256]{1,0:T(8,128)(2,1)S(1)}, bf16[144,256]{1,0:T(8,128)(2,1)}, u32[]{:S(2)}) copy-start(bf16[144,256]{1,0:T(8,128)(2,1)} %get-tuple-element.73.t0) | copy-start | bytes 221188
  19.0 4.3 %collective-permute-start.5 = (bf16[704,384]{1,0:T(8,128)(2,1)S(1)}, bf16[704,384]{1,0:T(8,128)(2,1)S(1)}, u32[]{:S(2)}, u32[]{:S(2)}) collective-permute-start(bf16[704,384]{1,0:T(8,128)(2,1)S(1)} %copy-done.2), channel_id=1, source_target_pairs={{0,1},{1,0},{2,3},{3,2},{4,5},{5,4},{6,7},{7,6},{8,9},{9,8},{10,11... | collective-permute-start | bytes 1622024 | tf_op jit(solution)/shard_map/ppermute | solution.py:24
  19.5 3.8 %collective-permute-start.7 = (bf16[704,384]{1,0:T(8,128)(2,1)S(1)}, bf16[704,384]{1,0:T(8,128)(2,1)S(1)}, u32[]{:S(2)}, u32[]{:S(2)}) collective-permute-start(bf16[704,384]{1,0:T(8,128)(2,1)S(1)} %collective-permute-done.6.b2), channel_id=1, source_target_pairs={{0,1},{1,0},{2,3},{3,2},{4,5},{5,4},{6,7},{7,6},{8,9},{9,8},{10,11... | collective-permute-start | bytes 1622024 | tf_op jit(solution)/shard_map/ppermute | solution.py:24
  19.7 3.5 %collective-permute-start.4 = (bf16[176,640]{1,0:T(8,128)(2,1)S(1)}, bf16[176,640]{1,0:T(8,128)(2,1)S(1)}, u32[]{:S(2)}, u32[]{:S(2)}) collective-permute-start(bf16[176,640]{1,0:T(8,128)(2,1)S(1)} %get-tuple-element.110.h0), channel_id=1, source_target_pairs={{0,1},{1,0},{2,3},{3,2},{4,5},{5,4},{6,7},{7,6},{8,9},{9,8},{10,11... | collective-permute-start | bytes 675848 | tf_op jit(solution)/shard_map/ppermute | solution.py:24
  20.0 9.8 %collective-permute-start.8 = (bf16[576,256]{1,0:T(8,128)(2,1)S(1)}, bf16[576,256]{1,0:T(8,128)(2,1)S(1)}, u32[]{:S(2)}, u32[]{:S(2)}) collective-permute-start(bf16[576,256]{1,0:T(8,128)(2,1)S(1)} %get-tuple-element.86.mine), channel_id=1, source_target_pairs={{0,4},{4,0},{8,12},{12,8},{16,20},{20,16},{24,28},{28,24},{1,5},{5... | collective-permute-start | bytes 884744 | tf_op jit(solution)/shard_map/ppermute | solution.py:24
  21.7 7.1 %collective-permute-start.9 = (bf16[176,640]{1,0:T(8,128)(2,1)S(1)}, bf16[176,640]{1,0:T(8,128)(2,1)S(1)}, u32[]{:S(2)}, u32[]{:S(2)}) collective-permute-start(bf16[176,640]{1,0:T(8,128)(2,1)S(1)} %get-tuple-element.110.h0), channel_id=1, source_target_pairs={{0,2},{1,3},{2,0},{3,1},{4,6},{5,7},{6,4},{7,5},{8,10},{9,11},{10,... | collective-permute-start | bytes 675848 | tf_op jit(solution)/shard_map/ppermute | solution.py:24
  25.4 12.4 %collective-permute-start.11 = (bf16[384,384]{1,0:T(8,128)(2,1)S(1)}, bf16[384,384]{1,0:T(8,128)(2,1)S(1)}, u32[]{:S(2)}, u32[]{:S(2)}) collective-permute-start(bf16[384,384]{1,0:T(8,128)(2,1)S(1)} %get-tuple-element.96.pre), channel_id=1, source_target_pairs={{0,4},{4,0},{8,12},{12,8},{16,20},{20,16},{24,28},{28,24},{1,5},{5... | collective-permute-start | bytes 884744 | tf_op jit(solution)/shard_map/ppermute | solution.py:24
  28.9 8.9 %collective-permute-start.10 = (bf16[176,640]{1,0:T(8,128)(2,1)S(1)}, bf16[176,640]{1,0:T(8,128)(2,1)S(1)}, u32[]{:S(2)}, u32[]{:S(2)}) collective-permute-start(bf16[176,640]{1,0:T(8,128)(2,1)S(1)} %collective-permute-done.9.h2), channel_id=1, source_target_pairs={{0,1},{1,0},{2,3},{3,2},{4,5},{5,4},{6,7},{7,6},{8,9},{9,8},{10,11... | collective-permute-start | bytes 675848 | tf_op jit(solution)/shard_map/ppermute | solution.py:24
  35.9 10.8 %collective-permute-start.13 = (f32[64,1408]{1,0:T(8,128)S(1)}, f32[64,1408]{1,0:T(8,128)S(1)}, u32[]{:S(2)}, u32[]{:S(2)}) collective-permute-start(f32[64,1408]{1,0:T(8,128)S(1)} %get-tuple-element.105.a), channel_id=1, source_target_pairs={{0,1},{1,0},{2,3},{3,2},{4,5},{5,4},{6,7},{7,6},{8,9},{9,8},{10,11... | collective-permute-start | bytes 1081352 | tf_op jit(solution)/shard_map/ppermute | solution.py:24
  36.0 9.9 %collective-permute-start.12 = (bf16[384,384]{1,0:T(8,128)(2,1)S(1)}, bf16[384,384]{1,0:T(8,128)(2,1)S(1)}, u32[]{:S(2)}, u32[]{:S(2)}) collective-permute-start(bf16[384,384]{1,0:T(8,128)(2,1)S(1)} %get-tuple-element.101.pre), channel_id=1, source_target_pairs={{0,4},{4,0},{8,12},{12,8},{16,20},{20,16},{24,28},{28,24},{1,5},{5... | collective-permute-start | bytes 884744 | tf_op jit(solution)/shard_map/ppermute | solution.py:24
  38.9 11.3 %collective-permute-start.14 = (bf16[352,384]{1,0:T(8,128)(2,1)S(1)}, bf16[352,384]{1,0:T(8,128)(2,1)S(1)}, u32[]{:S(2)}, u32[]{:S(2)}) collective-permute-start(bf16[352,384]{1,0:T(8,128)(2,1)S(1)} %get-tuple-element.99), channel_id=1, source_target_pairs={{0,8},{4,12},{8,0},{12,4},{16,24},{20,28},{24,16},{28,20},{1,9},{5... | collective-permute-start | bytes 811016 | tf_op jit(solution)/shard_map/ppermute | solution.py:24
  40.5 11.3 %collective-permute-start.15 = (bf16[512,256]{1,0:T(8,128)(2,1)S(1)}, bf16[512,256]{1,0:T(8,128)(2,1)S(1)}, u32[]{:S(2)}, u32[]{:S(2)}) collective-permute-start(bf16[512,256]{1,0:T(8,128)(2,1)S(1)} %get-tuple-element.109), channel_id=1, source_target_pairs={{0,2},{1,3},{2,0},{3,1},{4,6},{5,7},{6,4},{7,5},{8,10},{9,11},{10,... | collective-permute-start | bytes 786440 | tf_op jit(solution)/shard_map/ppermute | solution.py:24
  42.0 12.8 %collective-permute-start.17 = (bf16[384,384]{1,0:T(8,128)(2,1)S(1)}, bf16[384,384]{1,0:T(8,128)(2,1)S(1)}, u32[]{:S(2)}, u32[]{:S(2)}) collective-permute-start(bf16[384,384]{1,0:T(8,128)(2,1)S(1)} %get-tuple-element.112.pre), channel_id=1, source_target_pairs={{0,4},{4,0},{8,12},{12,8},{16,20},{20,16},{24,28},{28,24},{1,5},{5... | collective-permute-start | bytes 884744 | tf_op jit(solution)/shard_map/ppermute | solution.py:24
  46.7 5.8 %copy-start.1 = (bf16[1408,256]{1,0:T(8,128)(2,1)S(1)}, bf16[1408,256]{1,0:T(8,128)(2,1)}, u32[]{:S(2)}) copy-start(bf16[1408,256]{1,0:T(8,128)(2,1)} %ref_proj.1) | copy-start | bytes 2162692
  46.8 5.8 %collective-permute-start.16 = (bf16[64,1408]{1,0:T(8,128)(2,1)S(1)}, bf16[64,1408]{1,0:T(8,128)(2,1)S(1)}, u32[]{:S(2)}, u32[]{:S(2)}) collective-permute-start(bf16[64,1408]{1,0:T(8,128)(2,1)S(1)} %shard_map.113.a), channel_id=1, source_target_pairs={{0,2},{1,3},{2,0},{3,1},{4,6},{5,7},{6,4},{7,5},{8,10},{9,11},{10,... | collective-permute-start | bytes 540680 | tf_op jit(solution)/shard_map/ppermute | solution.py:24
  48.6 9.6 %collective-permute-start.18 = (bf16[352,384]{1,0:T(8,128)(2,1)S(1)}, bf16[352,384]{1,0:T(8,128)(2,1)S(1)}, u32[]{:S(2)}, u32[]{:S(2)}) collective-permute-start(bf16[352,384]{1,0:T(8,128)(2,1)S(1)} %get-tuple-element.104), channel_id=1, source_target_pairs={{0,8},{4,12},{8,0},{12,4},{16,24},{20,28},{24,16},{28,20},{1,9},{5... | collective-permute-start | bytes 811016 | tf_op jit(solution)/shard_map/ppermute | solution.py:24
  50.3 10.5 %collective-permute-start.20 = (bf16[384,384]{1,0:T(8,128)(2,1)S(1)}, bf16[384,384]{1,0:T(8,128)(2,1)S(1)}, u32[]{:S(2)}, u32[]{:S(2)}) collective-permute-start(bf16[384,384]{1,0:T(8,128)(2,1)S(1)} %get-tuple-element.120.pre), channel_id=1, source_target_pairs={{0,4},{4,0},{8,12},{12,8},{16,20},{20,16},{24,28},{28,24},{1,5},{5... | collective-permute-start | bytes 884744 | tf_op jit(solution)/shard_map/ppermute | solution.py:24
  51.8 8.1 %collective-permute-start.19 = (bf16[512,256]{1,0:T(8,128)(2,1)S(1)}, bf16[512,256]{1,0:T(8,128)(2,1)S(1)}, u32[]{:S(2)}, u32[]{:S(2)}) collective-permute-start(bf16[512,256]{1,0:T(8,128)(2,1)S(1)} %shard_map.115), channel_id=1, source_target_pairs={{0,1},{1,0},{2,3},{3,2},{4,5},{5,4},{6,7},{7,6},{8,9},{9,8},{10,11... | collective-permute-start | bytes 786440 | tf_op jit(solution)/shard_map/ppermute | solution.py:24
  53.0 7.6 %collective-permute-start.22 = (f32[192,256]{1,0:T(8,128)S(1)}, f32[192,256]{1,0:T(8,128)S(1)}, u32[]{:S(2)}, u32[]{:S(2)}) collective-permute-start(f32[192,256]{1,0:T(8,128)S(1)} %shard_map.116.e0), channel_id=1, source_target_pairs={{0,2},{1,3},{2,0},{3,1},{4,6},{5,7},{6,4},{7,5},{8,10},{9,11},{10,... | collective-permute-start | bytes 589832 | tf_op jit(solution)/shard_map/ppermute | solution.py:24
  54.8 7.7 %collective-permute-start.24 = (bf16[176,384]{1,0:T(8,128)(2,1)S(1)}, bf16[176,384]{1,0:T(8,128)(2,1)S(1)}, u32[]{:S(2)}, u32[]{:S(2)}) collective-permute-start(bf16[176,384]{1,0:T(8,128)(2,1)S(1)} %get-tuple-element.107), channel_id=1, source_target_pairs={{0,16},{4,20},{8,24},{12,28},{16,0},{20,4},{24,8},{28,12},{1,17},{... | collective-permute-start | bytes 405512 | tf_op jit(solution)/shard_map/ppermute | solution.py:24
  58.2 12.3 %collective-permute-start.25 = (bf16[352,384]{1,0:T(8,128)(2,1)S(1)}, bf16[352,384]{1,0:T(8,128)(2,1)S(1)}, u32[]{:S(2)}, u32[]{:S(2)}) collective-permute-start(bf16[352,384]{1,0:T(8,128)(2,1)S(1)} %get-tuple-element.113), channel_id=1, source_target_pairs={{0,8},{4,12},{8,0},{12,4},{16,24},{20,28},{24,16},{28,20},{1,9},{5... | collective-permute-start | bytes 811016 | tf_op jit(solution)/shard_map/ppermute | solution.py:24
  59.9 11.5 %collective-permute-start.27 = (bf16[176,384]{1,0:T(8,128)(2,1)S(1)}, bf16[176,384]{1,0:T(8,128)(2,1)S(1)}, u32[]{:S(2)}, u32[]{:S(2)}) collective-permute-start(bf16[176,384]{1,0:T(8,128)(2,1)S(1)} %get-tuple-element.115), channel_id=1, source_target_pairs={{0,16},{4,20},{8,24},{12,28},{16,0},{20,4},{24,8},{28,12},{1,17},{... | collective-permute-start | bytes 405512 | tf_op jit(solution)/shard_map/ppermute | solution.py:24
  60.6 3.8 %copy-start.5 = (s32[64]{0:T(128)S(1)}, s32[64]{0:T(128)}, u32[]{:S(2)}) copy-start(s32[64]{0:T(128)} %param.13) | copy-start | bytes 772
  60.6 3.8 %collective-permute-start.21 = (f32[192,256]{1,0:T(8,128)S(1)}, f32[192,256]{1,0:T(8,128)S(1)}, u32[]{:S(2)}, u32[]{:S(2)}) collective-permute-start(f32[192,256]{1,0:T(8,128)S(1)} %shard_map.116.e0), channel_id=1, source_target_pairs={{0,1},{1,0},{2,3},{3,2},{4,5},{5,4},{6,7},{7,6},{8,9},{9,8},{10,11... | collective-permute-start | bytes 589832 | tf_op jit(solution)/shard_map/ppermute | solution.py:24
  60.7 3.7 %collective-permute-start.23 = (f32[192,256]{1,0:T(8,128)S(1)}, f32[192,256]{1,0:T(8,128)S(1)}, u32[]{:S(2)}, u32[]{:S(2)}) collective-permute-start(f32[192,256]{1,0:T(8,128)S(1)} %collective-permute-done.22.e2), channel_id=1, source_target_pairs={{0,1},{1,0},{2,3},{3,2},{4,5},{5,4},{6,7},{7,6},{8,9},{9,8},{10,11... | collective-permute-start | bytes 589832 | tf_op jit(solution)/shard_map/ppermute | solution.py:24
  62.5 15.5 %collective-permute-start.28 = (bf16[352,384]{1,0:T(8,128)(2,1)S(1)}, bf16[352,384]{1,0:T(8,128)(2,1)S(1)}, u32[]{:S(2)}, u32[]{:S(2)}) collective-permute-start(bf16[352,384]{1,0:T(8,128)(2,1)S(1)} %get-tuple-element.122), channel_id=1, source_target_pairs={{0,8},{4,12},{8,0},{12,4},{16,24},{20,28},{24,16},{28,20},{1,9},{5... | collective-permute-start | bytes 811016 | tf_op jit(solution)/shard_map/ppermute | solution.py:24
  65.2 6.2 %collective-permute-start.26 = (f32[1,384]{1,0:T(1,128)S(1)}, f32[1,384]{1,0:T(1,128)S(1)}, u32[]{:S(2)}, u32[]{:S(2)}) collective-permute-start(f32[1,384]{1,0:T(1,128)S(1)} %shard_map.121.a), channel_id=1, source_target_pairs={{0,1},{1,0},{2,3},{3,2},{4,5},{5,4},{6,7},{7,6},{8,9},{9,8},{10,11... | collective-permute-start | bytes 4616 | tf_op jit(solution)/shard_map/ppermute | solution.py:24
  70.6 9.2 %collective-permute-start.30 = (bf16[176,384]{1,0:T(8,128)(2,1)S(1)}, bf16[176,384]{1,0:T(8,128)(2,1)S(1)}, u32[]{:S(2)}, u32[]{:S(2)}) collective-permute-start(bf16[176,384]{1,0:T(8,128)(2,1)S(1)} %get-tuple-element.126), channel_id=1, source_target_pairs={{0,16},{4,20},{8,24},{12,28},{16,0},{20,4},{24,8},{28,12},{1,17},{... | collective-permute-start | bytes 405512 | tf_op jit(solution)/shard_map/ppermute | solution.py:24
  71.5 8.4 %collective-permute-start.29 = (f32[1,384]{1,0:T(1,128)S(1)}, f32[1,384]{1,0:T(1,128)S(1)}, u32[]{:S(2)}, u32[]{:S(2)}) collective-permute-start(f32[1,384]{1,0:T(1,128)S(1)} %shard_map.123.a), channel_id=1, source_target_pairs={{0,2},{1,3},{2,0},{3,1},{4,6},{5,7},{6,4},{7,5},{8,10},{9,11},{10,... | collective-permute-start | bytes 4616 | tf_op jit(solution)/shard_map/ppermute | solution.py:24
  78.0 6.5 %collective-permute-start.31 = (bf16[176,384]{1,0:T(8,128)(2,1)S(1)}, bf16[176,384]{1,0:T(8,128)(2,1)S(1)}, u32[]{:S(2)}, u32[]{:S(2)}) collective-permute-start(bf16[176,384]{1,0:T(8,128)(2,1)S(1)} %get-tuple-element.130), channel_id=1, source_target_pairs={{0,16},{4,20},{8,24},{12,28},{16,0},{20,4},{24,8},{28,12},{1,17},{... | collective-permute-start | bytes 405512 | tf_op jit(solution)/shard_map/ppermute | solution.py:24

commit v5 on v4

--- a/solution.py
+++ b/solution.py
@@ -282,7 +282,7 @@
     pool[...] = (dot_rows(values, groups.astype(bf16)) * (1.0 / n_patch)).astype(bf16)
 
 
-def extras_body(half, pool, t0, t1, t2, t3, extras, texts):
+def extras_body(half, pool, t0, t1, t2, t3, extras, texts, dests):
     n_half, n_rows = half.shape
     n_ex = pool.shape[1]
     extras[:, 0:n_rows] = half[...]
@@ -291,36 +291,45 @@
     n_text = t0.shape[0]
     for r, piece in enumerate((t0, t1, t2, t3)):
         texts[r * n_text : (r + 1) * n_text, :] = piece[...]
-
-
-def text_body(k_dev, n_patch, mine, theirs, whole, send, weights):
+        k_dev = dests.shape[1] // 4
+        dests[:, r * k_dev : (r + 1) * k_dev] = piece[n_text - 16 :, 0:k_dev]
+
+
+def text_body(mine, theirs, whole, send):
     n_high = 4
     n_text = mine.shape[0] // n_high
     ex_dev = n_text - 16
     me = lax.axis_index("mdl")
     sel = lax.axis_index("sel")
     parity, high = lax.rem(sel, 2), lax.div(sel, 2)
-    shard = lax.broadcasted_iota(jnp.int32, (128, k_dev), 0).astype(f32)
-    ones = jnp.ones((8, k_dev), bf16)
-    counts = jnp.zeros((8, 128), f32)
-    named = []
     for which, place_in_pair in ((mine, parity), (theirs, 1 - parity)):
         for r in range(n_high):
             source = lax.rem(high + n_high - r, n_high)
             rows = place(source * 2 + place_in_pair, ex_dev)
             whole[rows, :] = which[r * n_text : r * n_text + ex_dev, :]
-            dest = which[r * n_text + ex_dev : (r + 1) * n_text, 0:k_dev].astype(f32)[0:1]
-            is_dest = (shard == dest).astype(bf16)
+    for i in range(2):
+        send[i * 2 * ex_dev : (i + 1) * 2 * ex_dev, :] = whole[place(me ^ (2 + i), 2 * ex_dev), :]
+
+
+def row_weights(n_patch, n_rows, pre, pre_pair):
+    k_dev = n_rows // n_patch
+    shard = lax.broadcasted_iota(jnp.int32, (128, k_dev), 0).astype(f32)
+    ones = jnp.ones((8, k_dev), bf16)
+    counts = jnp.zeros((8, 128), f32)
+    named = []
+    for which in (pre, pre_pair):
+        dests = which[n_rows:, :].astype(f32)
+        for r in range(4):
+            is_dest = (shard == dests[0:1, r * k_dev : (r + 1) * k_dev]).astype(bf16)
             counts = counts + dot_rows(ones, is_dest)
             if r == 0:
                 named.append(is_dest)
     member = group_mask(k_dev, n_patch)[0].astype(bf16)
-    n_rows = k_dev * n_patch
-    for i, is_dest in enumerate(named):
+    weights = []
+    for is_dest in named:
         count = dot_f32(counts.astype(bf16), is_dest).astype(bf16)
-        weights[:, i * n_rows : (i + 1) * n_rows] = 1.0 / dot_f32(count, member)
-    for i in range(2):
-        send[i * 2 * ex_dev : (i + 1) * 2 * ex_dev, :] = whole[place(me ^ (2 + i), 2 * ex_dev), :]
+        weights.append(1.0 / dot_f32(count, member)[0:1])
+    return weights
 
 
 def text_relay_body(whole, received, send):
@@ -361,7 +370,7 @@
     groups = group_mask(k_dev, n_patch)[0].astype(bf16)
     pre_act = dot_f32(tok[...], w_up[...])
     activated, gelu_slope = gelu_parts(pre_act)
-    pre[...] = (dot_rows(cot[...], w_down[...]) * gelu_slope).astype(bf16)
+    pre[0 : tok.shape[0], :] = (dot_rows(cot[...], w_down[...]) * gelu_slope).astype(bf16)
     pooled = dot_f32(groups, activated.astype(bf16))
     high = pooled.astype(bf16)
     low = (pooled - high.astype(f32)).astype(bf16)
@@ -370,7 +379,7 @@
 
 
 def first_chunk_body(
-    n_patch, n_mdl, b0, b1, b2, b3, w_up, w_down, pre, mixed, tok_full, tok, cot, cot_full
+    n_patch, n_mdl, dests, b0, b1, b2, b3, w_up, w_down, pre, mixed, tok_full, tok, cot, cot_full
 ):
     d_part, n_rows = b0.shape[0] // 2, b0.shape[1]
     groups = group_mask(n_rows // n_patch, n_patch)[0].astype(bf16)
@@ -382,10 +391,13 @@
     cot[...] = cot_full[...].T
     start = dot_f32(groups, tok[...]) * (1.0 / n_mdl)
     mixed[...] = chunk_work(n_patch, tok, cot, w_up, w_down, pre, start)
+    pre[n_rows:, :] = jnp.zeros((16, pre.shape[1]), bf16)
+    pre[n_rows:, 0 : dests.shape[1]] = dests[...]
 
 
 def next_chunk_body(n_patch, tok, cot, w_up, w_down, mixed_in, pre, mixed):
-    mixed[...] = chunk_work(n_patch, tok, cot, w_up, w_down, pre, mixed_in[...])
+    total = chunk_work(n_patch, tok, cot, w_up, w_down, pre, mixed_in[...])
+    mixed[...] = total.astype(mixed.dtype)
 
 
 def split_part(part, keep, send):
@@ -394,9 +406,10 @@
     send[...] = part[n_keep:].astype(bf16)
 
 
-def first_grad_body(tok_full, h0, h1, h2, h3, weights, pre, pre_pair, pair, keep, send):
+def first_grad_body(n_patch, tok_full, h0, h1, h2, h3, pre, pre_pair, pair, keep, send):
     n_rows = tok_full.shape[1]
     blk = h0.shape[0]
+    weights = row_weights(n_patch, n_rows, pre, pre_pair)
     me = lax.axis_index("mdl")
     sel = lax.axis_index("sel")
     parity, high = lax.rem(sel, 2), lax.div(sel, 2)
@@ -405,15 +418,16 @@
         apart = block ^ high
         rows = place(2 * lax.rem(apart, 2) + lax.div(apart, 2), blk)
         own_tok = tok_full[place(2 * block + parity, blk), :].astype(f32)
-        pair[rows, 0:n_rows] = (own_tok * weights[0:1, 0:n_rows]).astype(bf16)
+        pair[rows, 0:n_rows] = (own_tok * weights[0]).astype(bf16)
         pair_tok = piece[:, 0:n_rows].astype(f32)
-        pair[rows, n_rows:] = (pair_tok * weights[0:1, n_rows:]).astype(bf16)
+        pair[rows, n_rows:] = (pair_tok * weights[1]).astype(bf16)
     grad_body(pair, pre, pre_pair, keep, send)
 
 
 def grad_body(pair, pre, pre_pair, keep, send):
-    n_rows = pre.shape[0]
-    part = dot_f32(pair[:, 0:n_rows], pre[...]) + dot_f32(pair[:, n_rows:], pre_pair[...])
+    n_rows = pair.shape[1] // 2
+    part = dot_f32(pair[:, 0:n_rows], pre[0:n_rows, :])
+    part = part + dot_f32(pair[:, n_rows:], pre_pair[0:n_rows, :])
     split_part(part, keep, send)
 
 
@@ -422,7 +436,7 @@
 
 
 def mix_body(a, b, total):
-    total[...] = (a[...] + b[...]).astype(total.dtype)
+    total[...] = (a[...].astype(f32) + b[...].astype(f32)).astype(total.dtype)
 
 
 def heads_body(n_patch, h0, h1, h2, h3, a, b, ref_proj, emb, pooled):
@@ -555,7 +569,7 @@
             w_down,
             in_specs=[pl.BlockSpec(memory_space=pltpu.HBM)] * 2,
             scratch_shapes=[pltpu.SemaphoreType.DMA((2,))],
-            vmem=40 * 2**20,
+            vmem=32 * 2**20,
         )
 
 
@@ -567,6 +581,7 @@
             (
                 struct((d_part // 2, n_rows + 2 * ex_dev), bf16),
                 struct((n_high * (ex_dev + 16), emb_part), bf16),
+                struct((16, n_high * k_dev), bf16),
             ),
             half_pair,
             pool,
@@ -586,19 +601,33 @@
         return run(
             ties,
             functools.partial(first_chunk_body, n_patch, n_mdl),
-            (pre_struct, mixed_struct, struct((d_full, n_rows), bf16), row_struct, row_struct),
+            (
+                struct((n_rows + 16, size), bf16),
+                mixed_struct,
+                struct((d_full, n_rows), bf16),
+                row_struct,
+                row_struct,
+            ),
             *operands,
             grid=(1,),
-            in_specs=[whole((2 * d_part, n_rows))] * 4 + weight_specs(0),
-            out_specs=[pre_spec, mixed_spec, whole((d_full, n_rows)), row_spec, row_spec],
+            in_specs=[whole((16, n_high * k_dev))]
+            + [whole((2 * d_part, n_rows))] * 4 + weight_specs(0),
+            out_specs=[
+                whole((n_rows + 16, size)),
+                mixed_spec,
+                whole((d_full, n_rows)),
+                row_spec,
+                row_spec,
+            ],
             scratch_shapes=[pltpu.VMEM((d_full, n_rows), bf16)],
         )
 
     def forward(ties, c, tok, cot, held_up, held_down, mixed):
+        last = c == ff_dev // size - 1
         return run(
             ties,
             functools.partial(next_chunk_body, n_patch),
-            (pre_struct, mixed_struct),
+            (pre_struct, struct((k_dev, d_full), bf16 if last else f32)),
             tok,
             cot,
             held_up,
@@ -613,11 +642,10 @@
     def all_shards(ties, my_texts, pair_texts):
         return run(
             ties,
-            functools.partial(text_body, k_dev, n_patch),
+            text_body,
             (
                 struct((ex_dev * n_sel, emb_part), bf16),
                 struct((2 * n_share, emb_part), bf16),
-                struct((8, 2 * n_rows), f32),
             ),
             my_texts,
             pair_texts,
@@ -625,7 +653,7 @@
 
     def grad_first(ties, *operands):
         pair_struct = struct((blk * n_high, 2 * n_rows), bf16)
-        return run(ties, first_grad_body, (pair_struct,) + halves, *operands)
+        return run(ties, functools.partial(first_grad_body, n_patch), (pair_struct,) + halves, *operands)
 
     def grad(ties, *operands):
         return run(ties, grad_body, halves, *operands)
@@ -677,14 +705,15 @@
     both_core = swap(both, "mdl", 1)
     half_pair = swap(half, "sel", 1)
     held_up, held_down = stage((texts,))
-    extras, my_texts = make_extras((held_down,), half_pair, pool, texts)
+    extras, my_texts, dests = make_extras((held_down,), half_pair, pool, texts)
     both_diag = swap(after(both_x, extras), "mdl", 1)
     extras_x = swap(extras, "mdl", 2)
     extras_core = swap(extras, "mdl", 1)
     extras_diag = swap(extras_x, "mdl", 1)
     pair_texts = swap(my_texts, "sel", 1)
     pre0, mixed0, tok_full, tok, cot = forward_first(
-        (my_texts, extras_core),
+        (dests, extras_core),
+        dests,
         both,
         both_core,
         both_x,
@@ -693,53 +722,52 @@
         held_down,
     )
     pair_pre0 = swap(pre0, "sel", 1)
-    all_texts, text_send, weights = all_shards((cot,), my_texts, pair_texts)
+    pre1, mixed1 = forward((cot,), 1, tok, cot, held_up, held_down, mixed0)
+    pair_pre1 = swap(pre1, "sel", 1)
+    all_texts, text_send = all_shards((mixed1,), my_texts, pair_texts)
     text_x = swap(text_send, "mdl", 2)
-    pre1, mixed1 = forward((weights,), 1, tok, cot, held_up, held_down, mixed0)
-    pair_pre1 = swap(pre1, "sel", 1)
-    pre2, mixed2 = forward((mixed1,), 2, tok, cot, held_up, held_down, mixed1)
+    pre2, mixed2 = forward((text_send,), 2, tok, cot, held_up, held_down, mixed1)
     pair_pre2 = swap(pre2, "sel", 1)
-    pre3, mixed = forward((mixed2, extras_x), 3, tok, cot, held_up, held_down, mixed2)
+    pre3, mixed = forward((mixed2,), 3, tok, cot, held_up, held_down, mixed2)
     mixed_core = swap(mixed, "mdl", 1)
+    mixsum = run((mixed, extras_diag), mix_body, struct((k_dev, d_full), bf16), mixed, mixed_core)
+    mixsum_x = swap(mixsum, "mdl", 2)
+    relay = relay_text((mixsum,), all_texts, text_x)
+    text_core = swap(relay, "mdl", 1)
     pair, keep0, send0 = grad_first(
-        (mixed,),
+        (relay,),
         tok_full,
         extras,
         extras_core,
         extras_x,
         extras_diag,
-        weights,
         pre0,
         pair_pre0,
     )
     first0 = swap(send0, "sel", 2)
-    keep1, send1 = grad((send0,), pair, pre1, pair_pre1)
+    keep1, send1 = grad((send0, text_x), pair, pre1, pair_pre1)
     first1 = swap(send1, "sel", 2)
-    mixsum = run((send1,), mix_body, struct((k_dev, d_full), bf16), mixed, mixed_core)
-    mixsum_x = swap(mixsum, "mdl", 2)
-    own0, rest0 = add((mixsum,), keep0, first0)
-    pair_pre3 = swap(after(pre3, own0), "sel", 1)
-    second0 = swap(rest0, "sel", 4)
-    relay = relay_text((rest0,), all_texts, text_x)
-    text_core = swap(relay, "mdl", 1)
-    emb = heads((relay,), extras, extras_core, extras_x, extras_diag, mixsum, mixsum_x)
+    emb = heads((send1, first0), extras, extras_core, extras_x, extras_diag, mixsum, mixsum_x)
     emb_x = swap(emb, "mdl", 2)
     emb_core = swap(emb, "mdl", 1)
     emb_diag = swap(emb_x, "mdl", 1)
-    keep2, send2 = grad((emb,), pair, pre2, pair_pre2)
+    own0, rest0 = add((emb,), keep0, first0)
+    pair_pre3 = swap(after(pre3, own0), "sel", 1)
+    second0 = swap(rest0, "sel", 4)
+    keep2, send2 = grad((rest0,), pair, pre2, pair_pre2)
     first2 = swap(send2, "sel", 2)
     own1, rest1 = add((send2,), keep1, first1)
     second1 = swap(rest1, "sel", 4)
     share = share_text((rest1,), all_texts, text_x, text_core)
     keep3, send3 = grad((share,), pair, pre3, pair_pre3)
     first3 = swap(send3, "sel", 2)
-    sums = scores((send3,), emb, emb_core, emb_x, emb_diag, share)
+    own2, rest2 = add((send3,), keep2, first2)
+    second2 = swap(rest2, "sel", 4)
+    sums = scores((rest2,), emb, emb_core, emb_x, emb_diag, share)
     sums_core = swap(sums, "mdl", 1)
-    own2, rest2 = add((sums, second0), keep2, first2)
-    second2 = swap(rest2, "sel", 4)
-    total = run((rest2,), mix_body, struct((1, 2 * n_emb), f32), sums, sums_core)
-    total_x = swap(total, "mdl", 2)
-    own3, rest3 = add((total, second1), keep3, first3)
+    total = run((sums,), mix_body, struct((1, 2 * n_emb), f32), sums, sums_core)
+    own3, rest3 = add((total,), keep3, first3)
+    total_x = swap(after(total, own3), "mdl", 2)
     second3 = swap(rest3, "sel", 4)
     ref_loss, learnability = losses((rest3,), total, total_x)
 

time: 85.8 us -> 83.5 us (0.973)
  local copies, waits for them, and re-layouts: 2.25 us -> 4.57 us
  starting transfers between devices: 35.8 us -> 33.6 us
  Pallas kernels: 20.4 us -> 18.8 us
  waiting for transfers between devices: 25 us -> 24.1 us
    unnamed x12 -> x14, local copies, waits for them, and re-layouts: 2.25 us -> 4.57 us
    ppermute x29, starting transfers between devices: 30.3 us -> 28.1 us  [swap(): return lax.ppermute(value, axis, [(i, i ^ bit) for i in range(size)])]
    pallas_call x23, Pallas kernels: 20.4 us -> 18.8 us  [run(): call(body, out_shape, (2 ** 20, 2 ** 20), **kwargs)(first, *operands[1:])]
    ppermute x29, waiting for transfers between devices: 25 us -> 24.1 us  [swap(): return lax.ppermute(value, axis, [(i, i ^ bit) for i in range(size)])]
  transfers between devices with their start and end apart: 32 -> 32, of which waited for: 10 -> 10; matrix products, arithmetic and copies ran while one was open for 0% -> 0% of each run, Pallas kernels for 20% -> 19%
where the time goes in v5:
time: 83.5 us; the launch traced here: 83.3 us
  starting transfers between devices  33.6 us (40%)
  waiting for transfers between devices  24.1 us (29%)
  Pallas kernels  18.8 us (23%)
  local copies, waits for them, and re-layouts  4.57 us (5%)
  other arithmetic  1.23 us (1%)
  between operations  0.9 us (1%)
    ppermute x29, starting transfers between devices, swap(): return lax.ppermute(value, axis, [(i, i ^ bit) for i in range(size)])  28.1 us
    ppermute x29, waiting for transfers between devices, swap(): return lax.ppermute(value, axis, [(i, i ^ bit) for i in range(size)])  24.1 us
    pallas_call x23, Pallas kernels, run(): call(body, out_shape, (2 ** 20, 2 ** 20), **kwargs)(first, *operands[1:])  18.8 us
    ppermute x3, starting transfers between devices, rotate_pairs(): lax.ppermute(value, 'sel', [(i, (i + 2 * step) % size) for i in range(siz...  5.51 us
    unnamed x14, local copies, waits for them, and re-layouts  4.57 us
  transfers between devices with their start and end apart: 32, of which 10 were waited for; matrix products, arithmetic and copies ran while one was open for 0% of the time, Pallas kernels for 19%

profile of v5, /device:TPU:0, one launch (start us, length us, event | category | flops | bytes accessed | tf_op | source)
XLA Modules:
  0.0 83.3 jit_solution(6052353289739205848)
XLA Ops:
  0.6 3.3 %shard_map.103 = (bf16[704,384]{1,0:T(8,128)(2,1)}, bf16[176,384]{1,0:T(8,128)(2,1)}, bf16[352,128]{1,0:T(8,128)(2,1)}, bf16[144,256]{1,0:T(8,128)(2,1)}) custom-call(bf16[352,768]{1,0:T(8,128)(2,1)} %bitcast.9, bf16[352,384]{1,0:T(8,128)(2,1)} %bitcast.10, s32[1,64]{1,0:T(1,128)} %bitcast.6, s32[1,64]{1,0:T(1,128)} %bitcast.11, bf16[128,256]{1,0:T(8,128)(2,1)} %text_hbm.1), custom_call_target="tpu_custom_call" | custom-call | flops 1 | bytes 1 | tf_op jit(solution)/shard_map/pallas_call | solution.py:534
  4.0 3.0 %collective-permute-start.6 = (bf16[704,384]{1,0:T(8,128)(2,1)}, bf16[704,384]{1,0:T(8,128)(2,1)S(1)}, u32[]{:S(2)}, u32[]{:S(2)}) collective-permute-start(bf16[704,384]{1,0:T(8,128)(2,1)} %get-tuple-element.81.b0), channel_id=1, source_target_pairs={{0,2},{1,3},{2,0},{3,1},{4,6},{5,7},{6,4},{7,5},{8,10},{9,11},{10,... | collective-permute-start | bytes 1622024 | tf_op jit(solution)/shard_map/ppermute | solution.py:24
  7.0 1.5 %collective-permute-start = (bf16[176,384]{1,0:T(8,128)(2,1)}, bf16[176,384]{1,0:T(8,128)(2,1)S(1)}, u32[]{:S(2)}, u32[]{:S(2)}) collective-permute-start(bf16[176,384]{1,0:T(8,128)(2,1)} %get-tuple-element.72), channel_id=1, source_target_pairs={{0,4},{4,0},{8,12},{12,8},{16,20},{20,16},{24,28},{28,24},{1,5},{5... | collective-permute-start | bytes 405512 | tf_op jit(solution)/shard_map/ppermute | solution.py:24
  8.5 1.6 %collective-permute-start.1 = (bf16[144,256]{1,0:T(8,128)(2,1)}, bf16[144,256]{1,0:T(8,128)(2,1)S(1)}, u32[]{:S(2)}, u32[]{:S(2)}) collective-permute-start(bf16[144,256]{1,0:T(8,128)(2,1)} %get-tuple-element.73.t0), channel_id=1, source_target_pairs={{0,8},{4,12},{8,16},{12,20},{16,24},{20,28},{24,0},{28,4},{1,9},{5... | collective-permute-start | bytes 221192 | tf_op jit(solution)/shard_map/ppermute | solution.py:29
  10.1 2.6 %collective-permute-start.2 = (bf16[144,256]{1,0:T(8,128)(2,1)}, bf16[144,256]{1,0:T(8,128)(2,1)S(1)}, u32[]{:S(2)}, u32[]{:S(2)}) collective-permute-start(bf16[144,256]{1,0:T(8,128)(2,1)} %get-tuple-element.73.t0), channel_id=1, source_target_pairs={{0,16},{4,20},{8,24},{12,28},{16,0},{20,4},{24,8},{28,12},{1,17},{... | collective-permute-start | bytes 221192 | tf_op jit(solution)/shard_map/ppermute | solution.py:29
  12.6 1.3 %collective-permute-start.3 = (bf16[144,256]{1,0:T(8,128)(2,1)}, bf16[144,256]{1,0:T(8,128)(2,1)S(1)}, u32[]{:S(2)}, u32[]{:S(2)}) collective-permute-start(bf16[144,256]{1,0:T(8,128)(2,1)} %get-tuple-element.73.t0), channel_id=1, source_target_pairs={{0,24},{4,28},{8,0},{12,4},{16,8},{20,12},{24,16},{28,20},{1,25},{... | collective-permute-start | bytes 221192 | tf_op jit(solution)/shard_map/ppermute | solution.py:29
  14.0 2.2 %copy-done = bf16[1408,1536]{1,0:T(8,128)(2,1)S(1)} copy-done((bf16[1408,1536]{1,0:T(8,128)(2,1)S(1)}, bf16[1408,1536]{1,0:T(8,128)(2,1)}, u32[]{:S(2)}) %copy-start) | copy-done | bytes 4325400
  16.2 2.2 %copy-done.1 = bf16[1536,1408]{1,0:T(8,128)(2,1)S(1)} copy-done((bf16[1536,1408]{1,0:T(8,128)(2,1)S(1)}, bf16[1536,1408]{1,0:T(8,128)(2,1)}, u32[]{:S(2)}) %copy-start.1) | copy-done | bytes 4325400
  18.5 0.9 %shard_map.104 = (bf16[1408,1536]{1,0:T(8,128)(2,1)S(1)}, bf16[1536,1408]{1,0:T(8,128)(2,1)S(1)}) custom-call(bf16[1408,1536]{1,0:T(8,128)(2,1)S(1)} %copy-done, bf16[1536,1408]{1,0:T(8,128)(2,1)S(1)} %copy-done.1), custom_call_target="tpu_custom_call" | custom-call | flops 1 | bytes 1 | tf_op jit(solution)/shard_map/pallas_call | solution.py:534
  19.4 0.1 copy-done.3
  19.5 0.1 shard_map.105
  19.6 0.6 collective-permute-start.7
  20.2 1.0 %collective-permute-start.8 = (bf16[576,256]{1,0:T(8,128)(2,1)S(1)}, bf16[576,256]{1,0:T(8,128)(2,1)S(1)}, u32[]{:S(2)}, u32[]{:S(2)}) collective-permute-start(bf16[576,256]{1,0:T(8,128)(2,1)S(1)} %get-tuple-element.91.mine), channel_id=1, source_target_pairs={{0,4},{4,0},{8,12},{12,8},{16,20},{20,16},{24,28},{28,24},{1,5},{5... | collective-permute-start | bytes 884744 | tf_op jit(solution)/shard_map/ppermute | solution.py:24
  21.2 0.2 collective-permute-start.4
  21.4 1.5 %collective-permute-start.9 = (bf16[176,640]{1,0:T(8,128)(2,1)S(1)}, bf16[176,640]{1,0:T(8,128)(2,1)S(1)}, u32[]{:S(2)}, u32[]{:S(2)}) collective-permute-start(bf16[176,640]{1,0:T(8,128)(2,1)S(1)} %get-tuple-element.109.h0), channel_id=1, source_target_pairs={{0,2},{1,3},{2,0},{3,1},{4,6},{5,7},{6,4},{7,5},{8,10},{9,11},{10,... | collective-permute-start | bytes 675848 | tf_op jit(solution)/shard_map/ppermute | solution.py:24
  22.9 2.2 %shard_map.106 = (bf16[400,384]{1,0:T(8,128)(2,1)S(1)}, f32[64,1408]{1,0:T(8,128)S(1)}, bf16[1408,384]{1,0:T(8,128)(2,1)S(1)}, bf16[384,1408]{1,0:T(8,128)(2,1)S(1)}, bf16[384,1408]{1,0:T(8,128)(2,1)S(1)}) custom-call(bf16[16,256]{1,0:T(8,128)(2,1)S(1)} %get-tuple-element.80.dests, bf16[704,384]{1,0:T(8,128)(2,1)S(1)} %copy-done.3, ...), custom_call_target="tpu_custom_call" | custom-call | flops 1 | bytes 1 | tf_op jit(solution)/shard_map/pallas_call | solution.py:534
  25.2 0.8 collective-permute-start.13
  26.0 1.8 %shard_map.107 = (bf16[384,384]{1,0:T(8,128)(2,1)S(1)}, f32[64,1408]{1,0:T(8,128)S(1)}) custom-call(bf16[384,1408]{1,0:T(8,128)(2,1)S(1)} %get-tuple-element.96.tok, bf16[384,1408]{1,0:T(8,128)(2,1)S(1)} %get-tuple-element.87.cot, bf16[1408,1536]{1,0:T(8,128)(2,1)S(1)} %get-tuple-element.83.w_up, bf16[1536,1408]{1,0:T(8,128)(2,1)S(1)} %get-tuple-element.75.w_down, ...), custom_call_target="tpu_custom_call" | custom-call | flops 1 | bytes 1 | tf_op jit(solution)/shard_map/pallas_call | solution.py:534
  27.8 2.3 %collective-permute-done.8.theirs = bf16[576,256]{1,0:T(8,128)(2,1)S(1)} collective-permute-done((bf16[576,256]{1,0:T(8,128)(2,1)S(1)}, bf16[576,256]{1,0:T(8,128)(2,1)S(1)}, u32[]{:S(2)}, u32[]{:S(2)}) %collective-permute-start.8) | collective-permute-done | bytes 294944 | tf_op jit(solution)/shard_map/ppermute | solution.py:24
  30.0 0.1 shard_map.108
  30.1 1.0 %collective-permute-start.12 = (bf16[512,256]{1,0:T(8,128)(2,1)S(1)}, bf16[512,256]{1,0:T(8,128)(2,1)S(1)}, u32[]{:S(2)}, u32[]{:S(2)}) collective-permute-start(bf16[512,256]{1,0:T(8,128)(2,1)S(1)} %get-tuple-element.93), channel_id=1, source_target_pairs={{0,2},{1,3},{2,0},{3,1},{4,6},{5,7},{6,4},{7,5},{8,10},{9,11},{10,... | collective-permute-start | bytes 786440 | tf_op jit(solution)/shard_map/ppermute | solution.py:24
  31.2 1.8 %shard_map.109 = (bf16[384,384]{1,0:T(8,128)(2,1)S(1)}, f32[64,1408]{1,0:T(8,128)S(1)}) custom-call(bf16[384,1408]{1,0:T(8,128)(2,1)S(1)} %get-tuple-element.96.tok, bf16[384,1408]{1,0:T(8,128)(2,1)S(1)} %get-tuple-element.87.cot, bf16[1408,1536]{1,0:T(8,128)(2,1)S(1)} %get-tuple-element.83.w_up, bf16[1536,1408]{1,0:T(8,128)(2,1)S(1)} %get-tuple-element.75.w_down, ...), custom_call_target="tpu_custom_call" | custom-call | flops 1 | bytes 1 | tf_op jit(solution)/shard_map/pallas_call | solution.py:534
  32.9 1.8 %shard_map.110 = (bf16[384,384]{1,0:T(8,128)(2,1)S(1)}, bf16[64,1408]{1,0:T(8,128)(2,1)S(1)}) custom-call(bf16[384,1408]{1,0:T(8,128)(2,1)S(1)} %get-tuple-element.96.tok, bf16[384,1408]{1,0:T(8,128)(2,1)S(1)} %get-tuple-element.87.cot, bf16[1408,1536]{1,0:T(8,128)(2,1)S(1)} %get-tuple-element.83.w_up, bf16[1536,1408]{1,0:T(8,128)(2,1)S(1)} %get-tuple-element.75.w_down, ...), custom_call_target="tpu_custom_call" | custom-call | flops 1 | bytes 1 | tf_op jit(solution)/shard_map/pallas_call | solution.py:534
  34.7 0.5 collective-permute-start.11
  35.3 1.5 %collective-permute-start.14 = (bf16[384,384]{1,0:T(8,128)(2,1)S(1)}, bf16[384,384]{1,0:T(8,128)(2,1)S(1)}, u32[]{:S(2)}, u32[]{:S(2)}) collective-permute-start(bf16[384,384]{1,0:T(8,128)(2,1)S(1)} %get-tuple-element.105.pre), channel_id=1, source_target_pairs={{0,4},{4,0},{8,12},{12,8},{16,20},{20,16},{24,28},{28,24},{1,5},{5... | collective-permute-start | bytes 884744 | tf_op jit(solution)/shard_map/ppermute | solution.py:24
  36.9 0.1 collective-permute-done.12.received.from_x
  37.0 1.9 %shard_map.113 = (bf16[704,768]{1,0:T(8,128)(2,1)S(1)}, f32[352,384]{1,0:T(8,128)S(1)}, bf16[352,384]{1,0:T(8,128)(2,1)S(1)}) custom-call(bf16[1408,384]{1,0:T(8,128)(2,1)S(1)} %get-tuple-element.100.tok_full, bf16[176,640]{1,0:T(8,128)(2,1)S(1)} %get-tuple-element.109.h0, bf16[176,640]{1,0:T(8,128)(2,1)S(1)} %collective-permute-done.4.h1, ...), custom_call_target="tpu_custom_call" | custom-call | flops 1 | bytes 1 | tf_op jit(solution)/shard_map/pallas_call | solution.py:534
  38.9 0.0 copy-start.2
  38.9 1.9 %collective-permute-start.15 = (bf16[352,384]{1,0:T(8,128)(2,1)S(1)}, bf16[352,384]{1,0:T(8,128)(2,1)S(1)}, u32[]{:S(2)}, u32[]{:S(2)}) collective-permute-start(bf16[352,384]{1,0:T(8,128)(2,1)S(1)} %get-tuple-element.103), channel_id=1, source_target_pairs={{0,8},{4,12},{8,0},{12,4},{16,24},{20,28},{24,16},{28,20},{1,9},{5... | collective-permute-start | bytes 811016 | tf_op jit(solution)/shard_map/ppermute | solution.py:24
  40.8 1.5 %collective-permute-start.16 = (bf16[64,1408]{1,0:T(8,128)(2,1)S(1)}, bf16[64,1408]{1,0:T(8,128)(2,1)S(1)}, u32[]{:S(2)}, u32[]{:S(2)}) collective-permute-start(bf16[64,1408]{1,0:T(8,128)(2,1)S(1)} %shard_map.111.a), channel_id=1, source_target_pairs={{0,2},{1,3},{2,0},{3,1},{4,6},{5,7},{6,4},{7,5},{8,10},{9,11},{10,... | collective-permute-start | bytes 540680 | tf_op jit(solution)/shard_map/ppermute | solution.py:24
  42.3 1.5 %collective-permute-start.17 = (bf16[384,384]{1,0:T(8,128)(2,1)S(1)}, bf16[384,384]{1,0:T(8,128)(2,1)S(1)}, u32[]{:S(2)}, u32[]{:S(2)}) collective-permute-start(bf16[384,384]{1,0:T(8,128)(2,1)S(1)} %get-tuple-element.113.pre), channel_id=1, source_target_pairs={{0,4},{4,0},{8,12},{12,8},{16,20},{20,16},{24,28},{28,24},{1,5},{5... | collective-permute-start | bytes 884744 | tf_op jit(solution)/shard_map/ppermute | solution.py:24
  43.8 1.4 %collective-permute-done.14.pre_pair = bf16[384,384]{1,0:T(8,128)(2,1)S(1)} collective-permute-done((bf16[384,384]{1,0:T(8,128)(2,1)S(1)}, bf16[384,384]{1,0:T(8,128)(2,1)S(1)}, u32[]{:S(2)}, u32[]{:S(2)}) %collective-permute-start.14) | collective-permute-done | bytes 294944 | tf_op jit(solution)/shard_map/ppermute | solution.py:24
  45.1 0.8 shard_map.114
  46.0 1.6 %collective-permute-start.18 = (bf16[352,384]{1,0:T(8,128)(2,1)S(1)}, bf16[352,384]{1,0:T(8,128)(2,1)S(1)}, u32[]{:S(2)}, u32[]{:S(2)}) collective-permute-start(bf16[352,384]{1,0:T(8,128)(2,1)S(1)} %get-tuple-element.108), channel_id=1, source_target_pairs={{0,8},{4,12},{8,0},{12,4},{16,24},{20,28},{24,16},{28,20},{1,9},{5... | collective-permute-start | bytes 811016 | tf_op jit(solution)/shard_map/ppermute | solution.py:24
  47.6 0.5 shard_map.115.e0
  48.1 0.1 shard_map.116
  48.2 1.6 %collective-permute-start.20 = (bf16[384,384]{1,0:T(8,128)(2,1)S(1)}, bf16[384,384]{1,0:T(8,128)(2,1)S(1)}, u32[]{:S(2)}, u32[]{:S(2)}) collective-permute-start(bf16[384,384]{1,0:T(8,128)(2,1)S(1)} %get-tuple-element.121.pre), channel_id=1, source_target_pairs={{0,4},{4,0},{8,12},{12,8},{16,20},{20,16},{24,28},{28,24},{1,5},{5... | collective-permute-start | bytes 884744 | tf_op jit(solution)/shard_map/ppermute | solution.py:24
  49.8 0.5 collective-permute-start.23
  50.3 1.6 %collective-permute-done.17.pre_pair = bf16[384,384]{1,0:T(8,128)(2,1)S(1)} collective-permute-done((bf16[384,384]{1,0:T(8,128)(2,1)S(1)}, bf16[384,384]{1,0:T(8,128)(2,1)S(1)}, u32[]{:S(2)}, u32[]{:S(2)}) %collective-permute-start.17) | collective-permute-done | bytes 294944 | tf_op jit(solution)/shard_map/ppermute | solution.py:24
  51.8 2.9 %collective-permute-start.28 = (bf16[176,384]{1,0:T(8,128)(2,1)S(1)}, bf16[176,384]{1,0:T(8,128)(2,1)S(1)}, u32[]{:S(2)}, u32[]{:S(2)}) collective-permute-start(bf16[176,384]{1,0:T(8,128)(2,1)S(1)} %get-tuple-element.111), channel_id=1, source_target_pairs={{0,16},{4,20},{8,24},{12,28},{16,0},{20,4},{24,8},{28,12},{1,17},{... | collective-permute-start | bytes 405512 | tf_op jit(solution)/shard_map/ppermute | solution.py:24
  54.7 0.8 shard_map.117
  55.5 1.0 %collective-permute-start.21 = (bf16[352,384]{1,0:T(8,128)(2,1)S(1)}, bf16[352,384]{1,0:T(8,128)(2,1)S(1)}, u32[]{:S(2)}, u32[]{:S(2)}) collective-permute-start(bf16[352,384]{1,0:T(8,128)(2,1)S(1)} %get-tuple-element.114), channel_id=1, source_target_pairs={{0,8},{4,12},{8,0},{12,4},{16,24},{20,28},{24,16},{28,20},{1,9},{5... | collective-permute-start | bytes 811016 | tf_op jit(solution)/shard_map/ppermute | solution.py:24
  56.5 0.1 shard_map.118
  56.6 0.6 collective-permute-start.29
  57.3 0.2 shard_map.119.share
  57.5 0.1 collective-permute-start.22
  57.6 0.5 collective-permute-start.24
  58.1 0.8 shard_map.120
  58.9 1.6 %collective-permute-done.28 = bf16[176,384]{1,0:T(8,128)(2,1)S(1)} collective-permute-done((bf16[176,384]{1,0:T(8,128)(2,1)S(1)}, bf16[176,384]{1,0:T(8,128)(2,1)S(1)}, u32[]{:S(2)}, u32[]{:S(2)}) %collective-permute-start.28) | collective-permute-done | bytes 135200 | tf_op jit(solution)/shard_map/ppermute | solution.py:24
  60.5 0.7 collective-permute-start.26
  61.2 7.0 %collective-permute-done.21.received = bf16[352,384]{1,0:T(8,128)(2,1)S(1)} collective-permute-done((bf16[352,384]{1,0:T(8,128)(2,1)S(1)}, bf16[352,384]{1,0:T(8,128)(2,1)S(1)}, u32[]{:S(2)}, u32[]{:S(2)}) %collective-permute-start.21) | collective-permute-done | bytes 270368 | tf_op jit(solution)/shard_map/ppermute | solution.py:24
  68.2 0.1 shard_map.121
  68.3 0.4 collective-permute-start.30
  68.7 0.8 shard_map.122.a
  69.4 0.0 collective-permute-start.25
  69.5 1.1 %collective-permute-done.25.b = f32[1,384]{1,0:T(1,128)S(1)} collective-permute-done((f32[1,384]{1,0:T(1,128)S(1)}, f32[1,384]{1,0:T(1,128)S(1)}, u32[]{:S(2)}, u32[]{:S(2)}) %collective-permute-start.25) | collective-permute-done | bytes 1568 | tf_op jit(solution)/shard_map/ppermute | solution.py:24
  70.6 4.4 %collective-permute-done.26.received = bf16[352,384]{1,0:T(8,128)(2,1)S(1)} collective-permute-done((bf16[352,384]{1,0:T(8,128)(2,1)S(1)}, bf16[352,384]{1,0:T(8,128)(2,1)S(1)}, u32[]{:S(2)}, u32[]{:S(2)}) %collective-permute-start.26) | collective-permute-done | bytes 270368 | tf_op jit(solution)/shard_map/ppermute | solution.py:24
  75.0 0.1 shard_map.124
  75.0 0.6 collective-permute-start.31
  75.6 1.0 %collective-permute-start.27 = (f32[1,384]{1,0:T(1,128)S(1)}, f32[1,384]{1,0:T(1,128)S(1)}, u32[]{:S(2)}, u32[]{:S(2)}) collective-permute-start(f32[1,384]{1,0:T(1,128)S(1)} %shard_map.123.a), channel_id=1, source_target_pairs={{0,2},{1,3},{2,0},{3,1},{4,6},{5,7},{6,4},{7,5},{8,10},{9,11},{10,... | collective-permute-start | bytes 4616 | tf_op jit(solution)/shard_map/ppermute | solution.py:24
  76.7 2.5 %collective-permute-done.27.b = f32[1,384]{1,0:T(1,128)S(1)} collective-permute-done((f32[1,384]{1,0:T(1,128)S(1)}, f32[1,384]{1,0:T(1,128)S(1)}, u32[]{:S(2)}, u32[]{:S(2)}) %collective-permute-start.27) | collective-permute-done | bytes 1568 | tf_op jit(solution)/shard_map/ppermute | solution.py:24
  79.2 0.7 shard_map.125
  79.9 2.2 %collective-permute-done.31 = bf16[176,384]{1,0:T(8,128)(2,1)S(1)} collective-permute-done((bf16[176,384]{1,0:T(8,128)(2,1)S(1)}, bf16[176,384]{1,0:T(8,128)(2,1)S(1)}, u32[]{:S(2)}, u32[]{:S(2)}) %collective-permute-start.31) | collective-permute-done | bytes 135200 | tf_op jit(solution)/shard_map/ppermute | solution.py:24
  82.2 1.1 %pad_maximum_fusion = f32[176,1536]{1,0:T(8,128)} fusion(f32[176,384]{1,0:T(8,128)S(1)} %convert_add_fusion, f32[176,384]{1,0:T(8,128)S(1)} %convert_add_fusion.1, f32[176,384]{1,0:T(8,128)S(1)} %convert_add_fusion.2, f32[176,384]{1,0:T(8,128)S(1)} %convert_add_fusion.3), kind=kLoop, calls=%fused_computation | loop fusion | flops 811008 | bytes 2162688 | tf_op jit(solution)/shard_map/concatenate | solution.py:781
  (42 shorter events, 0.3 us)
Async XLA Ops:
  4.0 15.6 %collective-permute-start.6 = (bf16[704,384]{1,0:T(8,128)(2,1)}, bf16[704,384]{1,0:T(8,128)(2,1)S(1)}, u32[]{:S(2)}, u32[]{:S(2)}) collective-permute-start(bf16[704,384]{1,0:T(8,128)(2,1)} %get-tuple-element.81.b0), channel_id=1, source_target_pairs={{0,2},{1,3},{2,0},{3,1},{4,6},{5,7},{6,4},{7,5},{8,10},{9,11},{10,... | collective-permute-start | bytes 1622024 | tf_op jit(solution)/shard_map/ppermute | solution.py:24
  7.0 12.4 %collective-permute-start = (bf16[176,384]{1,0:T(8,128)(2,1)}, bf16[176,384]{1,0:T(8,128)(2,1)S(1)}, u32[]{:S(2)}, u32[]{:S(2)}) collective-permute-start(bf16[176,384]{1,0:T(8,128)(2,1)} %get-tuple-element.72), channel_id=1, source_target_pairs={{0,4},{4,0},{8,12},{12,8},{16,20},{20,16},{24,28},{28,24},{1,5},{5... | collective-permute-start | bytes 405512 | tf_op jit(solution)/shard_map/ppermute | solution.py:24
  8.5 11.0 %collective-permute-start.1 = (bf16[144,256]{1,0:T(8,128)(2,1)}, bf16[144,256]{1,0:T(8,128)(2,1)S(1)}, u32[]{:S(2)}, u32[]{:S(2)}) collective-permute-start(bf16[144,256]{1,0:T(8,128)(2,1)} %get-tuple-element.73.t0), channel_id=1, source_target_pairs={{0,8},{4,12},{8,16},{12,20},{16,24},{20,28},{24,0},{28,4},{1,9},{5... | collective-permute-start | bytes 221192 | tf_op jit(solution)/shard_map/ppermute | solution.py:29
  10.1 9.4 %collective-permute-start.2 = (bf16[144,256]{1,0:T(8,128)(2,1)}, bf16[144,256]{1,0:T(8,128)(2,1)S(1)}, u32[]{:S(2)}, u32[]{:S(2)}) collective-permute-start(bf16[144,256]{1,0:T(8,128)(2,1)} %get-tuple-element.73.t0), channel_id=1, source_target_pairs={{0,16},{4,20},{8,24},{12,28},{16,0},{20,4},{24,8},{28,12},{1,17},{... | collective-permute-start | bytes 221192 | tf_op jit(solution)/shard_map/ppermute | solution.py:29
  12.6 6.9 %collective-permute-start.3 = (bf16[144,256]{1,0:T(8,128)(2,1)}, bf16[144,256]{1,0:T(8,128)(2,1)S(1)}, u32[]{:S(2)}, u32[]{:S(2)}) collective-permute-start(bf16[144,256]{1,0:T(8,128)(2,1)} %get-tuple-element.73.t0), channel_id=1, source_target_pairs={{0,24},{4,28},{8,0},{12,4},{16,8},{20,12},{24,16},{28,20},{1,25},{... | collective-permute-start | bytes 221192 | tf_op jit(solution)/shard_map/ppermute | solution.py:29
  14.0 2.2 %copy-start = (bf16[1408,1536]{1,0:T(8,128)(2,1)S(1)}, bf16[1408,1536]{1,0:T(8,128)(2,1)}, u32[]{:S(2)}) copy-start(bf16[1408,1536]{1,0:T(8,128)(2,1)} %up) | copy-start | bytes 12976132
  16.2 2.2 %copy-start.1 = (bf16[1536,1408]{1,0:T(8,128)(2,1)S(1)}, bf16[1536,1408]{1,0:T(8,128)(2,1)}, u32[]{:S(2)}) copy-start(bf16[1536,1408]{1,0:T(8,128)(2,1)} %down.1) | copy-start | bytes 12976132
  18.4 1.0 %copy-start.3 = (bf16[704,384]{1,0:T(8,128)(2,1)S(1)}, bf16[704,384]{1,0:T(8,128)(2,1)}, u32[]{:S(2)}) copy-start(bf16[704,384]{1,0:T(8,128)(2,1)} %get-tuple-element.81.b0) | copy-start | bytes 1622020
  18.4 1.1 %copy-start.4 = (bf16[352,128]{1,0:T(8,128)(2,1)S(1)}, bf16[352,128]{1,0:T(8,128)(2,1)}, u32[]{:S(2)}) copy-start(bf16[352,128]{1,0:T(8,128)(2,1)} %get-tuple-element.77.pool) | copy-start | bytes 270340
  18.4 1.1 %copy-start.5 = (bf16[144,256]{1,0:T(8,128)(2,1)S(1)}, bf16[144,256]{1,0:T(8,128)(2,1)}, u32[]{:S(2)}) copy-start(bf16[144,256]{1,0:T(8,128)(2,1)} %get-tuple-element.73.t0) | copy-start | bytes 221188
  19.5 3.4 %collective-permute-start.5 = (bf16[704,384]{1,0:T(8,128)(2,1)S(1)}, bf16[704,384]{1,0:T(8,128)(2,1)S(1)}, u32[]{:S(2)}, u32[]{:S(2)}) collective-permute-start(bf16[704,384]{1,0:T(8,128)(2,1)S(1)} %copy-done.3), channel_id=1, source_target_pairs={{0,1},{1,0},{2,3},{3,2},{4,5},{5,4},{6,7},{7,6},{8,9},{9,8},{10,11... | collective-permute-start | bytes 1622024 | tf_op jit(solution)/shard_map/ppermute | solution.py:24
  19.6 3.3 %collective-permute-start.7 = (bf16[704,384]{1,0:T(8,128)(2,1)S(1)}, bf16[704,384]{1,0:T(8,128)(2,1)S(1)}, u32[]{:S(2)}, u32[]{:S(2)}) collective-permute-start(bf16[704,384]{1,0:T(8,128)(2,1)S(1)} %collective-permute-done.6.b2), channel_id=1, source_target_pairs={{0,1},{1,0},{2,3},{3,2},{4,5},{5,4},{6,7},{7,6},{8,9},{9,8},{10,11... | collective-permute-start | bytes 1622024 | tf_op jit(solution)/shard_map/ppermute | solution.py:24
  20.2 9.9 %collective-permute-start.8 = (bf16[576,256]{1,0:T(8,128)(2,1)S(1)}, bf16[576,256]{1,0:T(8,128)(2,1)S(1)}, u32[]{:S(2)}, u32[]{:S(2)}) collective-permute-start(bf16[576,256]{1,0:T(8,128)(2,1)S(1)} %get-tuple-element.91.mine), channel_id=1, source_target_pairs={{0,4},{4,0},{8,12},{12,8},{16,20},{20,16},{24,28},{28,24},{1,5},{5... | collective-permute-start | bytes 884744 | tf_op jit(solution)/shard_map/ppermute | solution.py:24
  21.2 1.7 %collective-permute-start.4 = (bf16[176,640]{1,0:T(8,128)(2,1)S(1)}, bf16[176,640]{1,0:T(8,128)(2,1)S(1)}, u32[]{:S(2)}, u32[]{:S(2)}) collective-permute-start(bf16[176,640]{1,0:T(8,128)(2,1)S(1)} %get-tuple-element.109.h0), channel_id=1, source_target_pairs={{0,1},{1,0},{2,3},{3,2},{4,5},{5,4},{6,7},{7,6},{8,9},{9,8},{10,11... | collective-permute-start | bytes 675848 | tf_op jit(solution)/shard_map/ppermute | solution.py:24
  21.4 9.7 %collective-permute-start.9 = (bf16[176,640]{1,0:T(8,128)(2,1)S(1)}, bf16[176,640]{1,0:T(8,128)(2,1)S(1)}, u32[]{:S(2)}, u32[]{:S(2)}) collective-permute-start(bf16[176,640]{1,0:T(8,128)(2,1)S(1)} %get-tuple-element.109.h0), channel_id=1, source_target_pairs={{0,2},{1,3},{2,0},{3,1},{4,6},{5,7},{6,4},{7,5},{8,10},{9,11},{10,... | collective-permute-start | bytes 675848 | tf_op jit(solution)/shard_map/ppermute | solution.py:24
  25.2 11.8 %collective-permute-start.13 = (bf16[400,384]{1,0:T(8,128)(2,1)S(1)}, bf16[400,384]{1,0:T(8,128)(2,1)S(1)}, u32[]{:S(2)}, u32[]{:S(2)}) collective-permute-start(bf16[400,384]{1,0:T(8,128)(2,1)S(1)} %get-tuple-element.101.pre), channel_id=1, source_target_pairs={{0,4},{4,0},{8,12},{12,8},{16,20},{20,16},{24,28},{28,24},{1,5},{5... | collective-permute-start | bytes 921608 | tf_op jit(solution)/shard_map/ppermute | solution.py:24
  30.1 6.9 %collective-permute-start.12 = (bf16[512,256]{1,0:T(8,128)(2,1)S(1)}, bf16[512,256]{1,0:T(8,128)(2,1)S(1)}, u32[]{:S(2)}, u32[]{:S(2)}) collective-permute-start(bf16[512,256]{1,0:T(8,128)(2,1)S(1)} %get-tuple-element.93), channel_id=1, source_target_pairs={{0,2},{1,3},{2,0},{3,1},{4,6},{5,7},{6,4},{7,5},{8,10},{9,11},{10,... | collective-permute-start | bytes 786440 | tf_op jit(solution)/shard_map/ppermute | solution.py:24
  31.2 5.7 %collective-permute-start.10 = (bf16[176,640]{1,0:T(8,128)(2,1)S(1)}, bf16[176,640]{1,0:T(8,128)(2,1)S(1)}, u32[]{:S(2)}, u32[]{:S(2)}) collective-permute-start(bf16[176,640]{1,0:T(8,128)(2,1)S(1)} %collective-permute-done.9.h2), channel_id=1, source_target_pairs={{0,1},{1,0},{2,3},{3,2},{4,5},{5,4},{6,7},{7,6},{8,9},{9,8},{10,11... | collective-permute-start | bytes 675848 | tf_op jit(solution)/shard_map/ppermute | solution.py:24
  34.7 2.1 %collective-permute-start.11 = (bf16[64,1408]{1,0:T(8,128)(2,1)S(1)}, bf16[64,1408]{1,0:T(8,128)(2,1)S(1)}, u32[]{:S(2)}, u32[]{:S(2)}) collective-permute-start(bf16[64,1408]{1,0:T(8,128)(2,1)S(1)} %get-tuple-element.98.a), channel_id=1, source_target_pairs={{0,1},{1,0},{2,3},{3,2},{4,5},{5,4},{6,7},{7,6},{8,9},{9,8},{10,11... | collective-permute-start | bytes 540680 | tf_op jit(solution)/shard_map/ppermute | solution.py:24
  35.3 9.9 %collective-permute-start.14 = (bf16[384,384]{1,0:T(8,128)(2,1)S(1)}, bf16[384,384]{1,0:T(8,128)(2,1)S(1)}, u32[]{:S(2)}, u32[]{:S(2)}) collective-permute-start(bf16[384,384]{1,0:T(8,128)(2,1)S(1)} %get-tuple-element.105.pre), channel_id=1, source_target_pairs={{0,4},{4,0},{8,12},{12,8},{16,20},{20,16},{24,28},{28,24},{1,5},{5... | collective-permute-start | bytes 884744 | tf_op jit(solution)/shard_map/ppermute | solution.py:24
  38.9 8.7 %copy-start.2 = (bf16[1408,256]{1,0:T(8,128)(2,1)S(1)}, bf16[1408,256]{1,0:T(8,128)(2,1)}, u32[]{:S(2)}) copy-start(bf16[1408,256]{1,0:T(8,128)(2,1)} %ref_proj.1) | copy-start | bytes 2162692
  38.9 8.7 %collective-permute-start.15 = (bf16[352,384]{1,0:T(8,128)(2,1)S(1)}, bf16[352,384]{1,0:T(8,128)(2,1)S(1)}, u32[]{:S(2)}, u32[]{:S(2)}) collective-permute-start(bf16[352,384]{1,0:T(8,128)(2,1)S(1)} %get-tuple-element.103), channel_id=1, source_target_pairs={{0,8},{4,12},{8,0},{12,4},{16,24},{20,28},{24,16},{28,20},{1,9},{5... | collective-permute-start | bytes 811016 | tf_op jit(solution)/shard_map/ppermute | solution.py:24
  40.8 6.8 %collective-permute-start.16 = (bf16[64,1408]{1,0:T(8,128)(2,1)S(1)}, bf16[64,1408]{1,0:T(8,128)(2,1)S(1)}, u32[]{:S(2)}, u32[]{:S(2)}) collective-permute-start(bf16[64,1408]{1,0:T(8,128)(2,1)S(1)} %shard_map.111.a), channel_id=1, source_target_pairs={{0,2},{1,3},{2,0},{3,1},{4,6},{5,7},{6,4},{7,5},{8,10},{9,11},{10,... | collective-permute-start | bytes 540680 | tf_op jit(solution)/shard_map/ppermute | solution.py:24
  42.3 9.6 %collective-permute-start.17 = (bf16[384,384]{1,0:T(8,128)(2,1)S(1)}, bf16[384,384]{1,0:T(8,128)(2,1)S(1)}, u32[]{:S(2)}, u32[]{:S(2)}) collective-permute-start(bf16[384,384]{1,0:T(8,128)(2,1)S(1)} %get-tuple-element.113.pre), channel_id=1, source_target_pairs={{0,4},{4,0},{8,12},{12,8},{16,20},{20,16},{24,28},{28,24},{1,5},{5... | collective-permute-start | bytes 884744 | tf_op jit(solution)/shard_map/ppermute | solution.py:24
  46.0 9.6 %collective-permute-start.18 = (bf16[352,384]{1,0:T(8,128)(2,1)S(1)}, bf16[352,384]{1,0:T(8,128)(2,1)S(1)}, u32[]{:S(2)}, u32[]{:S(2)}) collective-permute-start(bf16[352,384]{1,0:T(8,128)(2,1)S(1)} %get-tuple-element.108), channel_id=1, source_target_pairs={{0,8},{4,12},{8,0},{12,4},{16,24},{20,28},{24,16},{28,20},{1,9},{5... | collective-permute-start | bytes 811016 | tf_op jit(solution)/shard_map/ppermute | solution.py:24
  48.2 9.4 %collective-permute-start.20 = (bf16[384,384]{1,0:T(8,128)(2,1)S(1)}, bf16[384,384]{1,0:T(8,128)(2,1)S(1)}, u32[]{:S(2)}, u32[]{:S(2)}) collective-permute-start(bf16[384,384]{1,0:T(8,128)(2,1)S(1)} %get-tuple-element.121.pre), channel_id=1, source_target_pairs={{0,4},{4,0},{8,12},{12,8},{16,20},{20,16},{24,28},{28,24},{1,5},{5... | collective-permute-start | bytes 884744 | tf_op jit(solution)/shard_map/ppermute | solution.py:24
  49.8 6.8 %collective-permute-start.19 = (bf16[512,256]{1,0:T(8,128)(2,1)S(1)}, bf16[512,256]{1,0:T(8,128)(2,1)S(1)}, u32[]{:S(2)}, u32[]{:S(2)}) collective-permute-start(bf16[512,256]{1,0:T(8,128)(2,1)S(1)} %shard_map.112), channel_id=1, source_target_pairs={{0,1},{1,0},{2,3},{3,2},{4,5},{5,4},{6,7},{7,6},{8,9},{9,8},{10,11... | collective-permute-start | bytes 786440 | tf_op jit(solution)/shard_map/ppermute | solution.py:24
  49.8 7.7 %collective-permute-start.23 = (f32[192,256]{1,0:T(8,128)S(1)}, f32[192,256]{1,0:T(8,128)S(1)}, u32[]{:S(2)}, u32[]{:S(2)}) collective-permute-start(f32[192,256]{1,0:T(8,128)S(1)} %shard_map.115.e0), channel_id=1, source_target_pairs={{0,2},{1,3},{2,0},{3,1},{4,6},{5,7},{6,4},{7,5},{8,10},{9,11},{10,... | collective-permute-start | bytes 589832 | tf_op jit(solution)/shard_map/ppermute | solution.py:24
  51.8 8.7 %collective-permute-start.28 = (bf16[176,384]{1,0:T(8,128)(2,1)S(1)}, bf16[176,384]{1,0:T(8,128)(2,1)S(1)}, u32[]{:S(2)}, u32[]{:S(2)}) collective-permute-start(bf16[176,384]{1,0:T(8,128)(2,1)S(1)} %get-tuple-element.111), channel_id=1, source_target_pairs={{0,16},{4,20},{8,24},{12,28},{16,0},{20,4},{24,8},{28,12},{1,17},{... | collective-permute-start | bytes 405512 | tf_op jit(solution)/shard_map/ppermute | solution.py:24
  55.5 12.6 %collective-permute-start.21 = (bf16[352,384]{1,0:T(8,128)(2,1)S(1)}, bf16[352,384]{1,0:T(8,128)(2,1)S(1)}, u32[]{:S(2)}, u32[]{:S(2)}) collective-permute-start(bf16[352,384]{1,0:T(8,128)(2,1)S(1)} %get-tuple-element.114), channel_id=1, source_target_pairs={{0,8},{4,12},{8,0},{12,4},{16,24},{20,28},{24,16},{28,20},{1,9},{5... | collective-permute-start | bytes 811016 | tf_op jit(solution)/shard_map/ppermute | solution.py:24
  56.6 12.8 %collective-permute-start.29 = (bf16[176,384]{1,0:T(8,128)(2,1)S(1)}, bf16[176,384]{1,0:T(8,128)(2,1)S(1)}, u32[]{:S(2)}, u32[]{:S(2)}) collective-permute-start(bf16[176,384]{1,0:T(8,128)(2,1)S(1)} %get-tuple-element.116), channel_id=1, source_target_pairs={{0,16},{4,20},{8,24},{12,28},{16,0},{20,4},{24,8},{28,12},{1,17},{... | collective-permute-start | bytes 405512 | tf_op jit(solution)/shard_map/ppermute | solution.py:24
  57.5 11.1 %collective-permute-start.22 = (f32[192,256]{1,0:T(8,128)S(1)}, f32[192,256]{1,0:T(8,128)S(1)}, u32[]{:S(2)}, u32[]{:S(2)}) collective-permute-start(f32[192,256]{1,0:T(8,128)S(1)} %shard_map.115.e0), channel_id=1, source_target_pairs={{0,1},{1,0},{2,3},{3,2},{4,5},{5,4},{6,7},{7,6},{8,9},{9,8},{10,11... | collective-permute-start | bytes 589832 | tf_op jit(solution)/shard_map/ppermute | solution.py:24
  57.6 11.0 %collective-permute-start.24 = (f32[192,256]{1,0:T(8,128)S(1)}, f32[192,256]{1,0:T(8,128)S(1)}, u32[]{:S(2)}, u32[]{:S(2)}) collective-permute-start(f32[192,256]{1,0:T(8,128)S(1)} %collective-permute-done.23.e2), channel_id=1, source_target_pairs={{0,1},{1,0},{2,3},{3,2},{4,5},{5,4},{6,7},{7,6},{8,9},{9,8},{10,11... | collective-permute-start | bytes 589832 | tf_op jit(solution)/shard_map/ppermute | solution.py:24
  58.9 9.7 %copy-start.6 = (s32[64]{0:T(128)S(1)}, s32[64]{0:T(128)}, u32[]{:S(2)}) copy-start(s32[64]{0:T(128)} %param.13) | copy-start | bytes 772
  60.5 14.5 %collective-permute-start.26 = (bf16[352,384]{1,0:T(8,128)(2,1)S(1)}, bf16[352,384]{1,0:T(8,128)(2,1)S(1)}, u32[]{:S(2)}, u32[]{:S(2)}) collective-permute-start(bf16[352,384]{1,0:T(8,128)(2,1)S(1)} %get-tuple-element.124), channel_id=1, source_target_pairs={{0,8},{4,12},{8,0},{12,4},{16,24},{20,28},{24,16},{28,20},{1,9},{5... | collective-permute-start | bytes 811016 | tf_op jit(solution)/shard_map/ppermute | solution.py:24
  68.3 8.4 %collective-permute-start.30 = (bf16[176,384]{1,0:T(8,128)(2,1)S(1)}, bf16[176,384]{1,0:T(8,128)(2,1)S(1)}, u32[]{:S(2)}, u32[]{:S(2)}) collective-permute-start(bf16[176,384]{1,0:T(8,128)(2,1)S(1)} %get-tuple-element.126), channel_id=1, source_target_pairs={{0,16},{4,20},{8,24},{12,28},{16,0},{20,4},{24,8},{28,12},{1,17},{... | collective-permute-start | bytes 405512 | tf_op jit(solution)/shard_map/ppermute | solution.py:24
  69.4 1.2 %collective-permute-start.25 = (f32[1,384]{1,0:T(1,128)S(1)}, f32[1,384]{1,0:T(1,128)S(1)}, u32[]{:S(2)}, u32[]{:S(2)}) collective-permute-start(f32[1,384]{1,0:T(1,128)S(1)} %shard_map.122.a), channel_id=1, source_target_pairs={{0,1},{1,0},{2,3},{3,2},{4,5},{5,4},{6,7},{7,6},{8,9},{9,8},{10,11... | collective-permute-start | bytes 4616 | tf_op jit(solution)/shard_map/ppermute | solution.py:24
  75.0 7.1 %collective-permute-start.31 = (bf16[176,384]{1,0:T(8,128)(2,1)S(1)}, bf16[176,384]{1,0:T(8,128)(2,1)S(1)}, u32[]{:S(2)}, u32[]{:S(2)}) collective-permute-start(bf16[176,384]{1,0:T(8,128)(2,1)S(1)} %get-tuple-element.131), channel_id=1, source_target_pairs={{0,16},{4,20},{8,24},{12,28},{16,0},{20,4},{24,8},{28,12},{1,17},{... | collective-permute-start | bytes 405512 | tf_op jit(solution)/shard_map/ppermute | solution.py:24
  75.6 3.6 %collective-permute-start.27 = (f32[1,384]{1,0:T(1,128)S(1)}, f32[1,384]{1,0:T(1,128)S(1)}, u32[]{:S(2)}, u32[]{:S(2)}) collective-permute-start(f32[1,384]{1,0:T(1,128)S(1)} %shard_map.123.a), channel_id=1, source_target_pairs={{0,2},{1,3},{2,0},{3,1},{4,6},{5,7},{6,4},{7,5},{8,10},{9,11},{10,... | collective-permute-start | bytes 4616 | tf_op jit(solution)/shard_map/ppermute | solution.py:24

commit v6 on v5

--- a/solution.py
+++ b/solution.py
@@ -569,7 +569,7 @@
             w_down,
             in_specs=[pl.BlockSpec(memory_space=pltpu.HBM)] * 2,
             scratch_shapes=[pltpu.SemaphoreType.DMA((2,))],
-            vmem=32 * 2**20,
+            vmem=40 * 2**20,
         )
 
 
@@ -729,6 +729,7 @@
     pre2, mixed2 = forward((text_send,), 2, tok, cot, held_up, held_down, mixed1)
     pair_pre2 = swap(pre2, "sel", 1)
     pre3, mixed = forward((mixed2,), 3, tok, cot, held_up, held_down, mixed2)
+    pair_pre3 = swap(pre3, "sel", 1)
     mixed_core = swap(mixed, "mdl", 1)
     mixsum = run((mixed, extras_diag), mix_body, struct((k_dev, d_full), bf16), mixed, mixed_core)
     mixsum_x = swap(mixsum, "mdl", 2)
@@ -745,31 +746,30 @@
         pair_pre0,
     )
     first0 = swap(send0, "sel", 2)
-    keep1, send1 = grad((send0, text_x), pair, pre1, pair_pre1)
-    first1 = swap(send1, "sel", 2)
-    emb = heads((send1, first0), extras, extras_core, extras_x, extras_diag, mixsum, mixsum_x)
+    emb = heads((send0,), extras, extras_core, extras_x, extras_diag, mixsum, mixsum_x)
     emb_x = swap(emb, "mdl", 2)
     emb_core = swap(emb, "mdl", 1)
     emb_diag = swap(emb_x, "mdl", 1)
-    own0, rest0 = add((emb,), keep0, first0)
-    pair_pre3 = swap(after(pre3, own0), "sel", 1)
+    keep1, send1 = grad((emb, text_x), pair, pre1, pair_pre1)
+    first1 = swap(send1, "sel", 2)
+    own0, rest0 = add((send1,), keep0, first0)
     second0 = swap(rest0, "sel", 4)
     keep2, send2 = grad((rest0,), pair, pre2, pair_pre2)
     first2 = swap(send2, "sel", 2)
     own1, rest1 = add((send2,), keep1, first1)
     second1 = swap(rest1, "sel", 4)
     share = share_text((rest1,), all_texts, text_x, text_core)
-    keep3, send3 = grad((share,), pair, pre3, pair_pre3)
+    keep3, send3 = grad((share, emb_diag), pair, pre3, pair_pre3)
     first3 = swap(send3, "sel", 2)
     own2, rest2 = add((send3,), keep2, first2)
     second2 = swap(rest2, "sel", 4)
     sums = scores((rest2,), emb, emb_core, emb_x, emb_diag, share)
     sums_core = swap(sums, "mdl", 1)
     total = run((sums,), mix_body, struct((1, 2 * n_emb), f32), sums, sums_core)
-    own3, rest3 = add((total,), keep3, first3)
-    total_x = swap(after(total, own3), "mdl", 2)
+    total_x = swap(after(total, pair_texts), "mdl", 2)
+    ref_loss, learnability = losses((total,), total, total_x)
+    own3, rest3 = add((learnability,), keep3, first3)
     second3 = swap(rest3, "sel", 4)
-    ref_loss, learnability = losses((rest3,), total, total_x)
 
     own3, ref_loss, learnability = lax.optimization_barrier((own3, ref_loss, learnability))
     sums = [

time: 83.5 us -> 82.7 us (level)
  local copies, waits for them, and re-layouts: 4.57 us -> 2.25 us
  waiting for transfers between devices: 24.1 us -> 21.8 us
  starting transfers between devices: 33.6 us -> 35.8 us
  Pallas kernels: 18.8 us -> 20.5 us
    ppermute x29, waiting for transfers between devices: 24.1 us -> 21.8 us  [swap(): return lax.ppermute(value, axis, [(i, i ^ bit) for i in range(size)])]
    unnamed x14 -> x12, local copies, waits for them, and re-layouts: 4.57 us -> 2.25 us
    ppermute x29, starting transfers between devices: 28.1 us -> 30.3 us  [swap(): return lax.ppermute(value, axis, [(i, i ^ bit) for i in range(size)])]
    pallas_call x23, Pallas kernels: 18.8 us -> 20.5 us  [run(): call(body, out_shape, (2 ** 20, 2 ** 20), **kwargs)(first, *operands[1:])]
  transfers between devices with their start and end apart: 32 -> 32, of which waited for: 10 -> 10; matrix products, arithmetic and copies ran while one was open for 0% -> 0% of each run, Pallas kernels for 19% -> 21%
where the time goes in v6:
time: 82.7 us; the launch traced here: 82.5 us
  starting transfers between devices  35.8 us (43%)
  waiting for transfers between devices  21.8 us (26%)
  Pallas kernels  20.5 us (25%)
  local copies, waits for them, and re-layouts  2.25 us (3%)
  other arithmetic  1.23 us (1%)
  between operations  0.9 us (1%)
    ppermute x29, starting transfers between devices, swap(): return lax.ppermute(value, axis, [(i, i ^ bit) for i in range(size)])  30.3 us
    ppermute x29, waiting for transfers between devices, swap(): return lax.ppermute(value, axis, [(i, i ^ bit) for i in range(size)])  21.8 us
    pallas_call x23, Pallas kernels, run(): call(body, out_shape, (2 ** 20, 2 ** 20), **kwargs)(first, *operands[1:])  20.5 us
    ppermute x3, starting transfers between devices, rotate_pairs(): lax.ppermute(value, 'sel', [(i, (i + 2 * step) % size) for i in range(siz...  5.51 us
    unnamed x12, local copies, waits for them, and re-layouts  2.25 us
  transfers between devices with their start and end apart: 32, of which 10 were waited for; matrix products, arithmetic and copies ran while one was open for 0% of the time, Pallas kernels for 21%

profile of v6, /device:TPU:0, one launch (start us, length us, event | category | flops | bytes accessed | tf_op | source)
XLA Modules:
  0.0 82.5 jit_solution(4967202552806041834)
XLA Ops:
  0.6 3.3 %shard_map.103 = (bf16[704,384]{1,0:T(8,128)(2,1)}, bf16[176,384]{1,0:T(8,128)(2,1)}, bf16[352,128]{1,0:T(8,128)(2,1)}, bf16[144,256]{1,0:T(8,128)(2,1)}) custom-call(bf16[352,768]{1,0:T(8,128)(2,1)} %bitcast.9, bf16[352,384]{1,0:T(8,128)(2,1)} %bitcast.10, s32[1,64]{1,0:T(1,128)} %bitcast.6, s32[1,64]{1,0:T(1,128)} %bitcast.11, bf16[128,256]{1,0:T(8,128)(2,1)} %text_hbm.1), custom_call_target="tpu_custom_call" | custom-call | flops 1 | bytes 1 | tf_op jit(solution)/shard_map/pallas_call | solution.py:534
  4.0 3.0 %collective-permute-start.6 = (bf16[704,384]{1,0:T(8,128)(2,1)}, bf16[704,384]{1,0:T(8,128)(2,1)S(1)}, u32[]{:S(2)}, u32[]{:S(2)}) collective-permute-start(bf16[704,384]{1,0:T(8,128)(2,1)} %get-tuple-element.80.b0), channel_id=1, source_target_pairs={{0,2},{1,3},{2,0},{3,1},{4,6},{5,7},{6,4},{7,5},{8,10},{9,11},{10,... | collective-permute-start | bytes 1622024 | tf_op jit(solution)/shard_map/ppermute | solution.py:24
  7.0 1.5 %collective-permute-start = (bf16[176,384]{1,0:T(8,128)(2,1)}, bf16[176,384]{1,0:T(8,128)(2,1)S(1)}, u32[]{:S(2)}, u32[]{:S(2)}) collective-permute-start(bf16[176,384]{1,0:T(8,128)(2,1)} %get-tuple-element.71), channel_id=1, source_target_pairs={{0,4},{4,0},{8,12},{12,8},{16,20},{20,16},{24,28},{28,24},{1,5},{5... | collective-permute-start | bytes 405512 | tf_op jit(solution)/shard_map/ppermute | solution.py:24
  8.5 1.6 %collective-permute-start.1 = (bf16[144,256]{1,0:T(8,128)(2,1)}, bf16[144,256]{1,0:T(8,128)(2,1)S(1)}, u32[]{:S(2)}, u32[]{:S(2)}) collective-permute-start(bf16[144,256]{1,0:T(8,128)(2,1)} %get-tuple-element.72.t0), channel_id=1, source_target_pairs={{0,8},{4,12},{8,16},{12,20},{16,24},{20,28},{24,0},{28,4},{1,9},{5... | collective-permute-start | bytes 221192 | tf_op jit(solution)/shard_map/ppermute | solution.py:29
  10.1 2.6 %collective-permute-start.2 = (bf16[144,256]{1,0:T(8,128)(2,1)}, bf16[144,256]{1,0:T(8,128)(2,1)S(1)}, u32[]{:S(2)}, u32[]{:S(2)}) collective-permute-start(bf16[144,256]{1,0:T(8,128)(2,1)} %get-tuple-element.72.t0), channel_id=1, source_target_pairs={{0,16},{4,20},{8,24},{12,28},{16,0},{20,4},{24,8},{28,12},{1,17},{... | collective-permute-start | bytes 221192 | tf_op jit(solution)/shard_map/ppermute | solution.py:29
  12.7 1.3 %collective-permute-start.3 = (bf16[144,256]{1,0:T(8,128)(2,1)}, bf16[144,256]{1,0:T(8,128)(2,1)S(1)}, u32[]{:S(2)}, u32[]{:S(2)}) collective-permute-start(bf16[144,256]{1,0:T(8,128)(2,1)} %get-tuple-element.72.t0), channel_id=1, source_target_pairs={{0,24},{4,28},{8,0},{12,4},{16,8},{20,12},{24,16},{28,20},{1,25},{... | collective-permute-start | bytes 221192 | tf_op jit(solution)/shard_map/ppermute | solution.py:29
  14.0 2.2 %copy-done = bf16[1408,1536]{1,0:T(8,128)(2,1)S(1)} copy-done((bf16[1408,1536]{1,0:T(8,128)(2,1)S(1)}, bf16[1408,1536]{1,0:T(8,128)(2,1)}, u32[]{:S(2)}) %copy-start) | copy-done | bytes 4325400
  16.2 2.7 %shard_map.104 = (bf16[1408,1536]{1,0:T(8,128)(2,1)S(1)}, bf16[1536,1408]{1,0:T(8,128)(2,1)S(1)}) custom-call(bf16[1408,1536]{1,0:T(8,128)(2,1)S(1)} %copy-done, bf16[1536,1408]{1,0:T(8,128)(2,1)} %down.1), custom_call_target="tpu_custom_call" | custom-call | flops 1 | bytes 1 | tf_op jit(solution)/shard_map/pallas_call | solution.py:534
  18.9 0.0 collective-permute-done.half
  19.0 0.1 collective-permute-start.5
  19.1 0.1 shard_map.105
  19.2 0.3 collective-permute-done.6.b2
  19.5 0.2 collective-permute-start.7
  19.7 1.5 %collective-permute-start.8 = (bf16[576,256]{1,0:T(8,128)(2,1)S(1)}, bf16[576,256]{1,0:T(8,128)(2,1)S(1)}, u32[]{:S(2)}, u32[]{:S(2)}) collective-permute-start(bf16[576,256]{1,0:T(8,128)(2,1)S(1)} %get-tuple-element.90.mine), channel_id=1, source_target_pairs={{0,4},{4,0},{8,12},{12,8},{16,20},{20,16},{24,28},{28,24},{1,5},{5... | collective-permute-start | bytes 884744 | tf_op jit(solution)/shard_map/ppermute | solution.py:24
  21.2 0.2 collective-permute-start.4
  21.5 1.5 %collective-permute-start.9 = (bf16[176,640]{1,0:T(8,128)(2,1)S(1)}, bf16[176,640]{1,0:T(8,128)(2,1)S(1)}, u32[]{:S(2)}, u32[]{:S(2)}) collective-permute-start(bf16[176,640]{1,0:T(8,128)(2,1)S(1)} %get-tuple-element.103.h0), channel_id=1, source_target_pairs={{0,2},{1,3},{2,0},{3,1},{4,6},{5,7},{6,4},{7,5},{8,10},{9,11},{10,... | collective-permute-start | bytes 675848 | tf_op jit(solution)/shard_map/ppermute | solution.py:24
  23.0 2.2 %shard_map.106 = (bf16[400,384]{1,0:T(8,128)(2,1)S(1)}, f32[64,1408]{1,0:T(8,128)S(1)}, bf16[1408,384]{1,0:T(8,128)(2,1)S(1)}, bf16[384,1408]{1,0:T(8,128)(2,1)S(1)}, bf16[384,1408]{1,0:T(8,128)(2,1)S(1)}) custom-call(bf16[16,256]{1,0:T(8,128)(2,1)S(1)} %get-tuple-element.79.dests, bf16[704,384]{1,0:T(8,128)(2,1)S(1)} %copy-done.2, ...), custom_call_target="tpu_custom_call" | custom-call | flops 1 | bytes 1 | tf_op jit(solution)/shard_map/pallas_call | solution.py:534
  25.2 0.6 collective-permute-start.13
  25.8 1.8 %shard_map.107 = (bf16[384,384]{1,0:T(8,128)(2,1)S(1)}, f32[64,1408]{1,0:T(8,128)S(1)}) custom-call(bf16[384,1408]{1,0:T(8,128)(2,1)S(1)} %get-tuple-element.95.tok, bf16[384,1408]{1,0:T(8,128)(2,1)S(1)} %get-tuple-element.86.cot, bf16[1408,1536]{1,0:T(8,128)(2,1)S(1)} %get-tuple-element.82.w_up, bf16[1536,1408]{1,0:T(8,128)(2,1)S(1)} %get-tuple-element.74.w_down, ...), custom_call_target="tpu_custom_call" | custom-call | flops 1 | bytes 1 | tf_op jit(solution)/shard_map/pallas_call | solution.py:534
  27.6 2.0 %collective-permute-done.8.theirs = bf16[576,256]{1,0:T(8,128)(2,1)S(1)} collective-permute-done((bf16[576,256]{1,0:T(8,128)(2,1)S(1)}, bf16[576,256]{1,0:T(8,128)(2,1)S(1)}, u32[]{:S(2)}, u32[]{:S(2)}) %collective-permute-start.8) | collective-permute-done | bytes 294944 | tf_op jit(solution)/shard_map/ppermute | solution.py:24
  29.5 0.1 shard_map.108
  29.6 1.6 %collective-permute-start.12 = (bf16[512,256]{1,0:T(8,128)(2,1)S(1)}, bf16[512,256]{1,0:T(8,128)(2,1)S(1)}, u32[]{:S(2)}, u32[]{:S(2)}) collective-permute-start(bf16[512,256]{1,0:T(8,128)(2,1)S(1)} %get-tuple-element.92), channel_id=1, source_target_pairs={{0,2},{1,3},{2,0},{3,1},{4,6},{5,7},{6,4},{7,5},{8,10},{9,11},{10,... | collective-permute-start | bytes 786440 | tf_op jit(solution)/shard_map/ppermute | solution.py:24
  31.2 1.8 %shard_map.109 = (bf16[384,384]{1,0:T(8,128)(2,1)S(1)}, f32[64,1408]{1,0:T(8,128)S(1)}) custom-call(bf16[384,1408]{1,0:T(8,128)(2,1)S(1)} %get-tuple-element.95.tok, bf16[384,1408]{1,0:T(8,128)(2,1)S(1)} %get-tuple-element.86.cot, bf16[1408,1536]{1,0:T(8,128)(2,1)S(1)} %get-tuple-element.82.w_up, bf16[1536,1408]{1,0:T(8,128)(2,1)S(1)} %get-tuple-element.74.w_down, ...), custom_call_target="tpu_custom_call" | custom-call | flops 1 | bytes 1 | tf_op jit(solution)/shard_map/pallas_call | solution.py:534
  32.9 1.8 %shard_map.110 = (bf16[384,384]{1,0:T(8,128)(2,1)S(1)}, bf16[64,1408]{1,0:T(8,128)(2,1)S(1)}) custom-call(bf16[384,1408]{1,0:T(8,128)(2,1)S(1)} %get-tuple-element.95.tok, bf16[384,1408]{1,0:T(8,128)(2,1)S(1)} %get-tuple-element.86.cot, bf16[1408,1536]{1,0:T(8,128)(2,1)S(1)} %get-tuple-element.82.w_up, bf16[1536,1408]{1,0:T(8,128)(2,1)S(1)} %get-tuple-element.74.w_down, ...), custom_call_target="tpu_custom_call" | custom-call | flops 1 | bytes 1 | tf_op jit(solution)/shard_map/pallas_call | solution.py:534
  34.7 0.6 collective-permute-start.11
  35.3 1.5 %collective-permute-start.15 = (bf16[384,384]{1,0:T(8,128)(2,1)S(1)}, bf16[384,384]{1,0:T(8,128)(2,1)S(1)}, u32[]{:S(2)}, u32[]{:S(2)}) collective-permute-start(bf16[384,384]{1,0:T(8,128)(2,1)S(1)} %get-tuple-element.105.pre), channel_id=1, source_target_pairs={{0,4},{4,0},{8,12},{12,8},{16,20},{20,16},{24,28},{28,24},{1,5},{5... | collective-permute-start | bytes 884744 | tf_op jit(solution)/shard_map/ppermute | solution.py:24
  36.8 0.6 collective-permute-start.14
  37.5 0.0 copy-start.1
  37.5 1.9 %shard_map.113 = (bf16[704,768]{1,0:T(8,128)(2,1)S(1)}, f32[352,384]{1,0:T(8,128)S(1)}, bf16[352,384]{1,0:T(8,128)(2,1)S(1)}) custom-call(bf16[1408,384]{1,0:T(8,128)(2,1)S(1)} %get-tuple-element.99.tok_full, bf16[176,640]{1,0:T(8,128)(2,1)S(1)} %get-tuple-element.103.h0, bf16[176,640]{1,0:T(8,128)(2,1)S(1)} %collective-permute-done.4.h1, ...), custom_call_target="tpu_custom_call" | custom-call | flops 1 | bytes 1 | tf_op jit(solution)/shard_map/pallas_call | solution.py:534
  39.4 1.6 %collective-permute-start.16 = (bf16[352,384]{1,0:T(8,128)(2,1)S(1)}, bf16[352,384]{1,0:T(8,128)(2,1)S(1)}, u32[]{:S(2)}, u32[]{:S(2)}) collective-permute-start(bf16[352,384]{1,0:T(8,128)(2,1)S(1)} %get-tuple-element.102), channel_id=1, source_target_pairs={{0,8},{4,12},{8,0},{12,4},{16,24},{20,28},{24,16},{28,20},{1,9},{5... | collective-permute-start | bytes 811016 | tf_op jit(solution)/shard_map/ppermute | solution.py:24
  41.0 1.3 %collective-permute-start.17 = (bf16[384,384]{1,0:T(8,128)(2,1)S(1)}, bf16[384,384]{1,0:T(8,128)(2,1)S(1)}, u32[]{:S(2)}, u32[]{:S(2)}) collective-permute-start(bf16[384,384]{1,0:T(8,128)(2,1)S(1)} %get-tuple-element.112.pre), channel_id=1, source_target_pairs={{0,4},{4,0},{8,12},{12,8},{16,20},{20,16},{24,28},{28,24},{1,5},{5... | collective-permute-start | bytes 884744 | tf_op jit(solution)/shard_map/ppermute | solution.py:24
  42.3 1.0 %collective-permute-done.14.b = bf16[64,1408]{1,0:T(8,128)(2,1)S(1)} collective-permute-done((bf16[64,1408]{1,0:T(8,128)(2,1)S(1)}, bf16[64,1408]{1,0:T(8,128)(2,1)S(1)}, u32[]{:S(2)}, u32[]{:S(2)}) %collective-permute-start.14) | collective-permute-done | bytes 180256 | tf_op jit(solution)/shard_map/ppermute | solution.py:24
  43.3 0.5 shard_map.114.e0
  43.8 1.4 %collective-permute-done.15.pre_pair = bf16[384,384]{1,0:T(8,128)(2,1)S(1)} collective-permute-done((bf16[384,384]{1,0:T(8,128)(2,1)S(1)}, bf16[384,384]{1,0:T(8,128)(2,1)S(1)}, u32[]{:S(2)}, u32[]{:S(2)}) %collective-permute-start.15) | collective-permute-done | bytes 294944 | tf_op jit(solution)/shard_map/ppermute | solution.py:24
  45.2 0.8 shard_map.115
  46.0 1.6 %collective-permute-start.18 = (bf16[352,384]{1,0:T(8,128)(2,1)S(1)}, bf16[352,384]{1,0:T(8,128)(2,1)S(1)}, u32[]{:S(2)}, u32[]{:S(2)}) collective-permute-start(bf16[352,384]{1,0:T(8,128)(2,1)S(1)} %get-tuple-element.108), channel_id=1, source_target_pairs={{0,8},{4,12},{8,0},{12,4},{16,24},{20,28},{24,16},{28,20},{1,9},{5... | collective-permute-start | bytes 811016 | tf_op jit(solution)/shard_map/ppermute | solution.py:24
  47.6 0.5 collective-permute-start.20
  48.2 1.5 %collective-permute-start.22 = (bf16[384,384]{1,0:T(8,128)(2,1)S(1)}, bf16[384,384]{1,0:T(8,128)(2,1)S(1)}, u32[]{:S(2)}, u32[]{:S(2)}) collective-permute-start(bf16[384,384]{1,0:T(8,128)(2,1)S(1)} %get-tuple-element.118.pre), channel_id=1, source_target_pairs={{0,4},{4,0},{8,12},{12,8},{16,20},{20,16},{24,28},{28,24},{1,5},{5... | collective-permute-start | bytes 884744 | tf_op jit(solution)/shard_map/ppermute | solution.py:24
  49.6 0.1 shard_map.116
  49.7 1.8 %collective-permute-done.17.pre_pair = bf16[384,384]{1,0:T(8,128)(2,1)S(1)} collective-permute-done((bf16[384,384]{1,0:T(8,128)(2,1)S(1)}, bf16[384,384]{1,0:T(8,128)(2,1)S(1)}, u32[]{:S(2)}, u32[]{:S(2)}) %collective-permute-start.17) | collective-permute-done | bytes 294944 | tf_op jit(solution)/shard_map/ppermute | solution.py:24
  51.5 0.8 shard_map.117
  52.3 1.6 %collective-permute-start.23 = (bf16[352,384]{1,0:T(8,128)(2,1)S(1)}, bf16[352,384]{1,0:T(8,128)(2,1)S(1)}, u32[]{:S(2)}, u32[]{:S(2)}) collective-permute-start(bf16[352,384]{1,0:T(8,128)(2,1)S(1)} %get-tuple-element.113), channel_id=1, source_target_pairs={{0,8},{4,12},{8,0},{12,4},{16,24},{20,28},{24,16},{28,20},{1,9},{5... | collective-permute-start | bytes 811016 | tf_op jit(solution)/shard_map/ppermute | solution.py:24
  54.0 0.5 collective-permute-start.24
  54.5 2.6 %collective-permute-start.28 = (bf16[176,384]{1,0:T(8,128)(2,1)S(1)}, bf16[176,384]{1,0:T(8,128)(2,1)S(1)}, u32[]{:S(2)}, u32[]{:S(2)}) collective-permute-start(bf16[176,384]{1,0:T(8,128)(2,1)S(1)} %get-tuple-element.110), channel_id=1, source_target_pairs={{0,16},{4,20},{8,24},{12,28},{16,0},{20,4},{24,8},{28,12},{1,17},{... | collective-permute-start | bytes 405512 | tf_op jit(solution)/shard_map/ppermute | solution.py:24
  57.0 0.1 shard_map.118
  57.1 0.2 shard_map.119.share
  57.4 0.0 copy-start.5
  57.4 0.6 collective-permute-start.29
  58.0 0.8 shard_map.120
  58.8 0.6 collective-permute-start.27
  59.4 1.2 %collective-permute-done.23.received = bf16[352,384]{1,0:T(8,128)(2,1)S(1)} collective-permute-done((bf16[352,384]{1,0:T(8,128)(2,1)S(1)}, bf16[352,384]{1,0:T(8,128)(2,1)S(1)}, u32[]{:S(2)}, u32[]{:S(2)}) %collective-permute-start.23) | collective-permute-done | bytes 270368 | tf_op jit(solution)/shard_map/ppermute | solution.py:24
  60.6 0.1 shard_map.121
  60.7 0.8 shard_map.122.a
  61.5 0.0 collective-permute-start.25
  61.5 3.6 %collective-permute-done.28 = bf16[176,384]{1,0:T(8,128)(2,1)S(1)} collective-permute-done((bf16[176,384]{1,0:T(8,128)(2,1)S(1)}, bf16[176,384]{1,0:T(8,128)(2,1)S(1)}, u32[]{:S(2)}, u32[]{:S(2)}) %collective-permute-start.28) | collective-permute-done | bytes 135200 | tf_op jit(solution)/shard_map/ppermute | solution.py:24
  65.2 0.5 collective-permute-start.30
  65.6 2.6 %collective-permute-start.26 = (f32[1,384]{1,0:T(1,128)S(1)}, f32[1,384]{1,0:T(1,128)S(1)}, u32[]{:S(2)}, u32[]{:S(2)}) collective-permute-start(f32[1,384]{1,0:T(1,128)S(1)} %shard_map.123.a), channel_id=1, source_target_pairs={{0,2},{1,3},{2,0},{3,1},{4,6},{5,7},{6,4},{7,5},{8,10},{9,11},{10,... | collective-permute-start | bytes 4616 | tf_op jit(solution)/shard_map/ppermute | solution.py:24
  68.2 2.3 %collective-permute-done.29 = bf16[176,384]{1,0:T(8,128)(2,1)S(1)} collective-permute-done((bf16[176,384]{1,0:T(8,128)(2,1)S(1)}, bf16[176,384]{1,0:T(8,128)(2,1)S(1)}, u32[]{:S(2)}, u32[]{:S(2)}) %collective-permute-start.29) | collective-permute-done | bytes 135200 | tf_op jit(solution)/shard_map/ppermute | solution.py:24
  70.5 0.7 shard_map.124
  71.2 1.7 %collective-permute-done.27.received = bf16[352,384]{1,0:T(8,128)(2,1)S(1)} collective-permute-done((bf16[352,384]{1,0:T(8,128)(2,1)S(1)}, bf16[352,384]{1,0:T(8,128)(2,1)S(1)}, u32[]{:S(2)}, u32[]{:S(2)}) %collective-permute-start.27) | collective-permute-done | bytes 270368 | tf_op jit(solution)/shard_map/ppermute | solution.py:24
  72.9 0.1 shard_map.125
  73.0 1.9 %collective-permute-start.31 = (bf16[176,384]{1,0:T(8,128)(2,1)S(1)}, bf16[176,384]{1,0:T(8,128)(2,1)S(1)}, u32[]{:S(2)}, u32[]{:S(2)}) collective-permute-start(bf16[176,384]{1,0:T(8,128)(2,1)S(1)} %get-tuple-element.138), channel_id=1, source_target_pairs={{0,16},{4,20},{8,24},{12,28},{16,0},{20,4},{24,8},{28,12},{1,17},{... | collective-permute-start | bytes 405512 | tf_op jit(solution)/shard_map/ppermute | solution.py:24
  74.9 6.5 %collective-permute-done.31 = bf16[176,384]{1,0:T(8,128)(2,1)S(1)} collective-permute-done((bf16[176,384]{1,0:T(8,128)(2,1)S(1)}, bf16[176,384]{1,0:T(8,128)(2,1)S(1)}, u32[]{:S(2)}, u32[]{:S(2)}) %collective-permute-start.31) | collective-permute-done | bytes 135200 | tf_op jit(solution)/shard_map/ppermute | solution.py:24
  81.4 1.1 %pad_maximum_fusion = f32[176,1536]{1,0:T(8,128)} fusion(f32[176,384]{1,0:T(8,128)S(1)} %convert_add_fusion, f32[176,384]{1,0:T(8,128)S(1)} %convert_add_fusion.1, f32[176,384]{1,0:T(8,128)S(1)} %convert_add_fusion.2, f32[176,384]{1,0:T(8,128)S(1)} %convert_add_fusion.3), kind=kLoop, calls=%fused_computation | loop fusion | flops 811008 | bytes 2162688 | tf_op jit(solution)/shard_map/concatenate | solution.py:781
  (40 shorter events, 0.3 us)
Async XLA Ops:
  4.0 15.5 %collective-permute-start.6 = (bf16[704,384]{1,0:T(8,128)(2,1)}, bf16[704,384]{1,0:T(8,128)(2,1)S(1)}, u32[]{:S(2)}, u32[]{:S(2)}) collective-permute-start(bf16[704,384]{1,0:T(8,128)(2,1)} %get-tuple-element.80.b0), channel_id=1, source_target_pairs={{0,2},{1,3},{2,0},{3,1},{4,6},{5,7},{6,4},{7,5},{8,10},{9,11},{10,... | collective-permute-start | bytes 1622024 | tf_op jit(solution)/shard_map/ppermute | solution.py:24
  7.0 11.9 %collective-permute-start = (bf16[176,384]{1,0:T(8,128)(2,1)}, bf16[176,384]{1,0:T(8,128)(2,1)S(1)}, u32[]{:S(2)}, u32[]{:S(2)}) collective-permute-start(bf16[176,384]{1,0:T(8,128)(2,1)} %get-tuple-element.71), channel_id=1, source_target_pairs={{0,4},{4,0},{8,12},{12,8},{16,20},{20,16},{24,28},{28,24},{1,5},{5... | collective-permute-start | bytes 405512 | tf_op jit(solution)/shard_map/ppermute | solution.py:24
  8.5 10.5 %collective-permute-start.1 = (bf16[144,256]{1,0:T(8,128)(2,1)}, bf16[144,256]{1,0:T(8,128)(2,1)S(1)}, u32[]{:S(2)}, u32[]{:S(2)}) collective-permute-start(bf16[144,256]{1,0:T(8,128)(2,1)} %get-tuple-element.72.t0), channel_id=1, source_target_pairs={{0,8},{4,12},{8,16},{12,20},{16,24},{20,28},{24,0},{28,4},{1,9},{5... | collective-permute-start | bytes 221192 | tf_op jit(solution)/shard_map/ppermute | solution.py:29
  10.1 9.0 %collective-permute-start.2 = (bf16[144,256]{1,0:T(8,128)(2,1)}, bf16[144,256]{1,0:T(8,128)(2,1)S(1)}, u32[]{:S(2)}, u32[]{:S(2)}) collective-permute-start(bf16[144,256]{1,0:T(8,128)(2,1)} %get-tuple-element.72.t0), channel_id=1, source_target_pairs={{0,16},{4,20},{8,24},{12,28},{16,0},{20,4},{24,8},{28,12},{1,17},{... | collective-permute-start | bytes 221192 | tf_op jit(solution)/shard_map/ppermute | solution.py:29
  12.7 6.4 %collective-permute-start.3 = (bf16[144,256]{1,0:T(8,128)(2,1)}, bf16[144,256]{1,0:T(8,128)(2,1)S(1)}, u32[]{:S(2)}, u32[]{:S(2)}) collective-permute-start(bf16[144,256]{1,0:T(8,128)(2,1)} %get-tuple-element.72.t0), channel_id=1, source_target_pairs={{0,24},{4,28},{8,0},{12,4},{16,8},{20,12},{24,16},{28,20},{1,25},{... | collective-permute-start | bytes 221192 | tf_op jit(solution)/shard_map/ppermute | solution.py:29
  14.0 2.2 %copy-start = (bf16[1408,1536]{1,0:T(8,128)(2,1)S(1)}, bf16[1408,1536]{1,0:T(8,128)(2,1)}, u32[]{:S(2)}) copy-start(bf16[1408,1536]{1,0:T(8,128)(2,1)} %up) | copy-start | bytes 12976132
  16.2 2.7 %copy-start.2 = (bf16[704,384]{1,0:T(8,128)(2,1)S(1)}, bf16[704,384]{1,0:T(8,128)(2,1)}, u32[]{:S(2)}) copy-start(bf16[704,384]{1,0:T(8,128)(2,1)} %get-tuple-element.80.b0) | copy-start | bytes 1622020
  16.2 2.8 %copy-start.3 = (bf16[352,128]{1,0:T(8,128)(2,1)S(1)}, bf16[352,128]{1,0:T(8,128)(2,1)}, u32[]{:S(2)}) copy-start(bf16[352,128]{1,0:T(8,128)(2,1)} %get-tuple-element.76.pool) | copy-start | bytes 270340
  16.2 2.8 %copy-start.4 = (bf16[144,256]{1,0:T(8,128)(2,1)S(1)}, bf16[144,256]{1,0:T(8,128)(2,1)}, u32[]{:S(2)}) copy-start(bf16[144,256]{1,0:T(8,128)(2,1)} %get-tuple-element.72.t0) | copy-start | bytes 221188
  19.0 4.0 %collective-permute-start.5 = (bf16[704,384]{1,0:T(8,128)(2,1)S(1)}, bf16[704,384]{1,0:T(8,128)(2,1)S(1)}, u32[]{:S(2)}, u32[]{:S(2)}) collective-permute-start(bf16[704,384]{1,0:T(8,128)(2,1)S(1)} %copy-done.2), channel_id=1, source_target_pairs={{0,1},{1,0},{2,3},{3,2},{4,5},{5,4},{6,7},{7,6},{8,9},{9,8},{10,11... | collective-permute-start | bytes 1622024 | tf_op jit(solution)/shard_map/ppermute | solution.py:24
  19.5 3.5 %collective-permute-start.7 = (bf16[704,384]{1,0:T(8,128)(2,1)S(1)}, bf16[704,384]{1,0:T(8,128)(2,1)S(1)}, u32[]{:S(2)}, u32[]{:S(2)}) collective-permute-start(bf16[704,384]{1,0:T(8,128)(2,1)S(1)} %collective-permute-done.6.b2), channel_id=1, source_target_pairs={{0,1},{1,0},{2,3},{3,2},{4,5},{5,4},{6,7},{7,6},{8,9},{9,8},{10,11... | collective-permute-start | bytes 1622024 | tf_op jit(solution)/shard_map/ppermute | solution.py:24
  19.7 9.8 %collective-permute-start.8 = (bf16[576,256]{1,0:T(8,128)(2,1)S(1)}, bf16[576,256]{1,0:T(8,128)(2,1)S(1)}, u32[]{:S(2)}, u32[]{:S(2)}) collective-permute-start(bf16[576,256]{1,0:T(8,128)(2,1)S(1)} %get-tuple-element.90.mine), channel_id=1, source_target_pairs={{0,4},{4,0},{8,12},{12,8},{16,20},{20,16},{24,28},{28,24},{1,5},{5... | collective-permute-start | bytes 884744 | tf_op jit(solution)/shard_map/ppermute | solution.py:24
  21.2 1.7 %collective-permute-start.4 = (bf16[176,640]{1,0:T(8,128)(2,1)S(1)}, bf16[176,640]{1,0:T(8,128)(2,1)S(1)}, u32[]{:S(2)}, u32[]{:S(2)}) collective-permute-start(bf16[176,640]{1,0:T(8,128)(2,1)S(1)} %get-tuple-element.103.h0), channel_id=1, source_target_pairs={{0,1},{1,0},{2,3},{3,2},{4,5},{5,4},{6,7},{7,6},{8,9},{9,8},{10,11... | collective-permute-start | bytes 675848 | tf_op jit(solution)/shard_map/ppermute | solution.py:24
  21.5 9.7 %collective-permute-start.9 = (bf16[176,640]{1,0:T(8,128)(2,1)S(1)}, bf16[176,640]{1,0:T(8,128)(2,1)S(1)}, u32[]{:S(2)}, u32[]{:S(2)}) collective-permute-start(bf16[176,640]{1,0:T(8,128)(2,1)S(1)} %get-tuple-element.103.h0), channel_id=1, source_target_pairs={{0,2},{1,3},{2,0},{3,1},{4,6},{5,7},{6,4},{7,5},{8,10},{9,11},{10,... | collective-permute-start | bytes 675848 | tf_op jit(solution)/shard_map/ppermute | solution.py:24
  25.2 12.3 %collective-permute-start.13 = (bf16[400,384]{1,0:T(8,128)(2,1)S(1)}, bf16[400,384]{1,0:T(8,128)(2,1)S(1)}, u32[]{:S(2)}, u32[]{:S(2)}) collective-permute-start(bf16[400,384]{1,0:T(8,128)(2,1)S(1)} %get-tuple-element.100.pre), channel_id=1, source_target_pairs={{0,4},{4,0},{8,12},{12,8},{16,20},{20,16},{24,28},{28,24},{1,5},{5... | collective-permute-start | bytes 921608 | tf_op jit(solution)/shard_map/ppermute | solution.py:24
  29.6 7.8 %collective-permute-start.12 = (bf16[512,256]{1,0:T(8,128)(2,1)S(1)}, bf16[512,256]{1,0:T(8,128)(2,1)S(1)}, u32[]{:S(2)}, u32[]{:S(2)}) collective-permute-start(bf16[512,256]{1,0:T(8,128)(2,1)S(1)} %get-tuple-element.92), channel_id=1, source_target_pairs={{0,2},{1,3},{2,0},{3,1},{4,6},{5,7},{6,4},{7,5},{8,10},{9,11},{10,... | collective-permute-start | bytes 786440 | tf_op jit(solution)/shard_map/ppermute | solution.py:24
  31.2 5.6 %collective-permute-start.10 = (bf16[176,640]{1,0:T(8,128)(2,1)S(1)}, bf16[176,640]{1,0:T(8,128)(2,1)S(1)}, u32[]{:S(2)}, u32[]{:S(2)}) collective-permute-start(bf16[176,640]{1,0:T(8,128)(2,1)S(1)} %collective-permute-done.9.h2), channel_id=1, source_target_pairs={{0,1},{1,0},{2,3},{3,2},{4,5},{5,4},{6,7},{7,6},{8,9},{9,8},{10,11... | collective-permute-start | bytes 675848 | tf_op jit(solution)/shard_map/ppermute | solution.py:24
  34.7 2.1 %collective-permute-start.11 = (bf16[64,1408]{1,0:T(8,128)(2,1)S(1)}, bf16[64,1408]{1,0:T(8,128)(2,1)S(1)}, u32[]{:S(2)}, u32[]{:S(2)}) collective-permute-start(bf16[64,1408]{1,0:T(8,128)(2,1)S(1)} %get-tuple-element.97.a), channel_id=1, source_target_pairs={{0,1},{1,0},{2,3},{3,2},{4,5},{5,4},{6,7},{7,6},{8,9},{9,8},{10,11... | collective-permute-start | bytes 540680 | tf_op jit(solution)/shard_map/ppermute | solution.py:24
  35.3 9.9 %collective-permute-start.15 = (bf16[384,384]{1,0:T(8,128)(2,1)S(1)}, bf16[384,384]{1,0:T(8,128)(2,1)S(1)}, u32[]{:S(2)}, u32[]{:S(2)}) collective-permute-start(bf16[384,384]{1,0:T(8,128)(2,1)S(1)} %get-tuple-element.105.pre), channel_id=1, source_target_pairs={{0,4},{4,0},{8,12},{12,8},{16,20},{20,16},{24,28},{28,24},{1,5},{5... | collective-permute-start | bytes 884744 | tf_op jit(solution)/shard_map/ppermute | solution.py:24
  36.8 6.5 %collective-permute-start.14 = (bf16[64,1408]{1,0:T(8,128)(2,1)S(1)}, bf16[64,1408]{1,0:T(8,128)(2,1)S(1)}, u32[]{:S(2)}, u32[]{:S(2)}) collective-permute-start(bf16[64,1408]{1,0:T(8,128)(2,1)S(1)} %shard_map.111.a), channel_id=1, source_target_pairs={{0,2},{1,3},{2,0},{3,1},{4,6},{5,7},{6,4},{7,5},{8,10},{9,11},{10,... | collective-permute-start | bytes 540680 | tf_op jit(solution)/shard_map/ppermute | solution.py:24
  37.5 5.8 %copy-start.1 = (bf16[1408,256]{1,0:T(8,128)(2,1)S(1)}, bf16[1408,256]{1,0:T(8,128)(2,1)}, u32[]{:S(2)}) copy-start(bf16[1408,256]{1,0:T(8,128)(2,1)} %ref_proj.1) | copy-start | bytes 2162692
  39.4 8.8 %collective-permute-start.16 = (bf16[352,384]{1,0:T(8,128)(2,1)S(1)}, bf16[352,384]{1,0:T(8,128)(2,1)S(1)}, u32[]{:S(2)}, u32[]{:S(2)}) collective-permute-start(bf16[352,384]{1,0:T(8,128)(2,1)S(1)} %get-tuple-element.102), channel_id=1, source_target_pairs={{0,8},{4,12},{8,0},{12,4},{16,24},{20,28},{24,16},{28,20},{1,9},{5... | collective-permute-start | bytes 811016 | tf_op jit(solution)/shard_map/ppermute | solution.py:24
  41.0 10.5 %collective-permute-start.17 = (bf16[384,384]{1,0:T(8,128)(2,1)S(1)}, bf16[384,384]{1,0:T(8,128)(2,1)S(1)}, u32[]{:S(2)}, u32[]{:S(2)}) collective-permute-start(bf16[384,384]{1,0:T(8,128)(2,1)S(1)} %get-tuple-element.112.pre), channel_id=1, source_target_pairs={{0,4},{4,0},{8,12},{12,8},{16,20},{20,16},{24,28},{28,24},{1,5},{5... | collective-permute-start | bytes 884744 | tf_op jit(solution)/shard_map/ppermute | solution.py:24
  42.3 11.7 %collective-permute-start.19 = (bf16[512,256]{1,0:T(8,128)(2,1)S(1)}, bf16[512,256]{1,0:T(8,128)(2,1)S(1)}, u32[]{:S(2)}, u32[]{:S(2)}) collective-permute-start(bf16[512,256]{1,0:T(8,128)(2,1)S(1)} %shard_map.112), channel_id=1, source_target_pairs={{0,1},{1,0},{2,3},{3,2},{4,5},{5,4},{6,7},{7,6},{8,9},{9,8},{10,11... | collective-permute-start | bytes 786440 | tf_op jit(solution)/shard_map/ppermute | solution.py:24
  46.0 8.5 %collective-permute-start.18 = (bf16[352,384]{1,0:T(8,128)(2,1)S(1)}, bf16[352,384]{1,0:T(8,128)(2,1)S(1)}, u32[]{:S(2)}, u32[]{:S(2)}) collective-permute-start(bf16[352,384]{1,0:T(8,128)(2,1)S(1)} %get-tuple-element.108), channel_id=1, source_target_pairs={{0,8},{4,12},{8,0},{12,4},{16,24},{20,28},{24,16},{28,20},{1,9},{5... | collective-permute-start | bytes 811016 | tf_op jit(solution)/shard_map/ppermute | solution.py:24
  47.6 6.3 %collective-permute-start.20 = (f32[192,256]{1,0:T(8,128)S(1)}, f32[192,256]{1,0:T(8,128)S(1)}, u32[]{:S(2)}, u32[]{:S(2)}) collective-permute-start(f32[192,256]{1,0:T(8,128)S(1)} %shard_map.114.e0), channel_id=1, source_target_pairs={{0,2},{1,3},{2,0},{3,1},{4,6},{5,7},{6,4},{7,5},{8,10},{9,11},{10,... | collective-permute-start | bytes 589832 | tf_op jit(solution)/shard_map/ppermute | solution.py:24
  48.2 9.8 %collective-permute-start.22 = (bf16[384,384]{1,0:T(8,128)(2,1)S(1)}, bf16[384,384]{1,0:T(8,128)(2,1)S(1)}, u32[]{:S(2)}, u32[]{:S(2)}) collective-permute-start(bf16[384,384]{1,0:T(8,128)(2,1)S(1)} %get-tuple-element.118.pre), channel_id=1, source_target_pairs={{0,4},{4,0},{8,12},{12,8},{16,20},{20,16},{24,28},{28,24},{1,5},{5... | collective-permute-start | bytes 884744 | tf_op jit(solution)/shard_map/ppermute | solution.py:24
  52.3 8.3 %collective-permute-start.23 = (bf16[352,384]{1,0:T(8,128)(2,1)S(1)}, bf16[352,384]{1,0:T(8,128)(2,1)S(1)}, u32[]{:S(2)}, u32[]{:S(2)}) collective-permute-start(bf16[352,384]{1,0:T(8,128)(2,1)S(1)} %get-tuple-element.113), channel_id=1, source_target_pairs={{0,8},{4,12},{8,0},{12,4},{16,24},{20,28},{24,16},{28,20},{1,9},{5... | collective-permute-start | bytes 811016 | tf_op jit(solution)/shard_map/ppermute | solution.py:24
  54.0 3.4 %collective-permute-start.21 = (f32[192,256]{1,0:T(8,128)S(1)}, f32[192,256]{1,0:T(8,128)S(1)}, u32[]{:S(2)}, u32[]{:S(2)}) collective-permute-start(f32[192,256]{1,0:T(8,128)S(1)} %collective-permute-done.20.e2), channel_id=1, source_target_pairs={{0,1},{1,0},{2,3},{3,2},{4,5},{5,4},{6,7},{7,6},{8,9},{9,8},{10,11... | collective-permute-start | bytes 589832 | tf_op jit(solution)/shard_map/ppermute | solution.py:24
  54.0 6.7 %collective-permute-start.24 = (f32[192,256]{1,0:T(8,128)S(1)}, f32[192,256]{1,0:T(8,128)S(1)}, u32[]{:S(2)}, u32[]{:S(2)}) collective-permute-start(f32[192,256]{1,0:T(8,128)S(1)} %shard_map.114.e0), channel_id=1, source_target_pairs={{0,1},{1,0},{2,3},{3,2},{4,5},{5,4},{6,7},{7,6},{8,9},{9,8},{10,11... | collective-permute-start | bytes 589832 | tf_op jit(solution)/shard_map/ppermute | solution.py:24
  54.5 10.7 %collective-permute-start.28 = (bf16[176,384]{1,0:T(8,128)(2,1)S(1)}, bf16[176,384]{1,0:T(8,128)(2,1)S(1)}, u32[]{:S(2)}, u32[]{:S(2)}) collective-permute-start(bf16[176,384]{1,0:T(8,128)(2,1)S(1)} %get-tuple-element.110), channel_id=1, source_target_pairs={{0,16},{4,20},{8,24},{12,28},{16,0},{20,4},{24,8},{28,12},{1,17},{... | collective-permute-start | bytes 405512 | tf_op jit(solution)/shard_map/ppermute | solution.py:24
  57.4 3.3 %copy-start.5 = (s32[64]{0:T(128)S(1)}, s32[64]{0:T(128)}, u32[]{:S(2)}) copy-start(s32[64]{0:T(128)} %param.13) | copy-start | bytes 772
  57.4 13.1 %collective-permute-start.29 = (bf16[176,384]{1,0:T(8,128)(2,1)S(1)}, bf16[176,384]{1,0:T(8,128)(2,1)S(1)}, u32[]{:S(2)}, u32[]{:S(2)}) collective-permute-start(bf16[176,384]{1,0:T(8,128)(2,1)S(1)} %get-tuple-element.115), channel_id=1, source_target_pairs={{0,16},{4,20},{8,24},{12,28},{16,0},{20,4},{24,8},{28,12},{1,17},{... | collective-permute-start | bytes 405512 | tf_op jit(solution)/shard_map/ppermute | solution.py:24
  58.8 14.1 %collective-permute-start.27 = (bf16[352,384]{1,0:T(8,128)(2,1)S(1)}, bf16[352,384]{1,0:T(8,128)(2,1)S(1)}, u32[]{:S(2)}, u32[]{:S(2)}) collective-permute-start(bf16[352,384]{1,0:T(8,128)(2,1)S(1)} %get-tuple-element.121), channel_id=1, source_target_pairs={{0,8},{4,12},{8,0},{12,4},{16,24},{20,28},{24,16},{28,20},{1,9},{5... | collective-permute-start | bytes 811016 | tf_op jit(solution)/shard_map/ppermute | solution.py:24
  61.5 4.1 %collective-permute-start.25 = (f32[1,384]{1,0:T(1,128)S(1)}, f32[1,384]{1,0:T(1,128)S(1)}, u32[]{:S(2)}, u32[]{:S(2)}) collective-permute-start(f32[1,384]{1,0:T(1,128)S(1)} %shard_map.122.a), channel_id=1, source_target_pairs={{0,1},{1,0},{2,3},{3,2},{4,5},{5,4},{6,7},{7,6},{8,9},{9,8},{10,11... | collective-permute-start | bytes 4616 | tf_op jit(solution)/shard_map/ppermute | solution.py:24
  65.2 9.7 %collective-permute-start.30 = (bf16[176,384]{1,0:T(8,128)(2,1)S(1)}, bf16[176,384]{1,0:T(8,128)(2,1)S(1)}, u32[]{:S(2)}, u32[]{:S(2)}) collective-permute-start(bf16[176,384]{1,0:T(8,128)(2,1)S(1)} %get-tuple-element.123), channel_id=1, source_target_pairs={{0,16},{4,20},{8,24},{12,28},{16,0},{20,4},{24,8},{28,12},{1,17},{... | collective-permute-start | bytes 405512 | tf_op jit(solution)/shard_map/ppermute | solution.py:24
  65.6 4.9 %collective-permute-start.26 = (f32[1,384]{1,0:T(1,128)S(1)}, f32[1,384]{1,0:T(1,128)S(1)}, u32[]{:S(2)}, u32[]{:S(2)}) collective-permute-start(f32[1,384]{1,0:T(1,128)S(1)} %shard_map.123.a), channel_id=1, source_target_pairs={{0,2},{1,3},{2,0},{3,1},{4,6},{5,7},{6,4},{7,5},{8,10},{9,11},{10,... | collective-permute-start | bytes 4616 | tf_op jit(solution)/shard_map/ppermute | solution.py:24
  73.0 8.4 %collective-permute-start.31 = (bf16[176,384]{1,0:T(8,128)(2,1)S(1)}, bf16[176,384]{1,0:T(8,128)(2,1)S(1)}, u32[]{:S(2)}, u32[]{:S(2)}) collective-permute-start(bf16[176,384]{1,0:T(8,128)(2,1)S(1)} %get-tuple-element.138), channel_id=1, source_target_pairs={{0,16},{4,20},{8,24},{12,28},{16,0},{20,4},{24,8},{28,12},{1,17},{... | collective-permute-start | bytes 405512 | tf_op jit(solution)/shard_map/ppermute | solution.py:24

commit v7 on v6

--- a/solution.py
+++ b/solution.py
@@ -365,16 +365,17 @@
         copy.wait()
 
 
-def chunk_work(n_patch, tok, cot, w_up, w_down, pre, mixed):
+def chunk_work(n_patch, first, tok, cot, w_up, w_down, pre, mixed):
     k_dev = tok.shape[0] // n_patch
     groups = group_mask(k_dev, n_patch)[0].astype(bf16)
-    pre_act = dot_f32(tok[...], w_up[...])
+    size = pre.shape[1]
+    pre_act = dot_f32(tok[...], w_up[:, first : first + size])
     activated, gelu_slope = gelu_parts(pre_act)
-    pre[0 : tok.shape[0], :] = (dot_rows(cot[...], w_down[...]) * gelu_slope).astype(bf16)
+    pre[0 : tok.shape[0], :] = (dot_rows(cot[...], w_down[first : first + size, :]) * gelu_slope).astype(bf16)
     pooled = dot_f32(groups, activated.astype(bf16))
     high = pooled.astype(bf16)
     low = (pooled - high.astype(f32)).astype(bf16)
-    both = dot_f32(jnp.concatenate([high, low], axis=0), w_down[...])
+    both = dot_f32(jnp.concatenate([high, low], axis=0), w_down[first : first + size, :])
     return mixed + (both[:k_dev] + both[k_dev:])
 
 
@@ -390,13 +391,13 @@
     tok[...] = tok_full[...].T
     cot[...] = cot_full[...].T
     start = dot_f32(groups, tok[...]) * (1.0 / n_mdl)
-    mixed[...] = chunk_work(n_patch, tok, cot, w_up, w_down, pre, start)
+    mixed[...] = chunk_work(n_patch, 0, tok, cot, w_up, w_down, pre, start)
     pre[n_rows:, :] = jnp.zeros((16, pre.shape[1]), bf16)
     pre[n_rows:, 0 : dests.shape[1]] = dests[...]
 
 
-def next_chunk_body(n_patch, tok, cot, w_up, w_down, mixed_in, pre, mixed):
-    total = chunk_work(n_patch, tok, cot, w_up, w_down, pre, mixed_in[...])
+def next_chunk_body(n_patch, first, tok, cot, w_up, w_down, mixed_in, pre, mixed):
+    total = chunk_work(n_patch, first, tok, cot, w_up, w_down, pre, mixed_in[...])
     mixed[...] = total.astype(mixed.dtype)
 
 
@@ -519,15 +520,10 @@
     n_emb = ex_dev + k_dev
     kept_row = kept_index.reshape(1, k_dev)
     dest_row = dest.reshape(1, k_dev)
-    size = ff_dev // 4
-    whole = lambda shape: pl.BlockSpec(shape, lambda i: (0,) * len(shape))
+    widths = (384, 384, 384, 384)
+    starts = [sum(widths[:c]) for c in range(len(widths))]
     row_struct = struct((n_rows, d_full), bf16)
-    row_spec = whole((n_rows, d_full))
     mixed_struct = struct((k_dev, d_full), f32)
-    mixed_spec = whole((k_dev, d_full))
-    pre_struct = struct((n_rows, size), bf16)
-    pre_spec = whole((n_rows, size))
-    halves = (struct((2 * blk, size), f32), struct((2 * blk, size), bf16))
 
     def run(ties, body, out_shape, *operands, **kwargs):
         first = after(operands[0], *ties)
@@ -590,52 +586,35 @@
         )
 
 
-    def weight_specs(c):
-        return [
-            pl.BlockSpec((d_full, size), lambda i: (0, c)),
-            pl.BlockSpec((size, d_full), lambda i: (c, 0)),
-        ]
-
-
     def forward_first(ties, *operands):
         return run(
             ties,
             functools.partial(first_chunk_body, n_patch, n_mdl),
             (
-                struct((n_rows + 16, size), bf16),
+                struct((n_rows + 16, widths[0]), bf16),
                 mixed_struct,
                 struct((d_full, n_rows), bf16),
                 row_struct,
                 row_struct,
             ),
             *operands,
-            grid=(1,),
-            in_specs=[whole((16, n_high * k_dev))]
-            + [whole((2 * d_part, n_rows))] * 4 + weight_specs(0),
-            out_specs=[
-                whole((n_rows + 16, size)),
-                mixed_spec,
-                whole((d_full, n_rows)),
-                row_spec,
-                row_spec,
-            ],
             scratch_shapes=[pltpu.VMEM((d_full, n_rows), bf16)],
         )
 
     def forward(ties, c, tok, cot, held_up, held_down, mixed):
-        last = c == ff_dev // size - 1
-        return run(
-            ties,
-            functools.partial(next_chunk_body, n_patch),
-            (pre_struct, struct((k_dev, d_full), bf16 if last else f32)),
+        last = c == len(widths) - 1
+        return run(
+            ties,
+            functools.partial(next_chunk_body, n_patch, starts[c]),
+            (
+                struct((n_rows, widths[c]), bf16),
+                struct((k_dev, d_full), bf16 if last else f32),
+            ),
             tok,
             cot,
             held_up,
             held_down,
             mixed,
-            grid=(1,),
-            in_specs=[row_spec, row_spec] + weight_specs(c) + [mixed_spec],
-            out_specs=[pre_spec, mixed_spec],
         )
 
 
@@ -651,15 +630,19 @@
             pair_texts,
         )
 
+    def halves(width):
+        return (struct((2 * blk, width), f32), struct((2 * blk, width), bf16))
+
     def grad_first(ties, *operands):
         pair_struct = struct((blk * n_high, 2 * n_rows), bf16)
-        return run(ties, functools.partial(first_grad_body, n_patch), (pair_struct,) + halves, *operands)
-
-    def grad(ties, *operands):
-        return run(ties, grad_body, halves, *operands)
+        return run(ties, functools.partial(first_grad_body, n_patch), (pair_struct,) + halves(widths[0]), *operands)
+
+    def grad(ties, pair, pre, pair_pre):
+        return run(ties, grad_body, halves(pre.shape[1]), pair, pre, pair_pre)
 
     def add(ties, keep, received):
-        structs = (struct((blk, size), f32), struct((blk, size), bf16))
+        width = keep.shape[1]
+        structs = (struct((blk, width), f32), struct((blk, width), bf16))
         return run(ties, add_body, structs, keep, received)
 
     def relay_text(ties, all_texts, text_x):

time: 82.7 us -> 82.7 us (level)
  no operation moved by 1% of the time
where the time goes in v7:
time: 82.7 us; the launch traced here: 82.5 us
  starting transfers between devices  35.9 us (43%)
  waiting for transfers between devices  21.8 us (26%)
  Pallas kernels  20.4 us (25%)
  local copies, waits for them, and re-layouts  2.25 us (3%)
  other arithmetic  1.23 us (1%)
  between operations  0.9 us (1%)
    ppermute x29, starting transfers between devices, swap(): return lax.ppermute(value, axis, [(i, i ^ bit) for i in range(size)])  30.4 us
    ppermute x29, waiting for transfers between devices, swap(): return lax.ppermute(value, axis, [(i, i ^ bit) for i in range(size)])  21.8 us
    pallas_call x23, Pallas kernels, run(): call(body, out_shape, (2 ** 20, 2 ** 20), **kwargs)(first, *operands[1:])  20.4 us
    ppermute x3, starting transfers between devices, rotate_pairs(): lax.ppermute(value, 'sel', [(i, (i + 2 * step) % size) for i in range(siz...  5.51 us
    unnamed x12, local copies, waits for them, and re-layouts  2.25 us
  transfers between devices with their start and end apart: 32, of which 10 were waited for; matrix products, arithmetic and copies ran while one was open for 0% of the time, Pallas kernels for 21%

profile of v7, /device:TPU:0, one launch (start us, length us, event | category | flops | bytes accessed | tf_op | source)
XLA Modules:
  0.0 82.5 jit_solution(13207177242804377621)
XLA Ops:
  0.6 3.3 %shard_map.103 = (bf16[704,384]{1,0:T(8,128)(2,1)}, bf16[176,384]{1,0:T(8,128)(2,1)}, bf16[352,128]{1,0:T(8,128)(2,1)}, bf16[144,256]{1,0:T(8,128)(2,1)}) custom-call(bf16[352,768]{1,0:T(8,128)(2,1)} %bitcast.9, bf16[352,384]{1,0:T(8,128)(2,1)} %bitcast.10, s32[1,64]{1,0:T(1,128)} %bitcast.6, s32[1,64]{1,0:T(1,128)} %bitcast.11, bf16[128,256]{1,0:T(8,128)(2,1)} %text_hbm.1), custom_call_target="tpu_custom_call" | custom-call | flops 1 | bytes 1 | tf_op jit(solution)/shard_map/pallas_call | solution.py:530
  4.0 3.0 %collective-permute-start.6 = (bf16[704,384]{1,0:T(8,128)(2,1)}, bf16[704,384]{1,0:T(8,128)(2,1)S(1)}, u32[]{:S(2)}, u32[]{:S(2)}) collective-permute-start(bf16[704,384]{1,0:T(8,128)(2,1)} %get-tuple-element.80.b0), channel_id=1, source_target_pairs={{0,2},{1,3},{2,0},{3,1},{4,6},{5,7},{6,4},{7,5},{8,10},{9,11},{10,... | collective-permute-start | bytes 1622024 | tf_op jit(solution)/shard_map/ppermute | solution.py:24
  7.0 1.5 %collective-permute-start = (bf16[176,384]{1,0:T(8,128)(2,1)}, bf16[176,384]{1,0:T(8,128)(2,1)S(1)}, u32[]{:S(2)}, u32[]{:S(2)}) collective-permute-start(bf16[176,384]{1,0:T(8,128)(2,1)} %get-tuple-element.71), channel_id=1, source_target_pairs={{0,4},{4,0},{8,12},{12,8},{16,20},{20,16},{24,28},{28,24},{1,5},{5... | collective-permute-start | bytes 405512 | tf_op jit(solution)/shard_map/ppermute | solution.py:24
  8.5 1.6 %collective-permute-start.1 = (bf16[144,256]{1,0:T(8,128)(2,1)}, bf16[144,256]{1,0:T(8,128)(2,1)S(1)}, u32[]{:S(2)}, u32[]{:S(2)}) collective-permute-start(bf16[144,256]{1,0:T(8,128)(2,1)} %get-tuple-element.72.t0), channel_id=1, source_target_pairs={{0,8},{4,12},{8,16},{12,20},{16,24},{20,28},{24,0},{28,4},{1,9},{5... | collective-permute-start | bytes 221192 | tf_op jit(solution)/shard_map/ppermute | solution.py:29
  10.1 2.6 %collective-permute-start.2 = (bf16[144,256]{1,0:T(8,128)(2,1)}, bf16[144,256]{1,0:T(8,128)(2,1)S(1)}, u32[]{:S(2)}, u32[]{:S(2)}) collective-permute-start(bf16[144,256]{1,0:T(8,128)(2,1)} %get-tuple-element.72.t0), channel_id=1, source_target_pairs={{0,16},{4,20},{8,24},{12,28},{16,0},{20,4},{24,8},{28,12},{1,17},{... | collective-permute-start | bytes 221192 | tf_op jit(solution)/shard_map/ppermute | solution.py:29
  12.7 1.3 %collective-permute-start.3 = (bf16[144,256]{1,0:T(8,128)(2,1)}, bf16[144,256]{1,0:T(8,128)(2,1)S(1)}, u32[]{:S(2)}, u32[]{:S(2)}) collective-permute-start(bf16[144,256]{1,0:T(8,128)(2,1)} %get-tuple-element.72.t0), channel_id=1, source_target_pairs={{0,24},{4,28},{8,0},{12,4},{16,8},{20,12},{24,16},{28,20},{1,25},{... | collective-permute-start | bytes 221192 | tf_op jit(solution)/shard_map/ppermute | solution.py:29
  14.0 2.2 %copy-done = bf16[1408,1536]{1,0:T(8,128)(2,1)S(1)} copy-done((bf16[1408,1536]{1,0:T(8,128)(2,1)S(1)}, bf16[1408,1536]{1,0:T(8,128)(2,1)}, u32[]{:S(2)}) %copy-start) | copy-done | bytes 4325400
  16.2 2.7 %shard_map.104 = (bf16[1408,1536]{1,0:T(8,128)(2,1)S(1)}, bf16[1536,1408]{1,0:T(8,128)(2,1)S(1)}) custom-call(bf16[1408,1536]{1,0:T(8,128)(2,1)S(1)} %copy-done, bf16[1536,1408]{1,0:T(8,128)(2,1)} %down.1), custom_call_target="tpu_custom_call" | custom-call | flops 1 | bytes 1 | tf_op jit(solution)/shard_map/pallas_call | solution.py:530
  18.9 0.0 collective-permute-done.half
  19.0 0.1 collective-permute-start.5
  19.1 0.1 shard_map.105
  19.2 0.3 collective-permute-done.6.b2
  19.5 0.2 collective-permute-start.7
  19.7 1.5 %collective-permute-start.8 = (bf16[576,256]{1,0:T(8,128)(2,1)S(1)}, bf16[576,256]{1,0:T(8,128)(2,1)S(1)}, u32[]{:S(2)}, u32[]{:S(2)}) collective-permute-start(bf16[576,256]{1,0:T(8,128)(2,1)S(1)} %get-tuple-element.90.mine), channel_id=1, source_target_pairs={{0,4},{4,0},{8,12},{12,8},{16,20},{20,16},{24,28},{28,24},{1,5},{5... | collective-permute-start | bytes 884744 | tf_op jit(solution)/shard_map/ppermute | solution.py:24
  21.2 0.2 collective-permute-start.4
  21.5 1.5 %collective-permute-start.9 = (bf16[176,640]{1,0:T(8,128)(2,1)S(1)}, bf16[176,640]{1,0:T(8,128)(2,1)S(1)}, u32[]{:S(2)}, u32[]{:S(2)}) collective-permute-start(bf16[176,640]{1,0:T(8,128)(2,1)S(1)} %get-tuple-element.103.h0), channel_id=1, source_target_pairs={{0,2},{1,3},{2,0},{3,1},{4,6},{5,7},{6,4},{7,5},{8,10},{9,11},{10,... | collective-permute-start | bytes 675848 | tf_op jit(solution)/shard_map/ppermute | solution.py:24
  23.0 2.2 %shard_map.106 = (bf16[400,384]{1,0:T(8,128)(2,1)S(1)}, f32[64,1408]{1,0:T(8,128)S(1)}, bf16[1408,384]{1,0:T(8,128)(2,1)S(1)}, bf16[384,1408]{1,0:T(8,128)(2,1)S(1)}, bf16[384,1408]{1,0:T(8,128)(2,1)S(1)}) custom-call(bf16[16,256]{1,0:T(8,128)(2,1)S(1)} %get-tuple-element.79.dests, bf16[704,384]{1,0:T(8,128)(2,1)S(1)} %copy-done.2, ...), custom_call_target="tpu_custom_call" | custom-call | flops 1 | bytes 1 | tf_op jit(solution)/shard_map/pallas_call | solution.py:530
  25.1 0.6 collective-permute-start.13
  25.7 1.7 %shard_map.107 = (bf16[384,384]{1,0:T(8,128)(2,1)S(1)}, f32[64,1408]{1,0:T(8,128)S(1)}) custom-call(bf16[384,1408]{1,0:T(8,128)(2,1)S(1)} %get-tuple-element.95.tok, bf16[384,1408]{1,0:T(8,128)(2,1)S(1)} %get-tuple-element.86.cot, bf16[1408,1536]{1,0:T(8,128)(2,1)S(1)} %get-tuple-element.82.w_up, bf16[1536,1408]{1,0:T(8,128)(2,1)S(1)} %get-tuple-element.74.w_down, ...), custom_call_target="tpu_custom_call" | custom-call | flops 1 | bytes 1 | tf_op jit(solution)/shard_map/pallas_call | solution.py:530
  27.5 2.1 %collective-permute-done.8.theirs = bf16[576,256]{1,0:T(8,128)(2,1)S(1)} collective-permute-done((bf16[576,256]{1,0:T(8,128)(2,1)S(1)}, bf16[576,256]{1,0:T(8,128)(2,1)S(1)}, u32[]{:S(2)}, u32[]{:S(2)}) %collective-permute-start.8) | collective-permute-done | bytes 294944 | tf_op jit(solution)/shard_map/ppermute | solution.py:24
  29.5 0.1 shard_map.108
  29.6 1.6 %collective-permute-start.12 = (bf16[512,256]{1,0:T(8,128)(2,1)S(1)}, bf16[512,256]{1,0:T(8,128)(2,1)S(1)}, u32[]{:S(2)}, u32[]{:S(2)}) collective-permute-start(bf16[512,256]{1,0:T(8,128)(2,1)S(1)} %get-tuple-element.92), channel_id=1, source_target_pairs={{0,2},{1,3},{2,0},{3,1},{4,6},{5,7},{6,4},{7,5},{8,10},{9,11},{10,... | collective-permute-start | bytes 786440 | tf_op jit(solution)/shard_map/ppermute | solution.py:24
  31.2 1.7 %shard_map.109 = (bf16[384,384]{1,0:T(8,128)(2,1)S(1)}, f32[64,1408]{1,0:T(8,128)S(1)}) custom-call(bf16[384,1408]{1,0:T(8,128)(2,1)S(1)} %get-tuple-element.95.tok, bf16[384,1408]{1,0:T(8,128)(2,1)S(1)} %get-tuple-element.86.cot, bf16[1408,1536]{1,0:T(8,128)(2,1)S(1)} %get-tuple-element.82.w_up, bf16[1536,1408]{1,0:T(8,128)(2,1)S(1)} %get-tuple-element.74.w_down, ...), custom_call_target="tpu_custom_call" | custom-call | flops 1 | bytes 1 | tf_op jit(solution)/shard_map/pallas_call | solution.py:530
  32.9 1.7 %shard_map.110 = (bf16[384,384]{1,0:T(8,128)(2,1)S(1)}, bf16[64,1408]{1,0:T(8,128)(2,1)S(1)}) custom-call(bf16[384,1408]{1,0:T(8,128)(2,1)S(1)} %get-tuple-element.95.tok, bf16[384,1408]{1,0:T(8,128)(2,1)S(1)} %get-tuple-element.86.cot, bf16[1408,1536]{1,0:T(8,128)(2,1)S(1)} %get-tuple-element.82.w_up, bf16[1536,1408]{1,0:T(8,128)(2,1)S(1)} %get-tuple-element.74.w_down, ...), custom_call_target="tpu_custom_call" | custom-call | flops 1 | bytes 1 | tf_op jit(solution)/shard_map/pallas_call | solution.py:530
  34.6 0.6 collective-permute-start.11
  35.2 1.5 %collective-permute-start.15 = (bf16[384,384]{1,0:T(8,128)(2,1)S(1)}, bf16[384,384]{1,0:T(8,128)(2,1)S(1)}, u32[]{:S(2)}, u32[]{:S(2)}) collective-permute-start(bf16[384,384]{1,0:T(8,128)(2,1)S(1)} %get-tuple-element.105.pre), channel_id=1, source_target_pairs={{0,4},{4,0},{8,12},{12,8},{16,20},{20,16},{24,28},{28,24},{1,5},{5... | collective-permute-start | bytes 884744 | tf_op jit(solution)/shard_map/ppermute | solution.py:24
  36.8 0.6 collective-permute-start.14
  37.4 0.0 copy-start.1
  37.4 1.9 %shard_map.113 = (bf16[704,768]{1,0:T(8,128)(2,1)S(1)}, f32[352,384]{1,0:T(8,128)S(1)}, bf16[352,384]{1,0:T(8,128)(2,1)S(1)}) custom-call(bf16[1408,384]{1,0:T(8,128)(2,1)S(1)} %get-tuple-element.99.tok_full, bf16[176,640]{1,0:T(8,128)(2,1)S(1)} %get-tuple-element.103.h0, bf16[176,640]{1,0:T(8,128)(2,1)S(1)} %collective-permute-done.4.h1, ...), custom_call_target="tpu_custom_call" | custom-call | flops 1 | bytes 1 | tf_op jit(solution)/shard_map/pallas_call | solution.py:530
  39.3 1.6 %collective-permute-start.16 = (bf16[352,384]{1,0:T(8,128)(2,1)S(1)}, bf16[352,384]{1,0:T(8,128)(2,1)S(1)}, u32[]{:S(2)}, u32[]{:S(2)}) collective-permute-start(bf16[352,384]{1,0:T(8,128)(2,1)S(1)} %get-tuple-element.102), channel_id=1, source_target_pairs={{0,8},{4,12},{8,0},{12,4},{16,24},{20,28},{24,16},{28,20},{1,9},{5... | collective-permute-start | bytes 811016 | tf_op jit(solution)/shard_map/ppermute | solution.py:24
  40.9 1.4 %collective-permute-start.17 = (bf16[384,384]{1,0:T(8,128)(2,1)S(1)}, bf16[384,384]{1,0:T(8,128)(2,1)S(1)}, u32[]{:S(2)}, u32[]{:S(2)}) collective-permute-start(bf16[384,384]{1,0:T(8,128)(2,1)S(1)} %get-tuple-element.112.pre), channel_id=1, source_target_pairs={{0,4},{4,0},{8,12},{12,8},{16,20},{20,16},{24,28},{28,24},{1,5},{5... | collective-permute-start | bytes 884744 | tf_op jit(solution)/shard_map/ppermute | solution.py:24
  42.3 0.9 %collective-permute-done.14.b = bf16[64,1408]{1,0:T(8,128)(2,1)S(1)} collective-permute-done((bf16[64,1408]{1,0:T(8,128)(2,1)S(1)}, bf16[64,1408]{1,0:T(8,128)(2,1)S(1)}, u32[]{:S(2)}, u32[]{:S(2)}) %collective-permute-start.14) | collective-permute-done | bytes 180256 | tf_op jit(solution)/shard_map/ppermute | solution.py:24
  43.2 0.5 shard_map.114.e0
  43.7 1.4 %collective-permute-done.15.pre_pair = bf16[384,384]{1,0:T(8,128)(2,1)S(1)} collective-permute-done((bf16[384,384]{1,0:T(8,128)(2,1)S(1)}, bf16[384,384]{1,0:T(8,128)(2,1)S(1)}, u32[]{:S(2)}, u32[]{:S(2)}) %collective-permute-start.15) | collective-permute-done | bytes 294944 | tf_op jit(solution)/shard_map/ppermute | solution.py:24
  45.1 0.8 shard_map.115
  45.9 1.6 %collective-permute-start.18 = (bf16[352,384]{1,0:T(8,128)(2,1)S(1)}, bf16[352,384]{1,0:T(8,128)(2,1)S(1)}, u32[]{:S(2)}, u32[]{:S(2)}) collective-permute-start(bf16[352,384]{1,0:T(8,128)(2,1)S(1)} %get-tuple-element.108), channel_id=1, source_target_pairs={{0,8},{4,12},{8,0},{12,4},{16,24},{20,28},{24,16},{28,20},{1,9},{5... | collective-permute-start | bytes 811016 | tf_op jit(solution)/shard_map/ppermute | solution.py:24
  47.5 0.5 collective-permute-start.20
  48.1 1.5 %collective-permute-start.22 = (bf16[384,384]{1,0:T(8,128)(2,1)S(1)}, bf16[384,384]{1,0:T(8,128)(2,1)S(1)}, u32[]{:S(2)}, u32[]{:S(2)}) collective-permute-start(bf16[384,384]{1,0:T(8,128)(2,1)S(1)} %get-tuple-element.118.pre), channel_id=1, source_target_pairs={{0,4},{4,0},{8,12},{12,8},{16,20},{20,16},{24,28},{28,24},{1,5},{5... | collective-permute-start | bytes 884744 | tf_op jit(solution)/shard_map/ppermute | solution.py:24
  49.6 0.1 shard_map.116
  49.6 1.8 %collective-permute-done.17.pre_pair = bf16[384,384]{1,0:T(8,128)(2,1)S(1)} collective-permute-done((bf16[384,384]{1,0:T(8,128)(2,1)S(1)}, bf16[384,384]{1,0:T(8,128)(2,1)S(1)}, u32[]{:S(2)}, u32[]{:S(2)}) %collective-permute-start.17) | collective-permute-done | bytes 294944 | tf_op jit(solution)/shard_map/ppermute | solution.py:24
  51.4 0.8 shard_map.117
  52.2 1.6 %collective-permute-start.23 = (bf16[352,384]{1,0:T(8,128)(2,1)S(1)}, bf16[352,384]{1,0:T(8,128)(2,1)S(1)}, u32[]{:S(2)}, u32[]{:S(2)}) collective-permute-start(bf16[352,384]{1,0:T(8,128)(2,1)S(1)} %get-tuple-element.113), channel_id=1, source_target_pairs={{0,8},{4,12},{8,0},{12,4},{16,24},{20,28},{24,16},{28,20},{1,9},{5... | collective-permute-start | bytes 811016 | tf_op jit(solution)/shard_map/ppermute | solution.py:24
  53.9 0.5 collective-permute-start.24
  54.4 2.6 %collective-permute-start.28 = (bf16[176,384]{1,0:T(8,128)(2,1)S(1)}, bf16[176,384]{1,0:T(8,128)(2,1)S(1)}, u32[]{:S(2)}, u32[]{:S(2)}) collective-permute-start(bf16[176,384]{1,0:T(8,128)(2,1)S(1)} %get-tuple-element.110), channel_id=1, source_target_pairs={{0,16},{4,20},{8,24},{12,28},{16,0},{20,4},{24,8},{28,12},{1,17},{... | collective-permute-start | bytes 405512 | tf_op jit(solution)/shard_map/ppermute | solution.py:24
  57.0 0.1 shard_map.118
  57.0 0.2 shard_map.119.share
  57.3 0.0 copy-start.5
  57.3 0.6 collective-permute-start.29
  57.9 0.8 shard_map.120
  58.7 0.6 collective-permute-start.27
  59.3 1.3 %collective-permute-done.23.received = bf16[352,384]{1,0:T(8,128)(2,1)S(1)} collective-permute-done((bf16[352,384]{1,0:T(8,128)(2,1)S(1)}, bf16[352,384]{1,0:T(8,128)(2,1)S(1)}, u32[]{:S(2)}, u32[]{:S(2)}) %collective-permute-start.23) | collective-permute-done | bytes 270368 | tf_op jit(solution)/shard_map/ppermute | solution.py:24
  60.6 0.1 shard_map.121
  60.6 0.8 shard_map.122.a
  61.4 0.0 collective-permute-start.25
  61.4 3.6 %collective-permute-done.28 = bf16[176,384]{1,0:T(8,128)(2,1)S(1)} collective-permute-done((bf16[176,384]{1,0:T(8,128)(2,1)S(1)}, bf16[176,384]{1,0:T(8,128)(2,1)S(1)}, u32[]{:S(2)}, u32[]{:S(2)}) %collective-permute-start.28) | collective-permute-done | bytes 135200 | tf_op jit(solution)/shard_map/ppermute | solution.py:24
  65.1 0.4 collective-permute-start.30
  65.5 2.6 %collective-permute-start.26 = (f32[1,384]{1,0:T(1,128)S(1)}, f32[1,384]{1,0:T(1,128)S(1)}, u32[]{:S(2)}, u32[]{:S(2)}) collective-permute-start(f32[1,384]{1,0:T(1,128)S(1)} %shard_map.123.a), channel_id=1, source_target_pairs={{0,2},{1,3},{2,0},{3,1},{4,6},{5,7},{6,4},{7,5},{8,10},{9,11},{10,... | collective-permute-start | bytes 4616 | tf_op jit(solution)/shard_map/ppermute | solution.py:24
  68.1 2.3 %collective-permute-done.29 = bf16[176,384]{1,0:T(8,128)(2,1)S(1)} collective-permute-done((bf16[176,384]{1,0:T(8,128)(2,1)S(1)}, bf16[176,384]{1,0:T(8,128)(2,1)S(1)}, u32[]{:S(2)}, u32[]{:S(2)}) %collective-permute-start.29) | collective-permute-done | bytes 135200 | tf_op jit(solution)/shard_map/ppermute | solution.py:24
  70.4 0.7 shard_map.124
  71.1 1.7 %collective-permute-done.27.received = bf16[352,384]{1,0:T(8,128)(2,1)S(1)} collective-permute-done((bf16[352,384]{1,0:T(8,128)(2,1)S(1)}, bf16[352,384]{1,0:T(8,128)(2,1)S(1)}, u32[]{:S(2)}, u32[]{:S(2)}) %collective-permute-start.27) | collective-permute-done | bytes 270368 | tf_op jit(solution)/shard_map/ppermute | solution.py:24
  72.8 0.1 shard_map.125
  72.9 1.9 %collective-permute-start.31 = (bf16[176,384]{1,0:T(8,128)(2,1)S(1)}, bf16[176,384]{1,0:T(8,128)(2,1)S(1)}, u32[]{:S(2)}, u32[]{:S(2)}) collective-permute-start(bf16[176,384]{1,0:T(8,128)(2,1)S(1)} %get-tuple-element.138), channel_id=1, source_target_pairs={{0,16},{4,20},{8,24},{12,28},{16,0},{20,4},{24,8},{28,12},{1,17},{... | collective-permute-start | bytes 405512 | tf_op jit(solution)/shard_map/ppermute | solution.py:24
  74.8 6.5 %collective-permute-done.31 = bf16[176,384]{1,0:T(8,128)(2,1)S(1)} collective-permute-done((bf16[176,384]{1,0:T(8,128)(2,1)S(1)}, bf16[176,384]{1,0:T(8,128)(2,1)S(1)}, u32[]{:S(2)}, u32[]{:S(2)}) %collective-permute-start.31) | collective-permute-done | bytes 135200 | tf_op jit(solution)/shard_map/ppermute | solution.py:24
  81.4 1.1 %pad_maximum_fusion = f32[176,1536]{1,0:T(8,128)} fusion(f32[176,384]{1,0:T(8,128)S(1)} %convert_add_fusion, f32[176,384]{1,0:T(8,128)S(1)} %convert_add_fusion.1, f32[176,384]{1,0:T(8,128)S(1)} %convert_add_fusion.2, f32[176,384]{1,0:T(8,128)S(1)} %convert_add_fusion.3), kind=kLoop, calls=%fused_computation | loop fusion | flops 811008 | bytes 2162688 | tf_op jit(solution)/shard_map/concatenate | solution.py:764
  (40 shorter events, 0.3 us)
Async XLA Ops:
  4.0 15.5 %collective-permute-start.6 = (bf16[704,384]{1,0:T(8,128)(2,1)}, bf16[704,384]{1,0:T(8,128)(2,1)S(1)}, u32[]{:S(2)}, u32[]{:S(2)}) collective-permute-start(bf16[704,384]{1,0:T(8,128)(2,1)} %get-tuple-element.80.b0), channel_id=1, source_target_pairs={{0,2},{1,3},{2,0},{3,1},{4,6},{5,7},{6,4},{7,5},{8,10},{9,11},{10,... | collective-permute-start | bytes 1622024 | tf_op jit(solution)/shard_map/ppermute | solution.py:24
  7.0 11.9 %collective-permute-start = (bf16[176,384]{1,0:T(8,128)(2,1)}, bf16[176,384]{1,0:T(8,128)(2,1)S(1)}, u32[]{:S(2)}, u32[]{:S(2)}) collective-permute-start(bf16[176,384]{1,0:T(8,128)(2,1)} %get-tuple-element.71), channel_id=1, source_target_pairs={{0,4},{4,0},{8,12},{12,8},{16,20},{20,16},{24,28},{28,24},{1,5},{5... | collective-permute-start | bytes 405512 | tf_op jit(solution)/shard_map/ppermute | solution.py:24
  8.5 10.5 %collective-permute-start.1 = (bf16[144,256]{1,0:T(8,128)(2,1)}, bf16[144,256]{1,0:T(8,128)(2,1)S(1)}, u32[]{:S(2)}, u32[]{:S(2)}) collective-permute-start(bf16[144,256]{1,0:T(8,128)(2,1)} %get-tuple-element.72.t0), channel_id=1, source_target_pairs={{0,8},{4,12},{8,16},{12,20},{16,24},{20,28},{24,0},{28,4},{1,9},{5... | collective-permute-start | bytes 221192 | tf_op jit(solution)/shard_map/ppermute | solution.py:29
  10.1 9.0 %collective-permute-start.2 = (bf16[144,256]{1,0:T(8,128)(2,1)}, bf16[144,256]{1,0:T(8,128)(2,1)S(1)}, u32[]{:S(2)}, u32[]{:S(2)}) collective-permute-start(bf16[144,256]{1,0:T(8,128)(2,1)} %get-tuple-element.72.t0), channel_id=1, source_target_pairs={{0,16},{4,20},{8,24},{12,28},{16,0},{20,4},{24,8},{28,12},{1,17},{... | collective-permute-start | bytes 221192 | tf_op jit(solution)/shard_map/ppermute | solution.py:29
  12.7 6.4 %collective-permute-start.3 = (bf16[144,256]{1,0:T(8,128)(2,1)}, bf16[144,256]{1,0:T(8,128)(2,1)S(1)}, u32[]{:S(2)}, u32[]{:S(2)}) collective-permute-start(bf16[144,256]{1,0:T(8,128)(2,1)} %get-tuple-element.72.t0), channel_id=1, source_target_pairs={{0,24},{4,28},{8,0},{12,4},{16,8},{20,12},{24,16},{28,20},{1,25},{... | collective-permute-start | bytes 221192 | tf_op jit(solution)/shard_map/ppermute | solution.py:29
  14.0 2.2 %copy-start = (bf16[1408,1536]{1,0:T(8,128)(2,1)S(1)}, bf16[1408,1536]{1,0:T(8,128)(2,1)}, u32[]{:S(2)}) copy-start(bf16[1408,1536]{1,0:T(8,128)(2,1)} %up) | copy-start | bytes 12976132
  16.2 2.7 %copy-start.2 = (bf16[704,384]{1,0:T(8,128)(2,1)S(1)}, bf16[704,384]{1,0:T(8,128)(2,1)}, u32[]{:S(2)}) copy-start(bf16[704,384]{1,0:T(8,128)(2,1)} %get-tuple-element.80.b0) | copy-start | bytes 1622020
  16.2 2.8 %copy-start.3 = (bf16[352,128]{1,0:T(8,128)(2,1)S(1)}, bf16[352,128]{1,0:T(8,128)(2,1)}, u32[]{:S(2)}) copy-start(bf16[352,128]{1,0:T(8,128)(2,1)} %get-tuple-element.76.pool) | copy-start | bytes 270340
  16.2 2.8 %copy-start.4 = (bf16[144,256]{1,0:T(8,128)(2,1)S(1)}, bf16[144,256]{1,0:T(8,128)(2,1)}, u32[]{:S(2)}) copy-start(bf16[144,256]{1,0:T(8,128)(2,1)} %get-tuple-element.72.t0) | copy-start | bytes 221188
  19.0 4.0 %collective-permute-start.5 = (bf16[704,384]{1,0:T(8,128)(2,1)S(1)}, bf16[704,384]{1,0:T(8,128)(2,1)S(1)}, u32[]{:S(2)}, u32[]{:S(2)}) collective-permute-start(bf16[704,384]{1,0:T(8,128)(2,1)S(1)} %copy-done.2), channel_id=1, source_target_pairs={{0,1},{1,0},{2,3},{3,2},{4,5},{5,4},{6,7},{7,6},{8,9},{9,8},{10,11... | collective-permute-start | bytes 1622024 | tf_op jit(solution)/shard_map/ppermute | solution.py:24
  19.5 3.5 %collective-permute-start.7 = (bf16[704,384]{1,0:T(8,128)(2,1)S(1)}, bf16[704,384]{1,0:T(8,128)(2,1)S(1)}, u32[]{:S(2)}, u32[]{:S(2)}) collective-permute-start(bf16[704,384]{1,0:T(8,128)(2,1)S(1)} %collective-permute-done.6.b2), channel_id=1, source_target_pairs={{0,1},{1,0},{2,3},{3,2},{4,5},{5,4},{6,7},{7,6},{8,9},{9,8},{10,11... | collective-permute-start | bytes 1622024 | tf_op jit(solution)/shard_map/ppermute | solution.py:24
  19.7 9.8 %collective-permute-start.8 = (bf16[576,256]{1,0:T(8,128)(2,1)S(1)}, bf16[576,256]{1,0:T(8,128)(2,1)S(1)}, u32[]{:S(2)}, u32[]{:S(2)}) collective-permute-start(bf16[576,256]{1,0:T(8,128)(2,1)S(1)} %get-tuple-element.90.mine), channel_id=1, source_target_pairs={{0,4},{4,0},{8,12},{12,8},{16,20},{20,16},{24,28},{28,24},{1,5},{5... | collective-permute-start | bytes 884744 | tf_op jit(solution)/shard_map/ppermute | solution.py:24
  21.2 1.7 %collective-permute-start.4 = (bf16[176,640]{1,0:T(8,128)(2,1)S(1)}, bf16[176,640]{1,0:T(8,128)(2,1)S(1)}, u32[]{:S(2)}, u32[]{:S(2)}) collective-permute-start(bf16[176,640]{1,0:T(8,128)(2,1)S(1)} %get-tuple-element.103.h0), channel_id=1, source_target_pairs={{0,1},{1,0},{2,3},{3,2},{4,5},{5,4},{6,7},{7,6},{8,9},{9,8},{10,11... | collective-permute-start | bytes 675848 | tf_op jit(solution)/shard_map/ppermute | solution.py:24
  21.5 9.7 %collective-permute-start.9 = (bf16[176,640]{1,0:T(8,128)(2,1)S(1)}, bf16[176,640]{1,0:T(8,128)(2,1)S(1)}, u32[]{:S(2)}, u32[]{:S(2)}) collective-permute-start(bf16[176,640]{1,0:T(8,128)(2,1)S(1)} %get-tuple-element.103.h0), channel_id=1, source_target_pairs={{0,2},{1,3},{2,0},{3,1},{4,6},{5,7},{6,4},{7,5},{8,10},{9,11},{10,... | collective-permute-start | bytes 675848 | tf_op jit(solution)/shard_map/ppermute | solution.py:24
  25.1 12.3 %collective-permute-start.13 = (bf16[400,384]{1,0:T(8,128)(2,1)S(1)}, bf16[400,384]{1,0:T(8,128)(2,1)S(1)}, u32[]{:S(2)}, u32[]{:S(2)}) collective-permute-start(bf16[400,384]{1,0:T(8,128)(2,1)S(1)} %get-tuple-element.100.pre), channel_id=1, source_target_pairs={{0,4},{4,0},{8,12},{12,8},{16,20},{20,16},{24,28},{28,24},{1,5},{5... | collective-permute-start | bytes 921608 | tf_op jit(solution)/shard_map/ppermute | solution.py:24
  29.6 7.8 %collective-permute-start.12 = (bf16[512,256]{1,0:T(8,128)(2,1)S(1)}, bf16[512,256]{1,0:T(8,128)(2,1)S(1)}, u32[]{:S(2)}, u32[]{:S(2)}) collective-permute-start(bf16[512,256]{1,0:T(8,128)(2,1)S(1)} %get-tuple-element.92), channel_id=1, source_target_pairs={{0,2},{1,3},{2,0},{3,1},{4,6},{5,7},{6,4},{7,5},{8,10},{9,11},{10,... | collective-permute-start | bytes 786440 | tf_op jit(solution)/shard_map/ppermute | solution.py:24
  31.2 5.5 %collective-permute-start.10 = (bf16[176,640]{1,0:T(8,128)(2,1)S(1)}, bf16[176,640]{1,0:T(8,128)(2,1)S(1)}, u32[]{:S(2)}, u32[]{:S(2)}) collective-permute-start(bf16[176,640]{1,0:T(8,128)(2,1)S(1)} %collective-permute-done.9.h2), channel_id=1, source_target_pairs={{0,1},{1,0},{2,3},{3,2},{4,5},{5,4},{6,7},{7,6},{8,9},{9,8},{10,11... | collective-permute-start | bytes 675848 | tf_op jit(solution)/shard_map/ppermute | solution.py:24
  34.6 2.1 %collective-permute-start.11 = (bf16[64,1408]{1,0:T(8,128)(2,1)S(1)}, bf16[64,1408]{1,0:T(8,128)(2,1)S(1)}, u32[]{:S(2)}, u32[]{:S(2)}) collective-permute-start(bf16[64,1408]{1,0:T(8,128)(2,1)S(1)} %get-tuple-element.97.a), channel_id=1, source_target_pairs={{0,1},{1,0},{2,3},{3,2},{4,5},{5,4},{6,7},{7,6},{8,9},{9,8},{10,11... | collective-permute-start | bytes 540680 | tf_op jit(solution)/shard_map/ppermute | solution.py:24
  35.2 9.9 %collective-permute-start.15 = (bf16[384,384]{1,0:T(8,128)(2,1)S(1)}, bf16[384,384]{1,0:T(8,128)(2,1)S(1)}, u32[]{:S(2)}, u32[]{:S(2)}) collective-permute-start(bf16[384,384]{1,0:T(8,128)(2,1)S(1)} %get-tuple-element.105.pre), channel_id=1, source_target_pairs={{0,4},{4,0},{8,12},{12,8},{16,20},{20,16},{24,28},{28,24},{1,5},{5... | collective-permute-start | bytes 884744 | tf_op jit(solution)/shard_map/ppermute | solution.py:24
  36.8 6.4 %collective-permute-start.14 = (bf16[64,1408]{1,0:T(8,128)(2,1)S(1)}, bf16[64,1408]{1,0:T(8,128)(2,1)S(1)}, u32[]{:S(2)}, u32[]{:S(2)}) collective-permute-start(bf16[64,1408]{1,0:T(8,128)(2,1)S(1)} %shard_map.111.a), channel_id=1, source_target_pairs={{0,2},{1,3},{2,0},{3,1},{4,6},{5,7},{6,4},{7,5},{8,10},{9,11},{10,... | collective-permute-start | bytes 540680 | tf_op jit(solution)/shard_map/ppermute | solution.py:24
  37.4 5.8 %copy-start.1 = (bf16[1408,256]{1,0:T(8,128)(2,1)S(1)}, bf16[1408,256]{1,0:T(8,128)(2,1)}, u32[]{:S(2)}) copy-start(bf16[1408,256]{1,0:T(8,128)(2,1)} %ref_proj.1) | copy-start | bytes 2162692
  39.3 8.8 %collective-permute-start.16 = (bf16[352,384]{1,0:T(8,128)(2,1)S(1)}, bf16[352,384]{1,0:T(8,128)(2,1)S(1)}, u32[]{:S(2)}, u32[]{:S(2)}) collective-permute-start(bf16[352,384]{1,0:T(8,128)(2,1)S(1)} %get-tuple-element.102), channel_id=1, source_target_pairs={{0,8},{4,12},{8,0},{12,4},{16,24},{20,28},{24,16},{28,20},{1,9},{5... | collective-permute-start | bytes 811016 | tf_op jit(solution)/shard_map/ppermute | solution.py:24
  40.9 10.5 %collective-permute-start.17 = (bf16[384,384]{1,0:T(8,128)(2,1)S(1)}, bf16[384,384]{1,0:T(8,128)(2,1)S(1)}, u32[]{:S(2)}, u32[]{:S(2)}) collective-permute-start(bf16[384,384]{1,0:T(8,128)(2,1)S(1)} %get-tuple-element.112.pre), channel_id=1, source_target_pairs={{0,4},{4,0},{8,12},{12,8},{16,20},{20,16},{24,28},{28,24},{1,5},{5... | collective-permute-start | bytes 884744 | tf_op jit(solution)/shard_map/ppermute | solution.py:24
  42.3 11.6 %collective-permute-start.19 = (bf16[512,256]{1,0:T(8,128)(2,1)S(1)}, bf16[512,256]{1,0:T(8,128)(2,1)S(1)}, u32[]{:S(2)}, u32[]{:S(2)}) collective-permute-start(bf16[512,256]{1,0:T(8,128)(2,1)S(1)} %shard_map.112), channel_id=1, source_target_pairs={{0,1},{1,0},{2,3},{3,2},{4,5},{5,4},{6,7},{7,6},{8,9},{9,8},{10,11... | collective-permute-start | bytes 786440 | tf_op jit(solution)/shard_map/ppermute | solution.py:24
  45.9 8.5 %collective-permute-start.18 = (bf16[352,384]{1,0:T(8,128)(2,1)S(1)}, bf16[352,384]{1,0:T(8,128)(2,1)S(1)}, u32[]{:S(2)}, u32[]{:S(2)}) collective-permute-start(bf16[352,384]{1,0:T(8,128)(2,1)S(1)} %get-tuple-element.108), channel_id=1, source_target_pairs={{0,8},{4,12},{8,0},{12,4},{16,24},{20,28},{24,16},{28,20},{1,9},{5... | collective-permute-start | bytes 811016 | tf_op jit(solution)/shard_map/ppermute | solution.py:24
  47.5 6.3 %collective-permute-start.20 = (f32[192,256]{1,0:T(8,128)S(1)}, f32[192,256]{1,0:T(8,128)S(1)}, u32[]{:S(2)}, u32[]{:S(2)}) collective-permute-start(f32[192,256]{1,0:T(8,128)S(1)} %shard_map.114.e0), channel_id=1, source_target_pairs={{0,2},{1,3},{2,0},{3,1},{4,6},{5,7},{6,4},{7,5},{8,10},{9,11},{10,... | collective-permute-start | bytes 589832 | tf_op jit(solution)/shard_map/ppermute | solution.py:24
  48.1 9.8 %collective-permute-start.22 = (bf16[384,384]{1,0:T(8,128)(2,1)S(1)}, bf16[384,384]{1,0:T(8,128)(2,1)S(1)}, u32[]{:S(2)}, u32[]{:S(2)}) collective-permute-start(bf16[384,384]{1,0:T(8,128)(2,1)S(1)} %get-tuple-element.118.pre), channel_id=1, source_target_pairs={{0,4},{4,0},{8,12},{12,8},{16,20},{20,16},{24,28},{28,24},{1,5},{5... | collective-permute-start | bytes 884744 | tf_op jit(solution)/shard_map/ppermute | solution.py:24
  52.2 8.3 %collective-permute-start.23 = (bf16[352,384]{1,0:T(8,128)(2,1)S(1)}, bf16[352,384]{1,0:T(8,128)(2,1)S(1)}, u32[]{:S(2)}, u32[]{:S(2)}) collective-permute-start(bf16[352,384]{1,0:T(8,128)(2,1)S(1)} %get-tuple-element.113), channel_id=1, source_target_pairs={{0,8},{4,12},{8,0},{12,4},{16,24},{20,28},{24,16},{28,20},{1,9},{5... | collective-permute-start | bytes 811016 | tf_op jit(solution)/shard_map/ppermute | solution.py:24
  53.9 3.4 %collective-permute-start.21 = (f32[192,256]{1,0:T(8,128)S(1)}, f32[192,256]{1,0:T(8,128)S(1)}, u32[]{:S(2)}, u32[]{:S(2)}) collective-permute-start(f32[192,256]{1,0:T(8,128)S(1)} %collective-permute-done.20.e2), channel_id=1, source_target_pairs={{0,1},{1,0},{2,3},{3,2},{4,5},{5,4},{6,7},{7,6},{8,9},{9,8},{10,11... | collective-permute-start | bytes 589832 | tf_op jit(solution)/shard_map/ppermute | solution.py:24
  53.9 6.8 %collective-permute-start.24 = (f32[192,256]{1,0:T(8,128)S(1)}, f32[192,256]{1,0:T(8,128)S(1)}, u32[]{:S(2)}, u32[]{:S(2)}) collective-permute-start(f32[192,256]{1,0:T(8,128)S(1)} %shard_map.114.e0), channel_id=1, source_target_pairs={{0,1},{1,0},{2,3},{3,2},{4,5},{5,4},{6,7},{7,6},{8,9},{9,8},{10,11... | collective-permute-start | bytes 589832 | tf_op jit(solution)/shard_map/ppermute | solution.py:24
  54.4 10.7 %collective-permute-start.28 = (bf16[176,384]{1,0:T(8,128)(2,1)S(1)}, bf16[176,384]{1,0:T(8,128)(2,1)S(1)}, u32[]{:S(2)}, u32[]{:S(2)}) collective-permute-start(bf16[176,384]{1,0:T(8,128)(2,1)S(1)} %get-tuple-element.110), channel_id=1, source_target_pairs={{0,16},{4,20},{8,24},{12,28},{16,0},{20,4},{24,8},{28,12},{1,17},{... | collective-permute-start | bytes 405512 | tf_op jit(solution)/shard_map/ppermute | solution.py:24
  57.3 3.4 %copy-start.5 = (s32[64]{0:T(128)S(1)}, s32[64]{0:T(128)}, u32[]{:S(2)}) copy-start(s32[64]{0:T(128)} %param.13) | copy-start | bytes 772
  57.3 13.1 %collective-permute-start.29 = (bf16[176,384]{1,0:T(8,128)(2,1)S(1)}, bf16[176,384]{1,0:T(8,128)(2,1)S(1)}, u32[]{:S(2)}, u32[]{:S(2)}) collective-permute-start(bf16[176,384]{1,0:T(8,128)(2,1)S(1)} %get-tuple-element.115), channel_id=1, source_target_pairs={{0,16},{4,20},{8,24},{12,28},{16,0},{20,4},{24,8},{28,12},{1,17},{... | collective-permute-start | bytes 405512 | tf_op jit(solution)/shard_map/ppermute | solution.py:24
  58.7 14.1 %collective-permute-start.27 = (bf16[352,384]{1,0:T(8,128)(2,1)S(1)}, bf16[352,384]{1,0:T(8,128)(2,1)S(1)}, u32[]{:S(2)}, u32[]{:S(2)}) collective-permute-start(bf16[352,384]{1,0:T(8,128)(2,1)S(1)} %get-tuple-element.121), channel_id=1, source_target_pairs={{0,8},{4,12},{8,0},{12,4},{16,24},{20,28},{24,16},{28,20},{1,9},{5... | collective-permute-start | bytes 811016 | tf_op jit(solution)/shard_map/ppermute | solution.py:24
  61.4 4.1 %collective-permute-start.25 = (f32[1,384]{1,0:T(1,128)S(1)}, f32[1,384]{1,0:T(1,128)S(1)}, u32[]{:S(2)}, u32[]{:S(2)}) collective-permute-start(f32[1,384]{1,0:T(1,128)S(1)} %shard_map.122.a), channel_id=1, source_target_pairs={{0,1},{1,0},{2,3},{3,2},{4,5},{5,4},{6,7},{7,6},{8,9},{9,8},{10,11... | collective-permute-start | bytes 4616 | tf_op jit(solution)/shard_map/ppermute | solution.py:24
  65.1 9.7 %collective-permute-start.30 = (bf16[176,384]{1,0:T(8,128)(2,1)S(1)}, bf16[176,384]{1,0:T(8,128)(2,1)S(1)}, u32[]{:S(2)}, u32[]{:S(2)}) collective-permute-start(bf16[176,384]{1,0:T(8,128)(2,1)S(1)} %get-tuple-element.123), channel_id=1, source_target_pairs={{0,16},{4,20},{8,24},{12,28},{16,0},{20,4},{24,8},{28,12},{1,17},{... | collective-permute-start | bytes 405512 | tf_op jit(solution)/shard_map/ppermute | solution.py:24
  65.5 4.9 %collective-permute-start.26 = (f32[1,384]{1,0:T(1,128)S(1)}, f32[1,384]{1,0:T(1,128)S(1)}, u32[]{:S(2)}, u32[]{:S(2)}) collective-permute-start(f32[1,384]{1,0:T(1,128)S(1)} %shard_map.123.a), channel_id=1, source_target_pairs={{0,2},{1,3},{2,0},{3,1},{4,6},{5,7},{6,4},{7,5},{8,10},{9,11},{10,... | collective-permute-start | bytes 4616 | tf_op jit(solution)/shard_map/ppermute | solution.py:24
  72.9 8.4 %collective-permute-start.31 = (bf16[176,384]{1,0:T(8,128)(2,1)S(1)}, bf16[176,384]{1,0:T(8,128)(2,1)S(1)}, u32[]{:S(2)}, u32[]{:S(2)}) collective-permute-start(bf16[176,384]{1,0:T(8,128)(2,1)S(1)} %get-tuple-element.138), channel_id=1, source_target_pairs={{0,16},{4,20},{8,24},{12,28},{16,0},{20,4},{24,8},{28,12},{1,17},{... | collective-permute-start | bytes 405512 | tf_op jit(solution)/shard_map/ppermute | solution.py:24
